TPU v7x, 32 devices: a whole 2x2x4 slice. The times are simulated.
32 devices in a mesh: gx: 8 (over z, core), gy: 4 (over y, x).
Axes of the slice: x: 2, y: 2, z: 4, core: 2. Of those that a mesh axis runs over, the one named last changes fastest.
Arguments:
- temp_fluid: float32 [128, 256, 1024], P('gx', 'gy'), may hold values from -6 to 6
- velocity: bfloat16 [3, 128, 256, 1024], P(None, 'gx', 'gy'), may hold values from -1 to 1
- wall_old: float32 [128, 256, 128], P('gx', 'gy'), may hold values from -6 to 6
- wall_mask: int32 [128, 256, 128], P('gx', 'gy'), may hold values 0 or 1
- owner_map: int32 [32, 1024, 1], P(('gx', 'gy')), may hold values from 0 to 31; in each aligned block of 1024 rows (0 to 1023, 1024 to 2047, ..., all dimensions but the last counted through in order) at most 96 rows name the same one
- slot_map: int32 [32, 1024], P(('gx', 'gy')), may hold values from 0 to 511
- temp_solid: float32 [128, 128, 128], P('gx', 'gy'), may hold values from -6 to 6
- material: int32 [128, 128, 128], P('gx', 'gy'), may hold values from 0 to 3
Outputs:
- fluid_next: float32 [128, 256, 1024], P('gx', 'gy')
- wall_next: float32 [128, 256, 128], P('gx', 'gy')
- solid_next: float32 [128, 128, 128], P('gx', 'gy')
- stress_force: float32 [3, 128, 128, 128], P(None, 'gx', 'gy')
Inputs may be any that keep to these rules, and one draw needn't show every extreme that they name: `owner_map`: among the rows of one device, no owner is named by more than 96 rows, a bound that some block reaches.
All inputs are finite; a program needn't handle non-finite values. No bound on the sum of `wall_mask` on one device may be relied on, other than what follows from the above.
Results may differ from a plain program's by a relative error of at most 0.0003.
Values sent between devices are 32-bit elements; how exact they have to be, the bound alone decides.
No kernel may reach another device: no remote copies, remote signals or barrier semaphores. Data moves between devices by JAX's collectives and lax.ppermute only.
A program may use at most 128 MiB of HBM per device.

v0:
```python
import jax
import jax.numpy as jnp
from jax import lax
from jax.sharding import PartitionSpec as P

FSTEPS = 2
SSTEPS = 4
NMAT = 4


time_step = 0.1
diffusivity = 0.5
film_coef = 2.0
solid_step = 0.05
source_gain = 4.0
conduct_table = (0.4, 0.9, 1.5, 2.2)
modulus_table = (0.5, 1.0, 1.6, 2.4)


def extended(value, sides, width):
    for axis, dim in sides:
        size, length = (lax.axis_size(axis), value.shape[dim])
        up = [(i, (i + 1) % size) for i in range(size - 1)]
        down = [(j, i) for i, j in up]
        last = lax.slice_in_dim(value, length - width, length, axis=dim)
        first = lax.slice_in_dim(value, 0, width, axis=dim)
        before = lax.ppermute(last, axis, up)
        after = lax.ppermute(first, axis, down)
        value = jnp.concatenate([before, value, after], axis=dim)
    return value


def laplace(padded):
    center = padded[1:-1, 1:-1, 1:-1]
    beside = padded[2:, 1:-1, 1:-1] + padded[:-2, 1:-1, 1:-1]
    beside = beside + padded[1:-1, 2:, 1:-1] + padded[1:-1, :-2, 1:-1]
    beside = beside + padded[1:-1, 1:-1, 2:] + padded[1:-1, 1:-1, :-2]
    return beside - 6.0 * center


def advect(padded, velocity):
    center = padded[1:-1, 1:-1, 1:-1]
    uppers = (padded[2:, 1:-1, 1:-1], padded[1:-1, 2:, 1:-1], padded[1:-1, 1:-1, 2:])
    lowers = (padded[:-2, 1:-1, 1:-1], padded[1:-1, :-2, 1:-1], padded[1:-1, 1:-1, :-2])
    total = jnp.zeros_like(center)
    for comp in range(3):
        speed = velocity[comp].astype(jnp.float32)
        total = (
            total
            + jnp.maximum(speed, 0.0) * (center - lowers[comp])
            + jnp.minimum(speed, 0.0) * (uppers[comp] - center)
        )
    return total


def fluid_update(padded, velocity, sink):
    center = padded[1:-1, 1:-1, 1:-1]
    return (
        center
        + time_step * (diffusivity * laplace(padded) - advect(padded, velocity))
        - time_step * sink
    )


def table_lookup(material, table):
    out = jnp.zeros(material.shape, jnp.float32)
    for index in range(NMAT):
        out = out + jnp.where(material == index, table[index], 0.0).astype(jnp.float32)
    return out


def solid_update(padded, cond, heat):
    center = padded[1:-1, 1:-1, 1:-1]
    return center + solid_step * (cond * laplace(padded) + source_gain * heat)


def gradient(padded):
    first = 0.5 * (padded[2:, 1:-1, 1:-1] - padded[:-2, 1:-1, 1:-1])
    second = 0.5 * (padded[1:-1, 2:, 1:-1] - padded[1:-1, :-2, 1:-1])
    third = 0.5 * (padded[1:-1, 1:-1, 2:] - padded[1:-1, 1:-1, :-2])
    return jnp.stack([first, second, third])


def pad_depth(padded):
    return jnp.pad(padded, ((0, 0), (0, 0), (1, 1)))


def fluid_faces(field):
    return pad_depth(extended(field, (("gx", 0), ("gy", 1)), 1))


def solid_faces(field):
    return pad_depth(extended(field, (("gx", 0), ("gy", 1)), 1))


def body(temp_fluid, velocity, wall_old, wall_mask, owner_map, slot_map, temp_solid, material):
    cells_x, cells_y, depth = temp_fluid.shape
    row_len = wall_old.shape[2]
    solid_x, solid_y, solid_z = temp_solid.shape
    count_x = lax.axis_size("gx")
    count_y = lax.axis_size("gy")
    ndevices = count_x * count_y
    row_count = cells_x * cells_y
    capacity = max(2, (3 * row_count + ndevices - 1) // ndevices)
    flux = wall_mask.astype(jnp.float32) * film_coef * (temp_fluid[:, :, :row_len] - wall_old)
    flux_rows = flux.reshape(row_count, row_len)
    owner = owner_map[0, :, 0]
    slot = slot_map[0]
    onehot = (owner[:, None] == jnp.arange(ndevices, dtype=jnp.int32)[None, :]).astype(jnp.int32)
    ranks = jnp.cumsum(onehot, axis=0) - 1
    position = jnp.sum(onehot * ranks, axis=1)
    outgoing = (
        jnp.zeros((ndevices, capacity, row_len), jnp.float32).at[owner, position].set(flux_rows)
    )
    out_slots = (
        jnp.zeros((ndevices, capacity), jnp.float32)
        .at[owner, position]
        .set(slot.astype(jnp.float32))
    )
    incoming, in_slots = (
        lax.all_to_all(outgoing, ("gx", "gy"), split_axis=0, concat_axis=0, tiled=True),
        lax.all_to_all(out_slots, ("gx", "gy"), split_axis=0, concat_axis=0, tiled=True),
    )
    sink = jnp.concatenate(
        [flux, jnp.zeros((cells_x, cells_y, depth - row_len), jnp.float32)], axis=2
    )
    slot_index = in_slots.astype(jnp.int32).reshape(-1)
    heat = (
        jnp.zeros((solid_x * solid_y, row_len), jnp.float32)
        .at[slot_index]
        .add(incoming.reshape(-1, row_len))
    )
    heat = heat.reshape(solid_x, solid_y, solid_z)
    cond = table_lookup(material, conduct_table)
    modulus = table_lookup(material, modulus_table)
    fluid = temp_fluid
    for step in range(FSTEPS):
        fluid = fluid_update(fluid_faces(fluid), velocity, sink)
    solid = temp_solid
    for step in range(SSTEPS):
        solid = solid_update(solid_faces(solid), cond, heat)
    stress_pad = pad_depth(extended(modulus * solid, (("gx", 0), ("gy", 1)), 1))
    stress_force = gradient(stress_pad)
    replies = solid.reshape(solid_x * solid_y, row_len)[slot_index].reshape(
        ndevices, capacity, row_len
    )
    returned = lax.all_to_all(replies, ("gx", "gy"), split_axis=0, concat_axis=0, tiled=True)
    wall_next = returned[owner, position].reshape(cells_x, cells_y, row_len)
    return (fluid, wall_next, solid, stress_force)


def solution(mesh):
    placed = (
        P("gx", "gy", None),
        P(None, "gx", "gy", None),
        P("gx", "gy", None),
        P("gx", "gy", None),
        P(("gx", "gy"), None, None),
        P(("gx", "gy"), None),
        P("gx", "gy", None),
        P("gx", "gy", None),
    )
    return jax.shard_map(
        body,
        mesh=mesh,
        in_specs=placed,
        out_specs=(
            P("gx", "gy", None),
            P("gx", "gy", None),
            P("gx", "gy", None),
            P(None, "gx", "gy", None),
        ),
        check_vma=False,
    )
```

profile of v0, /device:TPU:11, one launch (start us, length us, event | category | flops | bytes accessed | tf_op | source)
XLA Modules:
  0.0 269.3 jit_solution(18044136182510359815)
XLA Ops:
  0.6 0.7 fusion.104
  1.4 9.0 %reduce-window.6 = s32[32,8,128]{2,1,0:T(8,128)S(1)} reduce-window(s32[32,8,128]{2,1,0:T(8,128)S(1)} %fusion.104, s32[]{:T(128)} %constant.27.clone.1), window={size=1x1x128 pad=0_0x0_0x127_0}, to_apply=%region_0.0 | reduce-window | flops 4161536 | bytes 262148 | tf_op jit(solution)/shard_map/reduce-window
  10.9 0.7 fusion.101
  11.6 0.7 shift-left_or_fusion
  12.3 0.8 and_reduce_fusion
  13.0 0.7 multiply_reduce_fusion
  13.8 0.7 convert_element_type.57
  14.5 4.3 %scatter_custom_fusion.1 = f32[3072]{0:T(1024)S(1)} fusion(s32[1024]{0:T(1024)S(1)} %broadcast_select_fusion, f32[1024]{0:T(1024)S(1)} %bitcast.146, f32[]{:T(128)} %constant.22.clone.1), kind=kCustom, calls=%fused_computation.244 | custom fusion | bytes 12292
  18.8 0.7 all_to_all.12
  19.5 6.3 %all-to-all-start = ((f32[32,1,96]{2,1,0:T(1,128)}), f32[32,1,96]{2,1,0:T(1,128)S(1)}, u32[]{:S(2)}, u32[]{:S(2)}) async-start(f32[32,1,96]{2,1,0:T(1,128)} %all_to_all.12), calls=%async_computation | async-start | bytes 32768 | tf_op jit(solution)/shard_map/all_to_all | solution.py:122
  25.9 1.5 subtract_multiply_fusion
  27.3 4.3 %scatter_custom_fusion.2 = f32[3072,128]{1,0:T(8,128)} fusion(s32[1024]{0:T(1024)S(1)} %broadcast_select_fusion, f32[1024,128]{1,0:T(8,128)S(1)} %bitcast.137, f32[]{:T(128)} %constant.22.clone.1), kind=kCustom, calls=%fused_computation.92 | custom fusion | bytes 1572868
  31.6 5.9 %all-to-all-start.1 = ((f32[32,96,128]{2,1,0:T(8,128)}), f32[32,96,128]{2,1,0:T(8,128)}, u32[]{:S(2)}, u32[]{:S(2)}) async-start(f32[32,96,128]{2,1,0:T(8,128)} %bitcast.15), calls=%async_computation.1 | async-start | bytes 3145728 | tf_op jit(solution)/shard_map/all_to_all | solution.py:121
  37.5 3.3 %collective-permute-start.9 = (f32[1,32,128]{2,1,0:T(8,128)S(1)}, f32[1,32,128]{2,1,0:T(8,128)S(1)}, u32[]{:S(2)}, u32[]{:S(2)}) collective-permute-start(f32[1,32,128]{2,1,0:T(8,128)S(1)} %get-tuple-element.44), channel_id=1, source_target_pairs={{0,4},{4,8},{8,12},{12,16},{16,20},{20,24},{24,28},{1,5},{5,9},{9,... | collective-permute-start | bytes 49160 | tf_op jit(solution)/shard_map/ppermute | solution.py:27
  40.9 1.1 fusion.110
  42.0 2.1 collective-permute-start.1
  44.0 2.3 collective-permute-start
  46.3 2.2 collective-permute-start.8
  48.5 23.5 %collective-permute-done.9 = f32[1,32,128]{2,1,0:T(8,128)S(1)} collective-permute-done((f32[1,32,128]{2,1,0:T(8,128)S(1)}, f32[1,32,128]{2,1,0:T(8,128)S(1)}, u32[]{:S(2)}, u32[]{:S(2)}) %collective-permute-start.9) | collective-permute-done | bytes 16416 | tf_op jit(solution)/shard_map/ppermute | solution.py:27
  72.1 4.4 %collective-permute-done.8 = f32[1,32,128]{2,1,0:T(8,128)S(1)} collective-permute-done((f32[1,32,128]{2,1,0:T(8,128)S(1)}, f32[1,32,128]{2,1,0:T(8,128)S(1)}, u32[]{:S(2)}, u32[]{:S(2)}) %collective-permute-start.8) | collective-permute-done | bytes 16416 | tf_op jit(solution)/shard_map/ppermute | solution.py:28
  76.5 2.1 collective-permute-start.10
  78.6 4.1 %collective-permute-start.11 = (f32[18,1,128]{2,1,0:T(1,128)S(1)}, f32[18,1,128]{2,1,0:T(1,128)S(1)}, u32[]{:S(2)}, u32[]{:S(2)}) collective-permute-start(f32[18,1,128]{2,1,0:T(1,128)S(1)} %get-tuple-element.33), channel_id=1, source_target_pairs={{0,1},{1,2},{2,3},{4,5},{5,6},{6,7},{8,9},{9,10},{10,11},{12,13},{... | collective-permute-start | bytes 27656 | tf_op jit(solution)/shard_map/ppermute | solution.py:27
  82.9 0.6 collective-permute-done.11
  83.5 0.3 select_maximum_fusion.22
  83.9 2.5 constant_dynamic-update-slice_fusion.1
  86.5 2.1 copy-done.4
  88.7 1.9 collective-permute-start.2
  90.7 4.5 %collective-permute-start.3 = (f32[18,1,1024]{2,0,1:T(8,128)S(1)}, f32[18,1,1024]{2,0,1:T(8,128)S(1)}, u32[]{:S(2)}, u32[]{:S(2)}) collective-permute-start(f32[18,1,1024]{2,0,1:T(8,128)S(1)} %copy.38), channel_id=1, source_target_pairs={{0,1},{1,2},{2,3},{4,5},{5,6},{6,7},{8,9},{9,10},{10,11},{12,13},{... | collective-permute-start | bytes 221192 | tf_op jit(solution)/shard_map/ppermute | solution.py:27
  95.2 20.6 %scatter_custom_fusion = f32[512,128]{1,0:T(8,128)S(1)} fusion(s32[3072]{0:T(1024)S(1)} %bitcast.140, f32[3072,128]{1,0:T(8,128)} %bitcast.16, f32[]{:T(128)} %constant.22.clone.1), kind=kCustom, calls=%fused_computation.208 | custom fusion | flops 393216 | bytes 262656 | tf_op jit(solution)/shard_map/scatter-add | solution.py:131
  115.8 0.4 fusion.96
  116.3 2.2 collective-permute-start.12
  118.4 3.6 %collective-permute-start.13 = (f32[1,32,128]{2,1,0:T(8,128)S(1)}, f32[1,32,128]{2,1,0:T(8,128)S(1)}, u32[]{:S(2)}, u32[]{:S(2)}) collective-permute-start(f32[1,32,128]{2,1,0:T(8,128)S(1)} %get-tuple-element.41), channel_id=1, source_target_pairs={{0,4},{4,8},{8,12},{12,16},{16,20},{20,24},{24,28},{1,5},{5,9},{9,... | collective-permute-start | bytes 49160 | tf_op jit(solution)/shard_map/ppermute | solution.py:27
  122.3 0.6 collective-permute-done.13
  123.0 1.9 collective-permute-start.14
  124.9 4.5 %collective-permute-start.15 = (f32[18,1,128]{2,1,0:T(1,128)S(1)}, f32[18,1,128]{2,1,0:T(1,128)S(1)}, u32[]{:S(2)}, u32[]{:S(2)}) collective-permute-start(f32[18,1,128]{2,1,0:T(1,128)S(1)} %get-tuple-element.31), channel_id=1, source_target_pairs={{0,1},{1,2},{2,3},{4,5},{5,6},{6,7},{8,9},{9,10},{10,11},{12,13},{... | collective-permute-start | bytes 27656 | tf_op jit(solution)/shard_map/ppermute | solution.py:27
  129.5 4.7 %select_maximum_fusion.4 = f32[18,66,1026]{2,1,0:T(8,128)S(1)} fusion(f32[18,1,1024]{2,1,0:T(1,128)S(1)} %copy.37, f32[18,64,1024]{2,1,0:T(8,128)} %copy-done.4, f32[18,1,1024]{2,1,0:T(1,128)S(1)} %copy.39), kind=kLoop, calls=%fused_computation.11 | loop fusion | flops 9751104 | bytes 9741600 | tf_op jit(solution)/shard_map/concatenate | solution.py:29
  134.5 0.3 fusion.88
  134.9 1.9 collective-permute-start.16
  136.8 4.9 %collective-permute-start.17 = (f32[1,32,128]{2,1,0:T(8,128)S(1)}, f32[1,32,128]{2,1,0:T(8,128)S(1)}, u32[]{:S(2)}, u32[]{:S(2)}) collective-permute-start(f32[1,32,128]{2,1,0:T(8,128)S(1)} %get-tuple-element.39), channel_id=1, source_target_pairs={{0,4},{4,8},{8,12},{12,16},{16,20},{20,24},{24,28},{1,5},{5,9},{9,... | collective-permute-start | bytes 49160 | tf_op jit(solution)/shard_map/ppermute | solution.py:27
  141.8 9.4 %fusion.12 = f32[16,64,1024]{2,1,0:T(8,128)S(1)} fusion(f32[16,64,1024]{2,1,0:T(8,128)S(1)} %copy-done.3, f32[1,64,1024]{2,1,0:T(8,128)S(1)} %collective-permute-done.1, f32[1,64,1024]{2,1,0:T(8,128)S(1)} %collective-permute-done, f32[16,64,128]{2,1,0:T(8,128)S(1)} %subtract_multiply_fusion, f32[18,66,1026]{2,1,0:T(8,128)S(1)} %select_maximum_fusion.4, ...), kind=kLoop, calls=%fused_computation.31 | loop fusion | flops 45088768 | bytes 28983296 | tf_op jit(solution)/shard_map/sub | solution.py:59
  151.3 1.9 collective-permute-start.18
  153.2 4.3 %collective-permute-start.19 = (f32[18,1,128]{2,1,0:T(1,128)S(1)}, f32[18,1,128]{2,1,0:T(1,128)S(1)}, u32[]{:S(2)}, u32[]{:S(2)}) collective-permute-start(f32[18,1,128]{2,1,0:T(1,128)S(1)} %get-tuple-element.29), channel_id=1, source_target_pairs={{0,1},{1,2},{2,3},{4,5},{5,6},{6,7},{8,9},{9,10},{10,11},{12,13},{... | collective-permute-start | bytes 27656 | tf_op jit(solution)/shard_map/ppermute | solution.py:27
  157.5 1.9 collective-permute-start.4
  159.4 3.6 %collective-permute-start.5 = (f32[1,64,1024]{2,1,0:T(8,128)S(1)}, f32[1,64,1024]{2,1,0:T(8,128)S(1)}, u32[]{:S(2)}, u32[]{:S(2)}) collective-permute-start(f32[1,64,1024]{2,1,0:T(8,128)S(1)} %get-tuple-element.19), channel_id=1, source_target_pairs={{0,4},{4,8},{8,12},{12,16},{16,20},{20,24},{24,28},{1,5},{5,9},{9,... | collective-permute-start | bytes 786440 | tf_op jit(solution)/shard_map/ppermute | solution.py:27
  163.5 0.3 fusion.80
  163.8 1.9 collective-permute-start.20
  165.7 3.6 %collective-permute-start.21 = (f32[1,32,128]{2,1,0:T(8,128)S(1)}, f32[1,32,128]{2,1,0:T(8,128)S(1)}, u32[]{:S(2)}, u32[]{:S(2)}) collective-permute-start(f32[1,32,128]{2,1,0:T(8,128)S(1)} %get-tuple-element.37), channel_id=1, source_target_pairs={{0,4},{4,8},{8,12},{12,16},{16,20},{20,24},{24,28},{1,5},{5,9},{9,... | collective-permute-start | bytes 49160 | tf_op jit(solution)/shard_map/ppermute | solution.py:27
  169.6 1.9 collective-permute-start.7
  171.5 3.4 %collective-permute-start.6 = (f32[18,1,1024]{2,0,1:T(8,128)S(1)}, f32[18,1,1024]{2,0,1:T(8,128)S(1)}, u32[]{:S(2)}, u32[]{:S(2)}) collective-permute-start(f32[18,1,1024]{2,0,1:T(8,128)S(1)} %copy.42), channel_id=1, source_target_pairs={{1,0},{2,1},{3,2},{5,4},{6,5},{7,6},{9,8},{10,9},{11,10},{13,12},{... | collective-permute-start | bytes 221192 | tf_op jit(solution)/shard_map/ppermute | solution.py:28
  174.9 1.9 collective-permute-start.22
  176.9 4.3 %collective-permute-start.23 = (f32[18,1,128]{2,1,0:T(1,128)S(1)}, f32[18,1,128]{2,1,0:T(1,128)S(1)}, u32[]{:S(2)}, u32[]{:S(2)}) collective-permute-start(f32[18,1,128]{2,1,0:T(1,128)S(1)} %get-tuple-element.27), channel_id=1, source_target_pairs={{0,1},{1,2},{2,3},{4,5},{5,6},{6,7},{8,9},{9,10},{10,11},{12,13},{... | collective-permute-start | bytes 27656 | tf_op jit(solution)/shard_map/ppermute | solution.py:27
  181.3 0.6 collective-permute-done.23
  182.3 0.4 add_multiply_fusion
  182.7 10.8 %gather_fusion = f32[3072,128]{1,0:T(8,128)} fusion(f32[512,128]{1,0:T(8,128)S(1)} %bitcast.129, s32[3072]{0:T(1024)S(1)} %broadcast_clamp_fusion), kind=kCustom, calls=%fused_computation | custom fusion | bytes 3158016 | tf_op jit(solution)/shard_map/gather | solution.py:144
  193.5 5.9 %all-to-all-start.2 = ((f32[32,96,128]{2,1,0:T(8,128)}), f32[32,96,128]{2,1,0:T(8,128)S(1)}, u32[]{:S(2)}, u32[]{:S(2)}) async-start(f32[32,96,128]{2,1,0:T(8,128)} %bitcast.19), calls=%async_computation.2 | async-start | bytes 3145728 | tf_op jit(solution)/shard_map/all_to_all | solution.py:147
  199.5 2.3 collective-permute-start.24
  201.8 3.6 %collective-permute-start.25 = (f32[1,32,128]{2,1,0:T(8,128)S(1)}, f32[1,32,128]{2,1,0:T(8,128)S(1)}, u32[]{:S(2)}, u32[]{:S(2)}) collective-permute-start(f32[1,32,128]{2,1,0:T(8,128)S(1)} %get-tuple-element.35), channel_id=1, source_target_pairs={{0,4},{4,8},{8,12},{12,16},{16,20},{20,24},{24,28},{1,5},{5,9},{9,... | collective-permute-start | bytes 49160 | tf_op jit(solution)/shard_map/ppermute | solution.py:27
  205.3 7.3 %select_maximum_fusion = f32[18,66,1026]{2,1,0:T(8,128)S(1)} fusion(f32[18,1,1024]{2,1,0:T(1,128)S(1)} %copy.43, f32[18,1,1024]{2,1,0:T(1,128)S(1)} %copy.45, f32[1,64,1024]{2,1,0:T(8,128)S(1)} %collective-permute-done.4, f32[16,64,1024]{2,1,0:T(8,128)} %copy-done.1, f32[1,64,1024]{2,1,0:T(8,128)S(1)} %collective-permute-done.5), kind=kLoop, calls=%fused_computation.7 | loop fusion | flops 14626656 | bytes 9741600 | tf_op jit(solution)/shard_map/concatenate | solution.py:29
  212.6 23.0 %collective-permute-done.24 = f32[1,32,128]{2,1,0:T(8,128)S(1)} collective-permute-done((f32[1,32,128]{2,1,0:T(8,128)S(1)}, f32[1,32,128]{2,1,0:T(8,128)S(1)}, u32[]{:S(2)}, u32[]{:S(2)}) %collective-permute-start.24) | collective-permute-done | bytes 16416 | tf_op jit(solution)/shard_map/ppermute | solution.py:28
  235.7 2.1 collective-permute-start.26
  237.8 4.3 %collective-permute-start.27 = (f32[18,1,128]{2,1,0:T(1,128)S(1)}, f32[18,1,128]{2,1,0:T(1,128)S(1)}, u32[]{:S(2)}, u32[]{:S(2)}) collective-permute-start(f32[18,1,128]{2,1,0:T(1,128)S(1)} %get-tuple-element.25), channel_id=1, source_target_pairs={{0,1},{1,2},{2,3},{4,5},{5,6},{6,7},{8,9},{9,10},{10,11},{12,13},{... | collective-permute-start | bytes 27656 | tf_op jit(solution)/shard_map/ppermute | solution.py:27
  242.1 14.1 %fusion.21 = f32[16,64,1024]{2,1,0:T(8,128)} fusion(f32[16,64,1024]{2,1,0:T(8,128)S(1)} %copy-done.2, f32[1,64,1024]{2,1,0:T(8,128)S(1)} %collective-permute-done.4, f32[1,64,1024]{2,1,0:T(8,128)S(1)} %collective-permute-done.5, f32[18,1,1024]{2,1,0:T(1,128)S(1)} %copy.45, f32[18,1,1024]{2,1,0:T(1,128)S(1)} %copy.43, ...), kind=kLoop, calls=%fused_computation.40 | loop fusion | flops 49283072 | bytes 24264704 | tf_op jit(solution)/shard_map/sub | solution.py:59
  256.8 0.9 pad_maximum_fusion.12
  257.7 11.6 %gather_fusion.1 = f32[1024,128]{1,0:T(8,128)} fusion(f32[32,96,128]{2,1,0:T(8,128)S(1)} %all-to-all-done.2, s32[1024]{0:T(1024)S(1)} %bitcast.130), kind=kCustom, calls=%fused_computation.1 | custom fusion | bytes 1056768 | tf_op jit(solution)/shard_map/gather | solution.py:148
  (89 shorter events, 3.1 us)
Async XLA Ops:
  0.6 36.9 %copy-start.6 = (f32[16,32,128]{2,1,0:T(8,128)S(1)}, f32[16,32,128]{2,1,0:T(8,128)}, u32[]{:S(2)}) copy-start(f32[16,32,128]{2,1,0:T(8,128)} %param.14) | copy-start | bytes 786436
  19.5 12.1 %all-to-all-start = ((f32[32,1,96]{2,1,0:T(1,128)}), f32[32,1,96]{2,1,0:T(1,128)S(1)}, u32[]{:S(2)}, u32[]{:S(2)}) async-start(f32[32,1,96]{2,1,0:T(1,128)} %all_to_all.12), calls=%async_computation | async-start | bytes 32768 | tf_op jit(solution)/shard_map/all_to_all | solution.py:122
  31.6 63.6 %all-to-all-start.1 = ((f32[32,96,128]{2,1,0:T(8,128)}), f32[32,96,128]{2,1,0:T(8,128)}, u32[]{:S(2)}, u32[]{:S(2)}) async-start(f32[32,96,128]{2,1,0:T(8,128)} %bitcast.15), calls=%async_computation.1 | async-start | bytes 3145728 | tf_op jit(solution)/shard_map/all_to_all | solution.py:121
  37.5 34.5 %collective-permute-start.9 = (f32[1,32,128]{2,1,0:T(8,128)S(1)}, f32[1,32,128]{2,1,0:T(8,128)S(1)}, u32[]{:S(2)}, u32[]{:S(2)}) collective-permute-start(f32[1,32,128]{2,1,0:T(8,128)S(1)} %get-tuple-element.44), channel_id=1, source_target_pairs={{0,4},{4,8},{8,12},{12,16},{16,20},{20,24},{24,28},{1,5},{5,9},{9,... | collective-permute-start | bytes 49160 | tf_op jit(solution)/shard_map/ppermute | solution.py:27
  42.0 41.9 %collective-permute-start.1 = (f32[1,64,1024]{2,1,0:T(8,128)S(1)}, f32[1,64,1024]{2,1,0:T(8,128)S(1)}, u32[]{:S(2)}, u32[]{:S(2)}) collective-permute-start(f32[1,64,1024]{2,1,0:T(8,128)S(1)} %get-tuple-element.22), channel_id=1, source_target_pairs={{0,4},{4,8},{8,12},{12,16},{16,20},{20,24},{24,28},{1,5},{5,9},{9,... | collective-permute-start | bytes 786440 | tf_op jit(solution)/shard_map/ppermute | solution.py:27
  44.0 42.4 %collective-permute-start = (f32[1,64,1024]{2,1,0:T(8,128)S(1)}, f32[1,64,1024]{2,1,0:T(8,128)S(1)}, u32[]{:S(2)}, u32[]{:S(2)}) collective-permute-start(f32[1,64,1024]{2,1,0:T(8,128)S(1)} %get-tuple-element.21), channel_id=1, source_target_pairs={{4,0},{8,4},{12,8},{16,12},{20,16},{24,20},{28,24},{5,1},{9,5},{13... | collective-permute-start | bytes 786440 | tf_op jit(solution)/shard_map/ppermute | solution.py:28
  46.3 30.2 %collective-permute-start.8 = (f32[1,32,128]{2,1,0:T(8,128)S(1)}, f32[1,32,128]{2,1,0:T(8,128)S(1)}, u32[]{:S(2)}, u32[]{:S(2)}) collective-permute-start(f32[1,32,128]{2,1,0:T(8,128)S(1)} %get-tuple-element.43), channel_id=1, source_target_pairs={{4,0},{8,4},{12,8},{16,12},{20,16},{24,20},{28,24},{5,1},{9,5},{13... | collective-permute-start | bytes 49160 | tf_op jit(solution)/shard_map/ppermute | solution.py:28
  76.5 6.4 %collective-permute-start.10 = (f32[18,1,128]{2,1,0:T(1,128)S(1)}, f32[18,1,128]{2,1,0:T(1,128)S(1)}, u32[]{:S(2)}, u32[]{:S(2)}) collective-permute-start(f32[18,1,128]{2,1,0:T(1,128)S(1)} %get-tuple-element.34), channel_id=1, source_target_pairs={{1,0},{2,1},{3,2},{5,4},{6,5},{7,6},{9,8},{10,9},{11,10},{13,12},{... | collective-permute-start | bytes 27656 | tf_op jit(solution)/shard_map/ppermute | solution.py:28
  78.6 4.9 %collective-permute-start.11 = (f32[18,1,128]{2,1,0:T(1,128)S(1)}, f32[18,1,128]{2,1,0:T(1,128)S(1)}, u32[]{:S(2)}, u32[]{:S(2)}) collective-permute-start(f32[18,1,128]{2,1,0:T(1,128)S(1)} %get-tuple-element.33), channel_id=1, source_target_pairs={{0,1},{1,2},{2,3},{4,5},{5,6},{6,7},{8,9},{9,10},{10,11},{12,13},{... | collective-permute-start | bytes 27656 | tf_op jit(solution)/shard_map/ppermute | solution.py:27
  83.9 32.0 %copy-start.7 = (s32[16,32,128]{2,1,0:T(8,128)S(1)}, s32[16,32,128]{2,1,0:T(8,128)}, u32[]{:S(2)}) copy-start(s32[16,32,128]{2,1,0:T(8,128)} %param.15) | copy-start | bytes 786436
  86.5 2.1 copy-start.4
  88.7 33.4 %collective-permute-start.2 = (f32[18,1,1024]{2,0,1:T(8,128)S(1)}, f32[18,1,1024]{2,0,1:T(8,128)S(1)}, u32[]{:S(2)}, u32[]{:S(2)}) collective-permute-start(f32[18,1,1024]{2,0,1:T(8,128)S(1)} %copy.36), channel_id=1, source_target_pairs={{1,0},{2,1},{3,2},{5,4},{6,5},{7,6},{9,8},{10,9},{11,10},{13,12},{... | collective-permute-start | bytes 221192 | tf_op jit(solution)/shard_map/ppermute | solution.py:28
  90.7 31.5 %collective-permute-start.3 = (f32[18,1,1024]{2,0,1:T(8,128)S(1)}, f32[18,1,1024]{2,0,1:T(8,128)S(1)}, u32[]{:S(2)}, u32[]{:S(2)}) collective-permute-start(f32[18,1,1024]{2,0,1:T(8,128)S(1)} %copy.38), channel_id=1, source_target_pairs={{0,1},{1,2},{2,3},{4,5},{5,6},{6,7},{8,9},{9,10},{10,11},{12,13},{... | collective-permute-start | bytes 221192 | tf_op jit(solution)/shard_map/ppermute | solution.py:27
  115.8 25.9 %copy-start.5 = (f32[18,64,1024]{2,1,0:T(8,128)S(1)}, f32[18,64,1024]{2,1,0:T(8,128)}, u32[]{:S(2)}) copy-start(f32[18,64,1024]{2,1,0:T(8,128)} %copy-done.4) | copy-start | bytes 14155780
  116.3 6.0 %collective-permute-start.12 = (f32[1,32,128]{2,1,0:T(8,128)S(1)}, f32[1,32,128]{2,1,0:T(8,128)S(1)}, u32[]{:S(2)}, u32[]{:S(2)}) collective-permute-start(f32[1,32,128]{2,1,0:T(8,128)S(1)} %get-tuple-element.42), channel_id=1, source_target_pairs={{4,0},{8,4},{12,8},{16,12},{20,16},{24,20},{28,24},{5,1},{9,5},{13... | collective-permute-start | bytes 49160 | tf_op jit(solution)/shard_map/ppermute | solution.py:28
  118.4 4.5 %collective-permute-start.13 = (f32[1,32,128]{2,1,0:T(8,128)S(1)}, f32[1,32,128]{2,1,0:T(8,128)S(1)}, u32[]{:S(2)}, u32[]{:S(2)}) collective-permute-start(f32[1,32,128]{2,1,0:T(8,128)S(1)} %get-tuple-element.41), channel_id=1, source_target_pairs={{0,4},{4,8},{8,12},{12,16},{16,20},{20,24},{24,28},{1,5},{5,9},{9,... | collective-permute-start | bytes 49160 | tf_op jit(solution)/shard_map/ppermute | solution.py:27
  123.0 11.2 %collective-permute-start.14 = (f32[18,1,128]{2,1,0:T(1,128)S(1)}, f32[18,1,128]{2,1,0:T(1,128)S(1)}, u32[]{:S(2)}, u32[]{:S(2)}) collective-permute-start(f32[18,1,128]{2,1,0:T(1,128)S(1)} %get-tuple-element.32), channel_id=1, source_target_pairs={{1,0},{2,1},{3,2},{5,4},{6,5},{7,6},{9,8},{10,9},{11,10},{13,12},{... | collective-permute-start | bytes 27656 | tf_op jit(solution)/shard_map/ppermute | solution.py:28
  124.9 16.9 %slice-start = ((s8[6291456]{0:T(1024)(128)(4,1)}), s8[4194304]{0:T(1024)(128)(4,1)S(1)}, s32[]{:S(2)}) async-start(s8[6291456]{0:T(1024)(128)(4,1)} %bitcast.131), calls=%async_computation.3 | async-start | bytes 8388608
  124.9 16.9 %slice-start.1 = ((s8[6291456]{0:T(1024)(128)(4,1)}), s8[2097152]{0:T(1024)(128)(4,1)S(1)}, s32[]{:S(2)}) async-start(s8[6291456]{0:T(1024)(128)(4,1)} %bitcast.131), calls=%async_computation.4 | async-start | bytes 4194304
  124.9 16.9 %copy-start.3 = (f32[16,64,1024]{2,1,0:T(8,128)S(1)}, f32[16,64,1024]{2,1,0:T(8,128)}, u32[]{:S(2)}) copy-start(f32[16,64,1024]{2,1,0:T(8,128)} %param.8) | copy-start | bytes 12582916
  124.9 9.2 %collective-permute-start.15 = (f32[18,1,128]{2,1,0:T(1,128)S(1)}, f32[18,1,128]{2,1,0:T(1,128)S(1)}, u32[]{:S(2)}, u32[]{:S(2)}) collective-permute-start(f32[18,1,128]{2,1,0:T(1,128)S(1)} %get-tuple-element.31), channel_id=1, source_target_pairs={{0,1},{1,2},{2,3},{4,5},{5,6},{6,7},{8,9},{9,10},{10,11},{12,13},{... | collective-permute-start | bytes 27656 | tf_op jit(solution)/shard_map/ppermute | solution.py:27
  134.9 16.3 %collective-permute-start.16 = (f32[1,32,128]{2,1,0:T(8,128)S(1)}, f32[1,32,128]{2,1,0:T(8,128)S(1)}, u32[]{:S(2)}, u32[]{:S(2)}) collective-permute-start(f32[1,32,128]{2,1,0:T(8,128)S(1)} %get-tuple-element.40), channel_id=1, source_target_pairs={{4,0},{8,4},{12,8},{16,12},{20,16},{24,20},{28,24},{5,1},{9,5},{13... | collective-permute-start | bytes 49160 | tf_op jit(solution)/shard_map/ppermute | solution.py:28
  136.8 14.4 %collective-permute-start.17 = (f32[1,32,128]{2,1,0:T(8,128)S(1)}, f32[1,32,128]{2,1,0:T(8,128)S(1)}, u32[]{:S(2)}, u32[]{:S(2)}) collective-permute-start(f32[1,32,128]{2,1,0:T(8,128)S(1)} %get-tuple-element.39), channel_id=1, source_target_pairs={{0,4},{4,8},{8,12},{12,16},{16,20},{20,24},{24,28},{1,5},{5,9},{9,... | collective-permute-start | bytes 49160 | tf_op jit(solution)/shard_map/ppermute | solution.py:27
  151.2 18.3 %copy-start.1 = (f32[16,64,1024]{2,1,0:T(8,128)}, f32[16,64,1024]{2,1,0:T(8,128)S(1)}, u32[]{:S(2)}) copy-start(f32[16,64,1024]{2,1,0:T(8,128)S(1)} %fusion.12) | copy-start | bytes 12582916
  151.3 11.8 %collective-permute-start.18 = (f32[18,1,128]{2,1,0:T(1,128)S(1)}, f32[18,1,128]{2,1,0:T(1,128)S(1)}, u32[]{:S(2)}, u32[]{:S(2)}) collective-permute-start(f32[18,1,128]{2,1,0:T(1,128)S(1)} %get-tuple-element.30), channel_id=1, source_target_pairs={{1,0},{2,1},{3,2},{5,4},{6,5},{7,6},{9,8},{10,9},{11,10},{13,12},{... | collective-permute-start | bytes 27656 | tf_op jit(solution)/shard_map/ppermute | solution.py:28
  153.2 9.9 %collective-permute-start.19 = (f32[18,1,128]{2,1,0:T(1,128)S(1)}, f32[18,1,128]{2,1,0:T(1,128)S(1)}, u32[]{:S(2)}, u32[]{:S(2)}) collective-permute-start(f32[18,1,128]{2,1,0:T(1,128)S(1)} %get-tuple-element.29), channel_id=1, source_target_pairs={{0,1},{1,2},{2,3},{4,5},{5,6},{6,7},{8,9},{9,10},{10,11},{12,13},{... | collective-permute-start | bytes 27656 | tf_op jit(solution)/shard_map/ppermute | solution.py:27
  157.5 11.9 %collective-permute-start.4 = (f32[1,64,1024]{2,1,0:T(8,128)S(1)}, f32[1,64,1024]{2,1,0:T(8,128)S(1)}, u32[]{:S(2)}, u32[]{:S(2)}) collective-permute-start(f32[1,64,1024]{2,1,0:T(8,128)S(1)} %get-tuple-element.20), channel_id=1, source_target_pairs={{4,0},{8,4},{12,8},{16,12},{20,16},{24,20},{28,24},{5,1},{9,5},{13... | collective-permute-start | bytes 786440 | tf_op jit(solution)/shard_map/ppermute | solution.py:28
  159.4 10.0 %collective-permute-start.5 = (f32[1,64,1024]{2,1,0:T(8,128)S(1)}, f32[1,64,1024]{2,1,0:T(8,128)S(1)}, u32[]{:S(2)}, u32[]{:S(2)}) collective-permute-start(f32[1,64,1024]{2,1,0:T(8,128)S(1)} %get-tuple-element.19), channel_id=1, source_target_pairs={{0,4},{4,8},{8,12},{12,16},{16,20},{20,24},{24,28},{1,5},{5,9},{9,... | collective-permute-start | bytes 786440 | tf_op jit(solution)/shard_map/ppermute | solution.py:27
  163.8 11.1 %collective-permute-start.20 = (f32[1,32,128]{2,1,0:T(8,128)S(1)}, f32[1,32,128]{2,1,0:T(8,128)S(1)}, u32[]{:S(2)}, u32[]{:S(2)}) collective-permute-start(f32[1,32,128]{2,1,0:T(8,128)S(1)} %get-tuple-element.38), channel_id=1, source_target_pairs={{4,0},{8,4},{12,8},{16,12},{20,16},{24,20},{28,24},{5,1},{9,5},{13... | collective-permute-start | bytes 49160 | tf_op jit(solution)/shard_map/ppermute | solution.py:28
  165.7 9.2 %collective-permute-start.21 = (f32[1,32,128]{2,1,0:T(8,128)S(1)}, f32[1,32,128]{2,1,0:T(8,128)S(1)}, u32[]{:S(2)}, u32[]{:S(2)}) collective-permute-start(f32[1,32,128]{2,1,0:T(8,128)S(1)} %get-tuple-element.37), channel_id=1, source_target_pairs={{0,4},{4,8},{8,12},{12,16},{16,20},{20,24},{24,28},{1,5},{5,9},{9,... | collective-permute-start | bytes 49160 | tf_op jit(solution)/shard_map/ppermute | solution.py:27
  169.6 11.6 %collective-permute-start.7 = (f32[18,1,1024]{2,0,1:T(8,128)S(1)}, f32[18,1,1024]{2,0,1:T(8,128)S(1)}, u32[]{:S(2)}, u32[]{:S(2)}) collective-permute-start(f32[18,1,1024]{2,0,1:T(8,128)S(1)} %copy.44), channel_id=1, source_target_pairs={{0,1},{1,2},{2,3},{4,5},{5,6},{6,7},{8,9},{9,10},{10,11},{12,13},{... | collective-permute-start | bytes 221192 | tf_op jit(solution)/shard_map/ppermute | solution.py:27
  171.5 9.7 %collective-permute-start.6 = (f32[18,1,1024]{2,0,1:T(8,128)S(1)}, f32[18,1,1024]{2,0,1:T(8,128)S(1)}, u32[]{:S(2)}, u32[]{:S(2)}) collective-permute-start(f32[18,1,1024]{2,0,1:T(8,128)S(1)} %copy.42), channel_id=1, source_target_pairs={{1,0},{2,1},{3,2},{5,4},{6,5},{7,6},{9,8},{10,9},{11,10},{13,12},{... | collective-permute-start | bytes 221192 | tf_op jit(solution)/shard_map/ppermute | solution.py:28
  174.9 6.4 %collective-permute-start.22 = (f32[18,1,128]{2,1,0:T(1,128)S(1)}, f32[18,1,128]{2,1,0:T(1,128)S(1)}, u32[]{:S(2)}, u32[]{:S(2)}) collective-permute-start(f32[18,1,128]{2,1,0:T(1,128)S(1)} %get-tuple-element.28), channel_id=1, source_target_pairs={{1,0},{2,1},{3,2},{5,4},{6,5},{7,6},{9,8},{10,9},{11,10},{13,12},{... | collective-permute-start | bytes 27656 | tf_op jit(solution)/shard_map/ppermute | solution.py:28
  176.9 5.0 %collective-permute-start.23 = (f32[18,1,128]{2,1,0:T(1,128)S(1)}, f32[18,1,128]{2,1,0:T(1,128)S(1)}, u32[]{:S(2)}, u32[]{:S(2)}) collective-permute-start(f32[18,1,128]{2,1,0:T(1,128)S(1)} %get-tuple-element.27), channel_id=1, source_target_pairs={{0,1},{1,2},{2,3},{4,5},{5,6},{6,7},{8,9},{9,10},{10,11},{12,13},{... | collective-permute-start | bytes 27656 | tf_op jit(solution)/shard_map/ppermute | solution.py:27
  182.7 10.8 %copy-start = (f32[16,32,128]{2,1,0:T(8,128)}, f32[16,32,128]{2,1,0:T(8,128)S(1)}, u32[]{:S(2)}) copy-start(f32[16,32,128]{2,1,0:T(8,128)S(1)} %get-tuple-element.9) | copy-start | bytes 786436
  193.5 64.2 %all-to-all-start.2 = ((f32[32,96,128]{2,1,0:T(8,128)}), f32[32,96,128]{2,1,0:T(8,128)S(1)}, u32[]{:S(2)}, u32[]{:S(2)}) async-start(f32[32,96,128]{2,1,0:T(8,128)} %bitcast.19), calls=%async_computation.2 | async-start | bytes 3145728 | tf_op jit(solution)/shard_map/all_to_all | solution.py:147
  199.5 36.2 %collective-permute-start.24 = (f32[1,32,128]{2,1,0:T(8,128)S(1)}, f32[1,32,128]{2,1,0:T(8,128)S(1)}, u32[]{:S(2)}, u32[]{:S(2)}) collective-permute-start(f32[1,32,128]{2,1,0:T(8,128)S(1)} %get-tuple-element.36), channel_id=1, source_target_pairs={{4,0},{8,4},{12,8},{16,12},{20,16},{24,20},{28,24},{5,1},{9,5},{13... | collective-permute-start | bytes 49160 | tf_op jit(solution)/shard_map/ppermute | solution.py:28
  201.7 40.4 %copy-start.2 = (f32[16,64,1024]{2,1,0:T(8,128)S(1)}, f32[16,64,1024]{2,1,0:T(8,128)}, u32[]{:S(2)}) copy-start(f32[16,64,1024]{2,1,0:T(8,128)} %copy-done.1) | copy-start | bytes 12582916
  201.8 33.9 %collective-permute-start.25 = (f32[1,32,128]{2,1,0:T(8,128)S(1)}, f32[1,32,128]{2,1,0:T(8,128)S(1)}, u32[]{:S(2)}, u32[]{:S(2)}) collective-permute-start(f32[1,32,128]{2,1,0:T(8,128)S(1)} %get-tuple-element.35), channel_id=1, source_target_pairs={{0,4},{4,8},{8,12},{12,16},{16,20},{20,24},{24,28},{1,5},{5,9},{9,... | collective-permute-start | bytes 49160 | tf_op jit(solution)/shard_map/ppermute | solution.py:27
  235.7 20.5 %collective-permute-start.26 = (f32[18,1,128]{2,1,0:T(1,128)S(1)}, f32[18,1,128]{2,1,0:T(1,128)S(1)}, u32[]{:S(2)}, u32[]{:S(2)}) collective-permute-start(f32[18,1,128]{2,1,0:T(1,128)S(1)} %get-tuple-element.26), channel_id=1, source_target_pairs={{1,0},{2,1},{3,2},{5,4},{6,5},{7,6},{9,8},{10,9},{11,10},{13,12},{... | collective-permute-start | bytes 27656 | tf_op jit(solution)/shard_map/ppermute | solution.py:28
  237.8 18.4 %collective-permute-start.27 = (f32[18,1,128]{2,1,0:T(1,128)S(1)}, f32[18,1,128]{2,1,0:T(1,128)S(1)}, u32[]{:S(2)}, u32[]{:S(2)}) collective-permute-start(f32[18,1,128]{2,1,0:T(1,128)S(1)} %get-tuple-element.25), channel_id=1, source_target_pairs={{0,1},{1,2},{2,3},{4,5},{5,6},{6,7},{8,9},{9,10},{10,11},{12,13},{... | collective-permute-start | bytes 27656 | tf_op jit(solution)/shard_map/ppermute | solution.py:27
where the time goes:
time: 271 us; the launch traced here: 269 us
  starting transfers between devices  101 us (37%)
  other arithmetic  75.7 us (28%)
  waiting for transfers between devices  52.8 us (19%)
  local copies, waits for them, and re-layouts  38.5 us (14%)
    ppermute x14, starting transfers between devices, extended(): before = lax.ppermute(last, axis, up)  52.7 us
    ppermute x14, starting transfers between devices, extended(): after = lax.ppermute(first, axis, down)  30 us
    ppermute x14, waiting for transfers between devices, extended(): after = lax.ppermute(first, axis, down)  27.4 us
    ppermute x14, waiting for transfers between devices, extended(): before = lax.ppermute(last, axis, up)  25.4 us
    sub x2, other arithmetic, fluid_update(): center + time_step * (diffusivity * laplace(padded) - advect(padded, velo...  23.5 us
    scatter-add x1, other arithmetic, body(): heat = jnp.zeros((solid_x * solid_y, row_len), jnp.float32).at[slot_index...  20.6 us
    concatenate x11, other arithmetic, extended(): value = jnp.concatenate([before, value, after], axis=dim)  13.8 us
    unnamed x26, local copies, waits for them, and re-layouts  13.4 us
  transfers between devices with their start and end apart: 31, of which 6 were waited for; matrix products, arithmetic and copies ran while one was open for 26% of the time, Pallas kernels for 0%

commit v1 on v0

v1 whole, which is shorter than its diff:
```python
import functools
import jax
import jax.numpy as jnp
from jax import lax
from jax.experimental import pallas as pl
from jax.experimental.pallas import tpu as pltpu
from jax.sharding import PartitionSpec as P

FSTEPS = 2
SSTEPS = 4
time_step = 0.1
diffusivity = 0.5
film_coef = 2.0
solid_step = 0.05
source_gain = 4.0
conduct_table = (0.4, 0.9, 1.5, 2.2)
modulus_table = (0.5, 1.0, 1.6, 2.4)
F32 = jnp.float32
BF16 = jnp.bfloat16
VMEM_LIMIT = 40 * 1024 * 1024
AXES = ("gx", "gy")


def params():
    return pltpu.CompilerParams(vmem_limit_bytes=VMEM_LIMIT)


def cost(flops, bytes_accessed):
    return pl.CostEstimate(flops=flops, bytes_accessed=bytes_accessed, transcendentals=0)


def halves(value):
    high = value.astype(BF16)
    low = (value - high.astype(F32)).astype(BF16)
    return high, low


def ones_where(test):
    return jnp.where(test, 1.0, 0.0).astype(BF16)


def neighbours(before, after, axis):
    size = lax.axis_size(axis)
    up = [(i, i + 1) for i in range(size - 1)]
    down = [(j, i) for i, j in up]
    return lax.ppermute(before, axis, up), lax.ppermute(after, axis, down)


def pack_kernel(ndev, cap, owner_ref, slot_ref, temp_ref, old_ref, mask_ref,
                out_ref, meta_ref, flux_ref, dest_ref, rhs_ref):
    rows = owner_ref.shape[1]
    row_len = temp_ref.shape[2]
    flux = mask_ref[...].astype(F32) * film_coef * (temp_ref[...] - old_ref[...])
    flux_ref[...] = flux
    high, low = halves(flux.reshape(rows, row_len))
    rhs_ref[:, :row_len] = high
    rhs_ref[:, row_len:] = low
    lane = 128
    tri = ones_where(
        lax.broadcasted_iota(jnp.int32, (lane, lane), 0)
        <= lax.broadcasted_iota(jnp.int32, (lane, lane), 1)
    )
    names = lax.broadcasted_iota(jnp.int32, (ndev, lane), 0)
    carry = jnp.zeros((ndev, 1), F32)
    for chunk in range(rows // lane):
        cols = slice(chunk * lane, (chunk + 1) * lane)
        own = owner_ref[:, cols]
        hit = jnp.where(names == own, 1.0, 0.0)
        ranks = jnp.dot(hit.astype(BF16), tri, preferred_element_type=F32) + carry
        carry = ranks[:, lane - 1:]
        place = jnp.sum(hit * ranks, axis=0, keepdims=True) - 1.0
        dest_ref[:, cols] = own * cap + place.astype(jnp.int32)
    dest = dest_ref[...]
    code = slot_ref[...] + 1
    pieces = jnp.concatenate(
        [(code // 32).astype(F32), (code % 32).astype(F32), jnp.zeros((6, rows), F32)], axis=0
    ).astype(BF16)
    block = 256

    def step(index, none):
        base = pl.multiple_of(index * block, block)
        pick = ones_where(
            lax.broadcasted_iota(jnp.int32, (block, rows), 0) + base == dest
        )
        both = jnp.dot(pick, rhs_ref[...], preferred_element_type=F32)
        out_ref[pl.ds(base, block), :] = both[:, :row_len] + both[:, row_len:]
        names2 = lax.dot_general(
            pieces, pick, (((1,), (1,)), ((), ())), preferred_element_type=F32
        )
        meta_ref[:, pl.ds(base, block)] = names2[0:1] * 32.0 + names2[1:2]
        return none

    lax.fori_loop(0, ndev * cap // block, step, 0)


def pack(owner, slot, temp, old, mask, ndev, cap):
    cx, cy, _ = temp.shape
    row_len = old.shape[2]
    rows = cx * cy
    total = ndev * cap
    whole = lambda shape: pl.BlockSpec(shape, lambda i: (0,) * len(shape))
    return pl.pallas_call(
        functools.partial(pack_kernel, ndev, cap),
        grid=(1,),
        in_specs=[
            whole((1, rows)),
            whole((1, rows)),
            whole((cx, cy, row_len)),
            whole((cx, cy, row_len)),
            whole((cx, cy, row_len)),
        ],
        out_specs=[
            whole((total, row_len)),
            whole((1, total)),
            whole((cx, cy, row_len)),
            whole((1, rows)),
        ],
        out_shape=[
            jax.ShapeDtypeStruct((total, row_len), F32),
            jax.ShapeDtypeStruct((1, total), F32),
            jax.ShapeDtypeStruct((cx, cy, row_len), F32),
            jax.ShapeDtypeStruct((1, rows), jnp.int32),
        ],
        scratch_shapes=[pltpu.VMEM((rows, 2 * row_len), BF16)],
        compiler_params=params(),
        cost_estimate=cost(4 * total * rows * row_len, 5 * rows * row_len * 4),
        name="pack",
    )(owner, slot, temp, old, mask)


def heat_kernel(rows_ref, code_ref, heat_ref):
    slots, row_len = heat_ref.shape
    total = rows_ref.shape[0]
    block = 512
    heat_ref[...] = jnp.zeros_like(heat_ref)

    def step(index, none):
        base = pl.multiple_of(index * block, block)
        high, low = halves(rows_ref[pl.ds(base, block), :])
        code = code_ref[:, pl.ds(base, block)].astype(jnp.int32) - 1
        pick = ones_where(lax.broadcasted_iota(jnp.int32, (slots, block), 0) == code)
        both = jnp.dot(
            pick, jnp.concatenate([high, low], axis=1), preferred_element_type=F32
        )
        heat_ref[...] += both[:, :row_len] + both[:, row_len:]
        return none

    lax.fori_loop(0, total // block, step, 0)


def heat_sum(incoming, code, slots):
    total, row_len = incoming.shape
    return pl.pallas_call(
        heat_kernel,
        in_specs=[pl.BlockSpec(memory_space=pltpu.VMEM)] * 2,
        out_specs=pl.BlockSpec(memory_space=pltpu.VMEM),
        out_shape=jax.ShapeDtypeStruct((slots, row_len), F32),
        compiler_params=params(),
        cost_estimate=cost(4 * total * slots * row_len, 4 * total * row_len),
        name="heat_sum",
    )(incoming, code)


def table(kind, values):
    out = jnp.zeros(kind.shape, F32)
    for index, value in enumerate(values):
        out = jnp.where(kind == index + 1.0, value, out)
    return out


OFF = 8


def solid_kernel(rim, state_ref, xlo_ref, xhi_ref, ylo_ref, yhi_ref,
                 heat_ref, hxlo_ref, hxhi_ref, hylo_ref, hyhi_ref, code_ref,
                 next_ref, sigma_ref, reply_ref, temp_ref, work_ref, cond_ref, src_ref, rhs_ref):
    _, sx, sy, sz = state_ref.shape
    wide = sx + 2 * rim
    thin = rim - 1
    temp_ref[...] = jnp.zeros_like(temp_ref)
    work_ref[...] = jnp.zeros_like(work_ref)
    cond_ref[...] = jnp.zeros_like(cond_ref)
    src_ref[...] = jnp.zeros_like(src_ref)
    for which, ref in ((0, temp_ref), (1, cond_ref)):
        ref[rim:rim + sx, OFF:OFF + sy, :] = state_ref[which]
        ref[0:rim, OFF:OFF + sy, :] = xlo_ref[which]
        ref[rim + sx:wide, OFF:OFF + sy, :] = xhi_ref[which]
        ref[:, OFF - rim:OFF, :] = ylo_ref[which]
        ref[:, OFF + sy:OFF + sy + rim, :] = yhi_ref[which]
    src_ref[rim:rim + sx, OFF:OFF + sy, :] = heat_ref[...]
    src_ref[1:rim, OFF:OFF + sy, :] = hxlo_ref[...]
    src_ref[rim + sx:wide - 1, OFF:OFF + sy, :] = hxhi_ref[...]
    src_ref[1:wide - 1, OFF - thin:OFF, :] = hylo_ref[...]
    src_ref[1:wide - 1, OFF + sy:OFF + sy + thin, :] = hyhi_ref[...]
    kind = cond_ref[...]
    sigma_ref[...] = table(kind[rim - 1:rim + sx + 1], modulus_table)
    cond_ref[...] = solid_step * table(kind, conduct_table)
    src_ref[...] = (solid_step * source_gain) * src_ref[...]
    height = temp_ref.shape[1]
    first = lax.broadcasted_iota(jnp.int32, (height, sz), 1) == 0
    last = lax.broadcasted_iota(jnp.int32, (height, sz), 1) == sz - 1
    pair = (temp_ref, work_ref)
    for turn in range(rim - 1):
        now, later = pair[turn % 2], pair[(turn + 1) % 2]

        def plane(x, none):
            centre = now[x]
            beside = now[x - 1] + now[x + 1]
            beside += pltpu.roll(centre, 1, 0) + pltpu.roll(centre, height - 1, 0)
            beside += jnp.where(first, 0.0, pltpu.roll(centre, 1, 1))
            beside += jnp.where(last, 0.0, pltpu.roll(centre, sz - 1, 1))
            later[x] = centre + (cond_ref[x] * (beside - 6.0 * centre) + src_ref[x])
            return none

        lax.fori_loop(1 + turn, wide - 1 - turn, plane, 0)
    final = pair[(rim - 1) % 2]
    solid = final[rim:rim + sx, OFF:OFF + sy, :]
    next_ref[...] = solid
    sigma_ref[...] = sigma_ref[...] * final[rim - 1:rim + sx + 1]
    high, low = halves(solid.reshape(sx * sy, sz))
    rhs_ref[:, :sz] = high
    rhs_ref[:, sz:] = low
    block = 256

    def answer(index, none):
        base = pl.multiple_of(index * block, block)
        code = code_ref[pl.ds(base, block), :].astype(jnp.int32) - 1
        pick = ones_where(lax.broadcasted_iota(jnp.int32, (block, sx * sy), 1) == code)
        both = jnp.dot(pick, rhs_ref[...], preferred_element_type=F32)
        reply_ref[pl.ds(base, block), :] = both[:, :sz] + both[:, sz:]
        return none

    lax.fori_loop(0, reply_ref.shape[0] // block, answer, 0)


def solid_steps(rim, state, state_rim, heat, heat_rim, code):
    _, sx, sy, sz = state.shape
    total = code.shape[0]
    wide, height = sx + 2 * rim, sy + 2 * OFF
    vmem = pl.BlockSpec(memory_space=pltpu.VMEM)
    return pl.pallas_call(
        functools.partial(solid_kernel, rim),
        in_specs=[vmem] * 11,
        out_specs=[vmem] * 3,
        out_shape=[
            jax.ShapeDtypeStruct((sx, sy, sz), F32),
            jax.ShapeDtypeStruct((sx + 2, height, sz), F32),
            jax.ShapeDtypeStruct((total, sz), F32),
        ],
        scratch_shapes=[pltpu.VMEM((wide, height, sz), F32)] * 4
        + [pltpu.VMEM((sx * sy, 2 * sz), BF16)],
        compiler_params=params(),
        cost_estimate=cost(4 * total * sx * sy * sz, 4 * total * sz),
        name="solid_steps",
    )(state, *state_rim, heat, *heat_rim, code)


def stress_kernel(sigma_ref, out_ref):
    _, sx, sy, sz = out_ref.shape
    height = sigma_ref.shape[1]
    first = lax.broadcasted_iota(jnp.int32, (height, sz), 1) == 0
    last = lax.broadcasted_iota(jnp.int32, (height, sz), 1) == sz - 1

    def plane(x, none):
        centre = sigma_ref[x + 1]
        out_ref[0, x] = 0.5 * (sigma_ref[x + 2] - sigma_ref[x])[OFF:OFF + sy]
        along = pltpu.roll(centre, height - 1, 0) - pltpu.roll(centre, 1, 0)
        out_ref[1, x] = 0.5 * along[OFF:OFF + sy]
        along = jnp.where(last, 0.0, pltpu.roll(centre, sz - 1, 1)) - jnp.where(
            first, 0.0, pltpu.roll(centre, 1, 1)
        )
        out_ref[2, x] = 0.5 * along[OFF:OFF + sy]
        return none

    lax.fori_loop(0, sx, plane, 0)


def stress(sigma, sx, sy):
    sz = sigma.shape[2]
    vmem = pl.BlockSpec(memory_space=pltpu.VMEM)
    return pl.pallas_call(
        stress_kernel,
        in_specs=[vmem],
        out_specs=vmem,
        out_shape=jax.ShapeDtypeStruct((3, sx, sy, sz), F32),
        compiler_params=params(),
        cost_estimate=cost(10 * sx * sy * sz, 16 * sx * sy * sz),
        name="stress",
    )(sigma)


def unpack_kernel(dest_ref, back_ref, out_ref):
    rows = out_ref.shape[0]

    def step(index, none):
        base = pl.multiple_of(index * 8, 8)
        lines = [back_ref[pl.ds(dest_ref[0, base + i], 1), :] for i in range(8)]
        out_ref[pl.ds(base, 8), :] = jnp.concatenate(lines, axis=0)
        return none

    lax.fori_loop(0, rows // 8, step, 0, unroll=2)


def unpack(dest, back):
    rows = dest.shape[1]
    vmem = pl.BlockSpec(memory_space=pltpu.VMEM)
    return pl.pallas_call(
        unpack_kernel,
        in_specs=[pl.BlockSpec(memory_space=pltpu.SMEM), vmem],
        out_specs=vmem,
        out_shape=jax.ShapeDtypeStruct((rows, back.shape[1]), F32),
        compiler_params=params(),
        cost_estimate=cost(rows * 128, 8 * rows * back.shape[1]),
        name="unpack",
    )(dest, back)


def fluid_kernel(before_ref, here_ref, after_ref, xlo_ref, xhi_ref, ylo_ref, yhi_ref,
                 speed_ref, flux_ref, out_ref, ext_ref):
    index, count = pl.program_id(0), pl.num_programs(0)
    _, cy, depth = here_ref.shape
    row_len = flux_ref.shape[2]
    ext_ref[OFF:OFF + cy, :] = here_ref[0]
    ext_ref[OFF - 1:OFF, :] = ylo_ref[0]
    ext_ref[OFF + cy:OFF + cy + 1, :] = yhi_ref[0]
    lanes = lax.broadcasted_iota(jnp.int32, (8, depth), 1)
    first, last = lanes == 0, lanes == depth - 1
    at_first, at_last = index == 0, index == count - 1
    rate = time_step * diffusivity

    def push(total, centre, lower, upper, speed):
        scaled = time_step * speed
        total = total + (rate + jnp.maximum(scaled, 0.0)) * (lower - centre)
        return total + (rate - jnp.minimum(scaled, 0.0)) * (upper - centre)

    for tile in range(cy // 16):
        speeds = [speed_ref[k, 0, tile * 16:tile * 16 + 16, :].astype(F32) for k in range(3)]
        for part in range(2):
            y = tile * 16 + part * 8
            u, v, w = [s[part * 8:part * 8 + 8] for s in speeds]
            centre = here_ref[0, y:y + 8, :]
            lower = jnp.where(at_first, xlo_ref[0, y:y + 8, :], before_ref[0, y:y + 8, :])
            upper = jnp.where(at_last, xhi_ref[0, y:y + 8, :], after_ref[0, y:y + 8, :])
            total = push(centre, centre, lower, upper, u)
            lower = ext_ref[OFF + y - 1:OFF + y + 7, :]
            upper = ext_ref[OFF + y + 1:OFF + y + 9, :]
            total = push(total, centre, lower, upper, v)
            lower = jnp.where(first, 0.0, pltpu.roll(centre, 1, 1))
            upper = jnp.where(last, 0.0, pltpu.roll(centre, depth - 1, 1))
            total = push(total, centre, lower, upper, w)
            out_ref[0, y:y + 8, row_len:] = total[:, row_len:]
            out_ref[0, y:y + 8, :row_len] = (
                total[:, :row_len] - time_step * flux_ref[0, y:y + 8, :]
            )


def fluid_step(temp, rims, velocity, flux):
    cx, cy, depth = temp.shape
    row_len = flux.shape[2]
    plane = (1, cy, depth)
    fixed = pl.BlockSpec(plane, lambda i: (0, 0, 0))
    line = pl.BlockSpec((1, 1, depth), lambda i: (i, 0, 0))
    return pl.pallas_call(
        fluid_kernel,
        grid=(cx,),
        in_specs=[
            pl.BlockSpec(plane, lambda i: (jnp.maximum(i - 1, 0), 0, 0)),
            pl.BlockSpec(plane, lambda i: (i, 0, 0)),
            pl.BlockSpec(plane, lambda i: (jnp.minimum(i + 1, cx - 1), 0, 0)),
            fixed,
            fixed,
            line,
            line,
            pl.BlockSpec((3, 1, cy, depth), lambda i: (0, i, 0, 0)),
            pl.BlockSpec((1, cy, row_len), lambda i: (i, 0, 0)),
        ],
        out_specs=pl.BlockSpec(plane, lambda i: (i, 0, 0)),
        out_shape=jax.ShapeDtypeStruct(temp.shape, F32),
        scratch_shapes=[pltpu.VMEM((cy + 2 * OFF, depth), F32)],
        compiler_params=params(),
        cost_estimate=cost(40 * cx * cy * depth, 22 * cx * cy * depth),
        name="fluid_step",
    )(temp, temp, temp, *rims, velocity, flux)


def fluid_rims(temp):
    xlo, xhi = neighbours(temp[-1:], temp[:1], "gx")
    ylo, yhi = neighbours(temp[:, -1:], temp[:, :1], "gy")
    return xlo, xhi, ylo, yhi


def body(temp_fluid, velocity, wall_old, wall_mask, owner_map, slot_map, temp_solid, material):
    cx, cy, depth = temp_fluid.shape
    row_len = wall_old.shape[2]
    sx, sy, sz = temp_solid.shape
    ndev = lax.axis_size("gx") * lax.axis_size("gy")
    rows = cx * cy
    cap = (3 * rows + ndev - 1) // ndev
    cap = -(-cap // 8) * 8
    total = ndev * cap
    rim = SSTEPS + 1

    outgoing, meta, flux, dest = pack(
        owner_map.reshape(1, rows), slot_map, temp_fluid, wall_old, wall_mask, ndev, cap
    )
    incoming = lax.all_to_all(
        outgoing.reshape(ndev, cap, row_len), AXES, split_axis=0, concat_axis=0, tiled=True
    )
    code = lax.all_to_all(meta.reshape(ndev, cap), AXES, split_axis=0, concat_axis=0, tiled=True)
    code_row = code.reshape(1, total)
    code_col = code.reshape(total, 1)

    state = jnp.stack([temp_solid, material.astype(F32) + 1.0])
    xlo, xhi = neighbours(state[:, sx - rim:], state[:, :rim], "gx")
    tall = lambda cut: jnp.concatenate([xlo[:, :, cut], state[:, :, cut], xhi[:, :, cut]], axis=1)
    ylo, yhi = neighbours(tall(slice(sy - rim, sy)), tall(slice(0, rim)), "gy")

    fluid = fluid_step(temp_fluid, fluid_rims(temp_fluid), velocity, flux)

    heat = heat_sum(incoming.reshape(total, row_len), code_row, sx * sy).reshape(sx, sy, sz)
    thin = rim - 1
    hxlo, hxhi = neighbours(heat[sx - thin:], heat[:thin], "gx")
    tall2 = lambda cut: jnp.concatenate([hxlo[:, cut], heat[:, cut], hxhi[:, cut]], axis=0)
    hylo, hyhi = neighbours(tall2(slice(sy - thin, sy)), tall2(slice(0, thin)), "gy")
    solid, sigma, replies = solid_steps(
        rim, state, (xlo, xhi, ylo, yhi), heat, (hxlo, hxhi, hylo, hyhi), code_col
    )
    returned = lax.all_to_all(
        replies.reshape(ndev, cap, sz), AXES, split_axis=0, concat_axis=0, tiled=True
    )
    fluid = fluid_step(fluid, fluid_rims(fluid), velocity, flux)
    force = stress(sigma, sx, sy)
    wall_next = unpack(dest, returned.reshape(total, sz)).reshape(cx, cy, row_len)
    return fluid, wall_next, solid, force


def solution(mesh):
    placed = (
        P("gx", "gy", None),
        P(None, "gx", "gy", None),
        P("gx", "gy", None),
        P("gx", "gy", None),
        P(("gx", "gy"), None, None),
        P(("gx", "gy"), None),
        P("gx", "gy", None),
        P("gx", "gy", None),
    )
    return jax.shard_map(
        body,
        mesh=mesh,
        in_specs=placed,
        out_specs=(
            P("gx", "gy", None),
            P("gx", "gy", None),
            P("gx", "gy", None),
            P(None, "gx", "gy", None),
        ),
        check_vma=False,
    )
```

time: 271 us -> 205 us (0.76)
  the two profiles are of different devices: /device:TPU:11 before, /device:TPU:13 now
where the time goes in v1:
time: 205 us; the launch traced here: 204 us
  waiting for transfers between devices  63.9 us (31%)
  starting transfers between devices  52.8 us (26%)
  Pallas kernels  49.5 us (24%)
  local copies, waits for them, and re-layouts  20 us (10%)
  blocking collectives  10.8 us (5%)
  other arithmetic  5.82 us (3%)
    ppermute x16, waiting for transfers between devices, neighbours(): return (lax.ppermute(before, axis, up), lax.ppermute(after, axis, down))  63.9 us
    ppermute x16, starting transfers between devices, neighbours(): return (lax.ppermute(before, axis, up), lax.ppermute(after, axis, down))  44.4 us
    pallas_call x2, Pallas kernels, fluid_step(): pl.pallas_call(fluid_kernel, grid=(cx,), in_specs=[pl.BlockSpec(plane, la...  22.3 us
    unnamed x44, local copies, waits for them, and re-layouts  14.6 us
    pallas_call x1, Pallas kernels, solid_steps(): pl.pallas_call(functools.partial(solid_kernel, rim), in_specs=[vmem] * 11...  12.7 us
    all_to_all x1, blocking collectives, body(): lax.all_to_all(meta.reshape(ndev, cap), AXES, split_axis=0, concat_axis=0...  10.8 us
    pallas_call x1, Pallas kernels, pack(): pl.pallas_call(functools.partial(pack_kernel, ndev, cap), grid=(1,), in_s...  7.13 us
    all_to_all x1, starting transfers between devices, body(): lax.all_to_all(outgoing.reshape(ndev, cap, row_len), AXES, split_axis=0,...  5.08 us
  transfers between devices with their start and end apart: 18, of which 6 were waited for; matrix products, arithmetic and copies ran while one was open for 5% of the time, Pallas kernels for 13%

profile of v1, /device:TPU:13, one launch (start us, length us, event | category | flops | bytes accessed | tf_op | source)
XLA Modules:
  0.0 203.9 jit_solution(4466204799052370712)
XLA Ops:
  0.6 0.0 copy-start
  0.6 2.2 %copy-done = f32[16,64,1024]{2,1,0:T(8,128)S(1)} copy-done((f32[16,64,1024]{2,1,0:T(8,128)S(1)}, f32[16,64,1024]{2,1,0:T(8,128)}, u32[]{:S(2)}) %copy-start) | copy-done | bytes 4194328
  2.8 1.0 copy-done.13
  3.9 1.0 copy-done.14
  4.9 0.7 copy-done.15
  5.6 0.7 copy-done.16
  6.3 7.1 %pack.1 = (f32[3072,128]{1,0:T(8,128)}, f32[1,3072]{1,0:T(1,128)S(1)}, f32[16,64,128]{2,1,0:T(8,128)S(1)}, s32[1,1024]{1,0:T(1,128)S(1)}) custom-call(s32[1,1024]{1,0:T(1,128)S(1)} %bitcast.20, s32[1,1024]{1,0:T(1,128)S(1)} %copy-done.16, f32[16,64,1024]{2,1,0:T(8,128)S(1)} %copy-done, f32[16,64,128]{2,1,0:T(8,128)S(1)} %copy-done.13, ...), custom_call_target="tpu_custom_call" | custom-call | flops 1610612736 | bytes 2621440 | tf_op jit(solution)/shard_map/pack/pallas_call | solution.py:102
  13.4 0.6 copy-done.11
  14.0 0.5 broadcast.8
  14.5 0.7 reduce.8
  15.2 0.1 all_to_all.13
  15.3 10.8 %all_to_all.19 = f32[32,1,96]{2,1,0:T(1,128)S(1)} all-to-all(f32[32,1,96]{2,1,0:T(1,128)S(1)} %bitcast.26), channel_id=1, replica_groups=mesh['gx'=8,'gy'=4] {'gx','gy'}, dimensions={0} | all-to-all | bytes 24576 | tf_op jit(solution)/shard_map/all_to_all | solution.py:409
  26.1 5.1 %all-to-all-start = ((f32[32,96,128]{2,1,0:T(8,128)}), f32[32,96,128]{2,1,0:T(8,128)S(1)}, u32[]{:S(2)}, u32[]{:S(2)}) async-start(f32[32,96,128]{2,1,0:T(8,128)} %bitcast.3), calls=%async_computation | async-start | bytes 3145728 | tf_op jit(solution)/shard_map/all_to_all | solution.py:406
  31.2 0.7 fusion.1
  32.0 2.3 %collective-permute-start.9 = (f32[2,5,32,128]{3,2,1,0:T(8,128)}, f32[2,5,32,128]{3,2,1,0:T(8,128)S(1)}, u32[]{:S(2)}, u32[]{:S(2)}) collective-permute-start(f32[2,5,32,128]{3,2,1,0:T(8,128)} %get-tuple-element.28), channel_id=1, source_target_pairs={{4,0},{8,4},{12,8},{16,12},{20,16},{24,20},{28,24},{5,1},{9,5},{13... | collective-permute-start | bytes 491528 | tf_op jit(solution)/shard_map/ppermute | solution.py:46
  34.3 3.3 %collective-permute-start.8 = (f32[2,5,32,128]{3,2,1,0:T(8,128)}, f32[2,5,32,128]{3,2,1,0:T(8,128)S(1)}, u32[]{:S(2)}, u32[]{:S(2)}) collective-permute-start(f32[2,5,32,128]{3,2,1,0:T(8,128)} %get-tuple-element.29), channel_id=1, source_target_pairs={{0,4},{4,8},{8,12},{12,16},{16,20},{20,24},{24,28},{1,5},{5,9},{9,... | collective-permute-start | bytes 491528 | tf_op jit(solution)/shard_map/ppermute | solution.py:46
  37.6 0.7 reduce.9
  38.3 0.1 reshape.46.code_ref
  38.4 30.9 %collective-permute-done.9.xhi_ref = f32[2,5,32,128]{3,2,1,0:T(8,128)S(1)} collective-permute-done((f32[2,5,32,128]{3,2,1,0:T(8,128)}, f32[2,5,32,128]{3,2,1,0:T(8,128)S(1)}, u32[]{:S(2)}, u32[]{:S(2)}) %collective-permute-start.9) | collective-permute-done | bytes 163872 | tf_op jit(solution)/shard_map/ppermute | solution.py:46
  69.3 0.0 copy-start.3
  69.3 0.7 pad_maximum_fusion.1
  70.0 2.8 %collective-permute-start.10 = (f32[2,26,5,128]{3,2,1,0:T(8,128)}, f32[2,26,5,128]{3,2,1,0:T(8,128)S(1)}, u32[]{:S(2)}, u32[]{:S(2)}) collective-permute-start(f32[2,26,5,128]{3,2,1,0:T(8,128)} %pad_maximum_fusion.1), channel_id=1, source_target_pairs={{0,1},{1,2},{2,3},{4,5},{5,6},{6,7},{8,9},{9,10},{10,11},{12,13},{... | collective-permute-start | bytes 399368 | tf_op jit(solution)/shard_map/ppermute | solution.py:46
  72.9 0.7 pad_maximum_fusion.2
  73.6 3.3 %collective-permute-start.11 = (f32[2,26,5,128]{3,2,1,0:T(8,128)}, f32[2,26,5,128]{3,2,1,0:T(8,128)S(1)}, u32[]{:S(2)}, u32[]{:S(2)}) collective-permute-start(f32[2,26,5,128]{3,2,1,0:T(8,128)} %pad_maximum_fusion.2), channel_id=1, source_target_pairs={{1,0},{2,1},{3,2},{5,4},{6,5},{7,6},{9,8},{10,9},{11,10},{13,12},{... | collective-permute-start | bytes 399368 | tf_op jit(solution)/shard_map/ppermute | solution.py:46
  76.9 1.8 heat_sum.1
  78.8 3.0 %collective-permute-start.12 = (f32[4,32,128]{2,1,0:T(8,128)S(1)}, f32[4,32,128]{2,1,0:T(8,128)S(1)}, u32[]{:S(2)}, u32[]{:S(2)}) collective-permute-start(f32[4,32,128]{2,1,0:T(8,128)S(1)} %bitcast.28), channel_id=1, source_target_pairs={{0,4},{4,8},{8,12},{12,16},{16,20},{20,24},{24,28},{1,5},{5,9},{9,... | collective-permute-start | bytes 196616 | tf_op jit(solution)/shard_map/ppermute | solution.py:46
  81.8 1.9 collective-permute-start.13
  83.7 3.6 %collective-permute-done.13.hxhi_ref = f32[4,32,128]{2,1,0:T(8,128)S(1)} collective-permute-done((f32[4,32,128]{2,1,0:T(8,128)S(1)}, f32[4,32,128]{2,1,0:T(8,128)S(1)}, u32[]{:S(2)}, u32[]{:S(2)}) %collective-permute-start.13) | collective-permute-done | bytes 65568 | tf_op jit(solution)/shard_map/ppermute | solution.py:46
  87.4 0.6 pad_maximum_fusion.3
  88.0 2.6 %collective-permute-start.14 = (f32[24,4,128]{2,1,0:T(4,128)}, f32[24,4,128]{2,1,0:T(4,128)}, u32[]{:S(2)}, u32[]{:S(2)}) collective-permute-start(f32[24,4,128]{2,1,0:T(4,128)} %pad_maximum_fusion.3), channel_id=1, source_target_pairs={{0,1},{1,2},{2,3},{4,5},{5,6},{6,7},{8,9},{9,10},{10,11},{12,13},{... | collective-permute-start | bytes 147464 | tf_op jit(solution)/shard_map/ppermute | solution.py:46
  90.6 0.6 pad_maximum_fusion.4
  91.2 3.5 %collective-permute-start.15 = (f32[24,4,128]{2,1,0:T(4,128)}, f32[24,4,128]{2,1,0:T(4,128)}, u32[]{:S(2)}, u32[]{:S(2)}) collective-permute-start(f32[24,4,128]{2,1,0:T(4,128)} %pad_maximum_fusion.4), channel_id=1, source_target_pairs={{1,0},{2,1},{3,2},{5,4},{6,5},{7,6},{9,8},{10,9},{11,10},{13,12},{... | collective-permute-start | bytes 147464 | tf_op jit(solution)/shard_map/ppermute | solution.py:46
  94.8 1.0 pad_maximum_fusion.state_ref
  95.8 2.2 %reshape.52.code_ref = f32[3072,1]{1,0:T(8,128)S(1)} reshape(f32[32,96]{1,0:T(8,128)} %bitcast.25) | data formatting | bytes 24576 | tf_op jit(solution)/shard_map/reshape | solution.py:411
  98.0 0.0 copy-start.5
  98.0 0.7 copy-done.5
  98.7 0.7 copy-done.7
  99.4 0.9 copy-done.4
  100.3 0.9 copy-done.6
  101.2 0.9 copy-done.8
  102.2 0.8 copy-done.10
  103.0 12.7 %solid_steps.1 = (f32[16,32,128]{2,1,0:T(8,128)}, f32[18,48,128]{2,1,0:T(8,128)S(1)}, f32[3072,128]{1,0:T(8,128)S(1)}) custom-call(f32[2,16,32,128]{3,2,1,0:T(8,128)S(1)} %pad_maximum_fusion.state_ref, f32[2,5,32,128]{3,2,1,0:T(8,128)S(1)} %copy-done.4, f32[2,5,32,128]{3,2,1,0:T(8,128)S(1)} %collective-permute-done.9.xhi_ref, ...), custom_call_target="tpu_custom_call" | custom-call | flops 805306368 | bytes 1572864 | tf_op jit(solution)/shard_map/solid_steps/pallas_call | solution.py:241
  115.7 1.1 copy-done.2
  116.9 3.3 %all-to-all-start.2 = ((f32[32,96,128]{2,1,0:T(8,128)}), f32[32,96,128]{2,1,0:T(8,128)}, u32[]{:S(2)}, u32[]{:S(2)}) async-start(f32[32,96,128]{2,1,0:T(8,128)} %bitcast.16), calls=%async_computation.2 | async-start | bytes 3145728 | tf_op jit(solution)/shard_map/all_to_all | solution.py:428
  120.2 1.1 fusion.7
  121.2 2.2 %collective-permute-start.1 = (f32[1,64,1024]{2,1,0:T(8,128)S(1)}, f32[1,64,1024]{2,1,0:T(8,128)S(1)}, u32[]{:S(2)}, u32[]{:S(2)}) collective-permute-start(f32[1,64,1024]{2,1,0:T(8,128)S(1)} %get-tuple-element.24), channel_id=1, source_target_pairs={{4,0},{8,4},{12,8},{16,12},{20,16},{24,20},{28,24},{5,1},{9,5},{13... | collective-permute-start | bytes 786440 | tf_op jit(solution)/shard_map/ppermute | solution.py:46
  123.5 3.4 %collective-permute-start = (f32[1,64,1024]{2,1,0:T(8,128)S(1)}, f32[1,64,1024]{2,1,0:T(8,128)S(1)}, u32[]{:S(2)}, u32[]{:S(2)}) collective-permute-start(f32[1,64,1024]{2,1,0:T(8,128)S(1)} %get-tuple-element.25), channel_id=1, source_target_pairs={{0,4},{4,8},{8,12},{12,16},{16,20},{20,24},{24,28},{1,5},{5,9},{9,... | collective-permute-start | bytes 786440 | tf_op jit(solution)/shard_map/ppermute | solution.py:46
  126.8 1.3 fusion.6
  128.1 3.0 %collective-permute-start.3 = (f32[16,1,1024]{2,1,0:T(1,128)S(1)}, f32[16,1,1024]{2,1,0:T(1,128)S(1)}, u32[]{:S(2)}, u32[]{:S(2)}) collective-permute-start(f32[16,1,1024]{2,1,0:T(1,128)S(1)} %get-tuple-element.22), channel_id=1, source_target_pairs={{1,0},{2,1},{3,2},{5,4},{6,5},{7,6},{9,8},{10,9},{11,10},{13,12},{... | collective-permute-start | bytes 196616 | tf_op jit(solution)/shard_map/ppermute | solution.py:46
  131.2 2.3 %collective-permute-start.2 = (f32[16,1,1024]{2,1,0:T(1,128)S(1)}, f32[16,1,1024]{2,1,0:T(1,128)S(1)}, u32[]{:S(2)}, u32[]{:S(2)}) collective-permute-start(f32[16,1,1024]{2,1,0:T(1,128)S(1)} %get-tuple-element.23), channel_id=1, source_target_pairs={{0,1},{1,2},{2,3},{4,5},{5,6},{6,7},{8,9},{9,10},{10,11},{12,13},{... | collective-permute-start | bytes 196616 | tf_op jit(solution)/shard_map/ppermute | solution.py:46
  133.4 2.0 collective-permute-done.3.yhi_ref
  135.4 3.3 %collective-permute-done.2.ylo_ref = f32[16,1,1024]{2,1,0:T(1,128)S(1)} collective-permute-done((f32[16,1,1024]{2,1,0:T(1,128)S(1)}, f32[16,1,1024]{2,1,0:T(1,128)S(1)}, u32[]{:S(2)}, u32[]{:S(2)}) %collective-permute-start.2) | collective-permute-done | bytes 65568 | tf_op jit(solution)/shard_map/ppermute | solution.py:46
  138.7 20.1 %collective-permute-done.1.xhi_ref = f32[1,64,1024]{2,1,0:T(8,128)S(1)} collective-permute-done((f32[1,64,1024]{2,1,0:T(8,128)S(1)}, f32[1,64,1024]{2,1,0:T(8,128)S(1)}, u32[]{:S(2)}, u32[]{:S(2)}) %collective-permute-start.1) | collective-permute-done | bytes 262176 | tf_op jit(solution)/shard_map/ppermute | solution.py:46
  158.8 2.2 %copy-done.1 = f32[16,64,1024]{2,1,0:T(8,128)S(1)} copy-done((f32[16,64,1024]{2,1,0:T(8,128)S(1)}, f32[16,64,1024]{2,1,0:T(8,128)}, u32[]{:S(2)}) %copy-start.1) | copy-done | bytes 4194328
  161.0 12.4 %fluid_step.2.before_ref.here_ref.after_ref = f32[16,64,1024]{2,1,0:T(8,128)S(1)} custom-call(f32[16,64,1024]{2,1,0:T(8,128)S(1)} %copy-done.1, f32[16,64,1024]{2,1,0:T(8,128)S(1)} %copy-done.1, f32[16,64,1024]{2,1,0:T(8,128)S(1)} %copy-done.1, f32[1,64,1024]{2,1,0:T(8,128)S(1)} %collective-permute-done.xlo_ref, ...), custom_call_target="tpu_custom_call" | custom-call | flops 41943040 | bytes 23068672 | tf_op jit(solution)/shard_map/fluid_step/pallas_call | solution.py:363
  173.5 1.9 collective-permute-start.5
  175.4 3.6 %collective-permute-start.4 = (f32[1,64,1024]{2,1,0:T(8,128)S(1)}, f32[1,64,1024]{2,1,0:T(8,128)S(1)}, u32[]{:S(2)}, u32[]{:S(2)}) collective-permute-start(f32[1,64,1024]{2,1,0:T(8,128)S(1)} %get-tuple-element.21), channel_id=1, source_target_pairs={{0,4},{4,8},{8,12},{12,16},{16,20},{20,24},{24,28},{1,5},{5,9},{9,... | collective-permute-start | bytes 786440 | tf_op jit(solution)/shard_map/ppermute | solution.py:46
  179.0 0.1 fusion.4
  179.1 3.2 %collective-permute-start.7 = (f32[16,1,1024]{2,1,0:T(1,128)S(1)}, f32[16,1,1024]{2,1,0:T(1,128)S(1)}, u32[]{:S(2)}, u32[]{:S(2)}) collective-permute-start(f32[16,1,1024]{2,1,0:T(1,128)S(1)} %get-tuple-element.18), channel_id=1, source_target_pairs={{1,0},{2,1},{3,2},{5,4},{6,5},{7,6},{9,8},{10,9},{11,10},{13,12},{... | collective-permute-start | bytes 196616 | tf_op jit(solution)/shard_map/ppermute | solution.py:46
  182.3 2.1 %collective-permute-start.6 = (f32[16,1,1024]{2,1,0:T(1,128)S(1)}, f32[16,1,1024]{2,1,0:T(1,128)S(1)}, u32[]{:S(2)}, u32[]{:S(2)}) collective-permute-start(f32[16,1,1024]{2,1,0:T(1,128)S(1)} %get-tuple-element.19), channel_id=1, source_target_pairs={{0,1},{1,2},{2,3},{4,5},{5,6},{6,7},{8,9},{9,10},{10,11},{12,13},{... | collective-permute-start | bytes 196616 | tf_op jit(solution)/shard_map/ppermute | solution.py:46
  184.5 4.0 %collective-permute-done.6.ylo_ref = f32[16,1,1024]{2,1,0:T(1,128)S(1)} collective-permute-done((f32[16,1,1024]{2,1,0:T(1,128)S(1)}, f32[16,1,1024]{2,1,0:T(1,128)S(1)}, u32[]{:S(2)}, u32[]{:S(2)}) %collective-permute-start.6) | collective-permute-done | bytes 65568 | tf_op jit(solution)/shard_map/ppermute | solution.py:46
  188.5 9.9 %fluid_step.3 = f32[16,64,1024]{2,1,0:T(8,128)} custom-call(f32[16,64,1024]{2,1,0:T(8,128)S(1)} %fluid_step.2.before_ref.here_ref.after_ref, f32[16,64,1024]{2,1,0:T(8,128)S(1)} %fluid_step.2.before_ref.here_ref.after_ref, f32[16,64,1024]{2,1,0:T(8,128)S(1)} %fluid_step.2.before_ref.here_ref.after_ref, f32[1,64,1024]{2,1,0:T(8,128)S(1)} %collective-permute-done.4.xlo_ref, ...), custom_call_target="tpu_custom_call" | custom-call | flops 41943040 | bytes 23068672 | tf_op jit(solution)/shard_map/fluid_step/pallas_call | solution.py:363
  198.4 2.1 %stress.1 = f32[3,16,32,128]{3,2,1,0:T(8,128)} custom-call(f32[18,48,128]{2,1,0:T(8,128)S(1)} %get-tuple-element.17.sigma_ref), custom_call_target="tpu_custom_call" | custom-call | flops 655360 | bytes 1048576 | tf_op jit(solution)/shard_map/stress/pallas_call | solution.py:281
  200.5 3.4 %unpack.1 = f32[1024,128]{1,0:T(8,128)} custom-call(s32[1,1024]{1,0:T(1,128)S(1)} %copy-done.12, f32[3072,128]{1,0:T(8,128)} %bitcast.10.back_ref), custom_call_target="tpu_custom_call" | custom-call | flops 131072 | bytes 1048576 | tf_op jit(solution)/shard_map/unpack/pallas_call | solution.py:307
  (49 shorter events, 0.2 us)
Async XLA Ops:
  0.6 2.2 %copy-start = (f32[16,64,1024]{2,1,0:T(8,128)S(1)}, f32[16,64,1024]{2,1,0:T(8,128)}, u32[]{:S(2)}) copy-start(f32[16,64,1024]{2,1,0:T(8,128)} %after_ref.1) | copy-start | bytes 12582916
  2.8 1.0 copy-start.13
  3.9 1.0 copy-start.14
  4.9 0.7 copy-start.15
  5.6 0.7 copy-start.16
  6.3 24.9 %copy-start.18 = (s32[16,32,128]{2,1,0:T(8,128)S(1)}, s32[16,32,128]{2,1,0:T(8,128)}, u32[]{:S(2)}) copy-start(s32[16,32,128]{2,1,0:T(8,128)} %param.15) | copy-start | bytes 786436
  6.3 25.0 %copy-start.17 = (f32[16,32,128]{2,1,0:T(8,128)S(1)}, f32[16,32,128]{2,1,0:T(8,128)}, u32[]{:S(2)}) copy-start(f32[16,32,128]{2,1,0:T(8,128)} %param.14) | copy-start | bytes 786436
  13.4 0.6 copy-start.11
  26.1 12.3 %copy-start.19 = (f32[32,1,96]{2,1,0:T(1,128)}, f32[32,1,96]{2,1,0:T(1,128)S(1)}, u32[]{:S(2)}) copy-start(f32[32,1,96]{2,1,0:T(1,128)S(1)} %all_to_all.19) | copy-start | bytes 36868
  26.1 50.8 %all-to-all-start = ((f32[32,96,128]{2,1,0:T(8,128)}), f32[32,96,128]{2,1,0:T(8,128)S(1)}, u32[]{:S(2)}, u32[]{:S(2)}) async-start(f32[32,96,128]{2,1,0:T(8,128)} %bitcast.3), calls=%async_computation | async-start | bytes 3145728 | tf_op jit(solution)/shard_map/all_to_all | solution.py:406
  32.0 37.3 %collective-permute-start.9 = (f32[2,5,32,128]{3,2,1,0:T(8,128)}, f32[2,5,32,128]{3,2,1,0:T(8,128)S(1)}, u32[]{:S(2)}, u32[]{:S(2)}) collective-permute-start(f32[2,5,32,128]{3,2,1,0:T(8,128)} %get-tuple-element.28), channel_id=1, source_target_pairs={{4,0},{8,4},{12,8},{16,12},{20,16},{24,20},{28,24},{5,1},{9,5},{13... | collective-permute-start | bytes 491528 | tf_op jit(solution)/shard_map/ppermute | solution.py:46
  34.3 35.0 %collective-permute-start.8 = (f32[2,5,32,128]{3,2,1,0:T(8,128)}, f32[2,5,32,128]{3,2,1,0:T(8,128)S(1)}, u32[]{:S(2)}, u32[]{:S(2)}) collective-permute-start(f32[2,5,32,128]{3,2,1,0:T(8,128)} %get-tuple-element.29), channel_id=1, source_target_pairs={{0,4},{4,8},{8,12},{12,16},{16,20},{20,24},{24,28},{1,5},{5,9},{9,... | collective-permute-start | bytes 491528 | tf_op jit(solution)/shard_map/ppermute | solution.py:46
  69.3 26.5 %copy-start.3 = (f32[2,5,32,128]{3,2,1,0:T(8,128)}, f32[2,5,32,128]{3,2,1,0:T(8,128)S(1)}, u32[]{:S(2)}) copy-start(f32[2,5,32,128]{3,2,1,0:T(8,128)S(1)} %collective-permute-done.8.xlo_ref) | copy-start | bytes 491524
  70.0 28.0 %collective-permute-start.10 = (f32[2,26,5,128]{3,2,1,0:T(8,128)}, f32[2,26,5,128]{3,2,1,0:T(8,128)S(1)}, u32[]{:S(2)}, u32[]{:S(2)}) collective-permute-start(f32[2,26,5,128]{3,2,1,0:T(8,128)} %pad_maximum_fusion.1), channel_id=1, source_target_pairs={{0,1},{1,2},{2,3},{4,5},{5,6},{6,7},{8,9},{9,10},{10,11},{12,13},{... | collective-permute-start | bytes 399368 | tf_op jit(solution)/shard_map/ppermute | solution.py:46
  73.6 25.1 %collective-permute-start.11 = (f32[2,26,5,128]{3,2,1,0:T(8,128)}, f32[2,26,5,128]{3,2,1,0:T(8,128)S(1)}, u32[]{:S(2)}, u32[]{:S(2)}) collective-permute-start(f32[2,26,5,128]{3,2,1,0:T(8,128)} %pad_maximum_fusion.2), channel_id=1, source_target_pairs={{1,0},{2,1},{3,2},{5,4},{6,5},{7,6},{9,8},{10,9},{11,10},{13,12},{... | collective-permute-start | bytes 399368 | tf_op jit(solution)/shard_map/ppermute | solution.py:46
  78.8 4.9 %collective-permute-start.12 = (f32[4,32,128]{2,1,0:T(8,128)S(1)}, f32[4,32,128]{2,1,0:T(8,128)S(1)}, u32[]{:S(2)}, u32[]{:S(2)}) collective-permute-start(f32[4,32,128]{2,1,0:T(8,128)S(1)} %bitcast.28), channel_id=1, source_target_pairs={{0,4},{4,8},{8,12},{12,16},{16,20},{20,24},{24,28},{1,5},{5,9},{9,... | collective-permute-start | bytes 196616 | tf_op jit(solution)/shard_map/ppermute | solution.py:46
  81.8 5.6 %collective-permute-start.13 = (f32[4,32,128]{2,1,0:T(8,128)S(1)}, f32[4,32,128]{2,1,0:T(8,128)S(1)}, u32[]{:S(2)}, u32[]{:S(2)}) collective-permute-start(f32[4,32,128]{2,1,0:T(8,128)S(1)} %bitcast.27), channel_id=1, source_target_pairs={{4,0},{8,4},{12,8},{16,12},{20,16},{24,20},{28,24},{5,1},{9,5},{13... | collective-permute-start | bytes 196616 | tf_op jit(solution)/shard_map/ppermute | solution.py:46
  87.3 8.5 %copy-start.9 = (f32[4,32,128]{2,1,0:T(8,128)}, f32[4,32,128]{2,1,0:T(8,128)S(1)}, u32[]{:S(2)}) copy-start(f32[4,32,128]{2,1,0:T(8,128)S(1)} %collective-permute-done.13.hxhi_ref) | copy-start | bytes 196612
  88.0 11.4 %collective-permute-start.14 = (f32[24,4,128]{2,1,0:T(4,128)}, f32[24,4,128]{2,1,0:T(4,128)}, u32[]{:S(2)}, u32[]{:S(2)}) collective-permute-start(f32[24,4,128]{2,1,0:T(4,128)} %pad_maximum_fusion.3), channel_id=1, source_target_pairs={{0,1},{1,2},{2,3},{4,5},{5,6},{6,7},{8,9},{9,10},{10,11},{12,13},{... | collective-permute-start | bytes 147464 | tf_op jit(solution)/shard_map/ppermute | solution.py:46
  91.2 8.1 %collective-permute-start.15 = (f32[24,4,128]{2,1,0:T(4,128)}, f32[24,4,128]{2,1,0:T(4,128)}, u32[]{:S(2)}, u32[]{:S(2)}) collective-permute-start(f32[24,4,128]{2,1,0:T(4,128)} %pad_maximum_fusion.4), channel_id=1, source_target_pairs={{1,0},{2,1},{3,2},{5,4},{6,5},{7,6},{9,8},{10,9},{11,10},{13,12},{... | collective-permute-start | bytes 147464 | tf_op jit(solution)/shard_map/ppermute | solution.py:46
  98.0 0.7 copy-start.5
  98.7 0.7 copy-start.7
  99.4 0.9 copy-start.4
  100.3 0.9 copy-start.6
  101.2 0.9 copy-start.8
  102.2 0.8 copy-start.10
  115.7 1.1 copy-start.2
  116.9 71.6 %slice-start = ((s8[6291456]{0:T(1024)(128)(4,1)}), s8[2097152]{0:T(1024)(128)(4,1)S(1)}, s32[]{:S(2)}) async-start(s8[6291456]{0:T(1024)(128)(4,1)} %bitcast.14), calls=%async_computation.3 | async-start | bytes 4194304
  116.9 83.7 %all-to-all-start.2 = ((f32[32,96,128]{2,1,0:T(8,128)}), f32[32,96,128]{2,1,0:T(8,128)}, u32[]{:S(2)}, u32[]{:S(2)}) async-start(f32[32,96,128]{2,1,0:T(8,128)} %bitcast.16), calls=%async_computation.2 | async-start | bytes 3145728 | tf_op jit(solution)/shard_map/all_to_all | solution.py:428
  121.2 37.6 %collective-permute-start.1 = (f32[1,64,1024]{2,1,0:T(8,128)S(1)}, f32[1,64,1024]{2,1,0:T(8,128)S(1)}, u32[]{:S(2)}, u32[]{:S(2)}) collective-permute-start(f32[1,64,1024]{2,1,0:T(8,128)S(1)} %get-tuple-element.24), channel_id=1, source_target_pairs={{4,0},{8,4},{12,8},{16,12},{20,16},{24,20},{28,24},{5,1},{9,5},{13... | collective-permute-start | bytes 786440 | tf_op jit(solution)/shard_map/ppermute | solution.py:46
  123.5 35.4 %collective-permute-start = (f32[1,64,1024]{2,1,0:T(8,128)S(1)}, f32[1,64,1024]{2,1,0:T(8,128)S(1)}, u32[]{:S(2)}, u32[]{:S(2)}) collective-permute-start(f32[1,64,1024]{2,1,0:T(8,128)S(1)} %get-tuple-element.25), channel_id=1, source_target_pairs={{0,4},{4,8},{8,12},{12,16},{16,20},{20,24},{24,28},{1,5},{5,9},{9,... | collective-permute-start | bytes 786440 | tf_op jit(solution)/shard_map/ppermute | solution.py:46
  128.1 7.3 %collective-permute-start.3 = (f32[16,1,1024]{2,1,0:T(1,128)S(1)}, f32[16,1,1024]{2,1,0:T(1,128)S(1)}, u32[]{:S(2)}, u32[]{:S(2)}) collective-permute-start(f32[16,1,1024]{2,1,0:T(1,128)S(1)} %get-tuple-element.22), channel_id=1, source_target_pairs={{1,0},{2,1},{3,2},{5,4},{6,5},{7,6},{9,8},{10,9},{11,10},{13,12},{... | collective-permute-start | bytes 196616 | tf_op jit(solution)/shard_map/ppermute | solution.py:46
  131.2 7.5 %collective-permute-start.2 = (f32[16,1,1024]{2,1,0:T(1,128)S(1)}, f32[16,1,1024]{2,1,0:T(1,128)S(1)}, u32[]{:S(2)}, u32[]{:S(2)}) collective-permute-start(f32[16,1,1024]{2,1,0:T(1,128)S(1)} %get-tuple-element.23), channel_id=1, source_target_pairs={{0,1},{1,2},{2,3},{4,5},{5,6},{6,7},{8,9},{9,10},{10,11},{12,13},{... | collective-permute-start | bytes 196616 | tf_op jit(solution)/shard_map/ppermute | solution.py:46
  158.8 2.2 %copy-start.1 = (f32[16,64,1024]{2,1,0:T(8,128)S(1)}, f32[16,64,1024]{2,1,0:T(8,128)}, u32[]{:S(2)}) copy-start(f32[16,64,1024]{2,1,0:T(8,128)} %after_ref.1) | copy-start | bytes 12582916
  161.0 27.5 %slice-start.1 = ((s8[6291456]{0:T(1024)(128)(4,1)}), s8[4194304]{0:T(1024)(128)(4,1)S(1)}, s32[]{:S(2)}) async-start(s8[6291456]{0:T(1024)(128)(4,1)} %bitcast.14), calls=%async_computation.4 | async-start | bytes 8388608
  173.5 15.0 %collective-permute-start.5 = (f32[1,64,1024]{2,1,0:T(8,128)S(1)}, f32[1,64,1024]{2,1,0:T(8,128)S(1)}, u32[]{:S(2)}, u32[]{:S(2)}) collective-permute-start(f32[1,64,1024]{2,1,0:T(8,128)S(1)} %get-tuple-element.20), channel_id=1, source_target_pairs={{4,0},{8,4},{12,8},{16,12},{20,16},{24,20},{28,24},{5,1},{9,5},{13... | collective-permute-start | bytes 786440 | tf_op jit(solution)/shard_map/ppermute | solution.py:46
  175.4 13.1 %collective-permute-start.4 = (f32[1,64,1024]{2,1,0:T(8,128)S(1)}, f32[1,64,1024]{2,1,0:T(8,128)S(1)}, u32[]{:S(2)}, u32[]{:S(2)}) collective-permute-start(f32[1,64,1024]{2,1,0:T(8,128)S(1)} %get-tuple-element.21), channel_id=1, source_target_pairs={{0,4},{4,8},{8,12},{12,16},{16,20},{20,24},{24,28},{1,5},{5,9},{9,... | collective-permute-start | bytes 786440 | tf_op jit(solution)/shard_map/ppermute | solution.py:46
  179.1 5.3 %collective-permute-start.7 = (f32[16,1,1024]{2,1,0:T(1,128)S(1)}, f32[16,1,1024]{2,1,0:T(1,128)S(1)}, u32[]{:S(2)}, u32[]{:S(2)}) collective-permute-start(f32[16,1,1024]{2,1,0:T(1,128)S(1)} %get-tuple-element.18), channel_id=1, source_target_pairs={{1,0},{2,1},{3,2},{5,4},{6,5},{7,6},{9,8},{10,9},{11,10},{13,12},{... | collective-permute-start | bytes 196616 | tf_op jit(solution)/shard_map/ppermute | solution.py:46
  182.3 18.2 %copy-start.12 = (s32[1,1024]{1,0:T(1,128)S(1)}, s32[1,1024]{1,0:T(1,128)}, u32[]{:S(2)}) copy-start(s32[1,1024]{1,0:T(1,128)} %copy-done.11) | copy-start | bytes 12292
  182.3 6.1 %collective-permute-start.6 = (f32[16,1,1024]{2,1,0:T(1,128)S(1)}, f32[16,1,1024]{2,1,0:T(1,128)S(1)}, u32[]{:S(2)}, u32[]{:S(2)}) collective-permute-start(f32[16,1,1024]{2,1,0:T(1,128)S(1)} %get-tuple-element.19), channel_id=1, source_target_pairs={{0,1},{1,2},{2,3},{4,5},{5,6},{6,7},{8,9},{9,10},{10,11},{12,13},{... | collective-permute-start | bytes 196616 | tf_op jit(solution)/shard_map/ppermute | solution.py:46

commit v2 on v1

--- a/solution.py
+++ b/solution.py
@@ -17,7 +17,7 @@
 modulus_table = (0.5, 1.0, 1.6, 2.4)
 F32 = jnp.float32
 BF16 = jnp.bfloat16
-VMEM_LIMIT = 40 * 1024 * 1024
+VMEM_LIMIT = 60 * 1024 * 1024
 AXES = ("gx", "gy")
 
 
@@ -46,10 +46,17 @@
     return lax.ppermute(before, axis, up), lax.ppermute(after, axis, down)
 
 
-def pack_kernel(ndev, cap, owner_ref, slot_ref, temp_ref, old_ref, mask_ref,
-                out_ref, meta_ref, flux_ref, dest_ref, rhs_ref):
+def whole(shape):
+    return pl.BlockSpec(shape, lambda i: (0,) * len(shape))
+
+
+anywhere = pl.BlockSpec(memory_space=pl.ANY)
+
+
+def pack_kernel(cap, owner_ref, slot_ref, temp_ref, old_ref, mask_ref,
+                out_ref, flux_ref, dest_ref, rhs_ref, where_ref):
     rows = owner_ref.shape[1]
-    row_len = temp_ref.shape[2]
+    ndev, tall, row_len = out_ref.shape
     flux = mask_ref[...].astype(F32) * film_coef * (temp_ref[...] - old_ref[...])
     flux_ref[...] = flux
     high, low = halves(flux.reshape(rows, row_len))
@@ -61,46 +68,51 @@
         <= lax.broadcasted_iota(jnp.int32, (lane, lane), 1)
     )
     names = lax.broadcasted_iota(jnp.int32, (ndev, lane), 0)
+    steps = lax.broadcasted_iota(jnp.int32, (lane, lane), 0)
     carry = jnp.zeros((ndev, 1), F32)
+    codes = jnp.zeros((2 * ndev, lane), F32)
     for chunk in range(rows // lane):
         cols = slice(chunk * lane, (chunk + 1) * lane)
         own = owner_ref[:, cols]
         hit = jnp.where(names == own, 1.0, 0.0)
         ranks = jnp.dot(hit.astype(BF16), tri, preferred_element_type=F32) + carry
         carry = ranks[:, lane - 1:]
-        place = jnp.sum(hit * ranks, axis=0, keepdims=True) - 1.0
-        dest_ref[:, cols] = own * cap + place.astype(jnp.int32)
-    dest = dest_ref[...]
-    code = slot_ref[...] + 1
-    pieces = jnp.concatenate(
-        [(code // 32).astype(F32), (code % 32).astype(F32), jnp.zeros((6, rows), F32)], axis=0
-    ).astype(BF16)
-    block = 256
+        place = jnp.sum(hit * ranks, axis=0, keepdims=True).astype(jnp.int32) - 1
+        dest_ref[:, cols] = own * cap + place
+        where_ref[:, cols] = own * tall + place
+        code = slot_ref[:, cols] + 1
+        pieces = jnp.concatenate(
+            [hit * (code // 32).astype(F32), hit * (code % 32).astype(F32)], axis=0
+        ).astype(BF16)
+        codes = codes + lax.dot_general(
+            pieces, ones_where(steps == place), (((1,), (1,)), ((), ())),
+            preferred_element_type=F32,
+        )
+    where = where_ref[...]
+    group = max(1, 256 // tall)
+    block = group * tall
 
     def step(index, none):
-        base = pl.multiple_of(index * block, block)
+        base = index * block
         pick = ones_where(
-            lax.broadcasted_iota(jnp.int32, (block, rows), 0) + base == dest
+            lax.broadcasted_iota(jnp.int32, (block, rows), 0) + base == where
         )
         both = jnp.dot(pick, rhs_ref[...], preferred_element_type=F32)
-        out_ref[pl.ds(base, block), :] = both[:, :row_len] + both[:, row_len:]
-        names2 = lax.dot_general(
-            pieces, pick, (((1,), (1,)), ((), ())), preferred_element_type=F32
-        )
-        meta_ref[:, pl.ds(base, block)] = names2[0:1] * 32.0 + names2[1:2]
+        lines = both[:, :row_len] + both[:, row_len:]
+        out_ref[pl.ds(index * group, group)] = lines.reshape(group, tall, row_len)
         return none
 
-    lax.fori_loop(0, ndev * cap // block, step, 0)
+    lax.fori_loop(0, ndev // group, step, 0)
+    out_ref[:, cap, :] = codes[:ndev] * 32.0 + codes[ndev:]
 
 
 def pack(owner, slot, temp, old, mask, ndev, cap):
     cx, cy, _ = temp.shape
     row_len = old.shape[2]
     rows = cx * cy
-    total = ndev * cap
-    whole = lambda shape: pl.BlockSpec(shape, lambda i: (0,) * len(shape))
-    return pl.pallas_call(
-        functools.partial(pack_kernel, ndev, cap),
+    tall = cap + 8
+    return pl.pallas_call(
+        functools.partial(pack_kernel, cap),
         grid=(1,),
         in_specs=[
             whole((1, rows)),
@@ -110,55 +122,69 @@
             whole((cx, cy, row_len)),
         ],
         out_specs=[
-            whole((total, row_len)),
-            whole((1, total)),
+            whole((ndev, tall, row_len)),
             whole((cx, cy, row_len)),
             whole((1, rows)),
         ],
         out_shape=[
-            jax.ShapeDtypeStruct((total, row_len), F32),
-            jax.ShapeDtypeStruct((1, total), F32),
+            jax.ShapeDtypeStruct((ndev, tall, row_len), F32),
             jax.ShapeDtypeStruct((cx, cy, row_len), F32),
             jax.ShapeDtypeStruct((1, rows), jnp.int32),
         ],
-        scratch_shapes=[pltpu.VMEM((rows, 2 * row_len), BF16)],
-        compiler_params=params(),
-        cost_estimate=cost(4 * total * rows * row_len, 5 * rows * row_len * 4),
+        scratch_shapes=[
+            pltpu.VMEM((rows, 2 * row_len), BF16),
+            pltpu.VMEM((1, rows), jnp.int32),
+        ],
+        compiler_params=params(),
+        cost_estimate=cost(4 * ndev * tall * rows * row_len, 5 * rows * row_len * 4),
         name="pack",
     )(owner, slot, temp, old, mask)
 
 
-def heat_kernel(rows_ref, code_ref, heat_ref):
-    slots, row_len = heat_ref.shape
-    total = rows_ref.shape[0]
-    block = 512
-    heat_ref[...] = jnp.zeros_like(heat_ref)
-
-    def step(index, none):
-        base = pl.multiple_of(index * block, block)
-        high, low = halves(rows_ref[pl.ds(base, block), :])
-        code = code_ref[:, pl.ds(base, block)].astype(jnp.int32) - 1
-        pick = ones_where(lax.broadcasted_iota(jnp.int32, (slots, block), 0) == code)
-        both = jnp.dot(
+def heat_kernel(cap, rows_ref, *refs):
+    heat_ref, code_ref = refs[-2:]
+    ndev, tall, row_len = rows_ref.shape
+    slots = heat_ref.shape[0]
+    codes = rows_ref[:, cap, :].astype(jnp.int32) - 1
+    turned = jnp.transpose(codes)
+    for source in range(ndev):
+        code_ref[source * cap:(source + 1) * cap, :] = jnp.broadcast_to(
+            turned[:cap, source:source + 1], (cap, row_len)
+        )
+    group = max(1, 256 // tall)
+    names = lax.broadcasted_iota(jnp.int32, (slots, tall), 0)
+    total = jnp.zeros((slots, 2 * row_len), F32)
+    for index in range(0, ndev, group):
+        lines = rows_ref[index:index + group].reshape(group * tall, row_len)
+        high, low = halves(lines)
+        pick = jnp.concatenate(
+            [
+                jnp.where(names == codes[index + i:index + i + 1, :tall], 1.0, 0.0)
+                for i in range(group)
+            ],
+            axis=1,
+        ).astype(BF16)
+        total = total + jnp.dot(
             pick, jnp.concatenate([high, low], axis=1), preferred_element_type=F32
         )
-        heat_ref[...] += both[:, :row_len] + both[:, row_len:]
-        return none
-
-    lax.fori_loop(0, total // block, step, 0)
-
-
-def heat_sum(incoming, code, slots):
-    total, row_len = incoming.shape
-    return pl.pallas_call(
-        heat_kernel,
-        in_specs=[pl.BlockSpec(memory_space=pltpu.VMEM)] * 2,
-        out_specs=pl.BlockSpec(memory_space=pltpu.VMEM),
-        out_shape=jax.ShapeDtypeStruct((slots, row_len), F32),
-        compiler_params=params(),
-        cost_estimate=cost(4 * total * slots * row_len, 4 * total * row_len),
+    heat_ref[...] = total[:, :row_len] + total[:, row_len:]
+
+
+def heat_sum(incoming, cap, slots, after):
+    ndev, tall, row_len = incoming.shape
+    return pl.pallas_call(
+        functools.partial(heat_kernel, cap),
+        grid=(1,),
+        in_specs=[whole(incoming.shape)] + [anywhere] * len(after),
+        out_specs=[whole((slots, row_len)), whole((ndev * cap, row_len))],
+        out_shape=[
+            jax.ShapeDtypeStruct((slots, row_len), F32),
+            jax.ShapeDtypeStruct((ndev * cap, row_len), jnp.int32),
+        ],
+        compiler_params=params(),
+        cost_estimate=cost(4 * ndev * tall * slots * row_len, 4 * ndev * tall * row_len),
         name="heat_sum",
-    )(incoming, code)
+    )(incoming, *after)
 
 
 def table(kind, values):
@@ -177,10 +203,6 @@
     _, sx, sy, sz = state_ref.shape
     wide = sx + 2 * rim
     thin = rim - 1
-    temp_ref[...] = jnp.zeros_like(temp_ref)
-    work_ref[...] = jnp.zeros_like(work_ref)
-    cond_ref[...] = jnp.zeros_like(cond_ref)
-    src_ref[...] = jnp.zeros_like(src_ref)
     for which, ref in ((0, temp_ref), (1, cond_ref)):
         ref[rim:rim + sx, OFF:OFF + sy, :] = state_ref[which]
         ref[0:rim, OFF:OFF + sy, :] = xlo_ref[which]
@@ -202,17 +224,13 @@
     pair = (temp_ref, work_ref)
     for turn in range(rim - 1):
         now, later = pair[turn % 2], pair[(turn + 1) % 2]
-
-        def plane(x, none):
+        for x in range(1 + turn, wide - 1 - turn):
             centre = now[x]
             beside = now[x - 1] + now[x + 1]
             beside += pltpu.roll(centre, 1, 0) + pltpu.roll(centre, height - 1, 0)
             beside += jnp.where(first, 0.0, pltpu.roll(centre, 1, 1))
             beside += jnp.where(last, 0.0, pltpu.roll(centre, sz - 1, 1))
             later[x] = centre + (cond_ref[x] * (beside - 6.0 * centre) + src_ref[x])
-            return none
-
-        lax.fori_loop(1 + turn, wide - 1 - turn, plane, 0)
     final = pair[(rim - 1) % 2]
     solid = final[rim:rim + sx, OFF:OFF + sy, :]
     next_ref[...] = solid
@@ -220,12 +238,16 @@
     high, low = halves(solid.reshape(sx * sy, sz))
     rhs_ref[:, :sz] = high
     rhs_ref[:, sz:] = low
-    block = 256
+    block = 512
+    slots = sx * sy
+    names = lax.broadcasted_iota(jnp.int32, (block, sz), 1)
 
     def answer(index, none):
         base = pl.multiple_of(index * block, block)
-        code = code_ref[pl.ds(base, block), :].astype(jnp.int32) - 1
-        pick = ones_where(lax.broadcasted_iota(jnp.int32, (block, sx * sy), 1) == code)
+        code = code_ref[pl.ds(base, block), :]
+        pick = jnp.concatenate(
+            [jnp.where(names + at == code, 1.0, 0.0) for at in range(0, slots, sz)], axis=1
+        ).astype(BF16)
         both = jnp.dot(pick, rhs_ref[...], preferred_element_type=F32)
         reply_ref[pl.ds(base, block), :] = both[:, :sz] + both[:, sz:]
         return none
@@ -237,11 +259,12 @@
     _, sx, sy, sz = state.shape
     total = code.shape[0]
     wide, height = sx + 2 * rim, sy + 2 * OFF
-    vmem = pl.BlockSpec(memory_space=pltpu.VMEM)
+    args = (state, *state_rim, heat, *heat_rim, code)
     return pl.pallas_call(
         functools.partial(solid_kernel, rim),
-        in_specs=[vmem] * 11,
-        out_specs=[vmem] * 3,
+        grid=(1,),
+        in_specs=[whole(x.shape) for x in args],
+        out_specs=[whole((sx, sy, sz)), whole((sx + 2, height, sz)), whole((total, sz))],
         out_shape=[
             jax.ShapeDtypeStruct((sx, sy, sz), F32),
             jax.ShapeDtypeStruct((sx + 2, height, sz), F32),
@@ -252,7 +275,7 @@
         compiler_params=params(),
         cost_estimate=cost(4 * total * sx * sy * sz, 4 * total * sz),
         name="solid_steps",
-    )(state, *state_rim, heat, *heat_rim, code)
+    )(*args)
 
 
 def stress_kernel(sigma_ref, out_ref):
@@ -277,11 +300,11 @@
 
 def stress(sigma, sx, sy):
     sz = sigma.shape[2]
-    vmem = pl.BlockSpec(memory_space=pltpu.VMEM)
     return pl.pallas_call(
         stress_kernel,
-        in_specs=[vmem],
-        out_specs=vmem,
+        grid=(1,),
+        in_specs=[whole(sigma.shape)],
+        out_specs=whole((3, sx, sy, sz)),
         out_shape=jax.ShapeDtypeStruct((3, sx, sy, sz), F32),
         compiler_params=params(),
         cost_estimate=cost(10 * sx * sy * sz, 16 * sx * sy * sz),
@@ -289,7 +312,8 @@
     )(sigma)
 
 
-def unpack_kernel(dest_ref, back_ref, out_ref):
+def unpack_kernel(dest_ref, back_ref, *refs):
+    out_ref = refs[-1]
     rows = out_ref.shape[0]
 
     def step(index, none):
@@ -298,21 +322,23 @@
         out_ref[pl.ds(base, 8), :] = jnp.concatenate(lines, axis=0)
         return none
 
-    lax.fori_loop(0, rows // 8, step, 0, unroll=2)
-
-
-def unpack(dest, back):
+    lax.fori_loop(0, rows // 8, step, 0, unroll=4)
+
+
+def unpack(dest, back, after):
     rows = dest.shape[1]
-    vmem = pl.BlockSpec(memory_space=pltpu.VMEM)
+    row_len = back.shape[1]
     return pl.pallas_call(
         unpack_kernel,
-        in_specs=[pl.BlockSpec(memory_space=pltpu.SMEM), vmem],
-        out_specs=vmem,
-        out_shape=jax.ShapeDtypeStruct((rows, back.shape[1]), F32),
-        compiler_params=params(),
-        cost_estimate=cost(rows * 128, 8 * rows * back.shape[1]),
+        grid=(1,),
+        in_specs=[pl.BlockSpec(memory_space=pltpu.SMEM), whole(back.shape)]
+        + [anywhere] * len(after),
+        out_specs=whole((rows, row_len)),
+        out_shape=jax.ShapeDtypeStruct((rows, row_len), F32),
+        compiler_params=params(),
+        cost_estimate=cost(rows * 128, 8 * rows * row_len),
         name="unpack",
-    )(dest, back)
+    )(dest, back, *after)
 
 
 def fluid_kernel(before_ref, here_ref, after_ref, xlo_ref, xhi_ref, ylo_ref, yhi_ref,
@@ -400,15 +426,10 @@
     total = ndev * cap
     rim = SSTEPS + 1
 
-    outgoing, meta, flux, dest = pack(
+    outgoing, flux, dest = pack(
         owner_map.reshape(1, rows), slot_map, temp_fluid, wall_old, wall_mask, ndev, cap
     )
-    incoming = lax.all_to_all(
-        outgoing.reshape(ndev, cap, row_len), AXES, split_axis=0, concat_axis=0, tiled=True
-    )
-    code = lax.all_to_all(meta.reshape(ndev, cap), AXES, split_axis=0, concat_axis=0, tiled=True)
-    code_row = code.reshape(1, total)
-    code_col = code.reshape(total, 1)
+    incoming = lax.all_to_all(outgoing, AXES, split_axis=0, concat_axis=0, tiled=True)
 
     state = jnp.stack([temp_solid, material.astype(F32) + 1.0])
     xlo, xhi = neighbours(state[:, sx - rim:], state[:, :rim], "gx")
@@ -417,21 +438,22 @@
 
     fluid = fluid_step(temp_fluid, fluid_rims(temp_fluid), velocity, flux)
 
-    heat = heat_sum(incoming.reshape(total, row_len), code_row, sx * sy).reshape(sx, sy, sz)
+    heat, code = heat_sum(incoming, cap, sx * sy, (fluid, xlo, xhi, ylo, yhi))
+    heat = heat.reshape(sx, sy, sz)
     thin = rim - 1
     hxlo, hxhi = neighbours(heat[sx - thin:], heat[:thin], "gx")
     tall2 = lambda cut: jnp.concatenate([hxlo[:, cut], heat[:, cut], hxhi[:, cut]], axis=0)
     hylo, hyhi = neighbours(tall2(slice(sy - thin, sy)), tall2(slice(0, thin)), "gy")
     solid, sigma, replies = solid_steps(
-        rim, state, (xlo, xhi, ylo, yhi), heat, (hxlo, hxhi, hylo, hyhi), code_col
+        rim, state, (xlo, xhi, ylo, yhi), heat, (hxlo, hxhi, hylo, hyhi), code
     )
     returned = lax.all_to_all(
         replies.reshape(ndev, cap, sz), AXES, split_axis=0, concat_axis=0, tiled=True
     )
     fluid = fluid_step(fluid, fluid_rims(fluid), velocity, flux)
     force = stress(sigma, sx, sy)
-    wall_next = unpack(dest, returned.reshape(total, sz)).reshape(cx, cy, row_len)
-    return fluid, wall_next, solid, force
+    wall_next = unpack(dest, returned.reshape(total, sz), (fluid, force))
+    return fluid, wall_next.reshape(cx, cy, row_len), solid, force
 
 
 def solution(mesh):

time: 205 us -> 189 us (0.922)
  the two profiles are of different devices: /device:TPU:13 before, /device:TPU:11 now
where the time goes in v2:
time: 189 us; the launch traced here: 187 us
  Pallas kernels  58.2 us (31%)
  waiting for transfers between devices  57.7 us (31%)
  starting transfers between devices  57.1 us (30%)
  local copies, waits for them, and re-layouts  12.5 us (7%)
    ppermute x16, waiting for transfers between devices, neighbours(): return (lax.ppermute(before, axis, up), lax.ppermute(after, axis, down))  57.7 us
    ppermute x16, starting transfers between devices, neighbours(): return (lax.ppermute(before, axis, up), lax.ppermute(after, axis, down))  46.9 us
    pallas_call x2, Pallas kernels, fluid_step(): pl.pallas_call(fluid_kernel, grid=(cx,), in_specs=[pl.BlockSpec(plane, la...  32.6 us
    pallas_call x1, Pallas kernels, pack(): pl.pallas_call(functools.partial(pack_kernel, cap), grid=(1,), in_specs=[...  8.44 us
    pallas_call x1, Pallas kernels, solid_steps(): pl.pallas_call(functools.partial(solid_kernel, rim), grid=(1,), in_specs=...  6.51 us
    all_to_all x1, starting transfers between devices, body(): lax.all_to_all(outgoing, AXES, split_axis=0, concat_axis=0, tiled=True)  6.33 us
    unnamed x40, local copies, waits for them, and re-layouts  5.95 us
    pallas_call x1, Pallas kernels, heat_sum(): pl.pallas_call(functools.partial(heat_kernel, cap), grid=(1,), in_specs=[...  4.3 us
  transfers between devices with their start and end apart: 18, of which 6 were waited for; matrix products, arithmetic and copies ran while one was open for 4% of the time, Pallas kernels for 19%

profile of v2, /device:TPU:11, one launch (start us, length us, event | category | flops | bytes accessed | tf_op | source)
XLA Modules:
  0.0 187.5 jit_solution(9893843542482295841)
XLA Ops:
  0.7 8.4 %pack.1 = (f32[32,104,128]{2,1,0:T(8,128)}, f32[16,64,128]{2,1,0:T(8,128)}, s32[1,1024]{1,0:T(1,128)}) custom-call(s32[1,1024]{1,0:T(1,128)} %bitcast.20, s32[1,1024]{1,0:T(1,128)} %slot_ref.1, f32[16,64,1024]{2,1,0:T(8,128)} %after_ref.1, f32[16,64,128]{2,1,0:T(8,128)} %old_ref.1, s32[16,64,128]{2,1,0:T(8,128)} %mask_ref.1), custom_call_target="tpu_custom_call" | custom-call | flops 1744830464 | bytes 2621440 | tf_op jit(solution)/shard_map/pack/pallas_call | solution.py:114
  9.1 6.3 %all-to-all-start = ((f32[32,104,128]{2,1,0:T(8,128)}), f32[32,104,128]{2,1,0:T(8,128)S(1)}, u32[]{:S(2)}, u32[]{:S(2)}) async-start(f32[32,104,128]{2,1,0:T(8,128)} %get-tuple-element.14), calls=%async_computation | async-start | bytes 3407872 | tf_op jit(solution)/shard_map/all_to_all | solution.py:432
  15.4 1.3 fusion.6
  16.7 2.2 %collective-permute-start.3 = (f32[16,1,1024]{2,1,0:T(1,128)S(1)}, f32[16,1,1024]{2,1,0:T(1,128)S(1)}, u32[]{:S(2)}, u32[]{:S(2)}) collective-permute-start(f32[16,1,1024]{2,1,0:T(1,128)S(1)} %get-tuple-element.24), channel_id=1, source_target_pairs={{1,0},{2,1},{3,2},{5,4},{6,5},{7,6},{9,8},{10,9},{11,10},{13,12},{... | collective-permute-start | bytes 196616 | tf_op jit(solution)/shard_map/ppermute | solution.py:46
  18.9 0.0 copy-done.11
  19.0 2.5 %collective-permute-start.9 = (f32[2,5,32,128]{3,2,1,0:T(8,128)S(1)}, f32[2,5,32,128]{3,2,1,0:T(8,128)S(1)}, u32[]{:S(2)}, u32[]{:S(2)}) collective-permute-start(f32[2,5,32,128]{3,2,1,0:T(8,128)S(1)} %get-tuple-element.30), channel_id=1, source_target_pairs={{4,0},{8,4},{12,8},{16,12},{20,16},{24,20},{28,24},{5,1},{9,5},{13... | collective-permute-start | bytes 491528 | tf_op jit(solution)/shard_map/ppermute | solution.py:46
  21.6 3.0 %collective-permute-start.8 = (f32[2,5,32,128]{3,2,1,0:T(8,128)S(1)}, f32[2,5,32,128]{3,2,1,0:T(8,128)S(1)}, u32[]{:S(2)}, u32[]{:S(2)}) collective-permute-start(f32[2,5,32,128]{3,2,1,0:T(8,128)S(1)} %get-tuple-element.31), channel_id=1, source_target_pairs={{0,4},{4,8},{8,12},{12,16},{16,20},{20,24},{24,28},{1,5},{5,9},{9,... | collective-permute-start | bytes 491528 | tf_op jit(solution)/shard_map/ppermute | solution.py:46
  24.6 1.1 fusion.7
  25.7 1.9 %collective-permute-start.1 = (f32[1,64,1024]{2,1,0:T(8,128)S(1)}, f32[1,64,1024]{2,1,0:T(8,128)S(1)}, u32[]{:S(2)}, u32[]{:S(2)}) collective-permute-start(f32[1,64,1024]{2,1,0:T(8,128)S(1)} %get-tuple-element.26), channel_id=1, source_target_pairs={{4,0},{8,4},{12,8},{16,12},{20,16},{24,20},{28,24},{5,1},{9,5},{13... | collective-permute-start | bytes 786440 | tf_op jit(solution)/shard_map/ppermute | solution.py:46
  27.6 3.6 %collective-permute-start = (f32[1,64,1024]{2,1,0:T(8,128)S(1)}, f32[1,64,1024]{2,1,0:T(8,128)S(1)}, u32[]{:S(2)}, u32[]{:S(2)}) collective-permute-start(f32[1,64,1024]{2,1,0:T(8,128)S(1)} %get-tuple-element.27), channel_id=1, source_target_pairs={{0,4},{4,8},{8,12},{12,16},{16,20},{20,24},{24,28},{1,5},{5,9},{9,... | collective-permute-start | bytes 786440 | tf_op jit(solution)/shard_map/ppermute | solution.py:46
  31.3 25.0 %collective-permute-done.9.refs_2_.xhi_ref = f32[2,5,32,128]{3,2,1,0:T(8,128)S(1)} collective-permute-done((f32[2,5,32,128]{3,2,1,0:T(8,128)S(1)}, f32[2,5,32,128]{3,2,1,0:T(8,128)S(1)}, u32[]{:S(2)}, u32[]{:S(2)}) %collective-permute-start.9) | collective-permute-done | bytes 163872 | tf_op jit(solution)/shard_map/ppermute | solution.py:46
  56.3 0.0 collective-permute-done.8.refs_1_.xlo_ref
  56.4 3.0 %collective-permute-start.10 = (f32[2,26,5,128]{3,2,1,0:T(8,128)S(1)}, f32[2,26,5,128]{3,2,1,0:T(8,128)S(1)}, u32[]{:S(2)}, u32[]{:S(2)}) collective-permute-start(f32[2,26,5,128]{3,2,1,0:T(8,128)S(1)} %pad_maximum_fusion.1), channel_id=1, source_target_pairs={{0,1},{1,2},{2,3},{4,5},{5,6},{6,7},{8,9},{9,10},{10,11},{12,13},{... | collective-permute-start | bytes 399368 | tf_op jit(solution)/shard_map/ppermute | solution.py:46
  59.5 2.3 %collective-permute-start.11 = (f32[2,26,5,128]{3,2,1,0:T(8,128)S(1)}, f32[2,26,5,128]{3,2,1,0:T(8,128)S(1)}, u32[]{:S(2)}, u32[]{:S(2)}) collective-permute-start(f32[2,26,5,128]{3,2,1,0:T(8,128)S(1)} %pad_maximum_fusion.2), channel_id=1, source_target_pairs={{1,0},{2,1},{3,2},{5,4},{6,5},{7,6},{9,8},{10,9},{11,10},{13,12},{... | collective-permute-start | bytes 399368 | tf_op jit(solution)/shard_map/ppermute | solution.py:46
  61.7 0.0 collective-permute-done.3.yhi_ref
  61.8 3.9 %collective-permute-start.2 = (f32[16,1,1024]{2,1,0:T(1,128)S(1)}, f32[16,1,1024]{2,1,0:T(1,128)S(1)}, u32[]{:S(2)}, u32[]{:S(2)}) collective-permute-start(f32[16,1,1024]{2,1,0:T(1,128)S(1)} %get-tuple-element.25), channel_id=1, source_target_pairs={{0,1},{1,2},{2,3},{4,5},{5,6},{6,7},{8,9},{9,10},{10,11},{12,13},{... | collective-permute-start | bytes 196616 | tf_op jit(solution)/shard_map/ppermute | solution.py:46
  65.7 1.3 collective-permute-done.2.ylo_ref
  67.0 0.0 collective-permute-done.1.xhi_ref
  67.0 0.0 collective-permute-done.xlo_ref
  67.0 0.0 copy-start.8
  67.0 0.6 copy-done.17
  67.6 0.1 copy-done.7
  67.7 0.1 copy-done.8
  67.8 16.3 %fluid_step.2.before_ref.here_ref.after_ref.refs_0_ = f32[16,64,1024]{2,1,0:T(8,128)} custom-call(f32[16,64,1024]{2,1,0:T(8,128)} %after_ref.1, f32[16,64,1024]{2,1,0:T(8,128)} %after_ref.1, f32[16,64,1024]{2,1,0:T(8,128)} %after_ref.1, f32[1,64,1024]{2,1,0:T(8,128)} %copy-done.8, f32[1,64,1024]{2,1,0:T(8,128)} %copy-done.7, f32[16,1,1024]{2,1,0:T(1,128)} %copy-done.17, ...), custom_call_target="tpu_custom_call" | custom-call | flops 41943040 | bytes 23068672 | tf_op jit(solution)/shard_map/fluid_step/pallas_call | solution.py:389
  84.1 0.0 copy-done.4
  84.1 0.0 collective-permute-done.10.refs_3_.ylo_ref
  84.1 0.0 collective-permute-done.11.refs_4_.yhi_ref
  84.2 0.0 all-to-all-done.rows_ref
  84.2 0.6 copy-done.5
  84.8 0.1 copy-done.6
  84.9 1.2 copy-done
  86.1 4.3 %heat_sum.1 = (f32[512,128]{1,0:T(8,128)}, s32[3072,128]{1,0:T(8,128)}) custom-call(f32[32,104,128]{2,1,0:T(8,128)} %copy-done, f32[16,64,1024]{2,1,0:T(8,128)} %fluid_step.2.before_ref.here_ref.after_ref.refs_0_, f32[2,5,32,128]{3,2,1,0:T(8,128)} %copy-done.4, f32[2,5,32,128]{3,2,1,0:T(8,128)} %copy-done.3, f32[2,26,5,128]{3,2,1,0:T(8,128)} %copy-done.5, ...), custom_call_target="tpu_custom_call" | custom-call | flops 872415232 | bytes 1703936 | tf_op jit(solution)/shard_map/heat_sum/pallas_call | solution.py:175
  90.4 0.9 fusion.9
  91.3 3.9 %collective-permute-start.12 = (f32[4,32,128]{2,1,0:T(8,128)S(1)}, f32[4,32,128]{2,1,0:T(8,128)S(1)}, u32[]{:S(2)}, u32[]{:S(2)}) collective-permute-start(f32[4,32,128]{2,1,0:T(8,128)S(1)} %bitcast.19), channel_id=1, source_target_pairs={{0,4},{4,8},{8,12},{12,16},{16,20},{20,24},{24,28},{1,5},{5,9},{9,... | collective-permute-start | bytes 196616 | tf_op jit(solution)/shard_map/ppermute | solution.py:46
  95.2 0.9 fusion.8
  96.1 1.9 %collective-permute-start.13 = (f32[4,32,128]{2,1,0:T(8,128)S(1)}, f32[4,32,128]{2,1,0:T(8,128)S(1)}, u32[]{:S(2)}, u32[]{:S(2)}) collective-permute-start(f32[4,32,128]{2,1,0:T(8,128)S(1)} %bitcast.18), channel_id=1, source_target_pairs={{4,0},{8,4},{12,8},{16,12},{20,16},{24,20},{28,24},{5,1},{9,5},{13... | collective-permute-start | bytes 196616 | tf_op jit(solution)/shard_map/ppermute | solution.py:46
  98.1 0.0 collective-permute-done.12.hxlo_ref
  98.1 0.0 copy-start.12
  98.1 3.6 %collective-permute-done.13.hxhi_ref = f32[4,32,128]{2,1,0:T(8,128)S(1)} collective-permute-done((f32[4,32,128]{2,1,0:T(8,128)S(1)}, f32[4,32,128]{2,1,0:T(8,128)S(1)}, u32[]{:S(2)}, u32[]{:S(2)}) %collective-permute-start.13) | collective-permute-done | bytes 65568 | tf_op jit(solution)/shard_map/ppermute | solution.py:46
  101.8 4.9 %collective-permute-start.14 = (f32[24,4,128]{2,1,0:T(4,128)S(1)}, f32[24,4,128]{2,1,0:T(4,128)S(1)}, u32[]{:S(2)}, u32[]{:S(2)}) collective-permute-start(f32[24,4,128]{2,1,0:T(4,128)S(1)} %pad_maximum_fusion.3), channel_id=1, source_target_pairs={{0,1},{1,2},{2,3},{4,5},{5,6},{6,7},{8,9},{9,10},{10,11},{12,13},{... | collective-permute-start | bytes 147464 | tf_op jit(solution)/shard_map/ppermute | solution.py:46
  106.7 1.9 %collective-permute-start.15 = (f32[24,4,128]{2,1,0:T(4,128)S(1)}, f32[24,4,128]{2,1,0:T(4,128)S(1)}, u32[]{:S(2)}, u32[]{:S(2)}) collective-permute-start(f32[24,4,128]{2,1,0:T(4,128)S(1)} %pad_maximum_fusion.4), channel_id=1, source_target_pairs={{1,0},{2,1},{3,2},{5,4},{6,5},{7,6},{9,8},{10,9},{11,10},{13,12},{... | collective-permute-start | bytes 147464 | tf_op jit(solution)/shard_map/ppermute | solution.py:46
  108.6 0.8 pad_maximum_fusion.state_ref
  109.4 0.0 collective-permute-done.14.hylo_ref
  109.4 3.0 %collective-permute-done.15.hyhi_ref = f32[24,4,128]{2,1,0:T(4,128)S(1)} collective-permute-done((f32[24,4,128]{2,1,0:T(4,128)S(1)}, f32[24,4,128]{2,1,0:T(4,128)S(1)}, u32[]{:S(2)}, u32[]{:S(2)}) %collective-permute-start.15) | collective-permute-done | bytes 49184 | tf_op jit(solution)/shard_map/ppermute | solution.py:46
  112.4 0.6 copy-done.19
  113.0 6.5 %solid_steps.1 = (f32[16,32,128]{2,1,0:T(8,128)}, f32[18,48,128]{2,1,0:T(8,128)}, f32[3072,128]{1,0:T(8,128)}) custom-call(f32[2,16,32,128]{3,2,1,0:T(8,128)} %pad_maximum_fusion.state_ref, f32[2,5,32,128]{3,2,1,0:T(8,128)} %copy-done.4, f32[2,5,32,128]{3,2,1,0:T(8,128)} %copy-done.3, f32[2,26,5,128]{3,2,1,0:T(8,128)} %copy-done.5, ...), custom_call_target="tpu_custom_call" | custom-call | flops 805306368 | bytes 1572864 | tf_op jit(solution)/shard_map/solid_steps/pallas_call | solution.py:263
  119.5 3.9 %all-to-all-start.1 = ((f32[32,96,128]{2,1,0:T(8,128)}), f32[32,96,128]{2,1,0:T(8,128)S(1)}, u32[]{:S(2)}, u32[]{:S(2)}) async-start(f32[32,96,128]{2,1,0:T(8,128)} %bitcast.14), calls=%async_computation.1 | async-start | bytes 3145728 | tf_op jit(solution)/shard_map/all_to_all | solution.py:450
  123.4 1.1 fusion.5
  124.5 2.3 %collective-permute-start.5 = (f32[1,64,1024]{2,1,0:T(8,128)S(1)}, f32[1,64,1024]{2,1,0:T(8,128)S(1)}, u32[]{:S(2)}, u32[]{:S(2)}) collective-permute-start(f32[1,64,1024]{2,1,0:T(8,128)S(1)} %get-tuple-element.22), channel_id=1, source_target_pairs={{4,0},{8,4},{12,8},{16,12},{20,16},{24,20},{28,24},{5,1},{9,5},{13... | collective-permute-start | bytes 786440 | tf_op jit(solution)/shard_map/ppermute | solution.py:46
  126.8 3.3 %collective-permute-start.4 = (f32[1,64,1024]{2,1,0:T(8,128)S(1)}, f32[1,64,1024]{2,1,0:T(8,128)S(1)}, u32[]{:S(2)}, u32[]{:S(2)}) collective-permute-start(f32[1,64,1024]{2,1,0:T(8,128)S(1)} %get-tuple-element.23), channel_id=1, source_target_pairs={{0,4},{4,8},{8,12},{12,16},{16,20},{20,24},{24,28},{1,5},{5,9},{9,... | collective-permute-start | bytes 786440 | tf_op jit(solution)/shard_map/ppermute | solution.py:46
  130.1 1.3 fusion.4
  131.4 2.2 %collective-permute-start.7 = (f32[16,1,1024]{2,1,0:T(1,128)S(1)}, f32[16,1,1024]{2,1,0:T(1,128)S(1)}, u32[]{:S(2)}, u32[]{:S(2)}) collective-permute-start(f32[16,1,1024]{2,1,0:T(1,128)S(1)} %get-tuple-element.20), channel_id=1, source_target_pairs={{1,0},{2,1},{3,2},{5,4},{6,5},{7,6},{9,8},{10,9},{11,10},{13,12},{... | collective-permute-start | bytes 196616 | tf_op jit(solution)/shard_map/ppermute | solution.py:46
  133.6 4.0 %collective-permute-start.6 = (f32[16,1,1024]{2,1,0:T(1,128)S(1)}, f32[16,1,1024]{2,1,0:T(1,128)S(1)}, u32[]{:S(2)}, u32[]{:S(2)}) collective-permute-start(f32[16,1,1024]{2,1,0:T(1,128)S(1)} %get-tuple-element.21), channel_id=1, source_target_pairs={{0,1},{1,2},{2,3},{4,5},{5,6},{6,7},{8,9},{9,10},{10,11},{12,13},{... | collective-permute-start | bytes 196616 | tf_op jit(solution)/shard_map/ppermute | solution.py:46
  137.6 3.1 %collective-permute-done.7.yhi_ref = f32[16,1,1024]{2,1,0:T(1,128)S(1)} collective-permute-done((f32[16,1,1024]{2,1,0:T(1,128)S(1)}, f32[16,1,1024]{2,1,0:T(1,128)S(1)}, u32[]{:S(2)}, u32[]{:S(2)}) %collective-permute-start.7) | collective-permute-done | bytes 65568 | tf_op jit(solution)/shard_map/ppermute | solution.py:46
  140.7 0.0 collective-permute-done.6.ylo_ref
  140.7 21.6 %collective-permute-done.5.xhi_ref = f32[1,64,1024]{2,1,0:T(8,128)S(1)} collective-permute-done((f32[1,64,1024]{2,1,0:T(8,128)S(1)}, f32[1,64,1024]{2,1,0:T(8,128)S(1)}, u32[]{:S(2)}, u32[]{:S(2)}) %collective-permute-start.5) | collective-permute-done | bytes 262176 | tf_op jit(solution)/shard_map/ppermute | solution.py:46
  162.3 0.0 collective-permute-done.4.xlo_ref
  162.3 0.7 copy-done.9
  163.0 0.7 copy-done.10
  163.7 16.3 %fluid_step.3.refs_0_ = f32[16,64,1024]{2,1,0:T(8,128)} custom-call(f32[16,64,1024]{2,1,0:T(8,128)} %fluid_step.2.before_ref.here_ref.after_ref.refs_0_, f32[16,64,1024]{2,1,0:T(8,128)} %fluid_step.2.before_ref.here_ref.after_ref.refs_0_, f32[16,64,1024]{2,1,0:T(8,128)} %fluid_step.2.before_ref.here_ref.after_ref.refs_0_, f32[1,64,1024]{2,1,0:T(8,128)} %copy-done.10, ...), custom_call_target="tpu_custom_call" | custom-call | flops 41943040 | bytes 23068672 | tf_op jit(solution)/shard_map/fluid_step/pallas_call | solution.py:389
  179.9 3.1 %stress.1.refs_1_ = f32[3,16,32,128]{3,2,1,0:T(8,128)} custom-call(f32[18,48,128]{2,1,0:T(8,128)} %get-tuple-element.18.sigma_ref), custom_call_target="tpu_custom_call" | custom-call | flops 655360 | bytes 1048576 | tf_op jit(solution)/shard_map/stress/pallas_call | solution.py:303
  183.1 0.0 all-to-all-done.1
  183.1 1.2 copy-done.1
  184.3 3.2 %unpack.1 = f32[1024,128]{1,0:T(8,128)} custom-call(s32[1,1024]{1,0:T(1,128)} %get-tuple-element.13.dest_ref, f32[3072,128]{1,0:T(8,128)} %bitcast.10, f32[16,64,1024]{2,1,0:T(8,128)} %fluid_step.3.refs_0_, f32[3,16,32,128]{3,2,1,0:T(8,128)} %stress.1.refs_1_), custom_call_target="tpu_custom_call" | custom-call | flops 131072 | bytes 1048576 | tf_op jit(solution)/shard_map/unpack/pallas_call | solution.py:331
  (37 shorter events, 0.2 us)
Async XLA Ops:
  0.6 18.3 %copy-start.11 = (s32[16,32,128]{2,1,0:T(8,128)S(1)}, s32[16,32,128]{2,1,0:T(8,128)}, u32[]{:S(2)}) copy-start(s32[16,32,128]{2,1,0:T(8,128)} %param.15) | copy-start | bytes 786436
  0.6 18.3 %copy-start.2 = (f32[16,32,128]{2,1,0:T(8,128)S(1)}, f32[16,32,128]{2,1,0:T(8,128)}, u32[]{:S(2)}) copy-start(f32[16,32,128]{2,1,0:T(8,128)} %param.14) | copy-start | bytes 786436
  9.1 75.1 %all-to-all-start = ((f32[32,104,128]{2,1,0:T(8,128)}), f32[32,104,128]{2,1,0:T(8,128)S(1)}, u32[]{:S(2)}, u32[]{:S(2)}) async-start(f32[32,104,128]{2,1,0:T(8,128)} %get-tuple-element.14), calls=%async_computation | async-start | bytes 3407872 | tf_op jit(solution)/shard_map/all_to_all | solution.py:432
  16.7 45.0 %collective-permute-start.3 = (f32[16,1,1024]{2,1,0:T(1,128)S(1)}, f32[16,1,1024]{2,1,0:T(1,128)S(1)}, u32[]{:S(2)}, u32[]{:S(2)}) collective-permute-start(f32[16,1,1024]{2,1,0:T(1,128)S(1)} %get-tuple-element.24), channel_id=1, source_target_pairs={{1,0},{2,1},{3,2},{5,4},{6,5},{7,6},{9,8},{10,9},{11,10},{13,12},{... | collective-permute-start | bytes 196616 | tf_op jit(solution)/shard_map/ppermute | solution.py:46
  19.0 37.3 %collective-permute-start.9 = (f32[2,5,32,128]{3,2,1,0:T(8,128)S(1)}, f32[2,5,32,128]{3,2,1,0:T(8,128)S(1)}, u32[]{:S(2)}, u32[]{:S(2)}) collective-permute-start(f32[2,5,32,128]{3,2,1,0:T(8,128)S(1)} %get-tuple-element.30), channel_id=1, source_target_pairs={{4,0},{8,4},{12,8},{16,12},{20,16},{24,20},{28,24},{5,1},{9,5},{13... | collective-permute-start | bytes 491528 | tf_op jit(solution)/shard_map/ppermute | solution.py:46
  21.6 34.8 %collective-permute-start.8 = (f32[2,5,32,128]{3,2,1,0:T(8,128)S(1)}, f32[2,5,32,128]{3,2,1,0:T(8,128)S(1)}, u32[]{:S(2)}, u32[]{:S(2)}) collective-permute-start(f32[2,5,32,128]{3,2,1,0:T(8,128)S(1)} %get-tuple-element.31), channel_id=1, source_target_pairs={{0,4},{4,8},{8,12},{12,16},{16,20},{20,24},{24,28},{1,5},{5,9},{9,... | collective-permute-start | bytes 491528 | tf_op jit(solution)/shard_map/ppermute | solution.py:46
  25.7 41.3 %collective-permute-start.1 = (f32[1,64,1024]{2,1,0:T(8,128)S(1)}, f32[1,64,1024]{2,1,0:T(8,128)S(1)}, u32[]{:S(2)}, u32[]{:S(2)}) collective-permute-start(f32[1,64,1024]{2,1,0:T(8,128)S(1)} %get-tuple-element.26), channel_id=1, source_target_pairs={{4,0},{8,4},{12,8},{16,12},{20,16},{24,20},{28,24},{5,1},{9,5},{13... | collective-permute-start | bytes 786440 | tf_op jit(solution)/shard_map/ppermute | solution.py:46
  27.6 39.4 %collective-permute-start = (f32[1,64,1024]{2,1,0:T(8,128)S(1)}, f32[1,64,1024]{2,1,0:T(8,128)S(1)}, u32[]{:S(2)}, u32[]{:S(2)}) collective-permute-start(f32[1,64,1024]{2,1,0:T(8,128)S(1)} %get-tuple-element.27), channel_id=1, source_target_pairs={{0,4},{4,8},{8,12},{12,16},{16,20},{20,24},{24,28},{1,5},{5,9},{9,... | collective-permute-start | bytes 786440 | tf_op jit(solution)/shard_map/ppermute | solution.py:46
  56.3 27.8 %copy-start.3 = (f32[2,5,32,128]{3,2,1,0:T(8,128)}, f32[2,5,32,128]{3,2,1,0:T(8,128)S(1)}, u32[]{:S(2)}) copy-start(f32[2,5,32,128]{3,2,1,0:T(8,128)S(1)} %collective-permute-done.9.refs_2_.xhi_ref) | copy-start | bytes 491524
  56.3 27.8 %copy-start.4 = (f32[2,5,32,128]{3,2,1,0:T(8,128)}, f32[2,5,32,128]{3,2,1,0:T(8,128)S(1)}, u32[]{:S(2)}) copy-start(f32[2,5,32,128]{3,2,1,0:T(8,128)S(1)} %collective-permute-done.8.refs_1_.xlo_ref) | copy-start | bytes 491524
  56.4 27.7 %collective-permute-start.10 = (f32[2,26,5,128]{3,2,1,0:T(8,128)S(1)}, f32[2,26,5,128]{3,2,1,0:T(8,128)S(1)}, u32[]{:S(2)}, u32[]{:S(2)}) collective-permute-start(f32[2,26,5,128]{3,2,1,0:T(8,128)S(1)} %pad_maximum_fusion.1), channel_id=1, source_target_pairs={{0,1},{1,2},{2,3},{4,5},{5,6},{6,7},{8,9},{9,10},{10,11},{12,13},{... | collective-permute-start | bytes 399368 | tf_op jit(solution)/shard_map/ppermute | solution.py:46
  59.5 24.7 %collective-permute-start.11 = (f32[2,26,5,128]{3,2,1,0:T(8,128)S(1)}, f32[2,26,5,128]{3,2,1,0:T(8,128)S(1)}, u32[]{:S(2)}, u32[]{:S(2)}) collective-permute-start(f32[2,26,5,128]{3,2,1,0:T(8,128)S(1)} %pad_maximum_fusion.2), channel_id=1, source_target_pairs={{1,0},{2,1},{3,2},{5,4},{6,5},{7,6},{9,8},{10,9},{11,10},{13,12},{... | collective-permute-start | bytes 399368 | tf_op jit(solution)/shard_map/ppermute | solution.py:46
  61.8 5.3 %copy-start.14 = (f32[16,1,1024]{2,1,0:T(1,128)}, f32[16,1,1024]{2,1,0:T(1,128)S(1)}, u32[]{:S(2)}) copy-start(f32[16,1,1024]{2,1,0:T(1,128)S(1)} %collective-permute-done.3.yhi_ref) | copy-start | bytes 196612
  61.8 5.2 %collective-permute-start.2 = (f32[16,1,1024]{2,1,0:T(1,128)S(1)}, f32[16,1,1024]{2,1,0:T(1,128)S(1)}, u32[]{:S(2)}, u32[]{:S(2)}) collective-permute-start(f32[16,1,1024]{2,1,0:T(1,128)S(1)} %get-tuple-element.25), channel_id=1, source_target_pairs={{0,1},{1,2},{2,3},{4,5},{5,6},{6,7},{8,9},{9,10},{10,11},{12,13},{... | collective-permute-start | bytes 196616 | tf_op jit(solution)/shard_map/ppermute | solution.py:46
  67.0 0.6 copy-start.17
  67.0 0.7 copy-start.7
  67.0 0.8 copy-start.8
  84.1 0.7 copy-start.5
  84.1 0.8 copy-start.6
  84.9 1.2 copy-start
  91.3 6.8 %collective-permute-start.12 = (f32[4,32,128]{2,1,0:T(8,128)S(1)}, f32[4,32,128]{2,1,0:T(8,128)S(1)}, u32[]{:S(2)}, u32[]{:S(2)}) collective-permute-start(f32[4,32,128]{2,1,0:T(8,128)S(1)} %bitcast.19), channel_id=1, source_target_pairs={{0,4},{4,8},{8,12},{12,16},{16,20},{20,24},{24,28},{1,5},{5,9},{9,... | collective-permute-start | bytes 196616 | tf_op jit(solution)/shard_map/ppermute | solution.py:46
  96.1 5.6 %collective-permute-start.13 = (f32[4,32,128]{2,1,0:T(8,128)S(1)}, f32[4,32,128]{2,1,0:T(8,128)S(1)}, u32[]{:S(2)}, u32[]{:S(2)}) collective-permute-start(f32[4,32,128]{2,1,0:T(8,128)S(1)} %bitcast.18), channel_id=1, source_target_pairs={{4,0},{8,4},{12,8},{16,12},{20,16},{24,20},{28,24},{5,1},{9,5},{13... | collective-permute-start | bytes 196616 | tf_op jit(solution)/shard_map/ppermute | solution.py:46
  98.1 14.3 %copy-start.12 = (f32[4,32,128]{2,1,0:T(8,128)}, f32[4,32,128]{2,1,0:T(8,128)S(1)}, u32[]{:S(2)}) copy-start(f32[4,32,128]{2,1,0:T(8,128)S(1)} %collective-permute-done.12.hxlo_ref) | copy-start | bytes 196612
  101.7 10.7 %copy-start.13 = (f32[4,32,128]{2,1,0:T(8,128)}, f32[4,32,128]{2,1,0:T(8,128)S(1)}, u32[]{:S(2)}) copy-start(f32[4,32,128]{2,1,0:T(8,128)S(1)} %collective-permute-done.13.hxhi_ref) | copy-start | bytes 196612
  101.8 7.7 %collective-permute-start.14 = (f32[24,4,128]{2,1,0:T(4,128)S(1)}, f32[24,4,128]{2,1,0:T(4,128)S(1)}, u32[]{:S(2)}, u32[]{:S(2)}) collective-permute-start(f32[24,4,128]{2,1,0:T(4,128)S(1)} %pad_maximum_fusion.3), channel_id=1, source_target_pairs={{0,1},{1,2},{2,3},{4,5},{5,6},{6,7},{8,9},{9,10},{10,11},{12,13},{... | collective-permute-start | bytes 147464 | tf_op jit(solution)/shard_map/ppermute | solution.py:46
  106.7 5.7 %collective-permute-start.15 = (f32[24,4,128]{2,1,0:T(4,128)S(1)}, f32[24,4,128]{2,1,0:T(4,128)S(1)}, u32[]{:S(2)}, u32[]{:S(2)}) collective-permute-start(f32[24,4,128]{2,1,0:T(4,128)S(1)} %pad_maximum_fusion.4), channel_id=1, source_target_pairs={{1,0},{2,1},{3,2},{5,4},{6,5},{7,6},{9,8},{10,9},{11,10},{13,12},{... | collective-permute-start | bytes 147464 | tf_op jit(solution)/shard_map/ppermute | solution.py:46
  109.4 3.0 %copy-start.18 = (f32[24,4,128]{2,1,0:T(4,128)}, f32[24,4,128]{2,1,0:T(4,128)S(1)}, u32[]{:S(2)}) copy-start(f32[24,4,128]{2,1,0:T(4,128)S(1)} %collective-permute-done.14.hylo_ref) | copy-start | bytes 147460
  112.4 0.6 copy-start.19
  119.5 63.6 %all-to-all-start.1 = ((f32[32,96,128]{2,1,0:T(8,128)}), f32[32,96,128]{2,1,0:T(8,128)S(1)}, u32[]{:S(2)}, u32[]{:S(2)}) async-start(f32[32,96,128]{2,1,0:T(8,128)} %bitcast.14), calls=%async_computation.1 | async-start | bytes 3145728 | tf_op jit(solution)/shard_map/all_to_all | solution.py:450
  124.5 37.8 %collective-permute-start.5 = (f32[1,64,1024]{2,1,0:T(8,128)S(1)}, f32[1,64,1024]{2,1,0:T(8,128)S(1)}, u32[]{:S(2)}, u32[]{:S(2)}) collective-permute-start(f32[1,64,1024]{2,1,0:T(8,128)S(1)} %get-tuple-element.22), channel_id=1, source_target_pairs={{4,0},{8,4},{12,8},{16,12},{20,16},{24,20},{28,24},{5,1},{9,5},{13... | collective-permute-start | bytes 786440 | tf_op jit(solution)/shard_map/ppermute | solution.py:46
  126.8 35.5 %collective-permute-start.4 = (f32[1,64,1024]{2,1,0:T(8,128)S(1)}, f32[1,64,1024]{2,1,0:T(8,128)S(1)}, u32[]{:S(2)}, u32[]{:S(2)}) collective-permute-start(f32[1,64,1024]{2,1,0:T(8,128)S(1)} %get-tuple-element.23), channel_id=1, source_target_pairs={{0,4},{4,8},{8,12},{12,16},{16,20},{20,24},{24,28},{1,5},{5,9},{9,... | collective-permute-start | bytes 786440 | tf_op jit(solution)/shard_map/ppermute | solution.py:46
  131.4 9.3 %collective-permute-start.7 = (f32[16,1,1024]{2,1,0:T(1,128)S(1)}, f32[16,1,1024]{2,1,0:T(1,128)S(1)}, u32[]{:S(2)}, u32[]{:S(2)}) collective-permute-start(f32[16,1,1024]{2,1,0:T(1,128)S(1)} %get-tuple-element.20), channel_id=1, source_target_pairs={{1,0},{2,1},{3,2},{5,4},{6,5},{7,6},{9,8},{10,9},{11,10},{13,12},{... | collective-permute-start | bytes 196616 | tf_op jit(solution)/shard_map/ppermute | solution.py:46
  133.6 7.1 %collective-permute-start.6 = (f32[16,1,1024]{2,1,0:T(1,128)S(1)}, f32[16,1,1024]{2,1,0:T(1,128)S(1)}, u32[]{:S(2)}, u32[]{:S(2)}) collective-permute-start(f32[16,1,1024]{2,1,0:T(1,128)S(1)} %get-tuple-element.21), channel_id=1, source_target_pairs={{0,1},{1,2},{2,3},{4,5},{5,6},{6,7},{8,9},{9,10},{10,11},{12,13},{... | collective-permute-start | bytes 196616 | tf_op jit(solution)/shard_map/ppermute | solution.py:46
  140.7 21.6 %copy-start.15 = (f32[16,1,1024]{2,1,0:T(1,128)}, f32[16,1,1024]{2,1,0:T(1,128)S(1)}, u32[]{:S(2)}) copy-start(f32[16,1,1024]{2,1,0:T(1,128)S(1)} %collective-permute-done.7.yhi_ref) | copy-start | bytes 196612
  140.7 21.6 %copy-start.16 = (f32[16,1,1024]{2,1,0:T(1,128)}, f32[16,1,1024]{2,1,0:T(1,128)S(1)}, u32[]{:S(2)}) copy-start(f32[16,1,1024]{2,1,0:T(1,128)S(1)} %collective-permute-done.6.ylo_ref) | copy-start | bytes 196612
  162.3 0.7 copy-start.9
  163.0 0.7 copy-start.10
  183.1 1.2 copy-start.1

commit v3 on v2

--- a/solution.py
+++ b/solution.py
@@ -17,12 +17,14 @@
 modulus_table = (0.5, 1.0, 1.6, 2.4)
 F32 = jnp.float32
 BF16 = jnp.bfloat16
-VMEM_LIMIT = 60 * 1024 * 1024
 AXES = ("gx", "gy")
-
-
-def params():
-    return pltpu.CompilerParams(vmem_limit_bytes=VMEM_LIMIT)
+LANE = 128
+PART = 16
+OFF = 8
+
+
+def params(mib):
+    return pltpu.CompilerParams(vmem_limit_bytes=mib * 1024 * 1024)
 
 
 def cost(flops, bytes_accessed):
@@ -89,7 +91,7 @@
             preferred_element_type=F32,
         )
     where = where_ref[...]
-    group = max(1, 256 // tall)
+    group = ndev // 4
     block = group * tall
 
     def step(index, none):
@@ -135,23 +137,20 @@
             pltpu.VMEM((rows, 2 * row_len), BF16),
             pltpu.VMEM((1, rows), jnp.int32),
         ],
-        compiler_params=params(),
+        compiler_params=params(60),
         cost_estimate=cost(4 * ndev * tall * rows * row_len, 5 * rows * row_len * 4),
         name="pack",
     )(owner, slot, temp, old, mask)
 
 
-def heat_kernel(cap, rows_ref, *refs):
-    heat_ref, code_ref = refs[-2:]
+def heat_kernel(cap, thin, rows_ref, *refs):
+    heat_ref, first_ref, last_ref, code_ref = refs[-4:]
     ndev, tall, row_len = rows_ref.shape
-    slots = heat_ref.shape[0]
+    sx, sy, _ = heat_ref.shape
+    slots = sx * sy
     codes = rows_ref[:, cap, :].astype(jnp.int32) - 1
-    turned = jnp.transpose(codes)
-    for source in range(ndev):
-        code_ref[source * cap:(source + 1) * cap, :] = jnp.broadcast_to(
-            turned[:cap, source:source + 1], (cap, row_len)
-        )
-    group = max(1, 256 // tall)
+    code_ref[...] = codes
+    group = ndev // 4
     names = lax.broadcasted_iota(jnp.int32, (slots, tall), 0)
     total = jnp.zeros((slots, 2 * row_len), F32)
     for index in range(0, ndev, group):
@@ -167,24 +166,146 @@
         total = total + jnp.dot(
             pick, jnp.concatenate([high, low], axis=1), preferred_element_type=F32
         )
-    heat_ref[...] = total[:, :row_len] + total[:, row_len:]
-
-
-def heat_sum(incoming, cap, slots, after):
+    heat = (total[:, :row_len] + total[:, row_len:]).reshape(sx, sy, row_len)
+    heat_ref[...] = heat
+    first_ref[...] = heat[:thin]
+    last_ref[...] = heat[sx - thin:]
+
+
+def heat_sum(incoming, cap, block, thin, after):
     ndev, tall, row_len = incoming.shape
-    return pl.pallas_call(
-        functools.partial(heat_kernel, cap),
+    sx, sy, _ = block
+    edge = (thin, sy, row_len)
+    return pl.pallas_call(
+        functools.partial(heat_kernel, cap, thin),
         grid=(1,),
         in_specs=[whole(incoming.shape)] + [anywhere] * len(after),
-        out_specs=[whole((slots, row_len)), whole((ndev * cap, row_len))],
+        out_specs=[whole(block), whole(edge), whole(edge), whole((ndev, row_len))],
         out_shape=[
-            jax.ShapeDtypeStruct((slots, row_len), F32),
-            jax.ShapeDtypeStruct((ndev * cap, row_len), jnp.int32),
-        ],
-        compiler_params=params(),
-        cost_estimate=cost(4 * ndev * tall * slots * row_len, 4 * ndev * tall * row_len),
+            jax.ShapeDtypeStruct(block, F32),
+            jax.ShapeDtypeStruct(edge, F32),
+            jax.ShapeDtypeStruct(edge, F32),
+            jax.ShapeDtypeStruct((ndev, row_len), jnp.int32),
+        ],
+        compiler_params=params(20),
+        cost_estimate=cost(4 * ndev * tall * sx * sy * row_len, 4 * ndev * tall * row_len),
         name="heat_sum",
     )(incoming, *after)
+
+
+def put_rim(ref, base, slabs):
+    across = ref.shape[1] // LANE
+    for n, slab in enumerate(slabs):
+        row = base + n // across * PART
+        ref[row:row + PART, n % across * LANE:(n % across + 1) * LANE] = slab
+
+
+def get_rim(ref, n):
+    across = ref.shape[1] // LANE
+    row = n // across * PART
+    return ref[row:row + PART, n % across * LANE:(n % across + 1) * LANE]
+
+
+def rim_rows(count, depth):
+    across = depth // LANE
+    return -(-count // across) * PART
+
+
+def x_faces_kernel(rim, bottom_ref, top_ref, temp_ref, kind_ref, low_ref, high_ref):
+    _, cy, _ = bottom_ref.shape
+    sx, sy, _ = temp_ref.shape
+    low_ref[:cy, :] = bottom_ref[0]
+    high_ref[:cy, :] = top_ref[0]
+    for ref, start in ((low_ref, 0), (high_ref, sx - rim)):
+        slabs = [
+            get(start + k, slice(h, h + PART))
+            for get in (
+                lambda x, cut: temp_ref[x, cut, :],
+                lambda x, cut: kind_ref[x, cut, :].astype(F32) + 1.0,
+            )
+            for k in range(rim)
+            for h in range(0, sy, PART)
+        ]
+        put_rim(ref, cy, slabs)
+
+
+def x_faces(rim, fluid, temp, kind):
+    cx, cy, depth = fluid.shape
+    sx, sy, sz = temp.shape
+    height = cy + rim_rows(2 * rim * (sy // PART), depth)
+    plane = (1, cy, depth)
+    return pl.pallas_call(
+        functools.partial(x_faces_kernel, rim),
+        grid=(1,),
+        in_specs=[
+            pl.BlockSpec(plane, lambda i: (0, 0, 0)),
+            pl.BlockSpec(plane, lambda i: (cx - 1, 0, 0)),
+            whole(temp.shape),
+            whole(temp.shape),
+        ],
+        out_specs=[whole((height, depth))] * 2,
+        out_shape=[jax.ShapeDtypeStruct((height, depth), F32)] * 2,
+        compiler_params=params(12),
+        cost_estimate=cost(1000, 4 * 4 * height * depth),
+        name="x_faces",
+    )(fluid, fluid, temp, kind)
+
+
+def fill_x(rim, ref, which, own, lo_ref, hi_ref):
+    sx, sy, _ = own.shape
+    pieces = sy // PART
+    ref[rim:rim + sx, OFF:OFF + sy, :] = own
+    for k in range(rim):
+        for h in range(pieces):
+            n = (which * rim + k) * pieces + h
+            cut = slice(OFF + h * PART, OFF + (h + 1) * PART)
+            ref[k, cut, :] = get_rim(lo_ref, n)
+            ref[rim + sx + k, cut, :] = get_rim(hi_ref, n)
+
+
+def y_faces_kernel(rim, near_ref, far_ref, temp_ref, kind_ref, lo_ref, hi_ref,
+                   left_ref, right_ref, work_ref):
+    cx, near, _ = near_ref.shape
+    sx, sy, _ = temp_ref.shape
+    left_ref[:cx, :] = near_ref[:, 0, :]
+    right_ref[:cx, :] = far_ref[:, near - 1, :]
+    slabs = ([], [])
+    long = work_ref.shape[1]
+    work_ref[...] = jnp.zeros_like(work_ref)
+    for which, own in enumerate((temp_ref[...], kind_ref[...].astype(F32) + 1.0)):
+        fill_x(rim, work_ref.at[which], which, own, lo_ref, hi_ref)
+        for into, start in zip(slabs, (OFF, OFF + sy - rim)):
+            for k in range(rim):
+                for h in range(0, long, PART):
+                    into.append(work_ref[which, h:h + PART, start + k, :])
+    put_rim(left_ref, cx, slabs[0])
+    put_rim(right_ref, cx, slabs[1])
+
+
+def y_faces(rim, fluid, temp, kind, lo, hi):
+    cx, cy, depth = fluid.shape
+    sx, sy, sz = temp.shape
+    long = -(-(sx + 2 * rim) // PART) * PART
+    height = cx + rim_rows(2 * rim * (long // PART), depth)
+    edge = (cx, 8, depth)
+    return pl.pallas_call(
+        functools.partial(y_faces_kernel, rim),
+        grid=(1,),
+        in_specs=[
+            pl.BlockSpec(edge, lambda i: (0, 0, 0)),
+            pl.BlockSpec(edge, lambda i: (0, cy // 8 - 1, 0)),
+            whole(temp.shape),
+            whole(temp.shape),
+            whole(lo.shape),
+            whole(hi.shape),
+        ],
+        out_specs=[whole((height, depth))] * 2,
+        out_shape=[jax.ShapeDtypeStruct((height, depth), F32)] * 2,
+        scratch_shapes=[pltpu.VMEM((2, long, sy + 2 * OFF, sz), F32)],
+        compiler_params=params(16),
+        cost_estimate=cost(1000, 4 * 4 * height * depth),
+        name="y_faces",
+    )(fluid, fluid, temp, kind, lo, hi)
 
 
 def table(kind, values):
@@ -194,21 +315,24 @@
     return out
 
 
-OFF = 8
-
-
-def solid_kernel(rim, state_ref, xlo_ref, xhi_ref, ylo_ref, yhi_ref,
+def solid_kernel(rim, cap, own_ref, kind_ref, xlo_ref, xhi_ref, ylo_ref, yhi_ref,
                  heat_ref, hxlo_ref, hxhi_ref, hylo_ref, hyhi_ref, code_ref,
                  next_ref, sigma_ref, reply_ref, temp_ref, work_ref, cond_ref, src_ref, rhs_ref):
-    _, sx, sy, sz = state_ref.shape
+    sx, sy, sz = own_ref.shape
     wide = sx + 2 * rim
     thin = rim - 1
-    for which, ref in ((0, temp_ref), (1, cond_ref)):
-        ref[rim:rim + sx, OFF:OFF + sy, :] = state_ref[which]
-        ref[0:rim, OFF:OFF + sy, :] = xlo_ref[which]
-        ref[rim + sx:wide, OFF:OFF + sy, :] = xhi_ref[which]
-        ref[:, OFF - rim:OFF, :] = ylo_ref[which]
-        ref[:, OFF + sy:OFF + sy + rim, :] = yhi_ref[which]
+    pieces = -(-wide // PART)
+    for which, (own, ref) in enumerate(
+        ((own_ref[...], temp_ref), (kind_ref[...].astype(F32) + 1.0, cond_ref))
+    ):
+        fill_x(rim, ref, which, own, xlo_ref, xhi_ref)
+        for k in range(rim):
+            for h in range(pieces):
+                n = (which * rim + k) * pieces + h
+                count = min(PART, wide - h * PART)
+                cut = slice(h * PART, h * PART + count)
+                ref[cut, OFF - rim + k, :] = get_rim(ylo_ref, n)[:count]
+                ref[cut, OFF + sy + k, :] = get_rim(yhi_ref, n)[:count]
     src_ref[rim:rim + sx, OFF:OFF + sy, :] = heat_ref[...]
     src_ref[1:rim, OFF:OFF + sy, :] = hxlo_ref[...]
     src_ref[rim + sx:wide - 1, OFF:OFF + sy, :] = hxhi_ref[...]
@@ -238,30 +362,30 @@
     high, low = halves(solid.reshape(sx * sy, sz))
     rhs_ref[:, :sz] = high
     rhs_ref[:, sz:] = low
-    block = 512
     slots = sx * sy
-    names = lax.broadcasted_iota(jnp.int32, (block, sz), 1)
-
-    def answer(index, none):
-        base = pl.multiple_of(index * block, block)
-        code = code_ref[pl.ds(base, block), :]
+    ndev = code_ref.shape[0]
+    turned = jnp.transpose(code_ref[...])
+    names = lax.broadcasted_iota(jnp.int32, (cap, slots), 1)
+    group = ndev // 4
+    for index in range(0, ndev, group):
         pick = jnp.concatenate(
-            [jnp.where(names + at == code, 1.0, 0.0) for at in range(0, slots, sz)], axis=1
-        ).astype(BF16)
+            [
+                ones_where(names == turned[:cap, index + i:index + i + 1])
+                for i in range(group)
+            ],
+            axis=0,
+        )
         both = jnp.dot(pick, rhs_ref[...], preferred_element_type=F32)
-        reply_ref[pl.ds(base, block), :] = both[:, :sz] + both[:, sz:]
-        return none
-
-    lax.fori_loop(0, reply_ref.shape[0] // block, answer, 0)
-
-
-def solid_steps(rim, state, state_rim, heat, heat_rim, code):
-    _, sx, sy, sz = state.shape
-    total = code.shape[0]
+        reply_ref[index * cap:(index + group) * cap, :] = both[:, :sz] + both[:, sz:]
+
+
+def solid_steps(rim, cap, temp, kind, state_rim, heat, heat_rim, code):
+    sx, sy, sz = temp.shape
+    total = code.shape[0] * cap
     wide, height = sx + 2 * rim, sy + 2 * OFF
-    args = (state, *state_rim, heat, *heat_rim, code)
-    return pl.pallas_call(
-        functools.partial(solid_kernel, rim),
+    args = (temp, kind, *state_rim, heat, *heat_rim, code)
+    return pl.pallas_call(
+        functools.partial(solid_kernel, rim, cap),
         grid=(1,),
         in_specs=[whole(x.shape) for x in args],
         out_specs=[whole((sx, sy, sz)), whole((sx + 2, height, sz)), whole((total, sz))],
@@ -272,7 +396,7 @@
         ],
         scratch_shapes=[pltpu.VMEM((wide, height, sz), F32)] * 4
         + [pltpu.VMEM((sx * sy, 2 * sz), BF16)],
-        compiler_params=params(),
+        compiler_params=params(24),
         cost_estimate=cost(4 * total * sx * sy * sz, 4 * total * sz),
         name="solid_steps",
     )(*args)
@@ -306,7 +430,7 @@
         in_specs=[whole(sigma.shape)],
         out_specs=whole((3, sx, sy, sz)),
         out_shape=jax.ShapeDtypeStruct((3, sx, sy, sz), F32),
-        compiler_params=params(),
+        compiler_params=params(8),
         cost_estimate=cost(10 * sx * sy * sz, 16 * sx * sy * sz),
         name="stress",
     )(sigma)
@@ -335,23 +459,36 @@
         + [anywhere] * len(after),
         out_specs=whole((rows, row_len)),
         out_shape=jax.ShapeDtypeStruct((rows, row_len), F32),
-        compiler_params=params(),
+        compiler_params=params(10),
         cost_estimate=cost(rows * 128, 8 * rows * row_len),
         name="unpack",
     )(dest, back, *after)
 
 
-def fluid_kernel(before_ref, here_ref, after_ref, xlo_ref, xhi_ref, ylo_ref, yhi_ref,
-                 speed_ref, flux_ref, out_ref, ext_ref):
+def fluid_kernel(here_ref, xlo_ref, xhi_ref, ylo_ref, yhi_ref, speed_ref, flux_ref,
+                 out_ref, ring_ref):
     index, count = pl.program_id(0), pl.num_programs(0)
+    cx = count - 1
     _, cy, depth = here_ref.shape
     row_len = flux_ref.shape[2]
-    ext_ref[OFF:OFF + cy, :] = here_ref[0]
-    ext_ref[OFF - 1:OFF, :] = ylo_ref[0]
-    ext_ref[OFF + cy:OFF + cy + 1, :] = yhi_ref[0]
-    lanes = lax.broadcasted_iota(jnp.int32, (8, depth), 1)
-    first, last = lanes == 0, lanes == depth - 1
-    at_first, at_last = index == 0, index == count - 1
+    rows = slice(OFF, OFF + cy)
+
+    @pl.when(index == 0)
+    def _():
+        ring_ref[2, rows, :] = xlo_ref[...]
+
+    new = lax.rem(index, 3)
+
+    @pl.when(index < cx)
+    def _():
+        ring_ref[new, rows, :] = here_ref[0]
+        ring_ref[new, OFF - 1:OFF, :] = ylo_ref[pl.ds(index, 1), :]
+        ring_ref[new, OFF + cy:OFF + cy + 1, :] = yhi_ref[pl.ds(index, 1), :]
+
+    @pl.when(index == cx)
+    def _():
+        ring_ref[new, rows, :] = xhi_ref[...]
+
     rate = time_step * diffusivity
 
     def push(total, centre, lower, upper, speed):
@@ -359,59 +496,65 @@
         total = total + (rate + jnp.maximum(scaled, 0.0)) * (lower - centre)
         return total + (rate - jnp.minimum(scaled, 0.0)) * (upper - centre)
 
-    for tile in range(cy // 16):
-        speeds = [speed_ref[k, 0, tile * 16:tile * 16 + 16, :].astype(F32) for k in range(3)]
-        for part in range(2):
-            y = tile * 16 + part * 8
-            u, v, w = [s[part * 8:part * 8 + 8] for s in speeds]
-            centre = here_ref[0, y:y + 8, :]
-            lower = jnp.where(at_first, xlo_ref[0, y:y + 8, :], before_ref[0, y:y + 8, :])
-            upper = jnp.where(at_last, xhi_ref[0, y:y + 8, :], after_ref[0, y:y + 8, :])
-            total = push(centre, centre, lower, upper, u)
-            lower = ext_ref[OFF + y - 1:OFF + y + 7, :]
-            upper = ext_ref[OFF + y + 1:OFF + y + 9, :]
-            total = push(total, centre, lower, upper, v)
-            lower = jnp.where(first, 0.0, pltpu.roll(centre, 1, 1))
-            upper = jnp.where(last, 0.0, pltpu.roll(centre, depth - 1, 1))
-            total = push(total, centre, lower, upper, w)
-            out_ref[0, y:y + 8, row_len:] = total[:, row_len:]
-            out_ref[0, y:y + 8, :row_len] = (
-                total[:, :row_len] - time_step * flux_ref[0, y:y + 8, :]
-            )
+    @pl.when(index > 0)
+    def _():
+        lanes = lax.broadcasted_iota(jnp.int32, (8, depth), 1)
+        first, last = lanes == 0, lanes == depth - 1
+        mid, old = lax.rem(index + 2, 3), lax.rem(index + 1, 3)
+        for tile in range(cy // 16):
+            speeds = [speed_ref[k, 0, tile * 16:tile * 16 + 16, :].astype(F32) for k in range(3)]
+            for part in range(2):
+                y = tile * 16 + part * 8
+                at = OFF + y
+                u, v, w = [s[part * 8:part * 8 + 8] for s in speeds]
+                centre = ring_ref[mid, at:at + 8, :]
+                total = push(
+                    centre, centre, ring_ref[old, at:at + 8, :], ring_ref[new, at:at + 8, :], u
+                )
+                total = push(
+                    total, centre, ring_ref[mid, at - 1:at + 7, :],
+                    ring_ref[mid, at + 1:at + 9, :], v,
+                )
+                lower = jnp.where(first, 0.0, pltpu.roll(centre, 1, 1))
+                upper = jnp.where(last, 0.0, pltpu.roll(centre, depth - 1, 1))
+                total = push(total, centre, lower, upper, w)
+                out_ref[0, y:y + 8, row_len:] = total[:, row_len:]
+                out_ref[0, y:y + 8, :row_len] = (
+                    total[:, :row_len] - time_step * flux_ref[0, y:y + 8, :]
+                )
 
 
 def fluid_step(temp, rims, velocity, flux):
     cx, cy, depth = temp.shape
     row_len = flux.shape[2]
     plane = (1, cy, depth)
-    fixed = pl.BlockSpec(plane, lambda i: (0, 0, 0))
-    line = pl.BlockSpec((1, 1, depth), lambda i: (i, 0, 0))
+    face = pl.BlockSpec((cy, depth), lambda i: (0, 0))
+    line = pl.BlockSpec((cx, depth), lambda i: (0, 0))
+    back = lambda i: (jnp.maximum(i - 1, 0), 0, 0)
     return pl.pallas_call(
         fluid_kernel,
-        grid=(cx,),
+        grid=(cx + 1,),
         in_specs=[
-            pl.BlockSpec(plane, lambda i: (jnp.maximum(i - 1, 0), 0, 0)),
-            pl.BlockSpec(plane, lambda i: (i, 0, 0)),
-            pl.BlockSpec(plane, lambda i: (jnp.minimum(i + 1, cx - 1), 0, 0)),
-            fixed,
-            fixed,
+            pl.BlockSpec(plane, lambda i: (jnp.minimum(i, cx - 1), 0, 0)),
+            face,
+            face,
             line,
             line,
-            pl.BlockSpec((3, 1, cy, depth), lambda i: (0, i, 0, 0)),
-            pl.BlockSpec((1, cy, row_len), lambda i: (i, 0, 0)),
-        ],
-        out_specs=pl.BlockSpec(plane, lambda i: (i, 0, 0)),
+            pl.BlockSpec((3, 1, cy, depth), lambda i: (0, jnp.maximum(i - 1, 0), 0, 0)),
+            pl.BlockSpec((1, cy, row_len), back),
+        ],
+        out_specs=pl.BlockSpec(plane, back),
         out_shape=jax.ShapeDtypeStruct(temp.shape, F32),
-        scratch_shapes=[pltpu.VMEM((cy + 2 * OFF, depth), F32)],
-        compiler_params=params(),
-        cost_estimate=cost(40 * cx * cy * depth, 22 * cx * cy * depth),
+        scratch_shapes=[pltpu.VMEM((3, cy + 2 * OFF, depth), F32)],
+        compiler_params=params(16),
+        cost_estimate=cost(40 * cx * cy * depth, 14 * cx * cy * depth),
         name="fluid_step",
-    )(temp, temp, temp, *rims, velocity, flux)
+    )(temp, *rims, velocity, flux)
 
 
 def fluid_rims(temp):
-    xlo, xhi = neighbours(temp[-1:], temp[:1], "gx")
-    ylo, yhi = neighbours(temp[:, -1:], temp[:, :1], "gy")
+    xlo, xhi = neighbours(temp[-1], temp[0], "gx")
+    ylo, yhi = neighbours(temp[:, -1], temp[:, 0], "gy")
     return xlo, xhi, ylo, yhi
 
 
@@ -431,21 +574,21 @@
     )
     incoming = lax.all_to_all(outgoing, AXES, split_axis=0, concat_axis=0, tiled=True)
 
-    state = jnp.stack([temp_solid, material.astype(F32) + 1.0])
-    xlo, xhi = neighbours(state[:, sx - rim:], state[:, :rim], "gx")
-    tall = lambda cut: jnp.concatenate([xlo[:, :, cut], state[:, :, cut], xhi[:, :, cut]], axis=1)
-    ylo, yhi = neighbours(tall(slice(sy - rim, sy)), tall(slice(0, rim)), "gy")
-
-    fluid = fluid_step(temp_fluid, fluid_rims(temp_fluid), velocity, flux)
-
-    heat, code = heat_sum(incoming, cap, sx * sy, (fluid, xlo, xhi, ylo, yhi))
-    heat = heat.reshape(sx, sy, sz)
+    first, last = x_faces(rim, temp_fluid, temp_solid, material)
+    xlo, xhi = neighbours(last, first, "gx")
+    first, last = y_faces(rim, temp_fluid, temp_solid, material, xlo[cy:], xhi[cy:])
+    ylo, yhi = neighbours(last, first, "gy")
+    rims = (xlo[cy:], xhi[cy:], ylo[cx:], yhi[cx:])
+
+    fluid = fluid_step(temp_fluid, (xlo, xhi, ylo, yhi), velocity, flux)
+
     thin = rim - 1
-    hxlo, hxhi = neighbours(heat[sx - thin:], heat[:thin], "gx")
-    tall2 = lambda cut: jnp.concatenate([hxlo[:, cut], heat[:, cut], hxhi[:, cut]], axis=0)
-    hylo, hyhi = neighbours(tall2(slice(sy - thin, sy)), tall2(slice(0, thin)), "gy")
+    heat, first, last, code = heat_sum(incoming, cap, temp_solid.shape, thin, (fluid, *rims))
+    hxlo, hxhi = neighbours(last, first, "gx")
+    tall = lambda cut: jnp.concatenate([hxlo[:, cut], heat[:, cut], hxhi[:, cut]], axis=0)
+    hylo, hyhi = neighbours(tall(slice(sy - thin, sy)), tall(slice(0, thin)), "gy")
     solid, sigma, replies = solid_steps(
-        rim, state, (xlo, xhi, ylo, yhi), heat, (hxlo, hxhi, hylo, hyhi), code
+        rim, cap, temp_solid, material, rims, heat, (hxlo, hxhi, hylo, hyhi), code
     )
     returned = lax.all_to_all(
         replies.reshape(ndev, cap, sz), AXES, split_axis=0, concat_axis=0, tiled=True

time: 189 us -> 172 us (0.910)
  Pallas kernels: 58.2 us -> 34.7 us
  waiting for transfers between devices: 57.7 us -> 74.2 us
  starting transfers between devices: 57.1 us -> 43.2 us
  local copies, waits for them, and re-layouts: 12.5 us -> 18.4 us
    pallas_call x4 -> x6, Pallas kernels: 43.4 us -> 23.8 us  [the longest x2 18.2 us: fluid_step(): pl.pallas_call(fluid_kernel, grid=(cx + 1,), in_specs=[pl.BlockSpec(plane...]
    ppermute x16 -> x12, waiting for transfers between devices: 57.7 us -> 74.2 us  [neighbours(): return (lax.ppermute(before, axis, up), lax.ppermute(after, axis, down))]
    ppermute x16 -> x12, starting transfers between devices: 46.9 us -> 33 us  [neighbours(): return (lax.ppermute(before, axis, up), lax.ppermute(after, axis, down))]
    unnamed x40 -> x32, local copies, waits for them, and re-layouts: 5.95 us -> 15.9 us
    slice x7 -> x5, local copies, waits for them, and re-layouts: 5.63 us -> 1.35 us  [the longest x1 1.3 us: fluid_rims(): ylo, yhi = neighbours(temp[:, -1], temp[:, 0], 'gy')]
    pallas_call x1, Pallas kernels: 8.44 us -> 6.33 us  [pack(): pl.pallas_call(functools.partial(pack_kernel, cap), grid=(1,), in_specs=[...]
  transfers between devices with their start and end apart: 18 -> 14, of which waited for: 6 -> 9; matrix products, arithmetic and copies ran while one was open for 4% -> 1% of each run, Pallas kernels for 19% -> 12%
where the time goes in v3:
time: 172 us; the launch traced here: 171 us
  waiting for transfers between devices  74.2 us (43%)
  starting transfers between devices  43.2 us (25%)
  Pallas kernels  34.7 us (20%)
  local copies, waits for them, and re-layouts  18.4 us (11%)
    ppermute x12, waiting for transfers between devices, neighbours(): return (lax.ppermute(before, axis, up), lax.ppermute(after, axis, down))  74.2 us
    ppermute x12, starting transfers between devices, neighbours(): return (lax.ppermute(before, axis, up), lax.ppermute(after, axis, down))  33 us
    pallas_call x2, Pallas kernels, fluid_step(): pl.pallas_call(fluid_kernel, grid=(cx + 1,), in_specs=[pl.BlockSpec(plane...  18.2 us
    unnamed x32, local copies, waits for them, and re-layouts  15.9 us
    all_to_all x1, starting transfers between devices, body(): lax.all_to_all(outgoing, AXES, split_axis=0, concat_axis=0, tiled=True)  6.33 us
    pallas_call x1, Pallas kernels, pack(): pl.pallas_call(functools.partial(pack_kernel, cap), grid=(1,), in_specs=[...  6.33 us
    all_to_all x1, starting transfers between devices, body(): lax.all_to_all(replies.reshape(ndev, cap, sz), AXES, split_axis=0, concat...  3.89 us
  transfers between devices with their start and end apart: 14, of which 9 were waited for; matrix products, arithmetic and copies ran while one was open for 1% of the time, Pallas kernels for 12%

profile of v3, /device:TPU:11, one launch (start us, length us, event | category | flops | bytes accessed | tf_op | source)
XLA Modules:
  0.0 171.5 jit_solution(8665628089491865546)
XLA Ops:
  0.6 0.0 copy-start.10
  0.6 0.0 copy-start.11
  0.7 6.3 %pack.1 = (f32[32,104,128]{2,1,0:T(8,128)}, f32[16,64,128]{2,1,0:T(8,128)}, s32[1,1024]{1,0:T(1,128)}) custom-call(s32[1,1024]{1,0:T(1,128)} %bitcast.21, s32[1,1024]{1,0:T(1,128)} %slot_ref.1, f32[16,64,1024]{2,1,0:T(8,128)} %here_ref.1, f32[16,64,128]{2,1,0:T(8,128)} %old_ref.1, s32[16,64,128]{2,1,0:T(8,128)} %mask_ref.1), custom_call_target="tpu_custom_call" | custom-call | flops 1744830464 | bytes 2621440 | tf_op jit(solution)/shard_map/pack/pallas_call | solution.py:116
  7.0 6.3 %all-to-all-start = ((f32[32,104,128]{2,1,0:T(8,128)}), f32[32,104,128]{2,1,0:T(8,128)S(1)}, u32[]{:S(2)}, u32[]{:S(2)}) async-start(f32[32,104,128]{2,1,0:T(8,128)} %get-tuple-element.24), calls=%async_computation | async-start | bytes 3407872 | tf_op jit(solution)/shard_map/all_to_all | solution.py:575
  13.3 0.0 copy-done.10
  13.3 0.0 copy-done.11
  13.3 0.0 copy-start
  13.4 2.2 %copy-done = f32[16,64,1024]{2,1,0:T(8,128)S(1)} copy-done((f32[16,64,1024]{2,1,0:T(8,128)S(1)}, f32[16,64,1024]{2,1,0:T(8,128)}, u32[]{:S(2)}) %copy-start) | copy-done | bytes 4194328
  15.5 0.0 copy-start.1
  15.5 0.0 slice-start
  15.5 0.1 x_faces.1
  15.6 3.6 %collective-permute-start = (f32[112,1024]{1,0:T(8,128)S(1)}, f32[112,1024]{1,0:T(8,128)S(1)}, u32[]{:S(2)}, u32[]{:S(2)}) collective-permute-start(f32[112,1024]{1,0:T(8,128)S(1)} %get-tuple-element.18), channel_id=1, source_target_pairs={{0,4},{4,8},{8,12},{12,16},{16,20},{20,24},{24,28},{1,5},{5,9},{9,... | collective-permute-start | bytes 1376264 | tf_op jit(solution)/shard_map/ppermute | solution.py:48
  19.2 1.9 %collective-permute-start.1 = (f32[112,1024]{1,0:T(8,128)S(1)}, f32[112,1024]{1,0:T(8,128)S(1)}, u32[]{:S(2)}, u32[]{:S(2)}) collective-permute-start(f32[112,1024]{1,0:T(8,128)S(1)} %get-tuple-element.19), channel_id=1, source_target_pairs={{4,0},{8,4},{12,8},{16,12},{20,16},{24,20},{28,24},{5,1},{9,5},{13... | collective-permute-start | bytes 1376264 | tf_op jit(solution)/shard_map/ppermute | solution.py:48
  21.1 34.2 %collective-permute-done.xlo_ref = f32[112,1024]{1,0:T(8,128)S(1)} collective-permute-done((f32[112,1024]{1,0:T(8,128)S(1)}, f32[112,1024]{1,0:T(8,128)S(1)}, u32[]{:S(2)}, u32[]{:S(2)}) %collective-permute-start) | collective-permute-done | bytes 458784 | tf_op jit(solution)/shard_map/ppermute | solution.py:48
  55.4 1.7 collective-permute-done.1.xhi_ref
  57.1 0.0 copy-done.1
  57.1 0.0 slice-start.1
  57.1 0.0 copy-start.8
  57.1 0.3 y_faces.1
  57.4 3.4 %collective-permute-start.2 = (f32[64,1024]{1,0:T(8,128)S(1)}, f32[64,1024]{1,0:T(8,128)S(1)}, u32[]{:S(2)}, u32[]{:S(2)}) collective-permute-start(f32[64,1024]{1,0:T(8,128)S(1)} %get-tuple-element.20), channel_id=1, source_target_pairs={{0,1},{1,2},{2,3},{4,5},{5,6},{6,7},{8,9},{9,10},{10,11},{12,13},{... | collective-permute-start | bytes 786440 | tf_op jit(solution)/shard_map/ppermute | solution.py:48
  60.9 2.0 %collective-permute-start.3 = (f32[64,1024]{1,0:T(8,128)S(1)}, f32[64,1024]{1,0:T(8,128)S(1)}, u32[]{:S(2)}, u32[]{:S(2)}) collective-permute-start(f32[64,1024]{1,0:T(8,128)S(1)} %get-tuple-element.21), channel_id=1, source_target_pairs={{1,0},{2,1},{3,2},{5,4},{6,5},{7,6},{9,8},{10,9},{11,10},{13,12},{... | collective-permute-start | bytes 786440 | tf_op jit(solution)/shard_map/ppermute | solution.py:48
  62.9 1.8 %collective-permute-done.2.ylo_ref = f32[64,1024]{1,0:T(8,128)S(1)} collective-permute-done((f32[64,1024]{1,0:T(8,128)S(1)}, f32[64,1024]{1,0:T(8,128)S(1)}, u32[]{:S(2)}, u32[]{:S(2)}) %collective-permute-start.2) | collective-permute-done | bytes 262176 | tf_op jit(solution)/shard_map/ppermute | solution.py:48
  64.7 4.2 %collective-permute-done.3.yhi_ref = f32[64,1024]{1,0:T(8,128)S(1)} collective-permute-done((f32[64,1024]{1,0:T(8,128)S(1)}, f32[64,1024]{1,0:T(8,128)S(1)}, u32[]{:S(2)}, u32[]{:S(2)}) %collective-permute-start.3) | collective-permute-done | bytes 262176 | tf_op jit(solution)/shard_map/ppermute | solution.py:48
  68.9 0.0 slice-done
  68.9 0.0 slice-done.1
  68.9 0.0 copy-done.8
  69.0 8.1 %fluid_step.2.here_ref.refs_0_ = f32[16,64,1024]{2,1,0:T(8,128)S(1)} custom-call(f32[16,64,1024]{2,1,0:T(8,128)S(1)} %copy-done.1, f32[112,1024]{1,0:T(8,128)S(1)} %collective-permute-done.xlo_ref, f32[112,1024]{1,0:T(8,128)S(1)} %collective-permute-done.1.xhi_ref, f32[64,1024]{1,0:T(8,128)S(1)} %collective-permute-done.2.ylo_ref, ...), custom_call_target="tpu_custom_call" | custom-call | flops 41943040 | bytes 14680064 | tf_op jit(solution)/shard_map/fluid_step/pallas_call | solution.py:534
  77.1 0.0 copy-start.2
  77.1 2.0 %copy-done.2 = f32[16,64,1024]{2,1,0:T(8,128)} copy-done((f32[16,64,1024]{2,1,0:T(8,128)}, f32[16,64,1024]{2,1,0:T(8,128)S(1)}, u32[]{:S(2)}) %copy-start.2) | copy-done | bytes 4194328
  79.1 0.0 all-to-all-done.rows_ref
  79.1 0.0 copy-start.3
  79.1 2.2 %copy-done.3 = f32[16,64,1024]{2,1,0:T(8,128)S(1)} copy-done((f32[16,64,1024]{2,1,0:T(8,128)S(1)}, f32[16,64,1024]{2,1,0:T(8,128)}, u32[]{:S(2)}) %copy-start.3) | copy-done | bytes 4194328
  81.3 2.1 %heat_sum.1 = (f32[16,32,128]{2,1,0:T(8,128)S(1)}, f32[4,32,128]{2,1,0:T(8,128)S(1)}, f32[4,32,128]{2,1,0:T(8,128)S(1)}, s32[32,128]{1,0:T(8,128)S(1)}) custom-call(f32[32,104,128]{2,1,0:T(8,128)S(1)} %all-to-all-done.rows_ref, f32[16,64,1024]{2,1,0:T(8,128)S(1)} %copy-done.3, f32[48,1024]{1,0:T(8,128)S(1)} %slice.58.lo_ref.refs_1_.xlo_ref, ...), custom_call_target="tpu_custom_call" | custom-call | flops 872415232 | bytes 1703936 | tf_op jit(solution)/shard_map/heat_sum/pallas_call | solution.py:179
  83.4 4.0 %collective-permute-start.8 = (f32[4,32,128]{2,1,0:T(8,128)S(1)}, f32[4,32,128]{2,1,0:T(8,128)S(1)}, u32[]{:S(2)}, u32[]{:S(2)}) collective-permute-start(f32[4,32,128]{2,1,0:T(8,128)S(1)} %get-tuple-element.26), channel_id=1, source_target_pairs={{0,4},{4,8},{8,12},{12,16},{16,20},{20,24},{24,28},{1,5},{5,9},{9,... | collective-permute-start | bytes 196616 | tf_op jit(solution)/shard_map/ppermute | solution.py:48
  87.4 1.9 %collective-permute-start.9 = (f32[4,32,128]{2,1,0:T(8,128)S(1)}, f32[4,32,128]{2,1,0:T(8,128)S(1)}, u32[]{:S(2)}, u32[]{:S(2)}) collective-permute-start(f32[4,32,128]{2,1,0:T(8,128)S(1)} %get-tuple-element.27), channel_id=1, source_target_pairs={{4,0},{8,4},{12,8},{16,12},{20,16},{24,20},{28,24},{5,1},{9,5},{13... | collective-permute-start | bytes 196616 | tf_op jit(solution)/shard_map/ppermute | solution.py:48
  89.3 0.0 collective-permute-done.8.hxlo_ref
  89.4 3.6 %collective-permute-done.9.hxhi_ref = f32[4,32,128]{2,1,0:T(8,128)S(1)} collective-permute-done((f32[4,32,128]{2,1,0:T(8,128)S(1)}, f32[4,32,128]{2,1,0:T(8,128)S(1)}, u32[]{:S(2)}, u32[]{:S(2)}) %collective-permute-start.9) | collective-permute-done | bytes 65568 | tf_op jit(solution)/shard_map/ppermute | solution.py:48
  93.0 2.7 %collective-permute-start.10 = (f32[24,4,128]{2,1,0:T(4,128)S(1)}, f32[24,4,128]{2,1,0:T(4,128)S(1)}, u32[]{:S(2)}, u32[]{:S(2)}) collective-permute-start(f32[24,4,128]{2,1,0:T(4,128)S(1)} %pad_maximum_fusion), channel_id=1, source_target_pairs={{0,1},{1,2},{2,3},{4,5},{5,6},{6,7},{8,9},{9,10},{10,11},{12,13},{... | collective-permute-start | bytes 147464 | tf_op jit(solution)/shard_map/ppermute | solution.py:48
  95.7 2.6 %collective-permute-start.11 = (f32[24,4,128]{2,1,0:T(4,128)S(1)}, f32[24,4,128]{2,1,0:T(4,128)S(1)}, u32[]{:S(2)}, u32[]{:S(2)}) collective-permute-start(f32[24,4,128]{2,1,0:T(4,128)S(1)} %pad_maximum_fusion.1), channel_id=1, source_target_pairs={{1,0},{2,1},{3,2},{5,4},{6,5},{7,6},{9,8},{10,9},{11,10},{13,12},{... | collective-permute-start | bytes 147464 | tf_op jit(solution)/shard_map/ppermute | solution.py:48
  98.3 0.0 collective-permute-done.10.hylo_ref
  98.3 3.1 %collective-permute-done.11.hyhi_ref = f32[24,4,128]{2,1,0:T(4,128)S(1)} collective-permute-done((f32[24,4,128]{2,1,0:T(4,128)S(1)}, f32[24,4,128]{2,1,0:T(4,128)S(1)}, u32[]{:S(2)}, u32[]{:S(2)}) %collective-permute-start.11) | collective-permute-done | bytes 49184 | tf_op jit(solution)/shard_map/ppermute | solution.py:48
  101.5 3.1 %solid_steps.1 = (f32[16,32,128]{2,1,0:T(8,128)}, f32[18,48,128]{2,1,0:T(8,128)S(1)}, f32[3072,128]{1,0:T(8,128)S(1)}) custom-call(f32[16,32,128]{2,1,0:T(8,128)S(1)} %copy-done.10, s32[16,32,128]{2,1,0:T(8,128)S(1)} %copy-done.11, f32[48,1024]{1,0:T(8,128)S(1)} %slice.58.lo_ref.refs_1_.xlo_ref, f32[48,1024]{1,0:T(8,128)S(1)} %slice.59.hi_ref.refs_2_.xhi_ref, ...), custom_call_target="tpu_custom_call" | custom-call | flops 805306368 | bytes 1572864 | tf_op jit(solution)/shard_map/solid_steps/pallas_call | solution.py:387
  104.6 1.2 copy-done.9
  105.8 3.9 %all-to-all-start.1 = ((f32[32,96,128]{2,1,0:T(8,128)}), f32[32,96,128]{2,1,0:T(8,128)S(1)}, u32[]{:S(2)}, u32[]{:S(2)}) async-start(f32[32,96,128]{2,1,0:T(8,128)} %bitcast.17), calls=%async_computation.1 | async-start | bytes 3145728 | tf_op jit(solution)/shard_map/all_to_all | solution.py:593
  109.7 1.1 slice_bitcast_fusion
  110.8 2.3 %collective-permute-start.5 = (f32[64,1024]{1,0:T(8,128)S(1)}, f32[64,1024]{1,0:T(8,128)S(1)}, u32[]{:S(2)}, u32[]{:S(2)}) collective-permute-start(f32[64,1024]{1,0:T(8,128)S(1)} %get-tuple-element.34), channel_id=1, source_target_pairs={{4,0},{8,4},{12,8},{16,12},{20,16},{24,20},{28,24},{5,1},{9,5},{13... | collective-permute-start | bytes 786440 | tf_op jit(solution)/shard_map/ppermute | solution.py:48
  113.0 3.3 %collective-permute-start.4 = (f32[64,1024]{1,0:T(8,128)S(1)}, f32[64,1024]{1,0:T(8,128)S(1)}, u32[]{:S(2)}, u32[]{:S(2)}) collective-permute-start(f32[64,1024]{1,0:T(8,128)S(1)} %get-tuple-element.35), channel_id=1, source_target_pairs={{0,4},{4,8},{8,12},{12,16},{16,20},{20,24},{24,28},{1,5},{5,9},{9,... | collective-permute-start | bytes 786440 | tf_op jit(solution)/shard_map/ppermute | solution.py:48
  116.3 1.3 fusion
  117.7 0.0 copy-start.12
  117.7 3.1 %collective-permute-start.6 = (f32[16,1024]{1,0:T(8,128)S(1)}, f32[16,1024]{1,0:T(8,128)S(1)}, u32[]{:S(2)}, u32[]{:S(2)}) collective-permute-start(f32[16,1024]{1,0:T(8,128)S(1)} %bitcast.20), channel_id=1, source_target_pairs={{0,1},{1,2},{2,3},{4,5},{5,6},{6,7},{8,9},{9,10},{10,11},{12,13},{... | collective-permute-start | bytes 196616 | tf_op jit(solution)/shard_map/ppermute | solution.py:48
  120.8 2.2 %collective-permute-start.7 = (f32[16,1024]{1,0:T(8,128)S(1)}, f32[16,1024]{1,0:T(8,128)S(1)}, u32[]{:S(2)}, u32[]{:S(2)}) collective-permute-start(f32[16,1024]{1,0:T(8,128)S(1)} %bitcast.19), channel_id=1, source_target_pairs={{1,0},{2,1},{3,2},{5,4},{6,5},{7,6},{9,8},{10,9},{11,10},{13,12},{... | collective-permute-start | bytes 196616 | tf_op jit(solution)/shard_map/ppermute | solution.py:48
  123.0 1.9 %collective-permute-done.6.ylo_ref = f32[16,1024]{1,0:T(8,128)S(1)} collective-permute-done((f32[16,1024]{1,0:T(8,128)S(1)}, f32[16,1024]{1,0:T(8,128)S(1)}, u32[]{:S(2)}, u32[]{:S(2)}) %collective-permute-start.6) | collective-permute-done | bytes 65568 | tf_op jit(solution)/shard_map/ppermute | solution.py:48
  124.9 4.5 %collective-permute-done.7.yhi_ref = f32[16,1024]{1,0:T(8,128)S(1)} collective-permute-done((f32[16,1024]{1,0:T(8,128)S(1)}, f32[16,1024]{1,0:T(8,128)S(1)}, u32[]{:S(2)}, u32[]{:S(2)}) %collective-permute-start.7) | collective-permute-done | bytes 65568 | tf_op jit(solution)/shard_map/ppermute | solution.py:48
  129.4 19.2 %collective-permute-done.5.xhi_ref = f32[64,1024]{1,0:T(8,128)S(1)} collective-permute-done((f32[64,1024]{1,0:T(8,128)S(1)}, f32[64,1024]{1,0:T(8,128)S(1)}, u32[]{:S(2)}, u32[]{:S(2)}) %collective-permute-start.5) | collective-permute-done | bytes 262176 | tf_op jit(solution)/shard_map/ppermute | solution.py:48
  148.5 0.0 collective-permute-done.4.xlo_ref
  148.5 2.2 %copy-done.4 = f32[16,64,1024]{2,1,0:T(8,128)S(1)} copy-done((f32[16,64,1024]{2,1,0:T(8,128)S(1)}, f32[16,64,1024]{2,1,0:T(8,128)}, u32[]{:S(2)}) %copy-start.4) | copy-done | bytes 4194328
  150.7 2.8 %copy-done.5 = bf16[3,16,64,1024]{3,2,1,0:T(8,128)(2,1)S(1)} copy-done((bf16[3,16,64,1024]{3,2,1,0:T(8,128)(2,1)S(1)}, bf16[3,16,64,1024]{3,2,1,0:T(8,128)(2,1)}, u32[]{:S(2)}) %copy-start.5) | copy-done | bytes 6291480
  153.5 10.1 %fluid_step.3.refs_0_ = f32[16,64,1024]{2,1,0:T(8,128)} custom-call(f32[16,64,1024]{2,1,0:T(8,128)S(1)} %copy-done.4, f32[64,1024]{1,0:T(8,128)S(1)} %collective-permute-done.4.xlo_ref, f32[64,1024]{1,0:T(8,128)S(1)} %collective-permute-done.5.xhi_ref, f32[16,1024]{1,0:T(8,128)S(1)} %collective-permute-done.6.ylo_ref, ...), custom_call_target="tpu_custom_call" | custom-call | flops 41943040 | bytes 14680064 | tf_op jit(solution)/shard_map/fluid_step/pallas_call | solution.py:534
  163.6 2.1 %stress.1.refs_1_ = f32[3,16,32,128]{3,2,1,0:T(8,128)} custom-call(f32[18,48,128]{2,1,0:T(8,128)S(1)} %get-tuple-element.30.sigma_ref), custom_call_target="tpu_custom_call" | custom-call | flops 655360 | bytes 1048576 | tf_op jit(solution)/shard_map/stress/pallas_call | solution.py:427
  165.8 0.0 all-to-all-done.1
  165.8 0.0 copy-done.12
  165.8 2.2 %copy-done.6 = f32[16,64,1024]{2,1,0:T(8,128)S(1)} copy-done((f32[16,64,1024]{2,1,0:T(8,128)S(1)}, f32[16,64,1024]{2,1,0:T(8,128)}, u32[]{:S(2)}) %copy-start.6) | copy-done | bytes 4194328
  168.0 1.1 copy-done.7
  169.1 2.4 %unpack.1 = f32[1024,128]{1,0:T(8,128)} custom-call(s32[1,1024]{1,0:T(1,128)S(1)} %copy-done.12, f32[3072,128]{1,0:T(8,128)S(1)} %bitcast.16, f32[16,64,1024]{2,1,0:T(8,128)S(1)} %copy-done.6, f32[3,16,32,128]{3,2,1,0:T(8,128)S(1)} %copy-done.7), custom_call_target="tpu_custom_call" | custom-call | flops 131072 | bytes 1048576 | tf_op jit(solution)/shard_map/unpack/pallas_call | solution.py:455
  (17 shorter events, 0.1 us)
Async XLA Ops:
  0.6 12.7 %copy-start.10 = (f32[16,32,128]{2,1,0:T(8,128)S(1)}, f32[16,32,128]{2,1,0:T(8,128)}, u32[]{:S(2)}) copy-start(f32[16,32,128]{2,1,0:T(8,128)} %own_ref.1) | copy-start | bytes 786436
  0.6 12.7 %copy-start.11 = (s32[16,32,128]{2,1,0:T(8,128)S(1)}, s32[16,32,128]{2,1,0:T(8,128)}, u32[]{:S(2)}) copy-start(s32[16,32,128]{2,1,0:T(8,128)} %kind_ref.5) | copy-start | bytes 786436
  7.0 72.1 %all-to-all-start = ((f32[32,104,128]{2,1,0:T(8,128)}), f32[32,104,128]{2,1,0:T(8,128)S(1)}, u32[]{:S(2)}, u32[]{:S(2)}) async-start(f32[32,104,128]{2,1,0:T(8,128)} %get-tuple-element.24), calls=%async_computation | async-start | bytes 3407872 | tf_op jit(solution)/shard_map/all_to_all | solution.py:575
  13.3 2.2 %copy-start = (f32[16,64,1024]{2,1,0:T(8,128)S(1)}, f32[16,64,1024]{2,1,0:T(8,128)}, u32[]{:S(2)}) copy-start(f32[16,64,1024]{2,1,0:T(8,128)} %here_ref.1) | copy-start | bytes 12582916
  15.5 41.6 %copy-start.1 = (f32[16,64,1024]{2,1,0:T(8,128)S(1)}, f32[16,64,1024]{2,1,0:T(8,128)}, u32[]{:S(2)}) copy-start(f32[16,64,1024]{2,1,0:T(8,128)} %here_ref.1) | copy-start | bytes 12582916
  15.5 53.4 %slice-start = ((s8[6291456]{0:T(1024)(128)(4,1)}), s8[4194304]{0:T(1024)(128)(4,1)S(1)}, s32[]{:S(2)}) async-start(s8[6291456]{0:T(1024)(128)(4,1)} %bitcast.14), calls=%async_computation.2 | async-start | bytes 8388608
  15.6 39.8 %collective-permute-start = (f32[112,1024]{1,0:T(8,128)S(1)}, f32[112,1024]{1,0:T(8,128)S(1)}, u32[]{:S(2)}, u32[]{:S(2)}) collective-permute-start(f32[112,1024]{1,0:T(8,128)S(1)} %get-tuple-element.18), channel_id=1, source_target_pairs={{0,4},{4,8},{8,12},{12,16},{16,20},{20,24},{24,28},{1,5},{5,9},{9,... | collective-permute-start | bytes 1376264 | tf_op jit(solution)/shard_map/ppermute | solution.py:48
  19.2 37.9 %collective-permute-start.1 = (f32[112,1024]{1,0:T(8,128)S(1)}, f32[112,1024]{1,0:T(8,128)S(1)}, u32[]{:S(2)}, u32[]{:S(2)}) collective-permute-start(f32[112,1024]{1,0:T(8,128)S(1)} %get-tuple-element.19), channel_id=1, source_target_pairs={{4,0},{8,4},{12,8},{16,12},{20,16},{24,20},{28,24},{5,1},{9,5},{13... | collective-permute-start | bytes 1376264 | tf_op jit(solution)/shard_map/ppermute | solution.py:48
  57.1 11.8 %slice-start.1 = ((s8[6291456]{0:T(1024)(128)(4,1)}), s8[2097152]{0:T(1024)(128)(4,1)S(1)}, s32[]{:S(2)}) async-start(s8[6291456]{0:T(1024)(128)(4,1)} %bitcast.14), calls=%async_computation.3 | async-start | bytes 4194304
  57.1 11.8 %copy-start.8 = (f32[16,64,128]{2,1,0:T(8,128)S(1)}, f32[16,64,128]{2,1,0:T(8,128)}, u32[]{:S(2)}) copy-start(f32[16,64,128]{2,1,0:T(8,128)} %get-tuple-element.22.flux_ref) | copy-start | bytes 1572868
  57.4 7.2 %collective-permute-start.2 = (f32[64,1024]{1,0:T(8,128)S(1)}, f32[64,1024]{1,0:T(8,128)S(1)}, u32[]{:S(2)}, u32[]{:S(2)}) collective-permute-start(f32[64,1024]{1,0:T(8,128)S(1)} %get-tuple-element.20), channel_id=1, source_target_pairs={{0,1},{1,2},{2,3},{4,5},{5,6},{6,7},{8,9},{9,10},{10,11},{12,13},{... | collective-permute-start | bytes 786440 | tf_op jit(solution)/shard_map/ppermute | solution.py:48
  60.9 8.0 %collective-permute-start.3 = (f32[64,1024]{1,0:T(8,128)S(1)}, f32[64,1024]{1,0:T(8,128)S(1)}, u32[]{:S(2)}, u32[]{:S(2)}) collective-permute-start(f32[64,1024]{1,0:T(8,128)S(1)} %get-tuple-element.21), channel_id=1, source_target_pairs={{1,0},{2,1},{3,2},{5,4},{6,5},{7,6},{9,8},{10,9},{11,10},{13,12},{... | collective-permute-start | bytes 786440 | tf_op jit(solution)/shard_map/ppermute | solution.py:48
  77.1 2.0 %copy-start.2 = (f32[16,64,1024]{2,1,0:T(8,128)}, f32[16,64,1024]{2,1,0:T(8,128)S(1)}, u32[]{:S(2)}) copy-start(f32[16,64,1024]{2,1,0:T(8,128)S(1)} %fluid_step.2.here_ref.refs_0_) | copy-start | bytes 12582916
  79.1 2.2 %copy-start.3 = (f32[16,64,1024]{2,1,0:T(8,128)S(1)}, f32[16,64,1024]{2,1,0:T(8,128)}, u32[]{:S(2)}) copy-start(f32[16,64,1024]{2,1,0:T(8,128)} %copy-done.2) | copy-start | bytes 12582916
  83.4 6.0 %collective-permute-start.8 = (f32[4,32,128]{2,1,0:T(8,128)S(1)}, f32[4,32,128]{2,1,0:T(8,128)S(1)}, u32[]{:S(2)}, u32[]{:S(2)}) collective-permute-start(f32[4,32,128]{2,1,0:T(8,128)S(1)} %get-tuple-element.26), channel_id=1, source_target_pairs={{0,4},{4,8},{8,12},{12,16},{16,20},{20,24},{24,28},{1,5},{5,9},{9,... | collective-permute-start | bytes 196616 | tf_op jit(solution)/shard_map/ppermute | solution.py:48
  87.4 5.6 %collective-permute-start.9 = (f32[4,32,128]{2,1,0:T(8,128)S(1)}, f32[4,32,128]{2,1,0:T(8,128)S(1)}, u32[]{:S(2)}, u32[]{:S(2)}) collective-permute-start(f32[4,32,128]{2,1,0:T(8,128)S(1)} %get-tuple-element.27), channel_id=1, source_target_pairs={{4,0},{8,4},{12,8},{16,12},{20,16},{24,20},{28,24},{5,1},{9,5},{13... | collective-permute-start | bytes 196616 | tf_op jit(solution)/shard_map/ppermute | solution.py:48
  93.0 5.3 %collective-permute-start.10 = (f32[24,4,128]{2,1,0:T(4,128)S(1)}, f32[24,4,128]{2,1,0:T(4,128)S(1)}, u32[]{:S(2)}, u32[]{:S(2)}) collective-permute-start(f32[24,4,128]{2,1,0:T(4,128)S(1)} %pad_maximum_fusion), channel_id=1, source_target_pairs={{0,1},{1,2},{2,3},{4,5},{5,6},{6,7},{8,9},{9,10},{10,11},{12,13},{... | collective-permute-start | bytes 147464 | tf_op jit(solution)/shard_map/ppermute | solution.py:48
  95.7 5.7 %collective-permute-start.11 = (f32[24,4,128]{2,1,0:T(4,128)S(1)}, f32[24,4,128]{2,1,0:T(4,128)S(1)}, u32[]{:S(2)}, u32[]{:S(2)}) collective-permute-start(f32[24,4,128]{2,1,0:T(4,128)S(1)} %pad_maximum_fusion.1), channel_id=1, source_target_pairs={{1,0},{2,1},{3,2},{5,4},{6,5},{7,6},{9,8},{10,9},{11,10},{13,12},{... | collective-permute-start | bytes 147464 | tf_op jit(solution)/shard_map/ppermute | solution.py:48
  104.6 1.2 copy-start.9
  105.8 60.0 %all-to-all-start.1 = ((f32[32,96,128]{2,1,0:T(8,128)}), f32[32,96,128]{2,1,0:T(8,128)S(1)}, u32[]{:S(2)}, u32[]{:S(2)}) async-start(f32[32,96,128]{2,1,0:T(8,128)} %bitcast.17), calls=%async_computation.1 | async-start | bytes 3145728 | tf_op jit(solution)/shard_map/all_to_all | solution.py:593
  110.8 37.8 %collective-permute-start.5 = (f32[64,1024]{1,0:T(8,128)S(1)}, f32[64,1024]{1,0:T(8,128)S(1)}, u32[]{:S(2)}, u32[]{:S(2)}) collective-permute-start(f32[64,1024]{1,0:T(8,128)S(1)} %get-tuple-element.34), channel_id=1, source_target_pairs={{4,0},{8,4},{12,8},{16,12},{20,16},{24,20},{28,24},{5,1},{9,5},{13... | collective-permute-start | bytes 786440 | tf_op jit(solution)/shard_map/ppermute | solution.py:48
  113.0 35.5 %collective-permute-start.4 = (f32[64,1024]{1,0:T(8,128)S(1)}, f32[64,1024]{1,0:T(8,128)S(1)}, u32[]{:S(2)}, u32[]{:S(2)}) collective-permute-start(f32[64,1024]{1,0:T(8,128)S(1)} %get-tuple-element.35), channel_id=1, source_target_pairs={{0,4},{4,8},{8,12},{12,16},{16,20},{20,24},{24,28},{1,5},{5,9},{9,... | collective-permute-start | bytes 786440 | tf_op jit(solution)/shard_map/ppermute | solution.py:48
  117.7 48.1 %copy-start.12 = (s32[1,1024]{1,0:T(1,128)S(1)}, s32[1,1024]{1,0:T(1,128)}, u32[]{:S(2)}) copy-start(s32[1,1024]{1,0:T(1,128)} %get-tuple-element.23.dest_ref) | copy-start | bytes 12292
  117.7 7.2 %collective-permute-start.6 = (f32[16,1024]{1,0:T(8,128)S(1)}, f32[16,1024]{1,0:T(8,128)S(1)}, u32[]{:S(2)}, u32[]{:S(2)}) collective-permute-start(f32[16,1024]{1,0:T(8,128)S(1)} %bitcast.20), channel_id=1, source_target_pairs={{0,1},{1,2},{2,3},{4,5},{5,6},{6,7},{8,9},{9,10},{10,11},{12,13},{... | collective-permute-start | bytes 196616 | tf_op jit(solution)/shard_map/ppermute | solution.py:48
  120.8 8.6 %collective-permute-start.7 = (f32[16,1024]{1,0:T(8,128)S(1)}, f32[16,1024]{1,0:T(8,128)S(1)}, u32[]{:S(2)}, u32[]{:S(2)}) collective-permute-start(f32[16,1024]{1,0:T(8,128)S(1)} %bitcast.19), channel_id=1, source_target_pairs={{1,0},{2,1},{3,2},{5,4},{6,5},{7,6},{9,8},{10,9},{11,10},{13,12},{... | collective-permute-start | bytes 196616 | tf_op jit(solution)/shard_map/ppermute | solution.py:48
  148.5 2.2 %copy-start.4 = (f32[16,64,1024]{2,1,0:T(8,128)S(1)}, f32[16,64,1024]{2,1,0:T(8,128)}, u32[]{:S(2)}) copy-start(f32[16,64,1024]{2,1,0:T(8,128)} %copy-done.2) | copy-start | bytes 12582916
  150.7 2.8 %copy-start.5 = (bf16[3,16,64,1024]{3,2,1,0:T(8,128)(2,1)S(1)}, bf16[3,16,64,1024]{3,2,1,0:T(8,128)(2,1)}, u32[]{:S(2)}) copy-start(bf16[3,16,64,1024]{3,2,1,0:T(8,128)(2,1)} %speed_ref.3) | copy-start | bytes 18874372
  165.8 2.2 %copy-start.6 = (f32[16,64,1024]{2,1,0:T(8,128)S(1)}, f32[16,64,1024]{2,1,0:T(8,128)}, u32[]{:S(2)}) copy-start(f32[16,64,1024]{2,1,0:T(8,128)} %fluid_step.3.refs_0_) | copy-start | bytes 12582916
  168.0 1.1 copy-start.7

commit v4 on v3

--- a/solution.py
+++ b/solution.py
@@ -55,30 +55,24 @@
 anywhere = pl.BlockSpec(memory_space=pl.ANY)
 
 
-def pack_kernel(cap, owner_ref, slot_ref, temp_ref, old_ref, mask_ref,
-                out_ref, flux_ref, dest_ref, rhs_ref, where_ref):
+def rank_kernel(cap, owner_ref, slot_ref, dest_ref, where_ref, code_ref):
     rows = owner_ref.shape[1]
-    ndev, tall, row_len = out_ref.shape
-    flux = mask_ref[...].astype(F32) * film_coef * (temp_ref[...] - old_ref[...])
-    flux_ref[...] = flux
-    high, low = halves(flux.reshape(rows, row_len))
-    rhs_ref[:, :row_len] = high
-    rhs_ref[:, row_len:] = low
-    lane = 128
+    ndev = code_ref.shape[0]
+    tall = cap + 8
     tri = ones_where(
-        lax.broadcasted_iota(jnp.int32, (lane, lane), 0)
-        <= lax.broadcasted_iota(jnp.int32, (lane, lane), 1)
+        lax.broadcasted_iota(jnp.int32, (LANE, LANE), 0)
+        <= lax.broadcasted_iota(jnp.int32, (LANE, LANE), 1)
     )
-    names = lax.broadcasted_iota(jnp.int32, (ndev, lane), 0)
-    steps = lax.broadcasted_iota(jnp.int32, (lane, lane), 0)
+    names = lax.broadcasted_iota(jnp.int32, (ndev, LANE), 0)
+    steps = lax.broadcasted_iota(jnp.int32, (LANE, LANE), 0)
     carry = jnp.zeros((ndev, 1), F32)
-    codes = jnp.zeros((2 * ndev, lane), F32)
-    for chunk in range(rows // lane):
-        cols = slice(chunk * lane, (chunk + 1) * lane)
+    codes = jnp.zeros((2 * ndev, LANE), F32)
+    for chunk in range(rows // LANE):
+        cols = slice(chunk * LANE, (chunk + 1) * LANE)
         own = owner_ref[:, cols]
         hit = jnp.where(names == own, 1.0, 0.0)
         ranks = jnp.dot(hit.astype(BF16), tri, preferred_element_type=F32) + carry
-        carry = ranks[:, lane - 1:]
+        carry = ranks[:, LANE - 1:]
         place = jnp.sum(hit * ranks, axis=0, keepdims=True).astype(jnp.int32) - 1
         dest_ref[:, cols] = own * cap + place
         where_ref[:, cols] = own * tall + place
@@ -90,6 +84,33 @@
             pieces, ones_where(steps == place), (((1,), (1,)), ((), ())),
             preferred_element_type=F32,
         )
+    code_ref[...] = codes[:ndev] * 32.0 + codes[ndev:]
+
+
+def rank(owner, slot, ndev, cap):
+    rows = owner.shape[1]
+    line = jax.ShapeDtypeStruct((1, rows), jnp.int32)
+    return pl.pallas_call(
+        functools.partial(rank_kernel, cap),
+        grid=(1,),
+        in_specs=[whole((1, rows))] * 2,
+        out_specs=[whole((1, rows))] * 2 + [whole((ndev, LANE))],
+        out_shape=[line, line, jax.ShapeDtypeStruct((ndev, LANE), F32)],
+        compiler_params=params(8),
+        cost_estimate=cost(8 * ndev * LANE * rows, 20 * rows),
+        name="rank",
+    )(owner, slot)
+
+
+def pack_kernel(cap, where_ref, code_ref, temp_ref, old_ref, mask_ref, *refs):
+    out_ref, flux_ref, rhs_ref = refs[-3:]
+    rows = where_ref.shape[1]
+    ndev, tall, row_len = out_ref.shape
+    flux = mask_ref[...].astype(F32) * film_coef * (temp_ref[...] - old_ref[...])
+    flux_ref[...] = flux
+    high, low = halves(flux.reshape(rows, row_len))
+    rhs_ref[:, :row_len] = high
+    rhs_ref[:, row_len:] = low
     where = where_ref[...]
     group = ndev // 4
     block = group * tall
@@ -105,42 +126,31 @@
         return none
 
     lax.fori_loop(0, ndev // group, step, 0)
-    out_ref[:, cap, :] = codes[:ndev] * 32.0 + codes[ndev:]
-
-
-def pack(owner, slot, temp, old, mask, ndev, cap):
+    out_ref[:, cap, :] = code_ref[...]
+
+
+def pack(where, code, temp, old, mask, cap, after):
     cx, cy, _ = temp.shape
     row_len = old.shape[2]
     rows = cx * cy
+    ndev = code.shape[0]
     tall = cap + 8
     return pl.pallas_call(
         functools.partial(pack_kernel, cap),
         grid=(1,),
-        in_specs=[
-            whole((1, rows)),
-            whole((1, rows)),
-            whole((cx, cy, row_len)),
-            whole((cx, cy, row_len)),
-            whole((cx, cy, row_len)),
-        ],
-        out_specs=[
-            whole((ndev, tall, row_len)),
-            whole((cx, cy, row_len)),
-            whole((1, rows)),
-        ],
+        in_specs=[whole((1, rows)), whole(code.shape)]
+        + [whole((cx, cy, row_len))] * 3
+        + [anywhere] * len(after),
+        out_specs=[whole((ndev, tall, row_len)), whole((cx, cy, row_len))],
         out_shape=[
             jax.ShapeDtypeStruct((ndev, tall, row_len), F32),
             jax.ShapeDtypeStruct((cx, cy, row_len), F32),
-            jax.ShapeDtypeStruct((1, rows), jnp.int32),
         ],
-        scratch_shapes=[
-            pltpu.VMEM((rows, 2 * row_len), BF16),
-            pltpu.VMEM((1, rows), jnp.int32),
-        ],
-        compiler_params=params(60),
+        scratch_shapes=[pltpu.VMEM((rows, 2 * row_len), BF16)],
+        compiler_params=params(61),
         cost_estimate=cost(4 * ndev * tall * rows * row_len, 5 * rows * row_len * 4),
         name="pack",
-    )(owner, slot, temp, old, mask)
+    )(where, code, temp, old, mask, *after)
 
 
 def heat_kernel(cap, thin, rows_ref, *refs):
@@ -245,7 +255,7 @@
         ],
         out_specs=[whole((height, depth))] * 2,
         out_shape=[jax.ShapeDtypeStruct((height, depth), F32)] * 2,
-        compiler_params=params(12),
+        compiler_params=params(61),
         cost_estimate=cost(1000, 4 * 4 * height * depth),
         name="x_faces",
     )(fluid, fluid, temp, kind)
@@ -263,8 +273,8 @@
             ref[rim + sx + k, cut, :] = get_rim(hi_ref, n)
 
 
-def y_faces_kernel(rim, near_ref, far_ref, temp_ref, kind_ref, lo_ref, hi_ref,
-                   left_ref, right_ref, work_ref):
+def y_faces_kernel(rim, near_ref, far_ref, temp_ref, kind_ref, lo_ref, hi_ref, *refs):
+    left_ref, right_ref, work_ref = refs[-3:]
     cx, near, _ = near_ref.shape
     sx, sy, _ = temp_ref.shape
     left_ref[:cx, :] = near_ref[:, 0, :]
@@ -282,7 +292,7 @@
     put_rim(right_ref, cx, slabs[1])
 
 
-def y_faces(rim, fluid, temp, kind, lo, hi):
+def y_faces(rim, fluid, temp, kind, lo, hi, after):
     cx, cy, depth = fluid.shape
     sx, sy, sz = temp.shape
     long = -(-(sx + 2 * rim) // PART) * PART
@@ -298,14 +308,15 @@
             whole(temp.shape),
             whole(lo.shape),
             whole(hi.shape),
-        ],
+        ]
+        + [anywhere] * len(after),
         out_specs=[whole((height, depth))] * 2,
         out_shape=[jax.ShapeDtypeStruct((height, depth), F32)] * 2,
         scratch_shapes=[pltpu.VMEM((2, long, sy + 2 * OFF, sz), F32)],
         compiler_params=params(16),
         cost_estimate=cost(1000, 4 * 4 * height * depth),
         name="y_faces",
-    )(fluid, fluid, temp, kind, lo, hi)
+    )(fluid, fluid, temp, kind, lo, hi, *after)
 
 
 def table(kind, values):
@@ -317,7 +328,8 @@
 
 def solid_kernel(rim, cap, own_ref, kind_ref, xlo_ref, xhi_ref, ylo_ref, yhi_ref,
                  heat_ref, hxlo_ref, hxhi_ref, hylo_ref, hyhi_ref, code_ref,
-                 next_ref, sigma_ref, reply_ref, temp_ref, work_ref, cond_ref, src_ref, rhs_ref):
+                 next_ref, sigma_ref, reply_ref, temp_ref, work_ref, cond_ref, src_ref, rhs_ref,
+                 stage_ref, sems):
     sx, sy, sz = own_ref.shape
     wide = sx + 2 * rim
     thin = rim - 1
@@ -376,7 +388,16 @@
             axis=0,
         )
         both = jnp.dot(pick, rhs_ref[...], preferred_element_type=F32)
-        reply_ref[index * cap:(index + group) * cap, :] = both[:, :sz] + both[:, sz:]
+        lines = slice(index * cap, (index + group) * cap)
+        stage_ref[lines, :] = both[:, :sz] + both[:, sz:]
+        pltpu.make_async_copy(
+            stage_ref.at[lines], reply_ref.at[lines], sems.at[index // group]
+        ).start()
+    for index in range(0, ndev, group):
+        lines = slice(index * cap, (index + group) * cap)
+        pltpu.make_async_copy(
+            stage_ref.at[lines], reply_ref.at[lines], sems.at[index // group]
+        ).wait()
 
 
 def solid_steps(rim, cap, temp, kind, state_rim, heat, heat_rim, code):
@@ -388,14 +409,22 @@
         functools.partial(solid_kernel, rim, cap),
         grid=(1,),
         in_specs=[whole(x.shape) for x in args],
-        out_specs=[whole((sx, sy, sz)), whole((sx + 2, height, sz)), whole((total, sz))],
+        out_specs=[
+            whole((sx, sy, sz)),
+            whole((sx + 2, height, sz)),
+            pl.BlockSpec(memory_space=pltpu.HBM),
+        ],
         out_shape=[
             jax.ShapeDtypeStruct((sx, sy, sz), F32),
             jax.ShapeDtypeStruct((sx + 2, height, sz), F32),
             jax.ShapeDtypeStruct((total, sz), F32),
         ],
         scratch_shapes=[pltpu.VMEM((wide, height, sz), F32)] * 4
-        + [pltpu.VMEM((sx * sy, 2 * sz), BF16)],
+        + [
+            pltpu.VMEM((sx * sy, 2 * sz), BF16),
+            pltpu.VMEM((total, sz), F32),
+            pltpu.SemaphoreType.DMA((4,)),
+        ],
         compiler_params=params(24),
         cost_estimate=cost(4 * total * sx * sy * sz, 4 * total * sz),
         name="solid_steps",
@@ -459,14 +488,14 @@
         + [anywhere] * len(after),
         out_specs=whole((rows, row_len)),
         out_shape=jax.ShapeDtypeStruct((rows, row_len), F32),
-        compiler_params=params(10),
+        compiler_params=params(61),
         cost_estimate=cost(rows * 128, 8 * rows * row_len),
         name="unpack",
     )(dest, back, *after)
 
 
-def fluid_kernel(here_ref, xlo_ref, xhi_ref, ylo_ref, yhi_ref, speed_ref, flux_ref,
-                 out_ref, ring_ref):
+def fluid_kernel(here_ref, xlo_ref, xhi_ref, ylo_ref, yhi_ref, speed_ref, flux_ref, *refs):
+    out_ref, xfirst_ref, xlast_ref, yfirst_ref, ylast_ref, ring_ref = refs[-6:]
     index, count = pl.program_id(0), pl.num_programs(0)
     cx = count - 1
     _, cy, depth = here_ref.shape
@@ -522,9 +551,19 @@
                 out_ref[0, y:y + 8, :row_len] = (
                     total[:, :row_len] - time_step * flux_ref[0, y:y + 8, :]
                 )
-
-
-def fluid_step(temp, rims, velocity, flux):
+        yfirst_ref[pl.ds(index - 1, 1), :] = out_ref[0, 0:1, :]
+        ylast_ref[pl.ds(index - 1, 1), :] = out_ref[0, cy - 1:cy, :]
+
+    @pl.when(index == 1)
+    def _():
+        xfirst_ref[...] = out_ref[0]
+
+    @pl.when(index == cx)
+    def _():
+        xlast_ref[...] = out_ref[0]
+
+
+def fluid_step(temp, rims, velocity, flux, after):
     cx, cy, depth = temp.shape
     row_len = flux.shape[2]
     plane = (1, cy, depth)
@@ -542,20 +581,21 @@
             line,
             pl.BlockSpec((3, 1, cy, depth), lambda i: (0, jnp.maximum(i - 1, 0), 0, 0)),
             pl.BlockSpec((1, cy, row_len), back),
+        ]
+        + [anywhere] * len(after),
+        out_specs=[pl.BlockSpec(plane, back), face, face, line, line],
+        out_shape=[
+            jax.ShapeDtypeStruct(temp.shape, F32),
+            jax.ShapeDtypeStruct((cy, depth), F32),
+            jax.ShapeDtypeStruct((cy, depth), F32),
+            jax.ShapeDtypeStruct((cx, depth), F32),
+            jax.ShapeDtypeStruct((cx, depth), F32),
         ],
-        out_specs=pl.BlockSpec(plane, back),
-        out_shape=jax.ShapeDtypeStruct(temp.shape, F32),
         scratch_shapes=[pltpu.VMEM((3, cy + 2 * OFF, depth), F32)],
-        compiler_params=params(16),
+        compiler_params=params(61),
         cost_estimate=cost(40 * cx * cy * depth, 14 * cx * cy * depth),
         name="fluid_step",
-    )(temp, *rims, velocity, flux)
-
-
-def fluid_rims(temp):
-    xlo, xhi = neighbours(temp[-1], temp[0], "gx")
-    ylo, yhi = neighbours(temp[:, -1], temp[:, 0], "gy")
-    return xlo, xhi, ylo, yhi
+    )(temp, *rims, velocity, flux, *after)
 
 
 def body(temp_fluid, velocity, wall_old, wall_mask, owner_map, slot_map, temp_solid, material):
@@ -569,21 +609,24 @@
     total = ndev * cap
     rim = SSTEPS + 1
 
-    outgoing, flux, dest = pack(
-        owner_map.reshape(1, rows), slot_map, temp_fluid, wall_old, wall_mask, ndev, cap
-    )
-    incoming = lax.all_to_all(outgoing, AXES, split_axis=0, concat_axis=0, tiled=True)
-
     first, last = x_faces(rim, temp_fluid, temp_solid, material)
     xlo, xhi = neighbours(last, first, "gx")
-    first, last = y_faces(rim, temp_fluid, temp_solid, material, xlo[cy:], xhi[cy:])
+    dest, where, codes = rank(owner_map.reshape(1, rows), slot_map, ndev, cap)
+    outgoing, flux = pack(where, codes, temp_fluid, wall_old, wall_mask, cap, (xlo, xhi))
+    incoming = lax.all_to_all(outgoing, AXES, split_axis=0, concat_axis=0, tiled=True)
+
+    first, last = y_faces(rim, temp_fluid, temp_solid, material, xlo[cy:], xhi[cy:], (flux,))
     ylo, yhi = neighbours(last, first, "gy")
     rims = (xlo[cy:], xhi[cy:], ylo[cx:], yhi[cx:])
-
-    fluid = fluid_step(temp_fluid, (xlo, xhi, ylo, yhi), velocity, flux)
+    faces = (xlo, xhi, ylo, yhi)
+    for turn in range(FSTEPS - 1):
+        fluid, xfirst, xlast, yfirst, ylast = fluid_step(
+            fluid if turn else temp_fluid, faces, velocity, flux, ()
+        )
+        faces = (*neighbours(xlast, xfirst, "gx"), *neighbours(ylast, yfirst, "gy"))
 
     thin = rim - 1
-    heat, first, last, code = heat_sum(incoming, cap, temp_solid.shape, thin, (fluid, *rims))
+    heat, first, last, code = heat_sum(incoming, cap, temp_solid.shape, thin, (*faces, *rims))
     hxlo, hxhi = neighbours(last, first, "gx")
     tall = lambda cut: jnp.concatenate([hxlo[:, cut], heat[:, cut], hxhi[:, cut]], axis=0)
     hylo, hyhi = neighbours(tall(slice(sy - thin, sy)), tall(slice(0, thin)), "gy")
@@ -593,7 +636,7 @@
     returned = lax.all_to_all(
         replies.reshape(ndev, cap, sz), AXES, split_axis=0, concat_axis=0, tiled=True
     )
-    fluid = fluid_step(fluid, fluid_rims(fluid), velocity, flux)
+    fluid = fluid_step(fluid, faces, velocity, flux, (sigma,))[0]
     force = stress(sigma, sx, sy)
     wall_next = unpack(dest, returned.reshape(total, sz), (fluid, force))
     return fluid, wall_next.reshape(cx, cy, row_len), solid, force

time: 172 us -> 167 us (0.971)
  the two profiles are of different devices: /device:TPU:11 before, /device:TPU:0 now
where the time goes in v4:
time: 167 us; the launch traced here: 166 us
  Pallas kernels  52.1 us (31%)
  waiting for transfers between devices  52 us (31%)
  starting transfers between devices  44.9 us (27%)
  local copies, waits for them, and re-layouts  15.8 us (9%)
    ppermute x12, waiting for transfers between devices, neighbours(): return (lax.ppermute(before, axis, up), lax.ppermute(after, axis, down))  32.4 us
    pallas_call x2, Pallas kernels, fluid_step(): pl.pallas_call(fluid_kernel, grid=(cx + 1,), in_specs=[pl.BlockSpec(plane...  31.5 us
    ppermute x12, starting transfers between devices, neighbours(): return (lax.ppermute(before, axis, up), lax.ppermute(after, axis, down))  25.9 us
    all_to_all x1, waiting for transfers between devices, body(): lax.all_to_all(replies.reshape(ndev, cap, sz), AXES, split_axis=0, concat...  19.6 us
    all_to_all x1, starting transfers between devices, body(): lax.all_to_all(outgoing, AXES, split_axis=0, concat_axis=0, tiled=True)  11 us
    unnamed x50, local copies, waits for them, and re-layouts  10.6 us
    all_to_all x1, starting transfers between devices, body(): lax.all_to_all(replies.reshape(ndev, cap, sz), AXES, split_axis=0, concat...  7.93 us
    pallas_call x1, Pallas kernels, pack(): pl.pallas_call(functools.partial(pack_kernel, cap), grid=(1,), in_specs=[...  5.25 us
  transfers between devices with their start and end apart: 14, of which 8 were waited for; matrix products, arithmetic and copies ran while one was open for 3% of the time, Pallas kernels for 21%

profile of v4, /device:TPU:0, one launch (start us, length us, event | category | flops | bytes accessed | tf_op | source)
XLA Modules:
  0.0 165.7 jit_solution(14659915920315120995)
XLA Ops:
  0.6 0.0 copy-start.18
  0.6 0.0 copy-start.17
  0.7 2.2 %x_faces.1 = (f32[112,1024]{1,0:T(8,128)}, f32[112,1024]{1,0:T(8,128)}) custom-call(f32[16,64,1024]{2,1,0:T(8,128)} %here_ref.1, f32[16,64,1024]{2,1,0:T(8,128)} %here_ref.1, f32[16,32,128]{2,1,0:T(8,128)} %own_ref.1, s32[16,32,128]{2,1,0:T(8,128)} %kind_ref.5), custom_call_target="tpu_custom_call" | custom-call | flops 1000 | bytes 1835008 | tf_op jit(solution)/shard_map/x_faces/pallas_call | solution.py:247
  2.8 2.4 %collective-permute-start = (f32[112,1024]{1,0:T(8,128)}, f32[112,1024]{1,0:T(8,128)S(1)}, u32[]{:S(2)}, u32[]{:S(2)}) collective-permute-start(f32[112,1024]{1,0:T(8,128)} %get-tuple-element.26), channel_id=1, source_target_pairs={{0,4},{4,8},{8,12},{12,16},{16,20},{20,24},{24,28},{1,5},{5,9},{9,... | collective-permute-start | bytes 1376264 | tf_op jit(solution)/shard_map/ppermute | solution.py:48
  5.2 1.3 collective-permute-start.1
  6.5 0.0 copy-done.18
  6.5 0.0 copy-done.17
  6.5 0.9 rank.1
  7.4 0.0 copy-start.16
  7.5 0.6 copy-done.16
  8.1 0.6 copy-done.19
  8.7 0.6 copy-done.20
  9.2 0.0 collective-permute-done.refs_0_.xlo_ref
  9.3 2.0 %collective-permute-done.1.refs_1_.xhi_ref = f32[112,1024]{1,0:T(8,128)S(1)} collective-permute-done((f32[112,1024]{1,0:T(8,128)}, f32[112,1024]{1,0:T(8,128)S(1)}, u32[]{:S(2)}, u32[]{:S(2)}) %collective-permute-start.1) | collective-permute-done | bytes 458784 | tf_op jit(solution)/shard_map/ppermute | solution.py:48
  11.3 0.8 copy-done.23
  12.1 5.3 %pack.1 = (f32[32,104,128]{2,1,0:T(8,128)}, f32[16,64,128]{2,1,0:T(8,128)}) custom-call(s32[1,1024]{1,0:T(1,128)} %copy-done.20, f32[32,128]{1,0:T(8,128)} %copy-done.19, f32[16,64,1024]{2,1,0:T(8,128)} %here_ref.1, f32[16,64,128]{2,1,0:T(8,128)} %old_ref.1, s32[16,64,128]{2,1,0:T(8,128)} %mask_ref.1, f32[112,1024]{1,0:T(8,128)} %copy-done.22, ...), custom_call_target="tpu_custom_call" | custom-call | flops 1744830464 | bytes 2621440 | tf_op jit(solution)/shard_map/pack/pallas_call | solution.py:138
  17.3 11.0 %all-to-all-start = ((f32[32,104,128]{2,1,0:T(8,128)}), f32[32,104,128]{2,1,0:T(8,128)S(1)}, u32[]{:S(2)}, u32[]{:S(2)}) async-start(f32[32,104,128]{2,1,0:T(8,128)} %get-tuple-element.38), calls=%async_computation | async-start | bytes 3407872 | tf_op jit(solution)/shard_map/all_to_all | solution.py:616
  28.4 0.9 slice.42.lo_ref.refs_4_.xlo_ref
  29.3 0.9 slice.43.hi_ref.refs_5_.xhi_ref
  30.2 0.0 copy-start.5
  30.3 0.0 copy-done.3
  30.3 0.0 copy-done.4
  30.3 0.0 copy-done.1
  30.3 0.0 copy-start
  30.3 2.2 %copy-done = f32[16,64,1024]{2,1,0:T(8,128)S(1)} copy-done((f32[16,64,1024]{2,1,0:T(8,128)S(1)}, f32[16,64,1024]{2,1,0:T(8,128)}, u32[]{:S(2)}) %copy-start) | copy-done | bytes 4194328
  32.5 0.3 y_faces.1
  32.8 3.7 %collective-permute-start.2 = (f32[64,1024]{1,0:T(8,128)S(1)}, f32[64,1024]{1,0:T(8,128)S(1)}, u32[]{:S(2)}, u32[]{:S(2)}) collective-permute-start(f32[64,1024]{1,0:T(8,128)S(1)} %get-tuple-element.31), channel_id=1, source_target_pairs={{0,1},{1,2},{2,3},{4,5},{5,6},{6,7},{8,9},{9,10},{10,11},{12,13},{... | collective-permute-start | bytes 786440 | tf_op jit(solution)/shard_map/ppermute | solution.py:48
  36.5 1.4 collective-permute-start.3
  38.0 11.9 %collective-permute-done.2.ylo_ref = f32[64,1024]{1,0:T(8,128)S(1)} collective-permute-done((f32[64,1024]{1,0:T(8,128)S(1)}, f32[64,1024]{1,0:T(8,128)S(1)}, u32[]{:S(2)}, u32[]{:S(2)}) %collective-permute-start.2) | collective-permute-done | bytes 262176 | tf_op jit(solution)/shard_map/ppermute | solution.py:48
  49.9 0.7 copy-done.24
  50.6 7.4 %collective-permute-done.3.yhi_ref = f32[64,1024]{1,0:T(8,128)} collective-permute-done((f32[64,1024]{1,0:T(8,128)S(1)}, f32[64,1024]{1,0:T(8,128)}, u32[]{:S(2)}, u32[]{:S(2)}) %collective-permute-start.3) | collective-permute-done | bytes 262176 | tf_op jit(solution)/shard_map/ppermute | solution.py:48
  58.0 15.8 %fluid_step.2 = (f32[16,64,1024]{2,1,0:T(8,128)}, f32[64,1024]{1,0:T(8,128)}, f32[64,1024]{1,0:T(8,128)}, f32[16,1024]{1,0:T(8,128)}, f32[16,1024]{1,0:T(8,128)}) custom-call(f32[16,64,1024]{2,1,0:T(8,128)} %here_ref.1, f32[112,1024]{1,0:T(8,128)} %copy-done.22, f32[112,1024]{1,0:T(8,128)} %copy-done.23, f32[64,1024]{1,0:T(8,128)} %copy-done.24, ...), custom_call_target="tpu_custom_call" | custom-call | flops 41943040 | bytes 14680064 | tf_op jit(solution)/shard_map/fluid_step/pallas_call | solution.py:573
  73.8 1.6 collective-permute-start.4
  75.4 1.3 collective-permute-start.5
  76.7 4.0 %collective-permute-start.6 = (f32[16,1024]{1,0:T(8,128)}, f32[16,1024]{1,0:T(8,128)S(1)}, u32[]{:S(2)}, u32[]{:S(2)}) collective-permute-start(f32[16,1024]{1,0:T(8,128)} %get-tuple-element.36), channel_id=1, source_target_pairs={{0,1},{1,2},{2,3},{4,5},{5,6},{6,7},{8,9},{9,10},{10,11},{12,13},{... | collective-permute-start | bytes 196616 | tf_op jit(solution)/shard_map/ppermute | solution.py:48
  80.8 1.3 collective-permute-start.7
  82.1 1.6 slice.44.refs_6_.ylo_ref
  83.7 1.6 slice.45.refs_7_.yhi_ref
  85.3 0.0 collective-permute-done.6.refs_2_.ylo_ref
  85.3 1.8 %collective-permute-done.7.refs_3_.yhi_ref = f32[16,1024]{1,0:T(8,128)S(1)} collective-permute-done((f32[16,1024]{1,0:T(8,128)}, f32[16,1024]{1,0:T(8,128)S(1)}, u32[]{:S(2)}, u32[]{:S(2)}) %collective-permute-start.7) | collective-permute-done | bytes 65568 | tf_op jit(solution)/shard_map/ppermute | solution.py:48
  87.1 0.0 collective-permute-done.4.refs_0_.xlo_ref
  87.1 0.0 collective-permute-done.5.refs_1_.xhi_ref
  87.2 0.0 all-to-all-done.rows_ref
  87.2 0.0 copy-start.10
  87.2 1.1 copy-done.10
  88.3 0.9 copy-done.12
  89.2 2.1 %heat_sum.1 = (f32[16,32,128]{2,1,0:T(8,128)S(1)}, f32[4,32,128]{2,1,0:T(8,128)S(1)}, f32[4,32,128]{2,1,0:T(8,128)S(1)}, s32[32,128]{1,0:T(8,128)S(1)}) custom-call(f32[32,104,128]{2,1,0:T(8,128)S(1)} %all-to-all-done.rows_ref, f32[64,1024]{1,0:T(8,128)S(1)} %collective-permute-done.4.refs_0_.xlo_ref, f32[64,1024]{1,0:T(8,128)S(1)} %collective-permute-done.5.refs_1_.xhi_ref, ...), custom_call_target="tpu_custom_call" | custom-call | flops 872415232 | bytes 1703936 | tf_op jit(solution)/shard_map/heat_sum/pallas_call | solution.py:189
  91.3 3.5 %collective-permute-start.8 = (f32[4,32,128]{2,1,0:T(8,128)S(1)}, f32[4,32,128]{2,1,0:T(8,128)S(1)}, u32[]{:S(2)}, u32[]{:S(2)}) collective-permute-start(f32[4,32,128]{2,1,0:T(8,128)S(1)} %get-tuple-element.40), channel_id=1, source_target_pairs={{0,4},{4,8},{8,12},{12,16},{16,20},{20,24},{24,28},{1,5},{5,9},{9,... | collective-permute-start | bytes 196616 | tf_op jit(solution)/shard_map/ppermute | solution.py:48
  94.8 1.3 collective-permute-start.9
  96.1 0.0 collective-permute-done.8.hxlo_ref
  96.2 4.5 %collective-permute-done.9.hxhi_ref = f32[4,32,128]{2,1,0:T(8,128)S(1)} collective-permute-done((f32[4,32,128]{2,1,0:T(8,128)S(1)}, f32[4,32,128]{2,1,0:T(8,128)S(1)}, u32[]{:S(2)}, u32[]{:S(2)}) %collective-permute-start.9) | collective-permute-done | bytes 65568 | tf_op jit(solution)/shard_map/ppermute | solution.py:48
  100.7 2.8 %collective-permute-start.10 = (f32[24,4,128]{2,1,0:T(4,128)S(1)}, f32[24,4,128]{2,1,0:T(4,128)S(1)}, u32[]{:S(2)}, u32[]{:S(2)}) collective-permute-start(f32[24,4,128]{2,1,0:T(4,128)S(1)} %pad_maximum_fusion), channel_id=1, source_target_pairs={{0,1},{1,2},{2,3},{4,5},{5,6},{6,7},{8,9},{9,10},{10,11},{12,13},{... | collective-permute-start | bytes 147464 | tf_op jit(solution)/shard_map/ppermute | solution.py:48
  103.5 1.3 collective-permute-start.11
  104.8 0.4 collective-permute-done.10.hylo_ref
  105.2 4.3 %collective-permute-done.11.hyhi_ref = f32[24,4,128]{2,1,0:T(4,128)S(1)} collective-permute-done((f32[24,4,128]{2,1,0:T(4,128)S(1)}, f32[24,4,128]{2,1,0:T(4,128)S(1)}, u32[]{:S(2)}, u32[]{:S(2)}) %collective-permute-start.11) | collective-permute-done | bytes 49184 | tf_op jit(solution)/shard_map/ppermute | solution.py:48
  109.5 0.9 copy-done.11
  110.4 0.9 copy-done.13
  111.4 4.5 %solid_steps.1 = (f32[16,32,128]{2,1,0:T(8,128)}, f32[18,48,128]{2,1,0:T(8,128)S(1)}, f32[3072,128]{1,0:T(8,128)}) custom-call(f32[16,32,128]{2,1,0:T(8,128)S(1)} %copy-done.3, s32[16,32,128]{2,1,0:T(8,128)S(1)} %copy-done.4, f32[48,1024]{1,0:T(8,128)S(1)} %slice.42.lo_ref.refs_4_.xlo_ref, f32[48,1024]{1,0:T(8,128)S(1)} %copy-done.7, ...), custom_call_target="tpu_custom_call" | custom-call | flops 805306368 | bytes 1572864 | tf_op jit(solution)/shard_map/solid_steps/pallas_call | solution.py:408
  115.9 7.9 %all-to-all-start.1 = ((f32[32,96,128]{2,1,0:T(8,128)}), f32[32,96,128]{2,1,0:T(8,128)S(1)}, u32[]{:S(2)}, u32[]{:S(2)}) async-start(f32[32,96,128]{2,1,0:T(8,128)} %bitcast.1), calls=%async_computation.1 | async-start | bytes 3145728 | tf_op jit(solution)/shard_map/all_to_all | solution.py:636
  123.8 2.1 %stress.1.refs_1_ = f32[3,16,32,128]{3,2,1,0:T(8,128)} custom-call(f32[18,48,128]{2,1,0:T(8,128)S(1)} %get-tuple-element.43.refs_0_.sigma_ref), custom_call_target="tpu_custom_call" | custom-call | flops 655360 | bytes 1048576 | tf_op jit(solution)/shard_map/stress/pallas_call | solution.py:456
  126.0 15.7 %fluid_step.3 = (f32[16,64,1024]{2,1,0:T(8,128)}, f32[64,1024]{1,0:T(8,128)}, f32[64,1024]{1,0:T(8,128)}, f32[16,1024]{1,0:T(8,128)}, f32[16,1024]{1,0:T(8,128)}) custom-call(f32[16,64,1024]{2,1,0:T(8,128)} %get-tuple-element.33.here_ref, f32[64,1024]{1,0:T(8,128)} %copy-done.8, f32[64,1024]{1,0:T(8,128)} %copy-done.9, f32[16,1024]{1,0:T(8,128)} %copy-done.14, ...), custom_call_target="tpu_custom_call" | custom-call | flops 41943040 | bytes 14680064 | tf_op jit(solution)/shard_map/fluid_step/pallas_call | solution.py:573
  141.7 19.6 %all-to-all-done.1 = f32[32,96,128]{2,1,0:T(8,128)S(1)} async-done(((f32[32,96,128]{2,1,0:T(8,128)}), f32[32,96,128]{2,1,0:T(8,128)S(1)}, u32[]{:S(2)}, u32[]{:S(2)}) %all-to-all-start.1) | async-done | bytes 1572896 | tf_op jit(solution)/shard_map/all_to_all | solution.py:636
  161.3 1.2 copy-done.21
  162.5 3.2 %unpack.1 = f32[1024,128]{1,0:T(8,128)} custom-call(s32[1,1024]{1,0:T(1,128)} %copy-done.16, f32[3072,128]{1,0:T(8,128)} %bitcast.5, f32[16,64,1024]{2,1,0:T(8,128)} %get-tuple-element.22.refs_0_, f32[3,16,32,128]{3,2,1,0:T(8,128)} %stress.1.refs_1_), custom_call_target="tpu_custom_call" | custom-call | flops 131072 | bytes 1048576 | tf_op jit(solution)/shard_map/unpack/pallas_call | solution.py:484
  (33 shorter events, 0.1 us)
Async XLA Ops:
  0.6 5.9 %copy-start.18 = (s32[1,1024]{1,0:T(1,128)S(1)}, s32[1,1024]{1,0:T(1,128)}, u32[]{:S(2)}) copy-start(s32[1,1024]{1,0:T(1,128)} %slot_ref.1) | copy-start | bytes 12292
  0.6 5.9 %copy-start.17 = (s32[1,1024,1]{1,2,0:T(1,128)S(1)}, s32[1,1024,1]{1,2,0:T(1,128)}, u32[]{:S(2)}) copy-start(s32[1,1024,1]{1,2,0:T(1,128)} %param.12) | copy-start | bytes 12292
  2.8 6.4 %collective-permute-start = (f32[112,1024]{1,0:T(8,128)}, f32[112,1024]{1,0:T(8,128)S(1)}, u32[]{:S(2)}, u32[]{:S(2)}) collective-permute-start(f32[112,1024]{1,0:T(8,128)} %get-tuple-element.26), channel_id=1, source_target_pairs={{0,4},{4,8},{8,12},{12,16},{16,20},{20,24},{24,28},{1,5},{5,9},{9,... | collective-permute-start | bytes 1376264 | tf_op jit(solution)/shard_map/ppermute | solution.py:48
  5.2 6.1 %collective-permute-start.1 = (f32[112,1024]{1,0:T(8,128)}, f32[112,1024]{1,0:T(8,128)S(1)}, u32[]{:S(2)}, u32[]{:S(2)}) collective-permute-start(f32[112,1024]{1,0:T(8,128)} %get-tuple-element.27), channel_id=1, source_target_pairs={{4,0},{8,4},{12,8},{16,12},{20,16},{24,20},{28,24},{5,1},{9,5},{13... | collective-permute-start | bytes 1376264 | tf_op jit(solution)/shard_map/ppermute | solution.py:48
  7.4 0.6 copy-start.16
  8.0 0.6 copy-start.19
  8.7 0.6 copy-start.20
  9.2 2.0 %copy-start.22 = (f32[112,1024]{1,0:T(8,128)}, f32[112,1024]{1,0:T(8,128)S(1)}, u32[]{:S(2)}) copy-start(f32[112,1024]{1,0:T(8,128)S(1)} %collective-permute-done.refs_0_.xlo_ref) | copy-start | bytes 1376260
  11.3 0.8 copy-start.23
  12.1 18.2 %copy-start.3 = (f32[16,32,128]{2,1,0:T(8,128)S(1)}, f32[16,32,128]{2,1,0:T(8,128)}, u32[]{:S(2)}) copy-start(f32[16,32,128]{2,1,0:T(8,128)} %own_ref.1) | copy-start | bytes 786436
  12.1 18.2 %copy-start.4 = (s32[16,32,128]{2,1,0:T(8,128)S(1)}, s32[16,32,128]{2,1,0:T(8,128)}, u32[]{:S(2)}) copy-start(s32[16,32,128]{2,1,0:T(8,128)} %kind_ref.5) | copy-start | bytes 786436
  17.3 13.0 %copy-start.1 = (f32[16,64,128]{2,1,0:T(8,128)S(1)}, f32[16,64,128]{2,1,0:T(8,128)}, u32[]{:S(2)}) copy-start(f32[16,64,128]{2,1,0:T(8,128)} %get-tuple-element.30.refs_0_.flux_ref) | copy-start | bytes 1572868
  17.3 69.8 %all-to-all-start = ((f32[32,104,128]{2,1,0:T(8,128)}), f32[32,104,128]{2,1,0:T(8,128)S(1)}, u32[]{:S(2)}, u32[]{:S(2)}) async-start(f32[32,104,128]{2,1,0:T(8,128)} %get-tuple-element.38), calls=%async_computation | async-start | bytes 3407872 | tf_op jit(solution)/shard_map/all_to_all | solution.py:616
  30.2 2.6 %copy-start.5 = (f32[48,1024]{1,0:T(8,128)}, f32[48,1024]{1,0:T(8,128)S(1)}, u32[]{:S(2)}) copy-start(f32[48,1024]{1,0:T(8,128)S(1)} %slice.43.hi_ref.refs_5_.xhi_ref) | copy-start | bytes 589828
  30.3 2.2 %copy-start = (f32[16,64,1024]{2,1,0:T(8,128)S(1)}, f32[16,64,1024]{2,1,0:T(8,128)}, u32[]{:S(2)}) copy-start(f32[16,64,1024]{2,1,0:T(8,128)} %here_ref.1) | copy-start | bytes 12582916
  32.8 17.0 %collective-permute-start.2 = (f32[64,1024]{1,0:T(8,128)S(1)}, f32[64,1024]{1,0:T(8,128)S(1)}, u32[]{:S(2)}, u32[]{:S(2)}) collective-permute-start(f32[64,1024]{1,0:T(8,128)S(1)} %get-tuple-element.31), channel_id=1, source_target_pairs={{0,1},{1,2},{2,3},{4,5},{5,6},{6,7},{8,9},{9,10},{10,11},{12,13},{... | collective-permute-start | bytes 786440 | tf_op jit(solution)/shard_map/ppermute | solution.py:48
  36.5 50.6 %copy-start.6 = (f32[48,1024]{1,0:T(8,128)S(1)}, f32[48,1024]{1,0:T(8,128)}, u32[]{:S(2)}) copy-start(f32[48,1024]{1,0:T(8,128)} %copy-done.5) | copy-start | bytes 589828
  36.5 21.5 %collective-permute-start.3 = (f32[64,1024]{1,0:T(8,128)S(1)}, f32[64,1024]{1,0:T(8,128)}, u32[]{:S(2)}, u32[]{:S(2)}) collective-permute-start(f32[64,1024]{1,0:T(8,128)S(1)} %get-tuple-element.32), channel_id=1, source_target_pairs={{1,0},{2,1},{3,2},{5,4},{6,5},{7,6},{9,8},{10,9},{11,10},{13,12},{... | collective-permute-start | bytes 786440 | tf_op jit(solution)/shard_map/ppermute | solution.py:48
  49.9 0.7 copy-start.24
  73.8 35.7 %copy-start.7 = (f32[48,1024]{1,0:T(8,128)S(1)}, f32[48,1024]{1,0:T(8,128)}, u32[]{:S(2)}) copy-start(f32[48,1024]{1,0:T(8,128)} %copy-done.5) | copy-start | bytes 589828
  73.8 13.3 %collective-permute-start.4 = (f32[64,1024]{1,0:T(8,128)}, f32[64,1024]{1,0:T(8,128)S(1)}, u32[]{:S(2)}, u32[]{:S(2)}) collective-permute-start(f32[64,1024]{1,0:T(8,128)} %get-tuple-element.34), channel_id=1, source_target_pairs={{0,4},{4,8},{8,12},{12,16},{16,20},{20,24},{24,28},{1,5},{5,9},{9,... | collective-permute-start | bytes 786440 | tf_op jit(solution)/shard_map/ppermute | solution.py:48
  75.4 11.7 %collective-permute-start.5 = (f32[64,1024]{1,0:T(8,128)}, f32[64,1024]{1,0:T(8,128)S(1)}, u32[]{:S(2)}, u32[]{:S(2)}) collective-permute-start(f32[64,1024]{1,0:T(8,128)} %get-tuple-element.35), channel_id=1, source_target_pairs={{4,0},{8,4},{12,8},{16,12},{20,16},{24,20},{28,24},{5,1},{9,5},{13... | collective-permute-start | bytes 786440 | tf_op jit(solution)/shard_map/ppermute | solution.py:48
  76.7 8.6 %collective-permute-start.6 = (f32[16,1024]{1,0:T(8,128)}, f32[16,1024]{1,0:T(8,128)S(1)}, u32[]{:S(2)}, u32[]{:S(2)}) collective-permute-start(f32[16,1024]{1,0:T(8,128)} %get-tuple-element.36), channel_id=1, source_target_pairs={{0,1},{1,2},{2,3},{4,5},{5,6},{6,7},{8,9},{9,10},{10,11},{12,13},{... | collective-permute-start | bytes 196616 | tf_op jit(solution)/shard_map/ppermute | solution.py:48
  80.8 6.4 %collective-permute-start.7 = (f32[16,1024]{1,0:T(8,128)}, f32[16,1024]{1,0:T(8,128)S(1)}, u32[]{:S(2)}, u32[]{:S(2)}) collective-permute-start(f32[16,1024]{1,0:T(8,128)} %get-tuple-element.37), channel_id=1, source_target_pairs={{1,0},{2,1},{3,2},{5,4},{6,5},{7,6},{9,8},{10,9},{11,10},{13,12},{... | collective-permute-start | bytes 196616 | tf_op jit(solution)/shard_map/ppermute | solution.py:48
  85.3 30.6 %copy-start.14 = (f32[16,1024]{1,0:T(8,128)}, f32[16,1024]{1,0:T(8,128)S(1)}, u32[]{:S(2)}) copy-start(f32[16,1024]{1,0:T(8,128)S(1)} %collective-permute-done.6.refs_2_.ylo_ref) | copy-start | bytes 196612
  87.1 28.7 %copy-start.15 = (f32[16,1024]{1,0:T(8,128)}, f32[16,1024]{1,0:T(8,128)S(1)}, u32[]{:S(2)}) copy-start(f32[16,1024]{1,0:T(8,128)S(1)} %collective-permute-done.7.refs_3_.yhi_ref) | copy-start | bytes 196612
  87.1 28.7 %copy-start.8 = (f32[64,1024]{1,0:T(8,128)}, f32[64,1024]{1,0:T(8,128)S(1)}, u32[]{:S(2)}) copy-start(f32[64,1024]{1,0:T(8,128)S(1)} %collective-permute-done.4.refs_0_.xlo_ref) | copy-start | bytes 786436
  87.2 22.4 %copy-start.9 = (f32[64,1024]{1,0:T(8,128)}, f32[64,1024]{1,0:T(8,128)S(1)}, u32[]{:S(2)}) copy-start(f32[64,1024]{1,0:T(8,128)S(1)} %collective-permute-done.5.refs_1_.xhi_ref) | copy-start | bytes 786436
  87.2 1.1 copy-start.10
  88.3 0.9 copy-start.12
  91.3 4.8 %collective-permute-start.8 = (f32[4,32,128]{2,1,0:T(8,128)S(1)}, f32[4,32,128]{2,1,0:T(8,128)S(1)}, u32[]{:S(2)}, u32[]{:S(2)}) collective-permute-start(f32[4,32,128]{2,1,0:T(8,128)S(1)} %get-tuple-element.40), channel_id=1, source_target_pairs={{0,4},{4,8},{8,12},{12,16},{16,20},{20,24},{24,28},{1,5},{5,9},{9,... | collective-permute-start | bytes 196616 | tf_op jit(solution)/shard_map/ppermute | solution.py:48
  94.8 5.8 %collective-permute-start.9 = (f32[4,32,128]{2,1,0:T(8,128)S(1)}, f32[4,32,128]{2,1,0:T(8,128)S(1)}, u32[]{:S(2)}, u32[]{:S(2)}) collective-permute-start(f32[4,32,128]{2,1,0:T(8,128)S(1)} %get-tuple-element.41), channel_id=1, source_target_pairs={{4,0},{8,4},{12,8},{16,12},{20,16},{24,20},{28,24},{5,1},{9,5},{13... | collective-permute-start | bytes 196616 | tf_op jit(solution)/shard_map/ppermute | solution.py:48
  100.7 4.6 %collective-permute-start.10 = (f32[24,4,128]{2,1,0:T(4,128)S(1)}, f32[24,4,128]{2,1,0:T(4,128)S(1)}, u32[]{:S(2)}, u32[]{:S(2)}) collective-permute-start(f32[24,4,128]{2,1,0:T(4,128)S(1)} %pad_maximum_fusion), channel_id=1, source_target_pairs={{0,1},{1,2},{2,3},{4,5},{5,6},{6,7},{8,9},{9,10},{10,11},{12,13},{... | collective-permute-start | bytes 147464 | tf_op jit(solution)/shard_map/ppermute | solution.py:48
  103.5 6.0 %collective-permute-start.11 = (f32[24,4,128]{2,1,0:T(4,128)S(1)}, f32[24,4,128]{2,1,0:T(4,128)S(1)}, u32[]{:S(2)}, u32[]{:S(2)}) collective-permute-start(f32[24,4,128]{2,1,0:T(4,128)S(1)} %pad_maximum_fusion.1), channel_id=1, source_target_pairs={{1,0},{2,1},{3,2},{5,4},{6,5},{7,6},{9,8},{10,9},{11,10},{13,12},{... | collective-permute-start | bytes 147464 | tf_op jit(solution)/shard_map/ppermute | solution.py:48
  109.5 0.9 copy-start.11
  110.4 0.9 copy-start.13
  115.9 10.1 %copy-start.2 = (f32[18,48,128]{2,1,0:T(8,128)}, f32[18,48,128]{2,1,0:T(8,128)S(1)}, u32[]{:S(2)}) copy-start(f32[18,48,128]{2,1,0:T(8,128)S(1)} %get-tuple-element.43.refs_0_.sigma_ref) | copy-start | bytes 1327108
  115.9 45.4 %all-to-all-start.1 = ((f32[32,96,128]{2,1,0:T(8,128)}), f32[32,96,128]{2,1,0:T(8,128)S(1)}, u32[]{:S(2)}, u32[]{:S(2)}) async-start(f32[32,96,128]{2,1,0:T(8,128)} %bitcast.1), calls=%async_computation.1 | async-start | bytes 3145728 | tf_op jit(solution)/shard_map/all_to_all | solution.py:636
  161.3 1.2 copy-start.21

commit v5 on v4

--- a/solution.py
+++ b/solution.py
@@ -147,7 +147,7 @@
             jax.ShapeDtypeStruct((cx, cy, row_len), F32),
         ],
         scratch_shapes=[pltpu.VMEM((rows, 2 * row_len), BF16)],
-        compiler_params=params(61),
+        compiler_params=params(40),
         cost_estimate=cost(4 * ndev * tall * rows * row_len, 5 * rows * row_len * 4),
         name="pack",
     )(where, code, temp, old, mask, *after)
@@ -210,9 +210,9 @@
         ref[row:row + PART, n % across * LANE:(n % across + 1) * LANE] = slab
 
 
-def get_rim(ref, n):
+def get_rim(ref, base, n):
     across = ref.shape[1] // LANE
-    row = n // across * PART
+    row = base + n // across * PART
     return ref[row:row + PART, n % across * LANE:(n % across + 1) * LANE]
 
 
@@ -221,8 +221,11 @@
     return -(-count // across) * PART
 
 
-def x_faces_kernel(rim, bottom_ref, top_ref, temp_ref, kind_ref, low_ref, high_ref):
+def x_faces_kernel(rim, bottom_ref, top_ref, near_ref, far_ref, temp_ref, kind_ref,
+                   low_ref, high_ref, left_ref, right_ref):
     _, cy, _ = bottom_ref.shape
+    left_ref[...] = near_ref[:, 0, :]
+    right_ref[...] = far_ref[:, near_ref.shape[1] - 1, :]
     sx, sy, _ = temp_ref.shape
     low_ref[:cy, :] = bottom_ref[0]
     high_ref[:cy, :] = top_ref[0]
@@ -250,35 +253,36 @@
         in_specs=[
             pl.BlockSpec(plane, lambda i: (0, 0, 0)),
             pl.BlockSpec(plane, lambda i: (cx - 1, 0, 0)),
+            pl.BlockSpec((cx, 8, depth), lambda i: (0, 0, 0)),
+            pl.BlockSpec((cx, 8, depth), lambda i: (0, cy // 8 - 1, 0)),
             whole(temp.shape),
             whole(temp.shape),
         ],
-        out_specs=[whole((height, depth))] * 2,
-        out_shape=[jax.ShapeDtypeStruct((height, depth), F32)] * 2,
+        out_specs=[whole((height, depth))] * 2 + [whole((cx, depth))] * 2,
+        out_shape=[jax.ShapeDtypeStruct((height, depth), F32)] * 2
+        + [jax.ShapeDtypeStruct((cx, depth), F32)] * 2,
         compiler_params=params(61),
         cost_estimate=cost(1000, 4 * 4 * height * depth),
         name="x_faces",
-    )(fluid, fluid, temp, kind)
+    )(fluid, fluid, fluid, fluid, temp, kind)
 
 
 def fill_x(rim, ref, which, own, lo_ref, hi_ref):
     sx, sy, _ = own.shape
     pieces = sy // PART
+    base = lo_ref.shape[0] - rim_rows(2 * rim * pieces, lo_ref.shape[1])
     ref[rim:rim + sx, OFF:OFF + sy, :] = own
     for k in range(rim):
         for h in range(pieces):
             n = (which * rim + k) * pieces + h
             cut = slice(OFF + h * PART, OFF + (h + 1) * PART)
-            ref[k, cut, :] = get_rim(lo_ref, n)
-            ref[rim + sx + k, cut, :] = get_rim(hi_ref, n)
-
-
-def y_faces_kernel(rim, near_ref, far_ref, temp_ref, kind_ref, lo_ref, hi_ref, *refs):
+            ref[k, cut, :] = get_rim(lo_ref, base, n)
+            ref[rim + sx + k, cut, :] = get_rim(hi_ref, base, n)
+
+
+def y_faces_kernel(rim, temp_ref, kind_ref, lo_ref, hi_ref, *refs):
     left_ref, right_ref, work_ref = refs[-3:]
-    cx, near, _ = near_ref.shape
     sx, sy, _ = temp_ref.shape
-    left_ref[:cx, :] = near_ref[:, 0, :]
-    right_ref[:cx, :] = far_ref[:, near - 1, :]
     slabs = ([], [])
     long = work_ref.shape[1]
     work_ref[...] = jnp.zeros_like(work_ref)
@@ -288,35 +292,26 @@
             for k in range(rim):
                 for h in range(0, long, PART):
                     into.append(work_ref[which, h:h + PART, start + k, :])
-    put_rim(left_ref, cx, slabs[0])
-    put_rim(right_ref, cx, slabs[1])
-
-
-def y_faces(rim, fluid, temp, kind, lo, hi, after):
-    cx, cy, depth = fluid.shape
+    put_rim(left_ref, 0, slabs[0])
+    put_rim(right_ref, 0, slabs[1])
+
+
+def y_faces(rim, temp, kind, lo, hi, after):
     sx, sy, sz = temp.shape
+    depth = lo.shape[1]
     long = -(-(sx + 2 * rim) // PART) * PART
-    height = cx + rim_rows(2 * rim * (long // PART), depth)
-    edge = (cx, 8, depth)
+    height = rim_rows(2 * rim * (long // PART), depth)
     return pl.pallas_call(
         functools.partial(y_faces_kernel, rim),
         grid=(1,),
-        in_specs=[
-            pl.BlockSpec(edge, lambda i: (0, 0, 0)),
-            pl.BlockSpec(edge, lambda i: (0, cy // 8 - 1, 0)),
-            whole(temp.shape),
-            whole(temp.shape),
-            whole(lo.shape),
-            whole(hi.shape),
-        ]
-        + [anywhere] * len(after),
+        in_specs=[whole(temp.shape)] * 2 + [whole(lo.shape)] * 2 + [anywhere] * len(after),
         out_specs=[whole((height, depth))] * 2,
         out_shape=[jax.ShapeDtypeStruct((height, depth), F32)] * 2,
         scratch_shapes=[pltpu.VMEM((2, long, sy + 2 * OFF, sz), F32)],
         compiler_params=params(16),
         cost_estimate=cost(1000, 4 * 4 * height * depth),
         name="y_faces",
-    )(fluid, fluid, temp, kind, lo, hi, *after)
+    )(temp, kind, lo, hi, *after)
 
 
 def table(kind, values):
@@ -343,8 +338,8 @@
                 n = (which * rim + k) * pieces + h
                 count = min(PART, wide - h * PART)
                 cut = slice(h * PART, h * PART + count)
-                ref[cut, OFF - rim + k, :] = get_rim(ylo_ref, n)[:count]
-                ref[cut, OFF + sy + k, :] = get_rim(yhi_ref, n)[:count]
+                ref[cut, OFF - rim + k, :] = get_rim(ylo_ref, 0, n)[:count]
+                ref[cut, OFF + sy + k, :] = get_rim(yhi_ref, 0, n)[:count]
     src_ref[rim:rim + sx, OFF:OFF + sy, :] = heat_ref[...]
     src_ref[1:rim, OFF:OFF + sy, :] = hxlo_ref[...]
     src_ref[rim + sx:wide - 1, OFF:OFF + sy, :] = hxhi_ref[...]
@@ -488,35 +483,40 @@
         + [anywhere] * len(after),
         out_specs=whole((rows, row_len)),
         out_shape=jax.ShapeDtypeStruct((rows, row_len), F32),
-        compiler_params=params(61),
+        compiler_params=params(10),
         cost_estimate=cost(rows * 128, 8 * rows * row_len),
         name="unpack",
     )(dest, back, *after)
 
 
+PLANES = 2
+RING = 3 * PLANES
+
+
 def fluid_kernel(here_ref, xlo_ref, xhi_ref, ylo_ref, yhi_ref, speed_ref, flux_ref, *refs):
     out_ref, xfirst_ref, xlast_ref, yfirst_ref, ylast_ref, ring_ref = refs[-6:]
     index, count = pl.program_id(0), pl.num_programs(0)
-    cx = count - 1
+    cx = (count - 1) * PLANES
     _, cy, depth = here_ref.shape
     row_len = flux_ref.shape[2]
     rows = slice(OFF, OFF + cy)
 
     @pl.when(index == 0)
     def _():
-        ring_ref[2, rows, :] = xlo_ref[...]
-
-    new = lax.rem(index, 3)
-
-    @pl.when(index < cx)
+        ring_ref[RING - 1, rows, :] = xlo_ref[...]
+
+    @pl.when(index < count - 1)
     def _():
-        ring_ref[new, rows, :] = here_ref[0]
-        ring_ref[new, OFF - 1:OFF, :] = ylo_ref[pl.ds(index, 1), :]
-        ring_ref[new, OFF + cy:OFF + cy + 1, :] = yhi_ref[pl.ds(index, 1), :]
-
-    @pl.when(index == cx)
+        for p in range(PLANES):
+            plane = index * PLANES + p
+            slot = lax.rem(plane, RING)
+            ring_ref[slot, rows, :] = here_ref[p]
+            ring_ref[slot, OFF - 1:OFF, :] = ylo_ref[pl.ds(plane, 1), :]
+            ring_ref[slot, OFF + cy:OFF + cy + 1, :] = yhi_ref[pl.ds(plane, 1), :]
+
+    @pl.when(index == count - 1)
     def _():
-        ring_ref[new, rows, :] = xhi_ref[...]
+        ring_ref[lax.rem(cx, RING), rows, :] = xhi_ref[...]
 
     rate = time_step * diffusivity
 
@@ -525,13 +525,16 @@
         total = total + (rate + jnp.maximum(scaled, 0.0)) * (lower - centre)
         return total + (rate - jnp.minimum(scaled, 0.0)) * (upper - centre)
 
-    @pl.when(index > 0)
-    def _():
+    def advance(p, none):
         lanes = lax.broadcasted_iota(jnp.int32, (8, depth), 1)
         first, last = lanes == 0, lanes == depth - 1
-        mid, old = lax.rem(index + 2, 3), lax.rem(index + 1, 3)
+        plane = (index - 1) * PLANES + p
+        mid = lax.rem(plane, RING)
+        old, new = lax.rem(plane + RING - 1, RING), lax.rem(plane + 1, RING)
         for tile in range(cy // 16):
-            speeds = [speed_ref[k, 0, tile * 16:tile * 16 + 16, :].astype(F32) for k in range(3)]
+            speeds = [
+                speed_ref[k, p, tile * 16:tile * 16 + 16, :].astype(F32) for k in range(3)
+            ]
             for part in range(2):
                 y = tile * 16 + part * 8
                 at = OFF + y
@@ -547,40 +550,46 @@
                 lower = jnp.where(first, 0.0, pltpu.roll(centre, 1, 1))
                 upper = jnp.where(last, 0.0, pltpu.roll(centre, depth - 1, 1))
                 total = push(total, centre, lower, upper, w)
-                out_ref[0, y:y + 8, row_len:] = total[:, row_len:]
-                out_ref[0, y:y + 8, :row_len] = (
-                    total[:, :row_len] - time_step * flux_ref[0, y:y + 8, :]
+                out_ref[p, y:y + 8, row_len:] = total[:, row_len:]
+                out_ref[p, y:y + 8, :row_len] = (
+                    total[:, :row_len] - time_step * flux_ref[p, y:y + 8, :]
                 )
-        yfirst_ref[pl.ds(index - 1, 1), :] = out_ref[0, 0:1, :]
-        ylast_ref[pl.ds(index - 1, 1), :] = out_ref[0, cy - 1:cy, :]
+        yfirst_ref[pl.ds(plane, 1), :] = out_ref[p, 0:1, :]
+        ylast_ref[pl.ds(plane, 1), :] = out_ref[p, cy - 1:cy, :]
+        return none
+
+    @pl.when(index > 0)
+    def _():
+        lax.fori_loop(0, PLANES, advance, 0)
 
     @pl.when(index == 1)
     def _():
         xfirst_ref[...] = out_ref[0]
 
-    @pl.when(index == cx)
+    @pl.when(index == count - 1)
     def _():
-        xlast_ref[...] = out_ref[0]
+        xlast_ref[...] = out_ref[PLANES - 1]
 
 
 def fluid_step(temp, rims, velocity, flux, after):
     cx, cy, depth = temp.shape
     row_len = flux.shape[2]
-    plane = (1, cy, depth)
+    plane = (PLANES, cy, depth)
+    steps = cx // PLANES
     face = pl.BlockSpec((cy, depth), lambda i: (0, 0))
     line = pl.BlockSpec((cx, depth), lambda i: (0, 0))
     back = lambda i: (jnp.maximum(i - 1, 0), 0, 0)
     return pl.pallas_call(
         fluid_kernel,
-        grid=(cx + 1,),
+        grid=(steps + 1,),
         in_specs=[
-            pl.BlockSpec(plane, lambda i: (jnp.minimum(i, cx - 1), 0, 0)),
+            pl.BlockSpec(plane, lambda i: (jnp.minimum(i, steps - 1), 0, 0)),
             face,
             face,
             line,
             line,
-            pl.BlockSpec((3, 1, cy, depth), lambda i: (0, jnp.maximum(i - 1, 0), 0, 0)),
-            pl.BlockSpec((1, cy, row_len), back),
+            pl.BlockSpec((3, PLANES, cy, depth), lambda i: (0, jnp.maximum(i - 1, 0), 0, 0)),
+            pl.BlockSpec((PLANES, cy, row_len), back),
         ]
         + [anywhere] * len(after),
         out_specs=[pl.BlockSpec(plane, back), face, face, line, line],
@@ -591,7 +600,7 @@
             jax.ShapeDtypeStruct((cx, depth), F32),
             jax.ShapeDtypeStruct((cx, depth), F32),
         ],
-        scratch_shapes=[pltpu.VMEM((3, cy + 2 * OFF, depth), F32)],
+        scratch_shapes=[pltpu.VMEM((RING, cy + 2 * OFF, depth), F32)],
         compiler_params=params(61),
         cost_estimate=cost(40 * cx * cy * depth, 14 * cx * cy * depth),
         name="fluid_step",
@@ -609,16 +618,16 @@
     total = ndev * cap
     rim = SSTEPS + 1
 
-    first, last = x_faces(rim, temp_fluid, temp_solid, material)
-    xlo, xhi = neighbours(last, first, "gx")
+    first, last, left, right = x_faces(rim, temp_fluid, temp_solid, material)
+    faces = (*neighbours(last, first, "gx"), *neighbours(right, left, "gy"))
+    xlo, xhi = faces[:2]
     dest, where, codes = rank(owner_map.reshape(1, rows), slot_map, ndev, cap)
-    outgoing, flux = pack(where, codes, temp_fluid, wall_old, wall_mask, cap, (xlo, xhi))
+    outgoing, flux = pack(where, codes, temp_fluid, wall_old, wall_mask, cap, faces)
     incoming = lax.all_to_all(outgoing, AXES, split_axis=0, concat_axis=0, tiled=True)
 
-    first, last = y_faces(rim, temp_fluid, temp_solid, material, xlo[cy:], xhi[cy:], (flux,))
+    first, last = y_faces(rim, temp_solid, material, xlo, xhi, (flux,))
     ylo, yhi = neighbours(last, first, "gy")
-    rims = (xlo[cy:], xhi[cy:], ylo[cx:], yhi[cx:])
-    faces = (xlo, xhi, ylo, yhi)
+    rims = (xlo, xhi, ylo, yhi)
     for turn in range(FSTEPS - 1):
         fluid, xfirst, xlast, yfirst, ylast = fluid_step(
             fluid if turn else temp_fluid, faces, velocity, flux, ()

time: 167 us -> 158 us (0.946)
  Pallas kernels: 52.1 us -> 42.8 us
  starting transfers between devices: 44.9 us -> 47.5 us
  waiting for transfers between devices: 52 us -> 49.6 us
    ppermute x12 -> x14, starting transfers between devices: 25.9 us -> 33.5 us  [neighbours(): return (lax.ppermute(before, axis, up), lax.ppermute(after, axis, down))]
    pallas_call x2, Pallas kernels: 31.5 us -> 24.5 us  [fluid_step(): pl.pallas_call(fluid_kernel, grid=(steps + 1,), in_specs=[pl.BlockSpec(pl...]
    ppermute x12 -> x14, waiting for transfers between devices: 32.4 us -> 26.5 us  [neighbours(): return (lax.ppermute(before, axis, up), lax.ppermute(after, axis, down))]
    slice x4 -> x0, local copies, waits for them, and re-layouts: 5.12 us -> none  [the longest x2 3.23 us: body(): rims = (xlo[cy:], xhi[cy:], ylo[cx:], yhi[cx:])]
    unnamed x50 -> x58, local copies, waits for them, and re-layouts: 10.6 us -> 15.4 us
    all_to_all x1, waiting for transfers between devices: 19.6 us -> 23.1 us  [body(): lax.all_to_all(replies.reshape(ndev, cap, sz), AXES, split_axis=0, concat...]
    all_to_all x1, starting transfers between devices: 11 us -> 8.3 us  [body(): lax.all_to_all(outgoing, AXES, split_axis=0, concat_axis=0, tiled=True)]
    pallas_call x1, Pallas kernels: 5.25 us -> 2.65 us  [pack(): pl.pallas_call(functools.partial(pack_kernel, cap), grid=(1,), in_specs=[...]
  transfers between devices with their start and end apart: 14 -> 16, of which waited for: 8 -> 7; matrix products, arithmetic and copies ran while one was open for 3% -> 0% of each run, Pallas kernels for 21% -> 18%
where the time goes in v5:
time: 158 us; the launch traced here: 156 us
  waiting for transfers between devices  49.6 us (31%)
  starting transfers between devices  47.5 us (30%)
  Pallas kernels  42.8 us (27%)
  local copies, waits for them, and re-layouts  15.5 us (10%)
    ppermute x14, starting transfers between devices, neighbours(): return (lax.ppermute(before, axis, up), lax.ppermute(after, axis, down))  33.5 us
    ppermute x14, waiting for transfers between devices, neighbours(): return (lax.ppermute(before, axis, up), lax.ppermute(after, axis, down))  26.5 us
    pallas_call x2, Pallas kernels, fluid_step(): pl.pallas_call(fluid_kernel, grid=(steps + 1,), in_specs=[pl.BlockSpec(pl...  24.5 us
    all_to_all x1, waiting for transfers between devices, body(): lax.all_to_all(replies.reshape(ndev, cap, sz), AXES, split_axis=0, concat...  23.1 us
    unnamed x58, local copies, waits for them, and re-layouts  15.4 us
    all_to_all x1, starting transfers between devices, body(): lax.all_to_all(outgoing, AXES, split_axis=0, concat_axis=0, tiled=True)  8.3 us
    all_to_all x1, starting transfers between devices, body(): lax.all_to_all(replies.reshape(ndev, cap, sz), AXES, split_axis=0, concat...  5.68 us
    pallas_call x1, Pallas kernels, solid_steps(): pl.pallas_call(functools.partial(solid_kernel, rim, cap), grid=(1,), in_s...  5.4 us
  transfers between devices with their start and end apart: 16, of which 7 were waited for; matrix products, arithmetic and copies ran while one was open for 0% of the time, Pallas kernels for 18%

profile of v5, /device:TPU:0, one launch (start us, length us, event | category | flops | bytes accessed | tf_op | source)
XLA Modules:
  0.0 156.4 jit_solution(9172089027630644463)
XLA Ops:
  0.7 2.6 %x_faces.1 = (f32[112,1024]{1,0:T(8,128)}, f32[112,1024]{1,0:T(8,128)}, f32[16,1024]{1,0:T(8,128)}, f32[16,1024]{1,0:T(8,128)}) custom-call(f32[16,64,1024]{2,1,0:T(8,128)} %here_ref.1, f32[16,64,1024]{2,1,0:T(8,128)} %here_ref.1, f32[16,64,1024]{2,1,0:T(8,128)} %here_ref.1, f32[16,64,1024]{2,1,0:T(8,128)} %here_ref.1, f32[16,32,128]{2,1,0:T(8,128)} %own_ref.1, ...), custom_call_target="tpu_custom_call" | custom-call | flops 1000 | bytes 1835008 | tf_op jit(solution)/shard_map/x_faces/pallas_call | solution.py:250
  3.3 2.4 %collective-permute-start = (f32[112,1024]{1,0:T(8,128)}, f32[112,1024]{1,0:T(8,128)S(1)}, u32[]{:S(2)}, u32[]{:S(2)}) collective-permute-start(f32[112,1024]{1,0:T(8,128)} %get-tuple-element.28), channel_id=1, source_target_pairs={{0,4},{4,8},{8,12},{12,16},{16,20},{20,24},{24,28},{1,5},{5,9},{9,... | collective-permute-start | bytes 1376264 | tf_op jit(solution)/shard_map/ppermute | solution.py:48
  5.6 1.3 collective-permute-start.1
  6.9 4.2 %collective-permute-start.2 = (f32[16,1024]{1,0:T(8,128)}, f32[16,1024]{1,0:T(8,128)S(1)}, u32[]{:S(2)}, u32[]{:S(2)}) collective-permute-start(f32[16,1024]{1,0:T(8,128)} %get-tuple-element.30), channel_id=1, source_target_pairs={{0,1},{1,2},{2,3},{4,5},{5,6},{6,7},{8,9},{9,10},{10,11},{12,13},{... | collective-permute-start | bytes 196616 | tf_op jit(solution)/shard_map/ppermute | solution.py:48
  11.2 1.3 collective-permute-start.3
  12.5 0.9 rank.1
  13.4 0.0 copy-start.23
  13.4 0.6 copy-done.23
  14.0 0.0 collective-permute-done.2.refs_2_.ylo_ref
  14.0 3.5 %collective-permute-done.3.refs_3_.yhi_ref = f32[16,1024]{1,0:T(8,128)S(1)} collective-permute-done((f32[16,1024]{1,0:T(8,128)}, f32[16,1024]{1,0:T(8,128)S(1)}, u32[]{:S(2)}, u32[]{:S(2)}) %collective-permute-start.3) | collective-permute-done | bytes 65568 | tf_op jit(solution)/shard_map/ppermute | solution.py:48
  17.6 0.0 collective-permute-done.refs_0_.xlo_ref.lo_ref.refs_4_
  17.6 0.0 collective-permute-done.1.refs_1_.xhi_ref.hi_ref.refs_5_
  17.6 0.0 copy-start
  17.6 2.5 %copy-done = f32[16,64,1024]{2,1,0:T(8,128)S(1)} copy-done((f32[16,64,1024]{2,1,0:T(8,128)S(1)}, f32[16,64,1024]{2,1,0:T(8,128)}, u32[]{:S(2)}) %copy-start) | copy-done | bytes 4194328
  20.1 2.6 %pack.1 = (f32[32,104,128]{2,1,0:T(8,128)S(1)}, f32[16,64,128]{2,1,0:T(8,128)S(1)}) custom-call(s32[1,1024]{1,0:T(1,128)S(1)} %get-tuple-element.32.where_ref, f32[32,128]{1,0:T(8,128)S(1)} %get-tuple-element.33.code_ref, f32[16,64,1024]{2,1,0:T(8,128)S(1)} %copy-done, f32[16,64,128]{2,1,0:T(8,128)S(1)} %copy-done.25, s32[16,64,128]{2,1,0:T(8,128)S(1)} %copy-done.26, ...), custom_call_target="tpu_custom_call" | custom-call | flops 1744830464 | bytes 2621440 | tf_op jit(solution)/shard_map/pack/pallas_call | solution.py:138
  22.8 0.0 copy-done.6
  22.8 0.0 copy-start.1
  22.8 0.8 copy-done.1
  23.6 1.2 copy-done.11
  24.8 0.0 copy-done.21
  24.8 8.3 %all-to-all-start = ((f32[32,104,128]{2,1,0:T(8,128)}), f32[32,104,128]{2,1,0:T(8,128)S(1)}, u32[]{:S(2)}, u32[]{:S(2)}) async-start(f32[32,104,128]{2,1,0:T(8,128)} %copy-done.11), calls=%async_computation | async-start | bytes 3407872 | tf_op jit(solution)/shard_map/all_to_all | solution.py:626
  33.1 0.0 copy-start.2
  33.1 0.0 copy-start.5
  33.1 0.0 copy-start.13
  33.1 12.2 %fluid_step.2 = (f32[16,64,1024]{2,1,0:T(8,128)}, f32[64,1024]{1,0:T(8,128)}, f32[64,1024]{1,0:T(8,128)}, f32[16,1024]{1,0:T(8,128)}, f32[16,1024]{1,0:T(8,128)}) custom-call(f32[16,64,1024]{2,1,0:T(8,128)} %here_ref.1, f32[112,1024]{1,0:T(8,128)} %copy-done.4, f32[112,1024]{1,0:T(8,128)} %copy-done.6, f32[16,1024]{1,0:T(8,128)} %copy-done.21, ...), custom_call_target="tpu_custom_call" | custom-call | flops 41943040 | bytes 14680064 | tf_op jit(solution)/shard_map/fluid_step/pallas_call | solution.py:582
  45.3 2.2 %collective-permute-start.4 = (f32[64,1024]{1,0:T(8,128)}, f32[64,1024]{1,0:T(8,128)S(1)}, u32[]{:S(2)}, u32[]{:S(2)}) collective-permute-start(f32[64,1024]{1,0:T(8,128)} %get-tuple-element.36), channel_id=1, source_target_pairs={{0,4},{4,8},{8,12},{12,16},{16,20},{20,24},{24,28},{1,5},{5,9},{9,... | collective-permute-start | bytes 786440 | tf_op jit(solution)/shard_map/ppermute | solution.py:48
  47.5 1.3 collective-permute-start.5
  48.9 1.0 copy-done.7
  49.9 0.9 copy-done.14
  50.8 0.2 y_faces.1
  51.0 3.6 %collective-permute-start.8 = (f32[48,1024]{1,0:T(8,128)S(1)}, f32[48,1024]{1,0:T(8,128)S(1)}, u32[]{:S(2)}, u32[]{:S(2)}) collective-permute-start(f32[48,1024]{1,0:T(8,128)S(1)} %get-tuple-element.40), channel_id=1, source_target_pairs={{0,1},{1,2},{2,3},{4,5},{5,6},{6,7},{8,9},{9,10},{10,11},{12,13},{... | collective-permute-start | bytes 589832 | tf_op jit(solution)/shard_map/ppermute | solution.py:48
  54.6 1.3 collective-permute-start.9
  55.9 4.5 %collective-permute-start.6 = (f32[16,1024]{1,0:T(8,128)}, f32[16,1024]{1,0:T(8,128)S(1)}, u32[]{:S(2)}, u32[]{:S(2)}) collective-permute-start(f32[16,1024]{1,0:T(8,128)} %get-tuple-element.38), channel_id=1, source_target_pairs={{0,1},{1,2},{2,3},{4,5},{5,6},{6,7},{8,9},{9,10},{10,11},{12,13},{... | collective-permute-start | bytes 196616 | tf_op jit(solution)/shard_map/ppermute | solution.py:48
  60.5 2.4 %collective-permute-done.6.refs_2_.ylo_ref = f32[16,1024]{1,0:T(8,128)S(1)} collective-permute-done((f32[16,1024]{1,0:T(8,128)}, f32[16,1024]{1,0:T(8,128)S(1)}, u32[]{:S(2)}, u32[]{:S(2)}) %collective-permute-start.6) | collective-permute-done | bytes 65568 | tf_op jit(solution)/shard_map/ppermute | solution.py:48
  62.9 1.3 collective-permute-start.7
  64.2 9.2 %collective-permute-done.7.refs_3_.yhi_ref = f32[16,1024]{1,0:T(8,128)S(1)} collective-permute-done((f32[16,1024]{1,0:T(8,128)}, f32[16,1024]{1,0:T(8,128)S(1)}, u32[]{:S(2)}, u32[]{:S(2)}) %collective-permute-start.7) | collective-permute-done | bytes 65568 | tf_op jit(solution)/shard_map/ppermute | solution.py:48
  73.4 0.0 collective-permute-done.8.refs_6_.ylo_ref
  73.4 0.0 collective-permute-done.9.refs_7_.yhi_ref
  73.4 0.0 collective-permute-done.4.refs_0_.xlo_ref
  73.5 0.0 collective-permute-done.5.refs_1_.xhi_ref
  73.5 0.7 copy-done.17
  74.2 0.0 all-to-all-done.rows_ref
  74.2 1.0 copy-done.8
  75.2 0.9 copy-done.18
  76.2 2.1 %heat_sum.1 = (f32[16,32,128]{2,1,0:T(8,128)S(1)}, f32[4,32,128]{2,1,0:T(8,128)S(1)}, f32[4,32,128]{2,1,0:T(8,128)S(1)}, s32[32,128]{1,0:T(8,128)S(1)}) custom-call(f32[32,104,128]{2,1,0:T(8,128)S(1)} %all-to-all-done.rows_ref, f32[64,1024]{1,0:T(8,128)S(1)} %collective-permute-done.4.refs_0_.xlo_ref, f32[64,1024]{1,0:T(8,128)S(1)} %copy-done.18, ...), custom_call_target="tpu_custom_call" | custom-call | flops 872415232 | bytes 1703936 | tf_op jit(solution)/shard_map/heat_sum/pallas_call | solution.py:189
  78.3 0.6 copy-done.19
  78.9 0.7 copy-done.20
  79.6 2.4 %collective-permute-start.10 = (f32[4,32,128]{2,1,0:T(8,128)S(1)}, f32[4,32,128]{2,1,0:T(8,128)S(1)}, u32[]{:S(2)}, u32[]{:S(2)}) collective-permute-start(f32[4,32,128]{2,1,0:T(8,128)S(1)} %get-tuple-element.44), channel_id=1, source_target_pairs={{0,4},{4,8},{8,12},{12,16},{16,20},{20,24},{24,28},{1,5},{5,9},{9,... | collective-permute-start | bytes 196616 | tf_op jit(solution)/shard_map/ppermute | solution.py:48
  82.0 1.3 collective-permute-start.11
  83.3 0.0 collective-permute-done.10.hxlo_ref
  83.3 6.1 %collective-permute-done.11.hxhi_ref = f32[4,32,128]{2,1,0:T(8,128)S(1)} collective-permute-done((f32[4,32,128]{2,1,0:T(8,128)S(1)}, f32[4,32,128]{2,1,0:T(8,128)S(1)}, u32[]{:S(2)}, u32[]{:S(2)}) %collective-permute-start.11) | collective-permute-done | bytes 65568 | tf_op jit(solution)/shard_map/ppermute | solution.py:48
  89.4 5.2 %collective-permute-start.12 = (f32[24,4,128]{2,1,0:T(4,128)S(1)}, f32[24,4,128]{2,1,0:T(4,128)S(1)}, u32[]{:S(2)}, u32[]{:S(2)}) collective-permute-start(f32[24,4,128]{2,1,0:T(4,128)S(1)} %pad_maximum_fusion), channel_id=1, source_target_pairs={{0,1},{1,2},{2,3},{4,5},{5,6},{6,7},{8,9},{9,10},{10,11},{12,13},{... | collective-permute-start | bytes 147464 | tf_op jit(solution)/shard_map/ppermute | solution.py:48
  94.6 1.3 collective-permute-start.13
  95.9 0.4 collective-permute-done.12.hylo_ref
  96.3 4.8 %collective-permute-done.13.hyhi_ref = f32[24,4,128]{2,1,0:T(4,128)S(1)} collective-permute-done((f32[24,4,128]{2,1,0:T(4,128)S(1)}, f32[24,4,128]{2,1,0:T(4,128)S(1)}, u32[]{:S(2)}, u32[]{:S(2)}) %collective-permute-start.13) | collective-permute-done | bytes 49184 | tf_op jit(solution)/shard_map/ppermute | solution.py:48
  101.1 0.9 copy-done.15
  102.1 5.4 %solid_steps.1 = (f32[16,32,128]{2,1,0:T(8,128)}, f32[18,48,128]{2,1,0:T(8,128)S(1)}, f32[3072,128]{1,0:T(8,128)S(1)}) custom-call(f32[16,32,128]{2,1,0:T(8,128)S(1)} %copy-done.13, s32[16,32,128]{2,1,0:T(8,128)S(1)} %copy-done.15, f32[112,1024]{1,0:T(8,128)S(1)} %copy-done.5, f32[112,1024]{1,0:T(8,128)S(1)} %copy-done.8, ...), custom_call_target="tpu_custom_call" | custom-call | flops 805306368 | bytes 1572864 | tf_op jit(solution)/shard_map/solid_steps/pallas_call | solution.py:403
  107.5 1.2 copy-done.12
  108.7 5.7 %all-to-all-start.1 = ((f32[32,96,128]{2,1,0:T(8,128)}), f32[32,96,128]{2,1,0:T(8,128)S(1)}, u32[]{:S(2)}, u32[]{:S(2)}) async-start(f32[32,96,128]{2,1,0:T(8,128)} %bitcast.5), calls=%async_computation.1 | async-start | bytes 3145728 | tf_op jit(solution)/shard_map/all_to_all | solution.py:645
  114.3 2.1 %stress.1.refs_1_ = f32[3,16,32,128]{3,2,1,0:T(8,128)} custom-call(f32[18,48,128]{2,1,0:T(8,128)S(1)} %get-tuple-element.47.refs_0_.sigma_ref), custom_call_target="tpu_custom_call" | custom-call | flops 655360 | bytes 1048576 | tf_op jit(solution)/shard_map/stress/pallas_call | solution.py:451
  116.5 12.2 %fluid_step.3 = (f32[16,64,1024]{2,1,0:T(8,128)}, f32[64,1024]{1,0:T(8,128)}, f32[64,1024]{1,0:T(8,128)}, f32[16,1024]{1,0:T(8,128)}, f32[16,1024]{1,0:T(8,128)}) custom-call(f32[16,64,1024]{2,1,0:T(8,128)} %get-tuple-element.35.here_ref, f32[64,1024]{1,0:T(8,128)} %copy-done.16, f32[64,1024]{1,0:T(8,128)} %copy-done.17, f32[16,1024]{1,0:T(8,128)} %copy-done.19, ...), custom_call_target="tpu_custom_call" | custom-call | flops 41943040 | bytes 14680064 | tf_op jit(solution)/shard_map/fluid_step/pallas_call | solution.py:582
  128.7 23.1 %all-to-all-done.1 = f32[32,96,128]{2,1,0:T(8,128)S(1)} async-done(((f32[32,96,128]{2,1,0:T(8,128)}), f32[32,96,128]{2,1,0:T(8,128)S(1)}, u32[]{:S(2)}, u32[]{:S(2)}) %all-to-all-start.1) | async-done | bytes 1572896 | tf_op jit(solution)/shard_map/all_to_all | solution.py:645
  151.8 2.2 %copy-done.3 = f32[16,64,1024]{2,1,0:T(8,128)S(1)} copy-done((f32[16,64,1024]{2,1,0:T(8,128)S(1)}, f32[16,64,1024]{2,1,0:T(8,128)}, u32[]{:S(2)}) %copy-start.3) | copy-done | bytes 4194328
  154.0 2.4 %unpack.1 = f32[1024,128]{1,0:T(8,128)} custom-call(s32[1,1024]{1,0:T(1,128)S(1)} %copy-done.24, f32[3072,128]{1,0:T(8,128)S(1)} %bitcast.4, f32[16,64,1024]{2,1,0:T(8,128)S(1)} %copy-done.3, f32[3,16,32,128]{3,2,1,0:T(8,128)S(1)} %copy-done.9), custom_call_target="tpu_custom_call" | custom-call | flops 131072 | bytes 1048576 | tf_op jit(solution)/shard_map/unpack/pallas_call | solution.py:479
  (41 shorter events, 0.1 us)
Async XLA Ops:
  0.6 11.9 %copy-start.28 = (s32[1,1024]{1,0:T(1,128)S(1)}, s32[1,1024]{1,0:T(1,128)}, u32[]{:S(2)}) copy-start(s32[1,1024]{1,0:T(1,128)} %slot_ref.1) | copy-start | bytes 12292
  0.6 11.9 %copy-start.27 = (s32[1,1024,1]{1,2,0:T(1,128)S(1)}, s32[1,1024,1]{1,2,0:T(1,128)}, u32[]{:S(2)}) copy-start(s32[1,1024,1]{1,2,0:T(1,128)} %param.12) | copy-start | bytes 12292
  0.7 16.9 %copy-start.26 = (s32[16,64,128]{2,1,0:T(8,128)S(1)}, s32[16,64,128]{2,1,0:T(8,128)}, u32[]{:S(2)}) copy-start(s32[16,64,128]{2,1,0:T(8,128)} %mask_ref.1) | copy-start | bytes 1572868
  0.7 16.9 %copy-start.25 = (f32[16,64,128]{2,1,0:T(8,128)S(1)}, f32[16,64,128]{2,1,0:T(8,128)}, u32[]{:S(2)}) copy-start(f32[16,64,128]{2,1,0:T(8,128)} %old_ref.1) | copy-start | bytes 1572868
  3.3 14.3 %collective-permute-start = (f32[112,1024]{1,0:T(8,128)}, f32[112,1024]{1,0:T(8,128)S(1)}, u32[]{:S(2)}, u32[]{:S(2)}) collective-permute-start(f32[112,1024]{1,0:T(8,128)} %get-tuple-element.28), channel_id=1, source_target_pairs={{0,4},{4,8},{8,12},{12,16},{16,20},{20,24},{24,28},{1,5},{5,9},{9,... | collective-permute-start | bytes 1376264 | tf_op jit(solution)/shard_map/ppermute | solution.py:48
  5.6 11.9 %collective-permute-start.1 = (f32[112,1024]{1,0:T(8,128)}, f32[112,1024]{1,0:T(8,128)S(1)}, u32[]{:S(2)}, u32[]{:S(2)}) collective-permute-start(f32[112,1024]{1,0:T(8,128)} %get-tuple-element.29), channel_id=1, source_target_pairs={{4,0},{8,4},{12,8},{16,12},{20,16},{24,20},{28,24},{5,1},{9,5},{13... | collective-permute-start | bytes 1376264 | tf_op jit(solution)/shard_map/ppermute | solution.py:48
  6.9 7.1 %collective-permute-start.2 = (f32[16,1024]{1,0:T(8,128)}, f32[16,1024]{1,0:T(8,128)S(1)}, u32[]{:S(2)}, u32[]{:S(2)}) collective-permute-start(f32[16,1024]{1,0:T(8,128)} %get-tuple-element.30), channel_id=1, source_target_pairs={{0,1},{1,2},{2,3},{4,5},{5,6},{6,7},{8,9},{9,10},{10,11},{12,13},{... | collective-permute-start | bytes 196616 | tf_op jit(solution)/shard_map/ppermute | solution.py:48
  11.2 6.4 %collective-permute-start.3 = (f32[16,1024]{1,0:T(8,128)}, f32[16,1024]{1,0:T(8,128)S(1)}, u32[]{:S(2)}, u32[]{:S(2)}) collective-permute-start(f32[16,1024]{1,0:T(8,128)} %get-tuple-element.31), channel_id=1, source_target_pairs={{1,0},{2,1},{3,2},{5,4},{6,5},{7,6},{9,8},{10,9},{11,10},{13,12},{... | collective-permute-start | bytes 196616 | tf_op jit(solution)/shard_map/ppermute | solution.py:48
  13.4 0.6 copy-start.23
  14.0 10.7 %copy-start.21 = (f32[16,1024]{1,0:T(8,128)}, f32[16,1024]{1,0:T(8,128)S(1)}, u32[]{:S(2)}) copy-start(f32[16,1024]{1,0:T(8,128)S(1)} %collective-permute-done.2.refs_2_.ylo_ref) | copy-start | bytes 196612
  17.6 7.2 %copy-start.22 = (f32[16,1024]{1,0:T(8,128)}, f32[16,1024]{1,0:T(8,128)S(1)}, u32[]{:S(2)}) copy-start(f32[16,1024]{1,0:T(8,128)S(1)} %collective-permute-done.3.refs_3_.yhi_ref) | copy-start | bytes 196612
  17.6 7.2 %copy-start.4 = (f32[112,1024]{1,0:T(8,128)}, f32[112,1024]{1,0:T(8,128)S(1)}, u32[]{:S(2)}) copy-start(f32[112,1024]{1,0:T(8,128)S(1)} %collective-permute-done.refs_0_.xlo_ref.lo_ref.refs_4_) | copy-start | bytes 1376260
  17.6 5.2 %copy-start.6 = (f32[112,1024]{1,0:T(8,128)}, f32[112,1024]{1,0:T(8,128)S(1)}, u32[]{:S(2)}) copy-start(f32[112,1024]{1,0:T(8,128)S(1)} %collective-permute-done.1.refs_1_.xhi_ref.hi_ref.refs_5_) | copy-start | bytes 1376260
  17.6 2.5 %copy-start = (f32[16,64,1024]{2,1,0:T(8,128)S(1)}, f32[16,64,1024]{2,1,0:T(8,128)}, u32[]{:S(2)}) copy-start(f32[16,64,1024]{2,1,0:T(8,128)} %here_ref.1) | copy-start | bytes 12582916
  22.8 0.8 copy-start.1
  23.6 1.2 copy-start.11
  24.8 49.5 %all-to-all-start = ((f32[32,104,128]{2,1,0:T(8,128)}), f32[32,104,128]{2,1,0:T(8,128)S(1)}, u32[]{:S(2)}, u32[]{:S(2)}) async-start(f32[32,104,128]{2,1,0:T(8,128)} %copy-done.11), calls=%async_computation | async-start | bytes 3407872 | tf_op jit(solution)/shard_map/all_to_all | solution.py:626
  33.1 15.8 %copy-start.2 = (f32[16,64,128]{2,1,0:T(8,128)S(1)}, f32[16,64,128]{2,1,0:T(8,128)}, u32[]{:S(2)}) copy-start(f32[16,64,128]{2,1,0:T(8,128)} %copy-done.1) | copy-start | bytes 1572868
  33.1 15.7 %copy-start.5 = (f32[112,1024]{1,0:T(8,128)S(1)}, f32[112,1024]{1,0:T(8,128)}, u32[]{:S(2)}) copy-start(f32[112,1024]{1,0:T(8,128)} %copy-done.4) | copy-start | bytes 1376260
  33.1 15.7 %copy-start.13 = (f32[16,32,128]{2,1,0:T(8,128)S(1)}, f32[16,32,128]{2,1,0:T(8,128)}, u32[]{:S(2)}) copy-start(f32[16,32,128]{2,1,0:T(8,128)} %own_ref.1) | copy-start | bytes 786436
  45.3 28.1 %collective-permute-start.4 = (f32[64,1024]{1,0:T(8,128)}, f32[64,1024]{1,0:T(8,128)S(1)}, u32[]{:S(2)}, u32[]{:S(2)}) collective-permute-start(f32[64,1024]{1,0:T(8,128)} %get-tuple-element.36), channel_id=1, source_target_pairs={{0,4},{4,8},{8,12},{12,16},{16,20},{20,24},{24,28},{1,5},{5,9},{9,... | collective-permute-start | bytes 786440 | tf_op jit(solution)/shard_map/ppermute | solution.py:48
  47.5 25.9 %collective-permute-start.5 = (f32[64,1024]{1,0:T(8,128)}, f32[64,1024]{1,0:T(8,128)S(1)}, u32[]{:S(2)}, u32[]{:S(2)}) collective-permute-start(f32[64,1024]{1,0:T(8,128)} %get-tuple-element.37), channel_id=1, source_target_pairs={{4,0},{8,4},{12,8},{16,12},{20,16},{24,20},{28,24},{5,1},{9,5},{13... | collective-permute-start | bytes 786440 | tf_op jit(solution)/shard_map/ppermute | solution.py:48
  48.9 1.0 copy-start.7
  49.9 0.9 copy-start.14
  51.0 22.4 %collective-permute-start.8 = (f32[48,1024]{1,0:T(8,128)S(1)}, f32[48,1024]{1,0:T(8,128)S(1)}, u32[]{:S(2)}, u32[]{:S(2)}) collective-permute-start(f32[48,1024]{1,0:T(8,128)S(1)} %get-tuple-element.40), channel_id=1, source_target_pairs={{0,1},{1,2},{2,3},{4,5},{5,6},{6,7},{8,9},{9,10},{10,11},{12,13},{... | collective-permute-start | bytes 589832 | tf_op jit(solution)/shard_map/ppermute | solution.py:48
  54.6 18.8 %collective-permute-start.9 = (f32[48,1024]{1,0:T(8,128)S(1)}, f32[48,1024]{1,0:T(8,128)S(1)}, u32[]{:S(2)}, u32[]{:S(2)}) collective-permute-start(f32[48,1024]{1,0:T(8,128)S(1)} %get-tuple-element.41), channel_id=1, source_target_pairs={{1,0},{2,1},{3,2},{5,4},{6,5},{7,6},{9,8},{10,9},{11,10},{13,12},{... | collective-permute-start | bytes 589832 | tf_op jit(solution)/shard_map/ppermute | solution.py:48
  55.9 7.0 %collective-permute-start.6 = (f32[16,1024]{1,0:T(8,128)}, f32[16,1024]{1,0:T(8,128)S(1)}, u32[]{:S(2)}, u32[]{:S(2)}) collective-permute-start(f32[16,1024]{1,0:T(8,128)} %get-tuple-element.38), channel_id=1, source_target_pairs={{0,1},{1,2},{2,3},{4,5},{5,6},{6,7},{8,9},{9,10},{10,11},{12,13},{... | collective-permute-start | bytes 196616 | tf_op jit(solution)/shard_map/ppermute | solution.py:48
  62.9 10.5 %collective-permute-start.7 = (f32[16,1024]{1,0:T(8,128)}, f32[16,1024]{1,0:T(8,128)S(1)}, u32[]{:S(2)}, u32[]{:S(2)}) collective-permute-start(f32[16,1024]{1,0:T(8,128)} %get-tuple-element.39), channel_id=1, source_target_pairs={{1,0},{2,1},{3,2},{5,4},{6,5},{7,6},{9,8},{10,9},{11,10},{13,12},{... | collective-permute-start | bytes 196616 | tf_op jit(solution)/shard_map/ppermute | solution.py:48
  73.4 27.7 %copy-start.16 = (f32[64,1024]{1,0:T(8,128)}, f32[64,1024]{1,0:T(8,128)S(1)}, u32[]{:S(2)}) copy-start(f32[64,1024]{1,0:T(8,128)S(1)} %collective-permute-done.4.refs_0_.xlo_ref) | copy-start | bytes 786436
  73.5 0.8 copy-start.17
  74.2 1.0 copy-start.8
  75.2 0.9 copy-start.18
  78.3 0.6 copy-start.19
  78.9 0.7 copy-start.20
  79.6 3.7 %collective-permute-start.10 = (f32[4,32,128]{2,1,0:T(8,128)S(1)}, f32[4,32,128]{2,1,0:T(8,128)S(1)}, u32[]{:S(2)}, u32[]{:S(2)}) collective-permute-start(f32[4,32,128]{2,1,0:T(8,128)S(1)} %get-tuple-element.44), channel_id=1, source_target_pairs={{0,4},{4,8},{8,12},{12,16},{16,20},{20,24},{24,28},{1,5},{5,9},{9,... | collective-permute-start | bytes 196616 | tf_op jit(solution)/shard_map/ppermute | solution.py:48
  82.0 7.4 %collective-permute-start.11 = (f32[4,32,128]{2,1,0:T(8,128)S(1)}, f32[4,32,128]{2,1,0:T(8,128)S(1)}, u32[]{:S(2)}, u32[]{:S(2)}) collective-permute-start(f32[4,32,128]{2,1,0:T(8,128)S(1)} %get-tuple-element.45), channel_id=1, source_target_pairs={{4,0},{8,4},{12,8},{16,12},{20,16},{24,20},{28,24},{5,1},{9,5},{13... | collective-permute-start | bytes 196616 | tf_op jit(solution)/shard_map/ppermute | solution.py:48
  89.4 6.9 %collective-permute-start.12 = (f32[24,4,128]{2,1,0:T(4,128)S(1)}, f32[24,4,128]{2,1,0:T(4,128)S(1)}, u32[]{:S(2)}, u32[]{:S(2)}) collective-permute-start(f32[24,4,128]{2,1,0:T(4,128)S(1)} %pad_maximum_fusion), channel_id=1, source_target_pairs={{0,1},{1,2},{2,3},{4,5},{5,6},{6,7},{8,9},{9,10},{10,11},{12,13},{... | collective-permute-start | bytes 147464 | tf_op jit(solution)/shard_map/ppermute | solution.py:48
  94.6 6.5 %collective-permute-start.13 = (f32[24,4,128]{2,1,0:T(4,128)S(1)}, f32[24,4,128]{2,1,0:T(4,128)S(1)}, u32[]{:S(2)}, u32[]{:S(2)}) collective-permute-start(f32[24,4,128]{2,1,0:T(4,128)S(1)} %pad_maximum_fusion.1), channel_id=1, source_target_pairs={{1,0},{2,1},{3,2},{5,4},{6,5},{7,6},{9,8},{10,9},{11,10},{13,12},{... | collective-permute-start | bytes 147464 | tf_op jit(solution)/shard_map/ppermute | solution.py:48
  101.1 1.0 copy-start.15
  107.5 1.2 copy-start.12
  108.7 7.8 %copy-start.10 = (f32[18,48,128]{2,1,0:T(8,128)}, f32[18,48,128]{2,1,0:T(8,128)S(1)}, u32[]{:S(2)}) copy-start(f32[18,48,128]{2,1,0:T(8,128)S(1)} %get-tuple-element.47.refs_0_.sigma_ref) | copy-start | bytes 1327108
  108.7 43.2 %all-to-all-start.1 = ((f32[32,96,128]{2,1,0:T(8,128)}), f32[32,96,128]{2,1,0:T(8,128)S(1)}, u32[]{:S(2)}, u32[]{:S(2)}) async-start(f32[32,96,128]{2,1,0:T(8,128)} %bitcast.5), calls=%async_computation.1 | async-start | bytes 3145728 | tf_op jit(solution)/shard_map/all_to_all | solution.py:645
  116.5 35.3 %copy-start.9 = (f32[3,16,32,128]{3,2,1,0:T(8,128)S(1)}, f32[3,16,32,128]{3,2,1,0:T(8,128)}, u32[]{:S(2)}) copy-start(f32[3,16,32,128]{3,2,1,0:T(8,128)} %stress.1.refs_1_) | copy-start | bytes 2359300
  116.5 35.3 %copy-start.24 = (s32[1,1024]{1,0:T(1,128)S(1)}, s32[1,1024]{1,0:T(1,128)}, u32[]{:S(2)}) copy-start(s32[1,1024]{1,0:T(1,128)} %copy-done.23) | copy-start | bytes 12292
  151.8 2.2 %copy-start.3 = (f32[16,64,1024]{2,1,0:T(8,128)S(1)}, f32[16,64,1024]{2,1,0:T(8,128)}, u32[]{:S(2)}) copy-start(f32[16,64,1024]{2,1,0:T(8,128)} %get-tuple-element.24.refs_0_) | copy-start | bytes 12582916

commit v6 on v5

--- a/solution.py
+++ b/solution.py
@@ -53,6 +53,12 @@
 
 
 anywhere = pl.BlockSpec(memory_space=pl.ANY)
+in_vmem = pl.BlockSpec(memory_space=pltpu.VMEM)
+in_hbm = pl.BlockSpec(memory_space=pltpu.HBM)
+
+
+def far(value):
+    return pltpu.with_memory_space_constraint(value, pltpu.HBM)
 
 
 def rank_kernel(cap, owner_ref, slot_ref, dest_ref, where_ref, code_ref):
@@ -102,31 +108,34 @@
     )(owner, slot)
 
 
+GROUPS = 4
+
+
 def pack_kernel(cap, where_ref, code_ref, temp_ref, old_ref, mask_ref, *refs):
-    out_ref, flux_ref, rhs_ref = refs[-3:]
+    out_ref, flux_ref, rhs_ref, stage_ref, sems = refs[-5:]
     rows = where_ref.shape[1]
-    ndev, tall, row_len = out_ref.shape
+    ndev, tall, row_len = stage_ref.shape
     flux = mask_ref[...].astype(F32) * film_coef * (temp_ref[...] - old_ref[...])
     flux_ref[...] = flux
     high, low = halves(flux.reshape(rows, row_len))
     rhs_ref[:, :row_len] = high
     rhs_ref[:, row_len:] = low
     where = where_ref[...]
-    group = ndev // 4
+    group = ndev // GROUPS
     block = group * tall
-
-    def step(index, none):
-        base = index * block
-        pick = ones_where(
-            lax.broadcasted_iota(jnp.int32, (block, rows), 0) + base == where
-        )
+    lines = lax.broadcasted_iota(jnp.int32, (block, rows), 0)
+    copies = []
+    for index in range(GROUPS):
+        cut = slice(index * group, (index + 1) * group)
+        pick = ones_where(lines == where - index * block)
         both = jnp.dot(pick, rhs_ref[...], preferred_element_type=F32)
-        lines = both[:, :row_len] + both[:, row_len:]
-        out_ref[pl.ds(index * group, group)] = lines.reshape(group, tall, row_len)
-        return none
-
-    lax.fori_loop(0, ndev // group, step, 0)
-    out_ref[:, cap, :] = code_ref[...]
+        both = both[:, :row_len] + both[:, row_len:]
+        stage_ref[cut] = both.reshape(group, tall, row_len)
+        stage_ref[cut, cap, :] = code_ref[cut, :]
+        copies.append(pltpu.make_async_copy(stage_ref.at[cut], out_ref.at[cut], sems.at[index]))
+        copies[-1].start()
+    for copy in copies:
+        copy.wait()
 
 
 def pack(where, code, temp, old, mask, cap, after):
@@ -141,16 +150,20 @@
         in_specs=[whole((1, rows)), whole(code.shape)]
         + [whole((cx, cy, row_len))] * 3
         + [anywhere] * len(after),
-        out_specs=[whole((ndev, tall, row_len)), whole((cx, cy, row_len))],
+        out_specs=[in_hbm, whole((cx, cy, row_len))],
         out_shape=[
-            jax.ShapeDtypeStruct((ndev, tall, row_len), F32),
+            pltpu.HBM((ndev, tall, row_len), F32),
             jax.ShapeDtypeStruct((cx, cy, row_len), F32),
         ],
-        scratch_shapes=[pltpu.VMEM((rows, 2 * row_len), BF16)],
-        compiler_params=params(40),
+        scratch_shapes=[
+            pltpu.VMEM((rows, 2 * row_len), BF16),
+            pltpu.VMEM((ndev, tall, row_len), F32),
+            pltpu.SemaphoreType.DMA((GROUPS,)),
+        ],
+        compiler_params=params(24),
         cost_estimate=cost(4 * ndev * tall * rows * row_len, 5 * rows * row_len * 4),
         name="pack",
-    )(where, code, temp, old, mask, *after)
+    )(where, code, far(temp), far(old), far(mask), *after)
 
 
 def heat_kernel(cap, thin, rows_ref, *refs):
@@ -188,9 +201,8 @@
     edge = (thin, sy, row_len)
     return pl.pallas_call(
         functools.partial(heat_kernel, cap, thin),
-        grid=(1,),
-        in_specs=[whole(incoming.shape)] + [anywhere] * len(after),
-        out_specs=[whole(block), whole(edge), whole(edge), whole((ndev, row_len))],
+        in_specs=[in_vmem] + [anywhere] * len(after),
+        out_specs=[in_vmem] * 4,
         out_shape=[
             jax.ShapeDtypeStruct(block, F32),
             jax.ShapeDtypeStruct(edge, F32),
@@ -261,10 +273,10 @@
         out_specs=[whole((height, depth))] * 2 + [whole((cx, depth))] * 2,
         out_shape=[jax.ShapeDtypeStruct((height, depth), F32)] * 2
         + [jax.ShapeDtypeStruct((cx, depth), F32)] * 2,
-        compiler_params=params(61),
+        compiler_params=params(16),
         cost_estimate=cost(1000, 4 * 4 * height * depth),
         name="x_faces",
-    )(fluid, fluid, fluid, fluid, temp, kind)
+    )(far(fluid), far(fluid), far(fluid), far(fluid), far(temp), far(kind))
 
 
 def fill_x(rim, ref, which, own, lo_ref, hi_ref):
@@ -280,38 +292,42 @@
             ref[rim + sx + k, cut, :] = get_rim(hi_ref, base, n)
 
 
-def y_faces_kernel(rim, temp_ref, kind_ref, lo_ref, hi_ref, *refs):
-    left_ref, right_ref, work_ref = refs[-3:]
+def y_faces_kernel(rim, near_ref, far_ref, temp_ref, kind_ref, lo_ref, hi_ref,
+                   left_ref, right_ref, state_ref):
+    cx = near_ref.shape[0]
     sx, sy, _ = temp_ref.shape
+    left_ref[:cx, :] = near_ref[...]
+    right_ref[:cx, :] = far_ref[...]
     slabs = ([], [])
-    long = work_ref.shape[1]
-    work_ref[...] = jnp.zeros_like(work_ref)
+    long = state_ref.shape[1]
+    state_ref[...] = jnp.zeros_like(state_ref)
     for which, own in enumerate((temp_ref[...], kind_ref[...].astype(F32) + 1.0)):
-        fill_x(rim, work_ref.at[which], which, own, lo_ref, hi_ref)
+        fill_x(rim, state_ref.at[which], which, own, lo_ref, hi_ref)
         for into, start in zip(slabs, (OFF, OFF + sy - rim)):
             for k in range(rim):
                 for h in range(0, long, PART):
-                    into.append(work_ref[which, h:h + PART, start + k, :])
-    put_rim(left_ref, 0, slabs[0])
-    put_rim(right_ref, 0, slabs[1])
-
-
-def y_faces(rim, temp, kind, lo, hi, after):
+                    into.append(state_ref[which, h:h + PART, start + k, :])
+    put_rim(left_ref, cx, slabs[0])
+    put_rim(right_ref, cx, slabs[1])
+
+
+def y_faces(rim, near, far_side, temp, kind, lo, hi):
+    cx, depth = near.shape
     sx, sy, sz = temp.shape
-    depth = lo.shape[1]
     long = -(-(sx + 2 * rim) // PART) * PART
-    height = rim_rows(2 * rim * (long // PART), depth)
+    height = cx + rim_rows(2 * rim * (long // PART), depth)
+    args = (near, far_side, far(temp), far(kind), lo, hi)
     return pl.pallas_call(
         functools.partial(y_faces_kernel, rim),
         grid=(1,),
-        in_specs=[whole(temp.shape)] * 2 + [whole(lo.shape)] * 2 + [anywhere] * len(after),
-        out_specs=[whole((height, depth))] * 2,
-        out_shape=[jax.ShapeDtypeStruct((height, depth), F32)] * 2,
-        scratch_shapes=[pltpu.VMEM((2, long, sy + 2 * OFF, sz), F32)],
+        in_specs=[whole(x.shape) for x in args],
+        out_specs=[whole((height, depth))] * 2 + [in_vmem],
+        out_shape=[jax.ShapeDtypeStruct((height, depth), F32)] * 2
+        + [jax.ShapeDtypeStruct((2, long, sy + 2 * OFF, sz), F32)],
         compiler_params=params(16),
         cost_estimate=cost(1000, 4 * 4 * height * depth),
         name="y_faces",
-    )(temp, kind, lo, hi, *after)
+    )(*args)
 
 
 def table(kind, values):
@@ -321,35 +337,36 @@
     return out
 
 
-def solid_kernel(rim, cap, own_ref, kind_ref, xlo_ref, xhi_ref, ylo_ref, yhi_ref,
+def solid_kernel(rim, cap, state_ref, ylo_ref, yhi_ref,
                  heat_ref, hxlo_ref, hxhi_ref, hylo_ref, hyhi_ref, code_ref,
-                 next_ref, sigma_ref, reply_ref, temp_ref, work_ref, cond_ref, src_ref, rhs_ref,
+                 next_ref, sigma_ref, reply_ref, work_ref, src_ref, rhs_ref,
                  stage_ref, sems):
-    sx, sy, sz = own_ref.shape
+    sx, sy, sz = heat_ref.shape
     wide = sx + 2 * rim
     thin = rim - 1
-    pieces = -(-wide // PART)
-    for which, (own, ref) in enumerate(
-        ((own_ref[...], temp_ref), (kind_ref[...].astype(F32) + 1.0, cond_ref))
-    ):
-        fill_x(rim, ref, which, own, xlo_ref, xhi_ref)
+    long = state_ref.shape[1]
+    pieces = long // PART
+    base = ylo_ref.shape[0] - rim_rows(2 * rim * pieces, ylo_ref.shape[1])
+    temp_ref, cond_ref = work_ref.at[0], work_ref.at[1]
+    work_ref, spare_ref = work_ref.at[2], work_ref
+    for which in range(2):
+        spare_ref[which] = state_ref[which]
         for k in range(rim):
             for h in range(pieces):
                 n = (which * rim + k) * pieces + h
-                count = min(PART, wide - h * PART)
-                cut = slice(h * PART, h * PART + count)
-                ref[cut, OFF - rim + k, :] = get_rim(ylo_ref, 0, n)[:count]
-                ref[cut, OFF + sy + k, :] = get_rim(yhi_ref, 0, n)[:count]
+                cut = slice(h * PART, (h + 1) * PART)
+                spare_ref[which, cut, OFF - rim + k, :] = get_rim(ylo_ref, base, n)
+                spare_ref[which, cut, OFF + sy + k, :] = get_rim(yhi_ref, base, n)
     src_ref[rim:rim + sx, OFF:OFF + sy, :] = heat_ref[...]
     src_ref[1:rim, OFF:OFF + sy, :] = hxlo_ref[...]
     src_ref[rim + sx:wide - 1, OFF:OFF + sy, :] = hxhi_ref[...]
     src_ref[1:wide - 1, OFF - thin:OFF, :] = hylo_ref[...]
     src_ref[1:wide - 1, OFF + sy:OFF + sy + thin, :] = hyhi_ref[...]
-    kind = cond_ref[...]
+    kind = cond_ref[:wide]
     sigma_ref[...] = table(kind[rim - 1:rim + sx + 1], modulus_table)
-    cond_ref[...] = solid_step * table(kind, conduct_table)
+    cond_ref[:wide] = solid_step * table(kind, conduct_table)
     src_ref[...] = (solid_step * source_gain) * src_ref[...]
-    height = temp_ref.shape[1]
+    height = state_ref.shape[2]
     first = lax.broadcasted_iota(jnp.int32, (height, sz), 1) == 0
     last = lax.broadcasted_iota(jnp.int32, (height, sz), 1) == sz - 1
     pair = (temp_ref, work_ref)
@@ -373,7 +390,7 @@
     ndev = code_ref.shape[0]
     turned = jnp.transpose(code_ref[...])
     names = lax.broadcasted_iota(jnp.int32, (cap, slots), 1)
-    group = ndev // 4
+    group = ndev // GROUPS
     for index in range(0, ndev, group):
         pick = jnp.concatenate(
             [
@@ -395,38 +412,34 @@
         ).wait()
 
 
-def solid_steps(rim, cap, temp, kind, state_rim, heat, heat_rim, code):
-    sx, sy, sz = temp.shape
+def solid_steps(rim, cap, state, state_rim, heat, heat_rim, code):
+    sx, sy, sz = heat.shape
+    _, long, height, _ = state.shape
     total = code.shape[0] * cap
-    wide, height = sx + 2 * rim, sy + 2 * OFF
-    args = (temp, kind, *state_rim, heat, *heat_rim, code)
     return pl.pallas_call(
         functools.partial(solid_kernel, rim, cap),
-        grid=(1,),
-        in_specs=[whole(x.shape) for x in args],
-        out_specs=[
-            whole((sx, sy, sz)),
-            whole((sx + 2, height, sz)),
-            pl.BlockSpec(memory_space=pltpu.HBM),
-        ],
+        in_specs=[in_vmem] * 9,
+        out_specs=[in_vmem, in_vmem, in_hbm],
         out_shape=[
             jax.ShapeDtypeStruct((sx, sy, sz), F32),
             jax.ShapeDtypeStruct((sx + 2, height, sz), F32),
-            jax.ShapeDtypeStruct((total, sz), F32),
+            pltpu.HBM((total, sz), F32),
         ],
-        scratch_shapes=[pltpu.VMEM((wide, height, sz), F32)] * 4
-        + [
+        scratch_shapes=[
+            pltpu.VMEM((3, long, height, sz), F32),
+            pltpu.VMEM((sx + 2 * rim, height, sz), F32),
             pltpu.VMEM((sx * sy, 2 * sz), BF16),
             pltpu.VMEM((total, sz), F32),
-            pltpu.SemaphoreType.DMA((4,)),
+            pltpu.SemaphoreType.DMA((GROUPS,)),
         ],
         compiler_params=params(24),
         cost_estimate=cost(4 * total * sx * sy * sz, 4 * total * sz),
         name="solid_steps",
-    )(*args)
-
-
-def stress_kernel(sigma_ref, out_ref):
+    )(state, *state_rim, heat, *heat_rim, code)
+
+
+def stress_kernel(sigma_ref, out_ref, tick_ref):
+    tick_ref[...] = jnp.zeros_like(tick_ref)
     _, sx, sy, sz = out_ref.shape
     height = sigma_ref.shape[1]
     first = lax.broadcasted_iota(jnp.int32, (height, sz), 1) == 0
@@ -452,8 +465,8 @@
         stress_kernel,
         grid=(1,),
         in_specs=[whole(sigma.shape)],
-        out_specs=whole((3, sx, sy, sz)),
-        out_shape=jax.ShapeDtypeStruct((3, sx, sy, sz), F32),
+        out_specs=[whole((3, sx, sy, sz)), whole((8, LANE))],
+        out_shape=[pltpu.HBM((3, sx, sy, sz), F32), jax.ShapeDtypeStruct((8, LANE), F32)],
         compiler_params=params(8),
         cost_estimate=cost(10 * sx * sy * sz, 16 * sx * sy * sz),
         name="stress",
@@ -594,17 +607,17 @@
         + [anywhere] * len(after),
         out_specs=[pl.BlockSpec(plane, back), face, face, line, line],
         out_shape=[
-            jax.ShapeDtypeStruct(temp.shape, F32),
+            pltpu.HBM(temp.shape, F32),
             jax.ShapeDtypeStruct((cy, depth), F32),
             jax.ShapeDtypeStruct((cy, depth), F32),
             jax.ShapeDtypeStruct((cx, depth), F32),
             jax.ShapeDtypeStruct((cx, depth), F32),
         ],
         scratch_shapes=[pltpu.VMEM((RING, cy + 2 * OFF, depth), F32)],
-        compiler_params=params(61),
+        compiler_params=params(24),
         cost_estimate=cost(40 * cx * cy * depth, 14 * cx * cy * depth),
         name="fluid_step",
-    )(temp, *rims, velocity, flux, *after)
+    )(far(temp), *rims, far(velocity), flux, *after)
 
 
 def body(temp_fluid, velocity, wall_old, wall_mask, owner_map, slot_map, temp_solid, material):
@@ -625,29 +638,26 @@
     outgoing, flux = pack(where, codes, temp_fluid, wall_old, wall_mask, cap, faces)
     incoming = lax.all_to_all(outgoing, AXES, split_axis=0, concat_axis=0, tiled=True)
 
-    first, last = y_faces(rim, temp_solid, material, xlo, xhi, (flux,))
-    ylo, yhi = neighbours(last, first, "gy")
-    rims = (xlo, xhi, ylo, yhi)
-    for turn in range(FSTEPS - 1):
-        fluid, xfirst, xlast, yfirst, ylast = fluid_step(
-            fluid if turn else temp_fluid, faces, velocity, flux, ()
-        )
-        faces = (*neighbours(xlast, xfirst, "gx"), *neighbours(ylast, yfirst, "gy"))
+    fluid, *edges = fluid_step(temp_fluid, faces, velocity, flux, ())
+    first, last, left, right = edges
+    left, right, state = y_faces(rim, left, right, temp_solid, material, xlo, xhi)
+    faces = (*neighbours(last, first, "gx"), *neighbours(right, left, "gy"))
+    rims = faces[2:]
 
     thin = rim - 1
-    heat, first, last, code = heat_sum(incoming, cap, temp_solid.shape, thin, (*faces, *rims))
+    heat, first, last, code = heat_sum(incoming, cap, temp_solid.shape, thin, faces)
     hxlo, hxhi = neighbours(last, first, "gx")
     tall = lambda cut: jnp.concatenate([hxlo[:, cut], heat[:, cut], hxhi[:, cut]], axis=0)
     hylo, hyhi = neighbours(tall(slice(sy - thin, sy)), tall(slice(0, thin)), "gy")
     solid, sigma, replies = solid_steps(
-        rim, cap, temp_solid, material, rims, heat, (hxlo, hxhi, hylo, hyhi), code
+        rim, cap, state, rims, heat, (hxlo, hxhi, hylo, hyhi), code
     )
     returned = lax.all_to_all(
         replies.reshape(ndev, cap, sz), AXES, split_axis=0, concat_axis=0, tiled=True
     )
-    fluid = fluid_step(fluid, faces, velocity, flux, (sigma,))[0]
-    force = stress(sigma, sx, sy)
-    wall_next = unpack(dest, returned.reshape(total, sz), (fluid, force))
+    force, tick = stress(sigma, sx, sy)
+    fluid, *edges = fluid_step(fluid, faces, velocity, flux, (tick,))
+    wall_next = unpack(dest, returned.reshape(total, sz), edges[2:])
     return fluid, wall_next.reshape(cx, cy, row_len), solid, force
 
 

time: 158 us -> 143 us (0.905)
  local copies, waits for them, and re-layouts: 15.5 us -> 3.54 us
  starting transfers between devices: 47.5 us -> 39.2 us
  waiting for transfers between devices: 49.6 us -> 53.3 us
  Pallas kernels: 42.8 us -> 44.4 us
    unnamed x58 -> x12, local copies, waits for them, and re-layouts: 15.4 us -> 3.51 us
    ppermute x14 -> x12, starting transfers between devices: 33.5 us -> 25.3 us  [neighbours(): return (lax.ppermute(before, axis, up), lax.ppermute(after, axis, down))]
    all_to_all x1, waiting for transfers between devices: 0.01 us -> 2.64 us  [body(): lax.all_to_all(outgoing, AXES, split_axis=0, concat_axis=0, tiled=True)]
    pallas_call x1, Pallas kernels: 2.65 us -> 4.38 us  [pack(): pl.pallas_call(functools.partial(pack_kernel, cap), grid=(1,), in_specs=[...]
    ppermute x14 -> x12, waiting for transfers between devices: 26.5 us -> 28.2 us  [neighbours(): return (lax.ppermute(before, axis, up), lax.ppermute(after, axis, down))]
  transfers between devices with their start and end apart: 16 -> 14, of which waited for: 7 -> 8; matrix products, arithmetic and copies ran while one was open for 0% -> 0% of each run, Pallas kernels for 18% -> 20%
where the time goes in v6:
time: 143 us; the launch traced here: 141 us
  waiting for transfers between devices  53.3 us (37%)
  Pallas kernels  44.4 us (31%)
  starting transfers between devices  39.2 us (27%)
  local copies, waits for them, and re-layouts  3.54 us (2%)
    ppermute x12, waiting for transfers between devices, neighbours(): return (lax.ppermute(before, axis, up), lax.ppermute(after, axis, down))  28.2 us
    ppermute x12, starting transfers between devices, neighbours(): return (lax.ppermute(before, axis, up), lax.ppermute(after, axis, down))  25.3 us
    pallas_call x2, Pallas kernels, fluid_step(): pl.pallas_call(fluid_kernel, grid=(steps + 1,), in_specs=[pl.BlockSpec(pl...  23.5 us
    all_to_all x1, waiting for transfers between devices, body(): lax.all_to_all(replies.reshape(ndev, cap, sz), AXES, split_axis=0, concat...  22.5 us
    all_to_all x1, starting transfers between devices, body(): lax.all_to_all(outgoing, AXES, split_axis=0, concat_axis=0, tiled=True)  8.42 us
    all_to_all x1, starting transfers between devices, body(): lax.all_to_all(replies.reshape(ndev, cap, sz), AXES, split_axis=0, concat...  5.53 us
    pallas_call x1, Pallas kernels, solid_steps(): pl.pallas_call(functools.partial(solid_kernel, rim, cap), in_specs=[in_vm...  4.58 us
    pallas_call x1, Pallas kernels, pack(): pl.pallas_call(functools.partial(pack_kernel, cap), grid=(1,), in_specs=[...  4.38 us
  transfers between devices with their start and end apart: 14, of which 8 were waited for; matrix products, arithmetic and copies ran while one was open for 0% of the time, Pallas kernels for 20%

profile of v6, /device:TPU:0, one launch (start us, length us, event | category | flops | bytes accessed | tf_op | source)
XLA Modules:
  0.0 141.4 jit_solution(17141411612958377782)
XLA Ops:
  0.6 0.0 copy-start.5
  0.6 0.0 copy-start.4
  0.7 1.6 %x_faces.1 = (f32[112,1024]{1,0:T(8,128)S(1)}, f32[112,1024]{1,0:T(8,128)S(1)}, f32[16,1024]{1,0:T(8,128)S(1)}, f32[16,1024]{1,0:T(8,128)S(1)}) custom-call(f32[16,64,1024]{2,1,0:T(8,128)} %here_ref.1, f32[16,64,1024]{2,1,0:T(8,128)} %here_ref.1, f32[16,64,1024]{2,1,0:T(8,128)} %here_ref.1, f32[16,64,1024]{2,1,0:T(8,128)} %here_ref.1, ...), custom_call_target="tpu_custom_call" | custom-call | flops 1000 | bytes 1835008 | tf_op jit(solution)/shard_map/x_faces/pallas_call | solution.py:262
  2.3 2.4 %collective-permute-start = (f32[112,1024]{1,0:T(8,128)S(1)}, f32[112,1024]{1,0:T(8,128)S(1)}, u32[]{:S(2)}, u32[]{:S(2)}) collective-permute-start(f32[112,1024]{1,0:T(8,128)S(1)} %get-tuple-element.33), channel_id=1, source_target_pairs={{0,4},{4,8},{8,12},{12,16},{16,20},{20,24},{24,28},{1,5},{5,9},{9,... | collective-permute-start | bytes 1376264 | tf_op jit(solution)/shard_map/ppermute | solution.py:48
  4.7 1.3 collective-permute-start.1
  6.0 4.2 %collective-permute-start.2 = (f32[16,1024]{1,0:T(8,128)S(1)}, f32[16,1024]{1,0:T(8,128)S(1)}, u32[]{:S(2)}, u32[]{:S(2)}) collective-permute-start(f32[16,1024]{1,0:T(8,128)S(1)} %get-tuple-element.35), channel_id=1, source_target_pairs={{0,1},{1,2},{2,3},{4,5},{5,6},{6,7},{8,9},{9,10},{10,11},{12,13},{... | collective-permute-start | bytes 196616 | tf_op jit(solution)/shard_map/ppermute | solution.py:48
  10.2 1.3 collective-permute-start.3
  11.5 0.0 copy-done.5
  11.5 0.0 copy-done.4
  11.5 0.9 rank.1
  12.4 0.0 collective-permute-done.2.refs_2_.ylo_ref
  12.4 3.9 %collective-permute-done.3.refs_3_.yhi_ref = f32[16,1024]{1,0:T(8,128)S(1)} collective-permute-done((f32[16,1024]{1,0:T(8,128)S(1)}, f32[16,1024]{1,0:T(8,128)S(1)}, u32[]{:S(2)}, u32[]{:S(2)}) %collective-permute-start.3) | collective-permute-done | bytes 65568 | tf_op jit(solution)/shard_map/ppermute | solution.py:48
  16.3 0.0 collective-permute-done.refs_0_.xlo_ref.lo_ref
  16.3 0.0 collective-permute-done.1.refs_1_.xhi_ref.hi_ref
  16.4 4.4 %pack.1 = (f32[32,104,128]{2,1,0:T(8,128)}, f32[16,64,128]{2,1,0:T(8,128)S(1)}) custom-call(s32[1,1024]{1,0:T(1,128)S(1)} %get-tuple-element.37.where_ref, f32[32,128]{1,0:T(8,128)S(1)} %get-tuple-element.38.code_ref, f32[16,64,1024]{2,1,0:T(8,128)} %here_ref.1, f32[16,64,128]{2,1,0:T(8,128)} %old_ref.1, s32[16,64,128]{2,1,0:T(8,128)} %mask_ref.1, ...), custom_call_target="tpu_custom_call" | custom-call | flops 1744830464 | bytes 2621440 | tf_op jit(solution)/shard_map/pack/pallas_call | solution.py:147
  20.7 8.4 %all-to-all-start = ((f32[32,104,128]{2,1,0:T(8,128)}), f32[32,104,128]{2,1,0:T(8,128)}, u32[]{:S(2)}, u32[]{:S(2)}) async-start(f32[32,104,128]{2,1,0:T(8,128)} %get-tuple-element.48), calls=%async_computation | async-start | bytes 3407872 | tf_op jit(solution)/shard_map/all_to_all | solution.py:639
  29.2 11.7 %fluid_step.2 = (f32[16,64,1024]{2,1,0:T(8,128)}, f32[64,1024]{1,0:T(8,128)S(1)}, f32[64,1024]{1,0:T(8,128)S(1)}, f32[16,1024]{1,0:T(8,128)S(1)}, f32[16,1024]{1,0:T(8,128)S(1)}) custom-call(f32[16,64,1024]{2,1,0:T(8,128)} %here_ref.1, f32[112,1024]{1,0:T(8,128)S(1)} %collective-permute-done.refs_0_.xlo_ref.lo_ref, ...), custom_call_target="tpu_custom_call" | custom-call | flops 41943040 | bytes 14680064 | tf_op jit(solution)/shard_map/fluid_step/pallas_call | solution.py:595
  40.9 2.1 %collective-permute-start.4 = (f32[64,1024]{1,0:T(8,128)S(1)}, f32[64,1024]{1,0:T(8,128)S(1)}, u32[]{:S(2)}, u32[]{:S(2)}) collective-permute-start(f32[64,1024]{1,0:T(8,128)S(1)} %get-tuple-element.41), channel_id=1, source_target_pairs={{0,4},{4,8},{8,12},{12,16},{16,20},{20,24},{24,28},{1,5},{5,9},{9,... | collective-permute-start | bytes 786440 | tf_op jit(solution)/shard_map/ppermute | solution.py:48
  43.0 1.3 collective-permute-start.5
  44.3 1.3 y_faces.1
  45.6 0.0 copy-start.2
  45.6 1.1 copy-done.2
  46.7 3.6 %collective-permute-start.6 = (f32[64,1024]{1,0:T(8,128)S(1)}, f32[64,1024]{1,0:T(8,128)S(1)}, u32[]{:S(2)}, u32[]{:S(2)}) collective-permute-start(f32[64,1024]{1,0:T(8,128)S(1)} %get-tuple-element.45), channel_id=1, source_target_pairs={{0,1},{1,2},{2,3},{4,5},{5,6},{6,7},{8,9},{9,10},{10,11},{12,13},{... | collective-permute-start | bytes 786440 | tf_op jit(solution)/shard_map/ppermute | solution.py:48
  50.3 1.3 collective-permute-start.7
  51.6 0.0 collective-permute-done.4.refs_0_.xlo_ref
  51.6 0.0 collective-permute-done.5.refs_1_.xhi_ref
  51.6 5.8 %collective-permute-done.6.refs_2_.ylo_ref = f32[64,1024]{1,0:T(8,128)S(1)} collective-permute-done((f32[64,1024]{1,0:T(8,128)S(1)}, f32[64,1024]{1,0:T(8,128)S(1)}, u32[]{:S(2)}, u32[]{:S(2)}) %collective-permute-start.6) | collective-permute-done | bytes 262176 | tf_op jit(solution)/shard_map/ppermute | solution.py:48
  57.4 9.4 %collective-permute-done.7.refs_3_.yhi_ref = f32[64,1024]{1,0:T(8,128)S(1)} collective-permute-done((f32[64,1024]{1,0:T(8,128)S(1)}, f32[64,1024]{1,0:T(8,128)S(1)}, u32[]{:S(2)}, u32[]{:S(2)}) %collective-permute-start.7) | collective-permute-done | bytes 262176 | tf_op jit(solution)/shard_map/ppermute | solution.py:48
  66.8 0.0 copy-start
  66.8 2.6 %all-to-all-done.rows_ref = f32[32,104,128]{2,1,0:T(8,128)} async-done(((f32[32,104,128]{2,1,0:T(8,128)}), f32[32,104,128]{2,1,0:T(8,128)}, u32[]{:S(2)}, u32[]{:S(2)}) %all-to-all-start) | async-done | bytes 1703968 | tf_op jit(solution)/shard_map/all_to_all | solution.py:639
  69.4 3.5 %heat_sum.1 = (f32[16,32,128]{2,1,0:T(8,128)S(1)}, f32[4,32,128]{2,1,0:T(8,128)S(1)}, f32[4,32,128]{2,1,0:T(8,128)S(1)}, s32[32,128]{1,0:T(8,128)S(1)}) custom-call(f32[32,104,128]{2,1,0:T(8,128)} %all-to-all-done.rows_ref, f32[64,1024]{1,0:T(8,128)S(1)} %collective-permute-done.4.refs_0_.xlo_ref, f32[64,1024]{1,0:T(8,128)S(1)} %collective-permute-done.5.refs_1_.xhi_ref, ...), custom_call_target="tpu_custom_call" | custom-call | flops 872415232 | bytes 1703936 | tf_op jit(solution)/shard_map/heat_sum/pallas_call | solution.py:202
  73.0 1.5 %collective-permute-start.8 = (f32[4,32,128]{2,1,0:T(8,128)S(1)}, f32[4,32,128]{2,1,0:T(8,128)S(1)}, u32[]{:S(2)}, u32[]{:S(2)}) collective-permute-start(f32[4,32,128]{2,1,0:T(8,128)S(1)} %get-tuple-element.50), channel_id=1, source_target_pairs={{0,4},{4,8},{8,12},{12,16},{16,20},{20,24},{24,28},{1,5},{5,9},{9,... | collective-permute-start | bytes 196616 | tf_op jit(solution)/shard_map/ppermute | solution.py:48
  74.6 1.3 collective-permute-start.9
  75.9 0.0 collective-permute-done.8.hxlo_ref
  75.9 4.4 %collective-permute-done.9.hxhi_ref = f32[4,32,128]{2,1,0:T(8,128)S(1)} collective-permute-done((f32[4,32,128]{2,1,0:T(8,128)S(1)}, f32[4,32,128]{2,1,0:T(8,128)S(1)}, u32[]{:S(2)}, u32[]{:S(2)}) %collective-permute-start.9) | collective-permute-done | bytes 65568 | tf_op jit(solution)/shard_map/ppermute | solution.py:48
  80.3 3.7 %collective-permute-start.10 = (f32[24,4,128]{2,1,0:T(4,128)S(1)}, f32[24,4,128]{2,1,0:T(4,128)S(1)}, u32[]{:S(2)}, u32[]{:S(2)}) collective-permute-start(f32[24,4,128]{2,1,0:T(4,128)S(1)} %pad_maximum_fusion), channel_id=1, source_target_pairs={{0,1},{1,2},{2,3},{4,5},{5,6},{6,7},{8,9},{9,10},{10,11},{12,13},{... | collective-permute-start | bytes 147464 | tf_op jit(solution)/shard_map/ppermute | solution.py:48
  84.0 1.3 collective-permute-start.11
  85.3 0.4 collective-permute-done.10.hylo_ref
  85.7 4.3 %collective-permute-done.11.hyhi_ref = f32[24,4,128]{2,1,0:T(4,128)S(1)} collective-permute-done((f32[24,4,128]{2,1,0:T(4,128)S(1)}, f32[24,4,128]{2,1,0:T(4,128)S(1)}, u32[]{:S(2)}, u32[]{:S(2)}) %collective-permute-start.11) | collective-permute-done | bytes 49184 | tf_op jit(solution)/shard_map/ppermute | solution.py:48
  90.0 0.0 copy-done
  90.0 0.0 copy-start.3
  90.0 1.4 copy-done.3
  91.4 4.6 %solid_steps.1 = (f32[16,32,128]{2,1,0:T(8,128)}, f32[18,48,128]{2,1,0:T(8,128)S(1)}, f32[3072,128]{1,0:T(8,128)}) custom-call(f32[2,32,48,128]{3,2,1,0:T(8,128)S(1)} %copy-done.3, f32[64,1024]{1,0:T(8,128)S(1)} %collective-permute-done.6.refs_2_.ylo_ref, f32[64,1024]{1,0:T(8,128)S(1)} %collective-permute-done.7.refs_3_.yhi_ref, ...), custom_call_target="tpu_custom_call" | custom-call | flops 805306368 | bytes 1572864 | tf_op jit(solution)/shard_map/solid_steps/pallas_call | solution.py:419
  96.0 5.5 %all-to-all-start.1 = ((f32[32,96,128]{2,1,0:T(8,128)}), f32[32,96,128]{2,1,0:T(8,128)S(1)}, u32[]{:S(2)}, u32[]{:S(2)}) async-start(f32[32,96,128]{2,1,0:T(8,128)} %bitcast.6), calls=%async_computation.1 | async-start | bytes 3145728 | tf_op jit(solution)/shard_map/all_to_all | solution.py:655
  101.6 2.1 %stress.1 = (f32[3,16,32,128]{3,2,1,0:T(8,128)}, f32[8,128]{1,0:T(8,128)S(1)}) custom-call(f32[18,48,128]{2,1,0:T(8,128)S(1)} %get-tuple-element.53.sigma_ref), custom_call_target="tpu_custom_call" | custom-call | flops 655360 | bytes 1048576 | tf_op jit(solution)/shard_map/stress/pallas_call | solution.py:464
  103.7 0.0 copy-start.1
  103.7 0.9 copy-done.1
  104.6 11.8 %fluid_step.3 = (f32[16,64,1024]{2,1,0:T(8,128)}, f32[64,1024]{1,0:T(8,128)}, f32[64,1024]{1,0:T(8,128)}, f32[16,1024]{1,0:T(8,128)S(1)}, f32[16,1024]{1,0:T(8,128)S(1)}) custom-call(f32[16,64,1024]{2,1,0:T(8,128)} %get-tuple-element.40.here_ref, f32[64,1024]{1,0:T(8,128)S(1)} %collective-permute-done.4.refs_0_.xlo_ref, ...), custom_call_target="tpu_custom_call" | custom-call | flops 41943040 | bytes 14680064 | tf_op jit(solution)/shard_map/fluid_step/pallas_call | solution.py:595
  116.5 22.5 %all-to-all-done.1 = f32[32,96,128]{2,1,0:T(8,128)S(1)} async-done(((f32[32,96,128]{2,1,0:T(8,128)}), f32[32,96,128]{2,1,0:T(8,128)S(1)}, u32[]{:S(2)}, u32[]{:S(2)}) %all-to-all-start.1) | async-done | bytes 1572896 | tf_op jit(solution)/shard_map/all_to_all | solution.py:655
  139.0 2.4 %unpack.1 = f32[1024,128]{1,0:T(8,128)} custom-call(s32[1,1024]{1,0:T(1,128)S(1)} %get-tuple-element.56.dest_ref, f32[3072,128]{1,0:T(8,128)S(1)} %bitcast.4, f32[16,1024]{1,0:T(8,128)S(1)} %get-tuple-element.58.refs_0_, f32[16,1024]{1,0:T(8,128)S(1)} %get-tuple-element.59.refs_1_), custom_call_target="tpu_custom_call" | custom-call | flops 131072 | bytes 1048576 | tf_op jit(solution)/shard_map/unpack/pallas_call | solution.py:492
  (5 shorter events, 0.1 us)
Async XLA Ops:
  0.6 10.9 %copy-start.5 = (s32[1,1024]{1,0:T(1,128)S(1)}, s32[1,1024]{1,0:T(1,128)}, u32[]{:S(2)}) copy-start(s32[1,1024]{1,0:T(1,128)} %slot_ref.1) | copy-start | bytes 12292
  0.6 10.9 %copy-start.4 = (s32[1,1024,1]{1,2,0:T(1,128)S(1)}, s32[1,1024,1]{1,2,0:T(1,128)}, u32[]{:S(2)}) copy-start(s32[1,1024,1]{1,2,0:T(1,128)} %param.12) | copy-start | bytes 12292
  2.3 14.1 %collective-permute-start = (f32[112,1024]{1,0:T(8,128)S(1)}, f32[112,1024]{1,0:T(8,128)S(1)}, u32[]{:S(2)}, u32[]{:S(2)}) collective-permute-start(f32[112,1024]{1,0:T(8,128)S(1)} %get-tuple-element.33), channel_id=1, source_target_pairs={{0,4},{4,8},{8,12},{12,16},{16,20},{20,24},{24,28},{1,5},{5,9},{9,... | collective-permute-start | bytes 1376264 | tf_op jit(solution)/shard_map/ppermute | solution.py:48
  4.7 11.7 %collective-permute-start.1 = (f32[112,1024]{1,0:T(8,128)S(1)}, f32[112,1024]{1,0:T(8,128)S(1)}, u32[]{:S(2)}, u32[]{:S(2)}) collective-permute-start(f32[112,1024]{1,0:T(8,128)S(1)} %get-tuple-element.34), channel_id=1, source_target_pairs={{4,0},{8,4},{12,8},{16,12},{20,16},{24,20},{28,24},{5,1},{9,5},{13... | collective-permute-start | bytes 1376264 | tf_op jit(solution)/shard_map/ppermute | solution.py:48
  6.0 6.5 %collective-permute-start.2 = (f32[16,1024]{1,0:T(8,128)S(1)}, f32[16,1024]{1,0:T(8,128)S(1)}, u32[]{:S(2)}, u32[]{:S(2)}) collective-permute-start(f32[16,1024]{1,0:T(8,128)S(1)} %get-tuple-element.35), channel_id=1, source_target_pairs={{0,1},{1,2},{2,3},{4,5},{5,6},{6,7},{8,9},{9,10},{10,11},{12,13},{... | collective-permute-start | bytes 196616 | tf_op jit(solution)/shard_map/ppermute | solution.py:48
  10.2 6.2 %collective-permute-start.3 = (f32[16,1024]{1,0:T(8,128)S(1)}, f32[16,1024]{1,0:T(8,128)S(1)}, u32[]{:S(2)}, u32[]{:S(2)}) collective-permute-start(f32[16,1024]{1,0:T(8,128)S(1)} %get-tuple-element.36), channel_id=1, source_target_pairs={{1,0},{2,1},{3,2},{5,4},{6,5},{7,6},{9,8},{10,9},{11,10},{13,12},{... | collective-permute-start | bytes 196616 | tf_op jit(solution)/shard_map/ppermute | solution.py:48
  20.7 48.7 %all-to-all-start = ((f32[32,104,128]{2,1,0:T(8,128)}), f32[32,104,128]{2,1,0:T(8,128)}, u32[]{:S(2)}, u32[]{:S(2)}) async-start(f32[32,104,128]{2,1,0:T(8,128)} %get-tuple-element.48), calls=%async_computation | async-start | bytes 3407872 | tf_op jit(solution)/shard_map/all_to_all | solution.py:639
  40.9 10.8 %collective-permute-start.4 = (f32[64,1024]{1,0:T(8,128)S(1)}, f32[64,1024]{1,0:T(8,128)S(1)}, u32[]{:S(2)}, u32[]{:S(2)}) collective-permute-start(f32[64,1024]{1,0:T(8,128)S(1)} %get-tuple-element.41), channel_id=1, source_target_pairs={{0,4},{4,8},{8,12},{12,16},{16,20},{20,24},{24,28},{1,5},{5,9},{9,... | collective-permute-start | bytes 786440 | tf_op jit(solution)/shard_map/ppermute | solution.py:48
  43.0 8.7 %collective-permute-start.5 = (f32[64,1024]{1,0:T(8,128)S(1)}, f32[64,1024]{1,0:T(8,128)S(1)}, u32[]{:S(2)}, u32[]{:S(2)}) collective-permute-start(f32[64,1024]{1,0:T(8,128)S(1)} %get-tuple-element.42), channel_id=1, source_target_pairs={{4,0},{8,4},{12,8},{16,12},{20,16},{24,20},{28,24},{5,1},{9,5},{13... | collective-permute-start | bytes 786440 | tf_op jit(solution)/shard_map/ppermute | solution.py:48
  45.6 1.2 copy-start.2
  46.7 10.7 %collective-permute-start.6 = (f32[64,1024]{1,0:T(8,128)S(1)}, f32[64,1024]{1,0:T(8,128)S(1)}, u32[]{:S(2)}, u32[]{:S(2)}) collective-permute-start(f32[64,1024]{1,0:T(8,128)S(1)} %get-tuple-element.45), channel_id=1, source_target_pairs={{0,1},{1,2},{2,3},{4,5},{5,6},{6,7},{8,9},{9,10},{10,11},{12,13},{... | collective-permute-start | bytes 786440 | tf_op jit(solution)/shard_map/ppermute | solution.py:48
  50.3 16.5 %collective-permute-start.7 = (f32[64,1024]{1,0:T(8,128)S(1)}, f32[64,1024]{1,0:T(8,128)S(1)}, u32[]{:S(2)}, u32[]{:S(2)}) collective-permute-start(f32[64,1024]{1,0:T(8,128)S(1)} %get-tuple-element.46), channel_id=1, source_target_pairs={{1,0},{2,1},{3,2},{5,4},{6,5},{7,6},{9,8},{10,9},{11,10},{13,12},{... | collective-permute-start | bytes 786440 | tf_op jit(solution)/shard_map/ppermute | solution.py:48
  66.8 23.2 %copy-start = (f32[64,1024]{1,0:T(8,128)}, f32[64,1024]{1,0:T(8,128)S(1)}, u32[]{:S(2)}) copy-start(f32[64,1024]{1,0:T(8,128)S(1)} %collective-permute-done.7.refs_3_.yhi_ref) | copy-start | bytes 786436
  73.0 2.9 %collective-permute-start.8 = (f32[4,32,128]{2,1,0:T(8,128)S(1)}, f32[4,32,128]{2,1,0:T(8,128)S(1)}, u32[]{:S(2)}, u32[]{:S(2)}) collective-permute-start(f32[4,32,128]{2,1,0:T(8,128)S(1)} %get-tuple-element.50), channel_id=1, source_target_pairs={{0,4},{4,8},{8,12},{12,16},{16,20},{20,24},{24,28},{1,5},{5,9},{9,... | collective-permute-start | bytes 196616 | tf_op jit(solution)/shard_map/ppermute | solution.py:48
  74.6 5.7 %collective-permute-start.9 = (f32[4,32,128]{2,1,0:T(8,128)S(1)}, f32[4,32,128]{2,1,0:T(8,128)S(1)}, u32[]{:S(2)}, u32[]{:S(2)}) collective-permute-start(f32[4,32,128]{2,1,0:T(8,128)S(1)} %get-tuple-element.51), channel_id=1, source_target_pairs={{4,0},{8,4},{12,8},{16,12},{20,16},{24,20},{28,24},{5,1},{9,5},{13... | collective-permute-start | bytes 196616 | tf_op jit(solution)/shard_map/ppermute | solution.py:48
  80.3 5.5 %collective-permute-start.10 = (f32[24,4,128]{2,1,0:T(4,128)S(1)}, f32[24,4,128]{2,1,0:T(4,128)S(1)}, u32[]{:S(2)}, u32[]{:S(2)}) collective-permute-start(f32[24,4,128]{2,1,0:T(4,128)S(1)} %pad_maximum_fusion), channel_id=1, source_target_pairs={{0,1},{1,2},{2,3},{4,5},{5,6},{6,7},{8,9},{9,10},{10,11},{12,13},{... | collective-permute-start | bytes 147464 | tf_op jit(solution)/shard_map/ppermute | solution.py:48
  84.0 6.0 %collective-permute-start.11 = (f32[24,4,128]{2,1,0:T(4,128)S(1)}, f32[24,4,128]{2,1,0:T(4,128)S(1)}, u32[]{:S(2)}, u32[]{:S(2)}) collective-permute-start(f32[24,4,128]{2,1,0:T(4,128)S(1)} %pad_maximum_fusion.1), channel_id=1, source_target_pairs={{1,0},{2,1},{3,2},{5,4},{6,5},{7,6},{9,8},{10,9},{11,10},{13,12},{... | collective-permute-start | bytes 147464 | tf_op jit(solution)/shard_map/ppermute | solution.py:48
  90.0 1.4 copy-start.3
  96.0 43.0 %all-to-all-start.1 = ((f32[32,96,128]{2,1,0:T(8,128)}), f32[32,96,128]{2,1,0:T(8,128)S(1)}, u32[]{:S(2)}, u32[]{:S(2)}) async-start(f32[32,96,128]{2,1,0:T(8,128)} %bitcast.6), calls=%async_computation.1 | async-start | bytes 3145728 | tf_op jit(solution)/shard_map/all_to_all | solution.py:655
  103.7 0.9 copy-start.1

commit v7 on v6

--- a/solution.py
+++ b/solution.py
@@ -59,6 +59,10 @@
 
 def far(value):
     return pltpu.with_memory_space_constraint(value, pltpu.HBM)
+
+
+def near(value):
+    return pltpu.with_memory_space_constraint(value, pltpu.VMEM)
 
 
 def rank_kernel(cap, owner_ref, slot_ref, dest_ref, where_ref, code_ref):
@@ -166,22 +170,28 @@
     )(where, code, far(temp), far(old), far(mask), *after)
 
 
-def heat_kernel(cap, thin, rows_ref, *refs):
-    heat_ref, first_ref, last_ref, code_ref = refs[-4:]
+def heat_kernel(cap, thin, far_ref, *refs):
+    heat_ref, first_ref, last_ref, code_ref, rows_ref, sems = refs[-6:]
     ndev, tall, row_len = rows_ref.shape
+    group = ndev // GROUPS
+    copies = []
+    for index in range(GROUPS):
+        cut = slice(index * group, (index + 1) * group)
+        copies.append(pltpu.make_async_copy(far_ref.at[cut], rows_ref.at[cut], sems.at[index]))
+        copies[-1].start()
     sx, sy, _ = heat_ref.shape
     slots = sx * sy
-    codes = rows_ref[:, cap, :].astype(jnp.int32) - 1
-    code_ref[...] = codes
-    group = ndev // 4
     names = lax.broadcasted_iota(jnp.int32, (slots, tall), 0)
     total = jnp.zeros((slots, 2 * row_len), F32)
-    for index in range(0, ndev, group):
+    for copy, index in zip(copies, range(0, ndev, group)):
+        copy.wait()
+        codes = rows_ref[index:index + group, cap, :].astype(jnp.int32) - 1
+        code_ref[index:index + group, :] = codes
         lines = rows_ref[index:index + group].reshape(group * tall, row_len)
         high, low = halves(lines)
         pick = jnp.concatenate(
             [
-                jnp.where(names == codes[index + i:index + i + 1, :tall], 1.0, 0.0)
+                jnp.where(names == codes[i:i + 1, :tall], 1.0, 0.0)
                 for i in range(group)
             ],
             axis=1,
@@ -201,7 +211,7 @@
     edge = (thin, sy, row_len)
     return pl.pallas_call(
         functools.partial(heat_kernel, cap, thin),
-        in_specs=[in_vmem] + [anywhere] * len(after),
+        in_specs=[in_hbm] + [anywhere] * len(after),
         out_specs=[in_vmem] * 4,
         out_shape=[
             jax.ShapeDtypeStruct(block, F32),
@@ -209,10 +219,14 @@
             jax.ShapeDtypeStruct(edge, F32),
             jax.ShapeDtypeStruct((ndev, row_len), jnp.int32),
         ],
+        scratch_shapes=[
+            pltpu.VMEM(incoming.shape, F32),
+            pltpu.SemaphoreType.DMA((GROUPS,)),
+        ],
         compiler_params=params(20),
         cost_estimate=cost(4 * ndev * tall * sx * sy * row_len, 4 * ndev * tall * row_len),
         name="heat_sum",
-    )(incoming, *after)
+    )(far(incoming), *after)
 
 
 def put_rim(ref, base, slabs):
@@ -311,19 +325,19 @@
     put_rim(right_ref, cx, slabs[1])
 
 
-def y_faces(rim, near, far_side, temp, kind, lo, hi):
-    cx, depth = near.shape
+def y_faces(rim, left, right, temp, kind, lo, hi):
+    cx, depth = left.shape
     sx, sy, sz = temp.shape
     long = -(-(sx + 2 * rim) // PART) * PART
     height = cx + rim_rows(2 * rim * (long // PART), depth)
-    args = (near, far_side, far(temp), far(kind), lo, hi)
+    args = (left, right, far(temp), far(kind), lo, hi)
     return pl.pallas_call(
         functools.partial(y_faces_kernel, rim),
         grid=(1,),
         in_specs=[whole(x.shape) for x in args],
         out_specs=[whole((height, depth))] * 2 + [in_vmem],
         out_shape=[jax.ShapeDtypeStruct((height, depth), F32)] * 2
-        + [jax.ShapeDtypeStruct((2, long, sy + 2 * OFF, sz), F32)],
+        + [pltpu.VMEM((2, long, sy + 2 * OFF, sz), F32)],
         compiler_params=params(16),
         cost_estimate=cost(1000, 4 * 4 * height * depth),
         name="y_faces",
@@ -435,7 +449,7 @@
         compiler_params=params(24),
         cost_estimate=cost(4 * total * sx * sy * sz, 4 * total * sz),
         name="solid_steps",
-    )(state, *state_rim, heat, *heat_rim, code)
+    )(near(state), *state_rim, heat, *heat_rim, code)
 
 
 def stress_kernel(sigma_ref, out_ref, tick_ref):
@@ -633,9 +647,10 @@
 
     first, last, left, right = x_faces(rim, temp_fluid, temp_solid, material)
     faces = (*neighbours(last, first, "gx"), *neighbours(right, left, "gy"))
+    dest, where, codes = rank(owner_map.reshape(1, rows), slot_map, ndev, cap)
+    outgoing, flux = pack(where, codes, temp_fluid, wall_old, wall_mask, cap, (first, last))
+    outgoing, *faces = lax.optimization_barrier((outgoing, *faces))
     xlo, xhi = faces[:2]
-    dest, where, codes = rank(owner_map.reshape(1, rows), slot_map, ndev, cap)
-    outgoing, flux = pack(where, codes, temp_fluid, wall_old, wall_mask, cap, faces)
     incoming = lax.all_to_all(outgoing, AXES, split_axis=0, concat_axis=0, tiled=True)
 
     fluid, *edges = fluid_step(temp_fluid, faces, velocity, flux, ())

time: 143 us -> 139 us (0.972)
  waiting for transfers between devices: 53.3 us -> 49.6 us
    ppermute x12, waiting for transfers between devices: 28.2 us -> 24.4 us  [neighbours(): return (lax.ppermute(before, axis, up), lax.ppermute(after, axis, down))]
  transfers between devices with their start and end apart: 14 -> 14, of which waited for: 8 -> 8; matrix products, arithmetic and copies ran while one was open for 0% -> 0% of each run, Pallas kernels for 20% -> 23%
where the time goes in v7:
time: 139 us; the launch traced here: 138 us
  waiting for transfers between devices  49.6 us (36%)
  Pallas kernels  45.1 us (32%)
  starting transfers between devices  39.1 us (28%)
  local copies, waits for them, and re-layouts  3.54 us (3%)
    ppermute x12, starting transfers between devices, neighbours(): return (lax.ppermute(before, axis, up), lax.ppermute(after, axis, down))  26.6 us
    ppermute x12, waiting for transfers between devices, neighbours(): return (lax.ppermute(before, axis, up), lax.ppermute(after, axis, down))  24.4 us
    pallas_call x2, Pallas kernels, fluid_step(): pl.pallas_call(fluid_kernel, grid=(steps + 1,), in_specs=[pl.BlockSpec(pl...  23.5 us
    all_to_all x1, waiting for transfers between devices, body(): lax.all_to_all(replies.reshape(ndev, cap, sz), AXES, split_axis=0, concat...  22.5 us
    all_to_all x1, starting transfers between devices, body(): lax.all_to_all(outgoing, AXES, split_axis=0, concat_axis=0, tiled=True)  7.01 us
    all_to_all x1, starting transfers between devices, body(): lax.all_to_all(replies.reshape(ndev, cap, sz), AXES, split_axis=0, concat...  5.54 us
    pallas_call x1, Pallas kernels, solid_steps(): pl.pallas_call(functools.partial(solid_kernel, rim, cap), in_specs=[in_vm...  4.58 us
    pallas_call x1, Pallas kernels, pack(): pl.pallas_call(functools.partial(pack_kernel, cap), grid=(1,), in_specs=[...  4.4 us
  transfers between devices with their start and end apart: 14, of which 8 were waited for; matrix products, arithmetic and copies ran while one was open for 0% of the time, Pallas kernels for 23%

profile of v7, /device:TPU:0, one launch (start us, length us, event | category | flops | bytes accessed | tf_op | source)
XLA Modules:
  0.0 138.2 jit_solution(16199277387443084329)
XLA Ops:
  0.6 0.0 copy-start.5
  0.6 0.0 copy-start.4
  0.7 1.6 %x_faces.1 = (f32[112,1024]{1,0:T(8,128)S(1)}, f32[112,1024]{1,0:T(8,128)S(1)}, f32[16,1024]{1,0:T(8,128)S(1)}, f32[16,1024]{1,0:T(8,128)S(1)}) custom-call(f32[16,64,1024]{2,1,0:T(8,128)} %here_ref.1, f32[16,64,1024]{2,1,0:T(8,128)} %here_ref.1, f32[16,64,1024]{2,1,0:T(8,128)} %here_ref.1, f32[16,64,1024]{2,1,0:T(8,128)} %here_ref.1, ...), custom_call_target="tpu_custom_call" | custom-call | flops 1000 | bytes 1835008 | tf_op jit(solution)/shard_map/x_faces/pallas_call | solution.py:276
  2.3 1.3 collective-permute-start.1
  3.6 3.1 %collective-permute-start = (f32[112,1024]{1,0:T(8,128)S(1)}, f32[112,1024]{1,0:T(8,128)S(1)}, u32[]{:S(2)}, u32[]{:S(2)}) collective-permute-start(f32[112,1024]{1,0:T(8,128)S(1)} %get-tuple-element.41.refs_1_), channel_id=1, source_target_pairs={{0,4},{4,8},{8,12},{12,16},{16,20},{20,24},{24,28},{1,5},{5,9},{9,... | collective-permute-start | bytes 1376264 | tf_op jit(solution)/shard_map/ppermute | solution.py:48
  6.6 4.8 %collective-permute-start.2 = (f32[16,1024]{1,0:T(8,128)S(1)}, f32[16,1024]{1,0:T(8,128)S(1)}, u32[]{:S(2)}, u32[]{:S(2)}) collective-permute-start(f32[16,1024]{1,0:T(8,128)S(1)} %get-tuple-element.43), channel_id=1, source_target_pairs={{0,1},{1,2},{2,3},{4,5},{5,6},{6,7},{8,9},{9,10},{10,11},{12,13},{... | collective-permute-start | bytes 196616 | tf_op jit(solution)/shard_map/ppermute | solution.py:48
  11.5 1.3 collective-permute-start.3
  12.8 0.0 copy-done.5
  12.8 0.0 copy-done.4
  12.8 0.9 rank.1
  13.7 4.4 %pack.1 = (f32[32,104,128]{2,1,0:T(8,128)}, f32[16,64,128]{2,1,0:T(8,128)S(1)}) custom-call(s32[1,1024]{1,0:T(1,128)S(1)} %get-tuple-element.38.where_ref, f32[32,128]{1,0:T(8,128)S(1)} %get-tuple-element.39.code_ref, f32[16,64,1024]{2,1,0:T(8,128)} %here_ref.1, f32[16,64,128]{2,1,0:T(8,128)} %old_ref.1, s32[16,64,128]{2,1,0:T(8,128)} %mask_ref.1, ...), custom_call_target="tpu_custom_call" | custom-call | flops 1744830464 | bytes 2621440 | tf_op jit(solution)/shard_map/pack/pallas_call | solution.py:151
  18.1 0.0 collective-permute-done.2.ylo_ref
  18.1 0.1 collective-permute-done.3.yhi_ref
  18.3 0.0 collective-permute-done.1.xhi_ref.hi_ref
  18.3 0.0 collective-permute-done.xlo_ref.lo_ref
  18.3 7.0 %all-to-all-start = ((f32[32,104,128]{2,1,0:T(8,128)}), f32[32,104,128]{2,1,0:T(8,128)}, u32[]{:S(2)}, u32[]{:S(2)}) async-start(f32[32,104,128]{2,1,0:T(8,128)} %get-tuple-element.58), calls=%async_computation | async-start | bytes 3407872 | tf_op jit(solution)/shard_map/all_to_all | solution.py:654
  25.3 11.7 %fluid_step.2 = (f32[16,64,1024]{2,1,0:T(8,128)}, f32[64,1024]{1,0:T(8,128)S(1)}, f32[64,1024]{1,0:T(8,128)S(1)}, f32[16,1024]{1,0:T(8,128)S(1)}, f32[16,1024]{1,0:T(8,128)S(1)}) custom-call(f32[16,64,1024]{2,1,0:T(8,128)} %here_ref.1, f32[112,1024]{1,0:T(8,128)S(1)} %collective-permute-done.xlo_ref.lo_ref, ...), custom_call_target="tpu_custom_call" | custom-call | flops 41943040 | bytes 14680064 | tf_op jit(solution)/shard_map/fluid_step/pallas_call | solution.py:609
  37.0 2.1 %collective-permute-start.4 = (f32[64,1024]{1,0:T(8,128)S(1)}, f32[64,1024]{1,0:T(8,128)S(1)}, u32[]{:S(2)}, u32[]{:S(2)}) collective-permute-start(f32[64,1024]{1,0:T(8,128)S(1)} %get-tuple-element.51), channel_id=1, source_target_pairs={{0,4},{4,8},{8,12},{12,16},{16,20},{20,24},{24,28},{1,5},{5,9},{9,... | collective-permute-start | bytes 786440 | tf_op jit(solution)/shard_map/ppermute | solution.py:48
  39.1 1.3 collective-permute-start.5
  40.4 1.3 y_faces.1
  41.7 0.0 copy-start.2
  41.7 1.1 copy-done.2
  42.9 3.6 %collective-permute-start.6 = (f32[64,1024]{1,0:T(8,128)S(1)}, f32[64,1024]{1,0:T(8,128)S(1)}, u32[]{:S(2)}, u32[]{:S(2)}) collective-permute-start(f32[64,1024]{1,0:T(8,128)S(1)} %get-tuple-element.55), channel_id=1, source_target_pairs={{0,1},{1,2},{2,3},{4,5},{5,6},{6,7},{8,9},{9,10},{10,11},{12,13},{... | collective-permute-start | bytes 786440 | tf_op jit(solution)/shard_map/ppermute | solution.py:48
  46.4 1.3 collective-permute-start.7
  47.7 0.0 collective-permute-done.4.refs_0_.xlo_ref
  47.7 0.0 collective-permute-done.5.refs_1_.xhi_ref
  47.8 5.8 %collective-permute-done.6.refs_2_.ylo_ref = f32[64,1024]{1,0:T(8,128)S(1)} collective-permute-done((f32[64,1024]{1,0:T(8,128)S(1)}, f32[64,1024]{1,0:T(8,128)S(1)}, u32[]{:S(2)}, u32[]{:S(2)}) %collective-permute-start.6) | collective-permute-done | bytes 262176 | tf_op jit(solution)/shard_map/ppermute | solution.py:48
  53.5 9.4 %collective-permute-done.7.refs_3_.yhi_ref = f32[64,1024]{1,0:T(8,128)S(1)} collective-permute-done((f32[64,1024]{1,0:T(8,128)S(1)}, f32[64,1024]{1,0:T(8,128)S(1)}, u32[]{:S(2)}, u32[]{:S(2)}) %collective-permute-start.7) | collective-permute-done | bytes 262176 | tf_op jit(solution)/shard_map/ppermute | solution.py:48
  62.9 0.0 copy-start
  62.9 2.6 %all-to-all-done.far_ref = f32[32,104,128]{2,1,0:T(8,128)} async-done(((f32[32,104,128]{2,1,0:T(8,128)}), f32[32,104,128]{2,1,0:T(8,128)}, u32[]{:S(2)}, u32[]{:S(2)}) %all-to-all-start) | async-done | bytes 1703968 | tf_op jit(solution)/shard_map/all_to_all | solution.py:654
  65.6 4.2 %heat_sum.1 = (f32[16,32,128]{2,1,0:T(8,128)S(1)}, f32[4,32,128]{2,1,0:T(8,128)S(1)}, f32[4,32,128]{2,1,0:T(8,128)S(1)}, s32[32,128]{1,0:T(8,128)S(1)}) custom-call(f32[32,104,128]{2,1,0:T(8,128)} %all-to-all-done.far_ref, f32[64,1024]{1,0:T(8,128)S(1)} %collective-permute-done.4.refs_0_.xlo_ref, f32[64,1024]{1,0:T(8,128)S(1)} %collective-permute-done.5.refs_1_.xhi_ref, ...), custom_call_target="tpu_custom_call" | custom-call | flops 872415232 | bytes 1703936 | tf_op jit(solution)/shard_map/heat_sum/pallas_call | solution.py:212
  69.8 1.5 %collective-permute-start.8 = (f32[4,32,128]{2,1,0:T(8,128)S(1)}, f32[4,32,128]{2,1,0:T(8,128)S(1)}, u32[]{:S(2)}, u32[]{:S(2)}) collective-permute-start(f32[4,32,128]{2,1,0:T(8,128)S(1)} %get-tuple-element.60), channel_id=1, source_target_pairs={{0,4},{4,8},{8,12},{12,16},{16,20},{20,24},{24,28},{1,5},{5,9},{9,... | collective-permute-start | bytes 196616 | tf_op jit(solution)/shard_map/ppermute | solution.py:48
  71.4 1.3 collective-permute-start.9
  72.7 0.0 collective-permute-done.8.hxlo_ref
  72.7 4.4 %collective-permute-done.9.hxhi_ref = f32[4,32,128]{2,1,0:T(8,128)S(1)} collective-permute-done((f32[4,32,128]{2,1,0:T(8,128)S(1)}, f32[4,32,128]{2,1,0:T(8,128)S(1)}, u32[]{:S(2)}, u32[]{:S(2)}) %collective-permute-start.9) | collective-permute-done | bytes 65568 | tf_op jit(solution)/shard_map/ppermute | solution.py:48
  77.1 3.7 %collective-permute-start.10 = (f32[24,4,128]{2,1,0:T(4,128)S(1)}, f32[24,4,128]{2,1,0:T(4,128)S(1)}, u32[]{:S(2)}, u32[]{:S(2)}) collective-permute-start(f32[24,4,128]{2,1,0:T(4,128)S(1)} %pad_maximum_fusion), channel_id=1, source_target_pairs={{0,1},{1,2},{2,3},{4,5},{5,6},{6,7},{8,9},{9,10},{10,11},{12,13},{... | collective-permute-start | bytes 147464 | tf_op jit(solution)/shard_map/ppermute | solution.py:48
  80.8 1.3 collective-permute-start.11
  82.1 0.4 collective-permute-done.10.hylo_ref
  82.5 4.3 %collective-permute-done.11.hyhi_ref = f32[24,4,128]{2,1,0:T(4,128)S(1)} collective-permute-done((f32[24,4,128]{2,1,0:T(4,128)S(1)}, f32[24,4,128]{2,1,0:T(4,128)S(1)}, u32[]{:S(2)}, u32[]{:S(2)}) %collective-permute-start.11) | collective-permute-done | bytes 49184 | tf_op jit(solution)/shard_map/ppermute | solution.py:48
  86.8 0.0 copy-done
  86.8 0.0 copy-start.3
  86.8 1.4 %copy-done.3 = f32[2,32,48,128]{3,2,1,0:T(8,128)S(1)} copy-done((f32[2,32,48,128]{3,2,1,0:T(8,128)S(1)}, f32[2,32,48,128]{3,2,1,0:T(8,128)}, u32[]{:S(2)}) %copy-start.3) | copy-done | bytes 1572888
  88.2 4.6 %solid_steps.1 = (f32[16,32,128]{2,1,0:T(8,128)}, f32[18,48,128]{2,1,0:T(8,128)S(1)}, f32[3072,128]{1,0:T(8,128)}) custom-call(f32[2,32,48,128]{3,2,1,0:T(8,128)S(1)} %copy-done.3, f32[64,1024]{1,0:T(8,128)S(1)} %collective-permute-done.6.refs_2_.ylo_ref, f32[64,1024]{1,0:T(8,128)S(1)} %collective-permute-done.7.refs_3_.yhi_ref, ...), custom_call_target="tpu_custom_call" | custom-call | flops 805306368 | bytes 1572864 | tf_op jit(solution)/shard_map/solid_steps/pallas_call | solution.py:433
  92.8 5.5 %all-to-all-start.1 = ((f32[32,96,128]{2,1,0:T(8,128)}), f32[32,96,128]{2,1,0:T(8,128)S(1)}, u32[]{:S(2)}, u32[]{:S(2)}) async-start(f32[32,96,128]{2,1,0:T(8,128)} %bitcast.6), calls=%async_computation.1 | async-start | bytes 3145728 | tf_op jit(solution)/shard_map/all_to_all | solution.py:670
  98.4 2.1 %stress.1 = (f32[3,16,32,128]{3,2,1,0:T(8,128)}, f32[8,128]{1,0:T(8,128)S(1)}) custom-call(f32[18,48,128]{2,1,0:T(8,128)S(1)} %get-tuple-element.63.sigma_ref), custom_call_target="tpu_custom_call" | custom-call | flops 655360 | bytes 1048576 | tf_op jit(solution)/shard_map/stress/pallas_call | solution.py:478
  100.5 0.0 copy-start.1
  100.5 0.9 copy-done.1
  101.4 11.8 %fluid_step.3 = (f32[16,64,1024]{2,1,0:T(8,128)}, f32[64,1024]{1,0:T(8,128)}, f32[64,1024]{1,0:T(8,128)}, f32[16,1024]{1,0:T(8,128)S(1)}, f32[16,1024]{1,0:T(8,128)S(1)}) custom-call(f32[16,64,1024]{2,1,0:T(8,128)} %get-tuple-element.50.here_ref, f32[64,1024]{1,0:T(8,128)S(1)} %collective-permute-done.4.refs_0_.xlo_ref, ...), custom_call_target="tpu_custom_call" | custom-call | flops 41943040 | bytes 14680064 | tf_op jit(solution)/shard_map/fluid_step/pallas_call | solution.py:609
  113.3 22.5 %all-to-all-done.1 = f32[32,96,128]{2,1,0:T(8,128)S(1)} async-done(((f32[32,96,128]{2,1,0:T(8,128)}), f32[32,96,128]{2,1,0:T(8,128)S(1)}, u32[]{:S(2)}, u32[]{:S(2)}) %all-to-all-start.1) | async-done | bytes 1572896 | tf_op jit(solution)/shard_map/all_to_all | solution.py:670
  135.8 2.4 %unpack.1 = f32[1024,128]{1,0:T(8,128)} custom-call(s32[1,1024]{1,0:T(1,128)S(1)} %get-tuple-element.66.dest_ref, f32[3072,128]{1,0:T(8,128)S(1)} %bitcast.4, f32[16,1024]{1,0:T(8,128)S(1)} %get-tuple-element.68.refs_0_, f32[16,1024]{1,0:T(8,128)S(1)} %get-tuple-element.69.refs_1_), custom_call_target="tpu_custom_call" | custom-call | flops 131072 | bytes 1048576 | tf_op jit(solution)/shard_map/unpack/pallas_call | solution.py:506
  (5 shorter events, 0.1 us)
Async XLA Ops:
  0.6 12.1 %copy-start.5 = (s32[1,1024]{1,0:T(1,128)S(1)}, s32[1,1024]{1,0:T(1,128)}, u32[]{:S(2)}) copy-start(s32[1,1024]{1,0:T(1,128)} %slot_ref.1) | copy-start | bytes 12292
  0.6 12.1 %copy-start.4 = (s32[1,1024,1]{1,2,0:T(1,128)S(1)}, s32[1,1024,1]{1,2,0:T(1,128)}, u32[]{:S(2)}) copy-start(s32[1,1024,1]{1,2,0:T(1,128)} %param.12) | copy-start | bytes 12292
  2.3 16.0 %collective-permute-start.1 = (f32[112,1024]{1,0:T(8,128)S(1)}, f32[112,1024]{1,0:T(8,128)S(1)}, u32[]{:S(2)}, u32[]{:S(2)}) collective-permute-start(f32[112,1024]{1,0:T(8,128)S(1)} %get-tuple-element.40.refs_0_), channel_id=1, source_target_pairs={{4,0},{8,4},{12,8},{16,12},{20,16},{24,20},{28,24},{5,1},{9,5},{13... | collective-permute-start | bytes 1376264 | tf_op jit(solution)/shard_map/ppermute | solution.py:48
  3.6 14.7 %collective-permute-start = (f32[112,1024]{1,0:T(8,128)S(1)}, f32[112,1024]{1,0:T(8,128)S(1)}, u32[]{:S(2)}, u32[]{:S(2)}) collective-permute-start(f32[112,1024]{1,0:T(8,128)S(1)} %get-tuple-element.41.refs_1_), channel_id=1, source_target_pairs={{0,4},{4,8},{8,12},{12,16},{16,20},{20,24},{24,28},{1,5},{5,9},{9,... | collective-permute-start | bytes 1376264 | tf_op jit(solution)/shard_map/ppermute | solution.py:48
  6.6 11.5 %collective-permute-start.2 = (f32[16,1024]{1,0:T(8,128)S(1)}, f32[16,1024]{1,0:T(8,128)S(1)}, u32[]{:S(2)}, u32[]{:S(2)}) collective-permute-start(f32[16,1024]{1,0:T(8,128)S(1)} %get-tuple-element.43), channel_id=1, source_target_pairs={{0,1},{1,2},{2,3},{4,5},{5,6},{6,7},{8,9},{9,10},{10,11},{12,13},{... | collective-permute-start | bytes 196616 | tf_op jit(solution)/shard_map/ppermute | solution.py:48
  11.5 6.8 %collective-permute-start.3 = (f32[16,1024]{1,0:T(8,128)S(1)}, f32[16,1024]{1,0:T(8,128)S(1)}, u32[]{:S(2)}, u32[]{:S(2)}) collective-permute-start(f32[16,1024]{1,0:T(8,128)S(1)} %get-tuple-element.44), channel_id=1, source_target_pairs={{1,0},{2,1},{3,2},{5,4},{6,5},{7,6},{9,8},{10,9},{11,10},{13,12},{... | collective-permute-start | bytes 196616 | tf_op jit(solution)/shard_map/ppermute | solution.py:48
  18.3 47.3 %all-to-all-start = ((f32[32,104,128]{2,1,0:T(8,128)}), f32[32,104,128]{2,1,0:T(8,128)}, u32[]{:S(2)}, u32[]{:S(2)}) async-start(f32[32,104,128]{2,1,0:T(8,128)} %get-tuple-element.58), calls=%async_computation | async-start | bytes 3407872 | tf_op jit(solution)/shard_map/all_to_all | solution.py:654
  37.0 10.8 %collective-permute-start.4 = (f32[64,1024]{1,0:T(8,128)S(1)}, f32[64,1024]{1,0:T(8,128)S(1)}, u32[]{:S(2)}, u32[]{:S(2)}) collective-permute-start(f32[64,1024]{1,0:T(8,128)S(1)} %get-tuple-element.51), channel_id=1, source_target_pairs={{0,4},{4,8},{8,12},{12,16},{16,20},{20,24},{24,28},{1,5},{5,9},{9,... | collective-permute-start | bytes 786440 | tf_op jit(solution)/shard_map/ppermute | solution.py:48
  39.1 8.7 %collective-permute-start.5 = (f32[64,1024]{1,0:T(8,128)S(1)}, f32[64,1024]{1,0:T(8,128)S(1)}, u32[]{:S(2)}, u32[]{:S(2)}) collective-permute-start(f32[64,1024]{1,0:T(8,128)S(1)} %get-tuple-element.52), channel_id=1, source_target_pairs={{4,0},{8,4},{12,8},{16,12},{20,16},{24,20},{28,24},{5,1},{9,5},{13... | collective-permute-start | bytes 786440 | tf_op jit(solution)/shard_map/ppermute | solution.py:48
  41.7 1.2 copy-start.2
  42.9 10.7 %collective-permute-start.6 = (f32[64,1024]{1,0:T(8,128)S(1)}, f32[64,1024]{1,0:T(8,128)S(1)}, u32[]{:S(2)}, u32[]{:S(2)}) collective-permute-start(f32[64,1024]{1,0:T(8,128)S(1)} %get-tuple-element.55), channel_id=1, source_target_pairs={{0,1},{1,2},{2,3},{4,5},{5,6},{6,7},{8,9},{9,10},{10,11},{12,13},{... | collective-permute-start | bytes 786440 | tf_op jit(solution)/shard_map/ppermute | solution.py:48
  46.4 16.5 %collective-permute-start.7 = (f32[64,1024]{1,0:T(8,128)S(1)}, f32[64,1024]{1,0:T(8,128)S(1)}, u32[]{:S(2)}, u32[]{:S(2)}) collective-permute-start(f32[64,1024]{1,0:T(8,128)S(1)} %get-tuple-element.56), channel_id=1, source_target_pairs={{1,0},{2,1},{3,2},{5,4},{6,5},{7,6},{9,8},{10,9},{11,10},{13,12},{... | collective-permute-start | bytes 786440 | tf_op jit(solution)/shard_map/ppermute | solution.py:48
  62.9 23.9 %copy-start = (f32[64,1024]{1,0:T(8,128)}, f32[64,1024]{1,0:T(8,128)S(1)}, u32[]{:S(2)}) copy-start(f32[64,1024]{1,0:T(8,128)S(1)} %collective-permute-done.7.refs_3_.yhi_ref) | copy-start | bytes 786436
  69.8 2.9 %collective-permute-start.8 = (f32[4,32,128]{2,1,0:T(8,128)S(1)}, f32[4,32,128]{2,1,0:T(8,128)S(1)}, u32[]{:S(2)}, u32[]{:S(2)}) collective-permute-start(f32[4,32,128]{2,1,0:T(8,128)S(1)} %get-tuple-element.60), channel_id=1, source_target_pairs={{0,4},{4,8},{8,12},{12,16},{16,20},{20,24},{24,28},{1,5},{5,9},{9,... | collective-permute-start | bytes 196616 | tf_op jit(solution)/shard_map/ppermute | solution.py:48
  71.4 5.7 %collective-permute-start.9 = (f32[4,32,128]{2,1,0:T(8,128)S(1)}, f32[4,32,128]{2,1,0:T(8,128)S(1)}, u32[]{:S(2)}, u32[]{:S(2)}) collective-permute-start(f32[4,32,128]{2,1,0:T(8,128)S(1)} %get-tuple-element.61), channel_id=1, source_target_pairs={{4,0},{8,4},{12,8},{16,12},{20,16},{24,20},{28,24},{5,1},{9,5},{13... | collective-permute-start | bytes 196616 | tf_op jit(solution)/shard_map/ppermute | solution.py:48
  77.1 5.5 %collective-permute-start.10 = (f32[24,4,128]{2,1,0:T(4,128)S(1)}, f32[24,4,128]{2,1,0:T(4,128)S(1)}, u32[]{:S(2)}, u32[]{:S(2)}) collective-permute-start(f32[24,4,128]{2,1,0:T(4,128)S(1)} %pad_maximum_fusion), channel_id=1, source_target_pairs={{0,1},{1,2},{2,3},{4,5},{5,6},{6,7},{8,9},{9,10},{10,11},{12,13},{... | collective-permute-start | bytes 147464 | tf_op jit(solution)/shard_map/ppermute | solution.py:48
  80.8 6.0 %collective-permute-start.11 = (f32[24,4,128]{2,1,0:T(4,128)S(1)}, f32[24,4,128]{2,1,0:T(4,128)S(1)}, u32[]{:S(2)}, u32[]{:S(2)}) collective-permute-start(f32[24,4,128]{2,1,0:T(4,128)S(1)} %pad_maximum_fusion.1), channel_id=1, source_target_pairs={{1,0},{2,1},{3,2},{5,4},{6,5},{7,6},{9,8},{10,9},{11,10},{13,12},{... | collective-permute-start | bytes 147464 | tf_op jit(solution)/shard_map/ppermute | solution.py:48
  86.8 1.4 %copy-start.3 = (f32[2,32,48,128]{3,2,1,0:T(8,128)S(1)}, f32[2,32,48,128]{3,2,1,0:T(8,128)}, u32[]{:S(2)}) copy-start(f32[2,32,48,128]{3,2,1,0:T(8,128)} %copy-done.2) | copy-start | bytes 4718596
  92.8 43.0 %all-to-all-start.1 = ((f32[32,96,128]{2,1,0:T(8,128)}), f32[32,96,128]{2,1,0:T(8,128)S(1)}, u32[]{:S(2)}, u32[]{:S(2)}) async-start(f32[32,96,128]{2,1,0:T(8,128)} %bitcast.6), calls=%async_computation.1 | async-start | bytes 3145728 | tf_op jit(solution)/shard_map/all_to_all | solution.py:670
  100.5 0.9 copy-start.1

commit v8 on v6

--- a/solution.py
+++ b/solution.py
@@ -59,6 +59,10 @@
 
 def far(value):
     return pltpu.with_memory_space_constraint(value, pltpu.HBM)
+
+
+def near(value):
+    return pltpu.with_memory_space_constraint(value, pltpu.VMEM)
 
 
 def rank_kernel(cap, owner_ref, slot_ref, dest_ref, where_ref, code_ref):
@@ -166,14 +170,25 @@
     )(where, code, far(temp), far(old), far(mask), *after)
 
 
-def heat_kernel(cap, thin, rows_ref, *refs):
-    heat_ref, first_ref, last_ref, code_ref = refs[-4:]
+def heat_kernel(cap, thin, rows_ref, xfirst_ref, xlast_ref, ylo_ref, yhi_ref,
+                yfirst_ref, ylast_ref, clo_ref, chi_ref,
+                heat_ref, low_ref, high_ref, left_ref, right_ref, code_ref):
     ndev, tall, row_len = rows_ref.shape
+    cx, depth = yfirst_ref.shape
     sx, sy, _ = heat_ref.shape
     slots = sx * sy
+    left = yfirst_ref[...] + clo_ref[...] * ylo_ref[:cx, :]
+    right = ylast_ref[...] + chi_ref[...] * yhi_ref[:cx, :]
+    left_ref[...] = left
+    right_ref[...] = right
+    edge = thin * sy
+    for ref, x in ((low_ref, 0), (high_ref, cx - 1)):
+        for at, line in ((edge, left[x:x + 1]), (edge + depth // LANE, right[x:x + 1])):
+            for i in range(depth // LANE):
+                ref[at + i:at + i + 1, :] = line[:, i * LANE:(i + 1) * LANE]
     codes = rows_ref[:, cap, :].astype(jnp.int32) - 1
     code_ref[...] = codes
-    group = ndev // 4
+    group = ndev // GROUPS
     names = lax.broadcasted_iota(jnp.int32, (slots, tall), 0)
     total = jnp.zeros((slots, 2 * row_len), F32)
     for index in range(0, ndev, group):
@@ -189,30 +204,33 @@
         total = total + jnp.dot(
             pick, jnp.concatenate([high, low], axis=1), preferred_element_type=F32
         )
-    heat = (total[:, :row_len] + total[:, row_len:]).reshape(sx, sy, row_len)
-    heat_ref[...] = heat
-    first_ref[...] = heat[:thin]
-    last_ref[...] = heat[sx - thin:]
-
-
-def heat_sum(incoming, cap, block, thin, after):
+    heat = total[:, :row_len] + total[:, row_len:]
+    heat_ref[...] = heat.reshape(sx, sy, row_len)
+    low_ref[:edge, :] = heat[:edge]
+    high_ref[:edge, :] = heat[slots - edge:]
+
+
+def heat_sum(incoming, cap, block, thin, faces, edges):
     ndev, tall, row_len = incoming.shape
     sx, sy, _ = block
-    edge = (thin, sy, row_len)
+    line = edges[2].shape
+    edge = (thin * sy + 2 * (line[1] // LANE), row_len)
     return pl.pallas_call(
         functools.partial(heat_kernel, cap, thin),
-        in_specs=[in_vmem] + [anywhere] * len(after),
-        out_specs=[in_vmem] * 4,
+        in_specs=[in_vmem] + [anywhere] * 2 + [in_vmem] * 6,
+        out_specs=[in_vmem] * 6,
         out_shape=[
             jax.ShapeDtypeStruct(block, F32),
             jax.ShapeDtypeStruct(edge, F32),
             jax.ShapeDtypeStruct(edge, F32),
+            jax.ShapeDtypeStruct(line, F32),
+            jax.ShapeDtypeStruct(line, F32),
             jax.ShapeDtypeStruct((ndev, row_len), jnp.int32),
         ],
         compiler_params=params(20),
         cost_estimate=cost(4 * ndev * tall * sx * sy * row_len, 4 * ndev * tall * row_len),
         name="heat_sum",
-    )(incoming, *after)
+    )(near(incoming), *faces, *edges)
 
 
 def put_rim(ref, base, slabs):
@@ -311,23 +329,59 @@
     put_rim(right_ref, cx, slabs[1])
 
 
-def y_faces(rim, near, far_side, temp, kind, lo, hi):
-    cx, depth = near.shape
+def y_faces(rim, left, right, temp, kind, lo, hi):
+    cx, depth = left.shape
     sx, sy, sz = temp.shape
     long = -(-(sx + 2 * rim) // PART) * PART
     height = cx + rim_rows(2 * rim * (long // PART), depth)
-    args = (near, far_side, far(temp), far(kind), lo, hi)
+    args = (left, right, far(temp), far(kind), lo, hi)
     return pl.pallas_call(
         functools.partial(y_faces_kernel, rim),
         grid=(1,),
         in_specs=[whole(x.shape) for x in args],
-        out_specs=[whole((height, depth))] * 2 + [in_vmem],
+        out_specs=[whole((height, depth))] * 2 + [whole((2, long, sy + 2 * OFF, sz))],
         out_shape=[jax.ShapeDtypeStruct((height, depth), F32)] * 2
-        + [jax.ShapeDtypeStruct((2, long, sy + 2 * OFF, sz), F32)],
+        + [pltpu.HBM((2, long, sy + 2 * OFF, sz), F32)],
         compiler_params=params(16),
         cost_estimate=cost(1000, 4 * 4 * height * depth),
         name="y_faces",
     )(*args)
+
+
+def strips_kernel(thin, heat_ref, lo_ref, hi_ref, near_ref, away_ref,
+                  left_ref, right_ref, work_ref):
+    cx = near_ref.shape[0]
+    sx, sy, sz = heat_ref.shape
+    edge = thin * sy
+    left_ref[:cx, :] = near_ref[...]
+    right_ref[:cx, :] = away_ref[...]
+    work_ref[...] = jnp.zeros_like(work_ref)
+    work_ref[:thin] = lo_ref[:edge, :].reshape(thin, sy, sz)
+    work_ref[thin:thin + sx] = heat_ref[...]
+    work_ref[thin + sx:2 * thin + sx] = hi_ref[:edge, :].reshape(thin, sy, sz)
+    long = work_ref.shape[0]
+    for ref, start in ((left_ref, 0), (right_ref, sy - thin)):
+        slabs = [
+            work_ref[h:h + PART, start + k, :] for k in range(thin) for h in range(0, long, PART)
+        ]
+        put_rim(ref, cx, slabs)
+
+
+def strips(thin, heat, lo, hi, left, right):
+    cx, depth = left.shape
+    sx, sy, sz = heat.shape
+    long = -(-(sx + 2 * thin) // PART) * PART
+    height = cx + rim_rows(thin * (long // PART), depth)
+    return pl.pallas_call(
+        functools.partial(strips_kernel, thin),
+        in_specs=[in_vmem] * 5,
+        out_specs=[in_vmem] * 2,
+        out_shape=[jax.ShapeDtypeStruct((height, depth), F32)] * 2,
+        scratch_shapes=[pltpu.VMEM((long, sy, sz), F32)],
+        compiler_params=params(8),
+        cost_estimate=cost(1000, 16 * height * depth),
+        name="strips",
+    )(heat, lo, hi, left, right)
 
 
 def table(kind, values):
@@ -340,28 +394,45 @@
 def solid_kernel(rim, cap, state_ref, ylo_ref, yhi_ref,
                  heat_ref, hxlo_ref, hxhi_ref, hylo_ref, hyhi_ref, code_ref,
                  next_ref, sigma_ref, reply_ref, work_ref, src_ref, rhs_ref,
-                 stage_ref, sems):
+                 pick_ref, stage_ref, load, sems):
     sx, sy, sz = heat_ref.shape
+    ndev = code_ref.shape[0]
+    slots = sx * sy
     wide = sx + 2 * rim
     thin = rim - 1
     long = state_ref.shape[1]
     pieces = long // PART
+    loading = pltpu.make_async_copy(state_ref, work_ref.at[:2], load)
+    loading.start()
+    turned = jnp.transpose(code_ref[...])
+    names = lax.broadcasted_iota(jnp.int32, (cap, slots), 1)
+    for source in range(ndev):
+        pick_ref[source * cap:(source + 1) * cap, :] = ones_where(
+            names == turned[:cap, source:source + 1]
+        )
+    edge = thin * sy
+    src_ref[rim:rim + sx, OFF:OFF + sy, :] = heat_ref[...]
+    src_ref[1:rim, OFF:OFF + sy, :] = hxlo_ref[:edge, :].reshape(thin, sy, sz)
+    src_ref[rim + sx:wide - 1, OFF:OFF + sy, :] = hxhi_ref[:edge, :].reshape(thin, sy, sz)
+    parts = -(-(sx + 2 * thin) // PART)
+    base = hylo_ref.shape[0] - rim_rows(thin * parts, hylo_ref.shape[1])
+    for k in range(thin):
+        for h in range(parts):
+            n = k * parts + h
+            count = min(PART, sx + 2 * thin - h * PART)
+            cut = slice(1 + h * PART, 1 + h * PART + count)
+            src_ref[cut, OFF - thin + k, :] = get_rim(hylo_ref, base, n)[:count]
+            src_ref[cut, OFF + sy + k, :] = get_rim(hyhi_ref, base, n)[:count]
+    loading.wait()
     base = ylo_ref.shape[0] - rim_rows(2 * rim * pieces, ylo_ref.shape[1])
-    temp_ref, cond_ref = work_ref.at[0], work_ref.at[1]
-    work_ref, spare_ref = work_ref.at[2], work_ref
     for which in range(2):
-        spare_ref[which] = state_ref[which]
         for k in range(rim):
             for h in range(pieces):
                 n = (which * rim + k) * pieces + h
                 cut = slice(h * PART, (h + 1) * PART)
-                spare_ref[which, cut, OFF - rim + k, :] = get_rim(ylo_ref, base, n)
-                spare_ref[which, cut, OFF + sy + k, :] = get_rim(yhi_ref, base, n)
-    src_ref[rim:rim + sx, OFF:OFF + sy, :] = heat_ref[...]
-    src_ref[1:rim, OFF:OFF + sy, :] = hxlo_ref[...]
-    src_ref[rim + sx:wide - 1, OFF:OFF + sy, :] = hxhi_ref[...]
-    src_ref[1:wide - 1, OFF - thin:OFF, :] = hylo_ref[...]
-    src_ref[1:wide - 1, OFF + sy:OFF + sy + thin, :] = hyhi_ref[...]
+                work_ref[which, cut, OFF - rim + k, :] = get_rim(ylo_ref, base, n)
+                work_ref[which, cut, OFF + sy + k, :] = get_rim(yhi_ref, base, n)
+    temp_ref, cond_ref, work_ref = work_ref.at[0], work_ref.at[1], work_ref.at[2]
     kind = cond_ref[:wide]
     sigma_ref[...] = table(kind[rim - 1:rim + sx + 1], modulus_table)
     cond_ref[:wide] = solid_step * table(kind, conduct_table)
@@ -386,30 +457,16 @@
     high, low = halves(solid.reshape(sx * sy, sz))
     rhs_ref[:, :sz] = high
     rhs_ref[:, sz:] = low
-    slots = sx * sy
-    ndev = code_ref.shape[0]
-    turned = jnp.transpose(code_ref[...])
-    names = lax.broadcasted_iota(jnp.int32, (cap, slots), 1)
-    group = ndev // GROUPS
-    for index in range(0, ndev, group):
-        pick = jnp.concatenate(
-            [
-                ones_where(names == turned[:cap, index + i:index + i + 1])
-                for i in range(group)
-            ],
-            axis=0,
-        )
-        both = jnp.dot(pick, rhs_ref[...], preferred_element_type=F32)
-        lines = slice(index * cap, (index + group) * cap)
-        stage_ref[lines, :] = both[:, :sz] + both[:, sz:]
-        pltpu.make_async_copy(
-            stage_ref.at[lines], reply_ref.at[lines], sems.at[index // group]
-        ).start()
-    for index in range(0, ndev, group):
-        lines = slice(index * cap, (index + group) * cap)
-        pltpu.make_async_copy(
-            stage_ref.at[lines], reply_ref.at[lines], sems.at[index // group]
-        ).wait()
+    block = ndev // GROUPS * cap
+    copies = []
+    for index in range(GROUPS):
+        cut = slice(index * block, (index + 1) * block)
+        both = jnp.dot(pick_ref[cut, :], rhs_ref[...], preferred_element_type=F32)
+        stage_ref[cut, :] = both[:, :sz] + both[:, sz:]
+        copies.append(pltpu.make_async_copy(stage_ref.at[cut], reply_ref.at[cut], sems.at[index]))
+        copies[-1].start()
+    for copy in copies:
+        copy.wait()
 
 
 def solid_steps(rim, cap, state, state_rim, heat, heat_rim, code):
@@ -418,7 +475,7 @@
     total = code.shape[0] * cap
     return pl.pallas_call(
         functools.partial(solid_kernel, rim, cap),
-        in_specs=[in_vmem] * 9,
+        in_specs=[in_hbm] + [in_vmem] * 8,
         out_specs=[in_vmem, in_vmem, in_hbm],
         out_shape=[
             jax.ShapeDtypeStruct((sx, sy, sz), F32),
@@ -429,13 +486,15 @@
             pltpu.VMEM((3, long, height, sz), F32),
             pltpu.VMEM((sx + 2 * rim, height, sz), F32),
             pltpu.VMEM((sx * sy, 2 * sz), BF16),
+            pltpu.VMEM((total, sx * sy), BF16),
             pltpu.VMEM((total, sz), F32),
+            pltpu.SemaphoreType.DMA,
             pltpu.SemaphoreType.DMA((GROUPS,)),
         ],
         compiler_params=params(24),
         cost_estimate=cost(4 * total * sx * sy * sz, 4 * total * sz),
         name="solid_steps",
-    )(state, *state_rim, heat, *heat_rim, code)
+    )(far(state), *state_rim, heat, *heat_rim, code)
 
 
 def stress_kernel(sigma_ref, out_ref, tick_ref):
@@ -506,17 +565,37 @@
 RING = 3 * PLANES
 
 
-def fluid_kernel(here_ref, xlo_ref, xhi_ref, ylo_ref, yhi_ref, speed_ref, flux_ref, *refs):
-    out_ref, xfirst_ref, xlast_ref, yfirst_ref, ylast_ref, ring_ref = refs[-6:]
+def fluid_kernel(opening, here_ref, xlo_ref, xhi_ref, speed_ref, flux_ref, *refs):
     index, count = pl.program_id(0), pl.num_programs(0)
     cx = (count - 1) * PLANES
     _, cy, depth = here_ref.shape
     row_len = flux_ref.shape[2]
     rows = slice(OFF, OFF + cy)
+    if opening:
+        out_ref, xfirst_ref, xlast_ref, yfirst_ref, ylast_ref, clo_ref, chi_ref, ring_ref = refs
+    else:
+        lo_ref, hi_ref, left_ref, right_ref, ylo_ref, yhi_ref = refs[:6]
+        out_ref, tick_ref, ring_ref = refs[-3:]
+        tick_ref[...] = jnp.zeros_like(tick_ref)
+
+    def patch(slot, corner_ref):
+        wide = depth // LANE
+        base = corner_ref.shape[0] - 2 * wide
+        for row, at in ((OFF, base), (OFF + cy - 1, base + wide)):
+            for i in range(wide):
+                ring_ref[slot, row:row + 1, i * LANE:(i + 1) * LANE] = (
+                    corner_ref[at + i:at + i + 1, :]
+                )
 
     @pl.when(index == 0)
     def _():
         ring_ref[RING - 1, rows, :] = xlo_ref[...]
+        if opening:
+            for slot in range(RING):
+                ring_ref[slot, OFF - 8:OFF, :] = jnp.zeros((8, depth), F32)
+                ring_ref[slot, OFF + cy:OFF + cy + 8, :] = jnp.zeros((8, depth), F32)
+        else:
+            patch(RING - 1, lo_ref)
 
     @pl.when(index < count - 1)
     def _():
@@ -524,12 +603,18 @@
             plane = index * PLANES + p
             slot = lax.rem(plane, RING)
             ring_ref[slot, rows, :] = here_ref[p]
-            ring_ref[slot, OFF - 1:OFF, :] = ylo_ref[pl.ds(plane, 1), :]
-            ring_ref[slot, OFF + cy:OFF + cy + 1, :] = yhi_ref[pl.ds(plane, 1), :]
+            if not opening:
+                one = pl.ds(plane, 1)
+                ring_ref[slot, OFF:OFF + 1, :] = left_ref[one, :]
+                ring_ref[slot, OFF + cy - 1:OFF + cy, :] = right_ref[one, :]
+                ring_ref[slot, OFF - 1:OFF, :] = ylo_ref[one, :]
+                ring_ref[slot, OFF + cy:OFF + cy + 1, :] = yhi_ref[one, :]
 
     @pl.when(index == count - 1)
     def _():
         ring_ref[lax.rem(cx, RING), rows, :] = xhi_ref[...]
+        if not opening:
+            patch(lax.rem(cx, RING), hi_ref)
 
     rate = time_step * diffusivity
 
@@ -567,24 +652,32 @@
                 out_ref[p, y:y + 8, :row_len] = (
                     total[:, :row_len] - time_step * flux_ref[p, y:y + 8, :]
                 )
-        yfirst_ref[pl.ds(plane, 1), :] = out_ref[p, 0:1, :]
-        ylast_ref[pl.ds(plane, 1), :] = out_ref[p, cy - 1:cy, :]
+        if opening:
+            one = pl.ds(plane, 1)
+            yfirst_ref[one, :] = out_ref[p, 0:1, :]
+            ylast_ref[one, :] = out_ref[p, cy - 1:cy, :]
+            edge = time_step * speed_ref[1, p, 0:16, :].astype(F32)
+            clo_ref[one, :] = rate + jnp.maximum(edge[0:1], 0.0)
+            edge = time_step * speed_ref[1, p, cy - 16:cy, :].astype(F32)
+            chi_ref[one, :] = rate - jnp.minimum(edge[15:16], 0.0)
         return none
 
     @pl.when(index > 0)
     def _():
         lax.fori_loop(0, PLANES, advance, 0)
 
-    @pl.when(index == 1)
-    def _():
-        xfirst_ref[...] = out_ref[0]
-
-    @pl.when(index == count - 1)
-    def _():
-        xlast_ref[...] = out_ref[PLANES - 1]
-
-
-def fluid_step(temp, rims, velocity, flux, after):
+    if opening:
+
+        @pl.when(index == 1)
+        def _():
+            xfirst_ref[...] = out_ref[0]
+
+        @pl.when(index == count - 1)
+        def _():
+            xlast_ref[...] = out_ref[PLANES - 1]
+
+
+def fluid_step(opening, temp, sides, velocity, flux, lines, after):
     cx, cy, depth = temp.shape
     row_len = flux.shape[2]
     plane = (PLANES, cy, depth)
@@ -592,32 +685,34 @@
     face = pl.BlockSpec((cy, depth), lambda i: (0, 0))
     line = pl.BlockSpec((cx, depth), lambda i: (0, 0))
     back = lambda i: (jnp.maximum(i - 1, 0), 0, 0)
-    return pl.pallas_call(
-        fluid_kernel,
+    shape = jax.ShapeDtypeStruct
+    outs = [pl.BlockSpec(plane, back)]
+    outs += [face, face] + [line] * 4 if opening else [whole((8, LANE))]
+    shapes = [pltpu.HBM(temp.shape, F32)]
+    if opening:
+        shapes += [shape((cy, depth), F32)] * 2 + [shape((cx, depth), F32)] * 4
+    else:
+        shapes += [shape((8, LANE), F32)]
+    extra = [whole(x.shape) for x in lines[:2]] + [line] * len(lines[2:])
+    return pl.pallas_call(
+        functools.partial(fluid_kernel, opening),
         grid=(steps + 1,),
         in_specs=[
             pl.BlockSpec(plane, lambda i: (jnp.minimum(i, steps - 1), 0, 0)),
             face,
             face,
-            line,
-            line,
             pl.BlockSpec((3, PLANES, cy, depth), lambda i: (0, jnp.maximum(i - 1, 0), 0, 0)),
             pl.BlockSpec((PLANES, cy, row_len), back),
         ]
+        + extra
         + [anywhere] * len(after),
-        out_specs=[pl.BlockSpec(plane, back), face, face, line, line],
-        out_shape=[
-            pltpu.HBM(temp.shape, F32),
-            jax.ShapeDtypeStruct((cy, depth), F32),
-            jax.ShapeDtypeStruct((cy, depth), F32),
-            jax.ShapeDtypeStruct((cx, depth), F32),
-            jax.ShapeDtypeStruct((cx, depth), F32),
-        ],
+        out_specs=outs,
+        out_shape=shapes,
         scratch_shapes=[pltpu.VMEM((RING, cy + 2 * OFF, depth), F32)],
         compiler_params=params(24),
         cost_estimate=cost(40 * cx * cy * depth, 14 * cx * cy * depth),
         name="fluid_step",
-    )(far(temp), *rims, far(velocity), flux, *after)
+    )(far(temp), *sides, far(velocity), flux, *lines, *after)
 
 
 def body(temp_fluid, velocity, wall_old, wall_mask, owner_map, slot_map, temp_solid, material):
@@ -632,32 +727,37 @@
     rim = SSTEPS + 1
 
     first, last, left, right = x_faces(rim, temp_fluid, temp_solid, material)
-    faces = (*neighbours(last, first, "gx"), *neighbours(right, left, "gy"))
-    xlo, xhi = faces[:2]
+    xlo, xhi = neighbours(last, first, "gx")
     dest, where, codes = rank(owner_map.reshape(1, rows), slot_map, ndev, cap)
-    outgoing, flux = pack(where, codes, temp_fluid, wall_old, wall_mask, cap, faces)
+    outgoing, flux = pack(where, codes, temp_fluid, wall_old, wall_mask, cap, (first, last))
+    outgoing, xlo, xhi = lax.optimization_barrier((outgoing, xlo, xhi))
     incoming = lax.all_to_all(outgoing, AXES, split_axis=0, concat_axis=0, tiled=True)
 
-    fluid, *edges = fluid_step(temp_fluid, faces, velocity, flux, ())
-    first, last, left, right = edges
     left, right, state = y_faces(rim, left, right, temp_solid, material, xlo, xhi)
-    faces = (*neighbours(last, first, "gx"), *neighbours(right, left, "gy"))
-    rims = faces[2:]
+    ylo, yhi = neighbours(right, left, "gy")
+    fluid, first, last, *edges = fluid_step(
+        True, temp_fluid, (xlo, xhi), velocity, flux, (), ()
+    )
+    sides = neighbours(last, first, "gx")
 
     thin = rim - 1
-    heat, first, last, code = heat_sum(incoming, cap, temp_solid.shape, thin, faces)
+    heat, first, last, left, right, code = heat_sum(
+        incoming, cap, temp_solid.shape, thin, sides, (ylo, yhi, *edges)
+    )
     hxlo, hxhi = neighbours(last, first, "gx")
-    tall = lambda cut: jnp.concatenate([hxlo[:, cut], heat[:, cut], hxhi[:, cut]], axis=0)
-    hylo, hyhi = neighbours(tall(slice(sy - thin, sy)), tall(slice(0, thin)), "gy")
+    first, last = strips(thin, heat, hxlo, hxhi, left, right)
+    hylo, hyhi = neighbours(last, first, "gy")
     solid, sigma, replies = solid_steps(
-        rim, cap, state, rims, heat, (hxlo, hxhi, hylo, hyhi), code
+        rim, cap, state, (ylo, yhi), heat, (hxlo, hxhi, hylo, hyhi), code
     )
     returned = lax.all_to_all(
         replies.reshape(ndev, cap, sz), AXES, split_axis=0, concat_axis=0, tiled=True
     )
     force, tick = stress(sigma, sx, sy)
-    fluid, *edges = fluid_step(fluid, faces, velocity, flux, (tick,))
-    wall_next = unpack(dest, returned.reshape(total, sz), edges[2:])
+    fluid, tick = fluid_step(
+        False, fluid, sides, velocity, flux, (hxlo, hxhi, left, right, hylo, hyhi), (tick,)
+    )
+    wall_next = unpack(dest, returned.reshape(total, sz), (tick,))
     return fluid, wall_next.reshape(cx, cy, row_len), solid, force
 
 

time: 143 us -> 135 us (0.944)
  starting transfers between devices: 39.2 us -> 35.2 us
  local copies, waits for them, and re-layouts: 3.54 us -> 0.92 us
  waiting for transfers between devices: 53.3 us -> 50.7 us
  Pallas kernels: 44.4 us -> 46.5 us
    ppermute x12 -> x10, waiting for transfers between devices: 28.2 us -> 17 us  [neighbours(): return (lax.ppermute(before, axis, up), lax.ppermute(after, axis, down))]
    all_to_all x1, waiting for transfers between devices: 2.64 us -> 10.9 us  [body(): lax.all_to_all(outgoing, AXES, split_axis=0, concat_axis=0, tiled=True)]
    ppermute x12 -> x10, starting transfers between devices: 25.3 us -> 18.2 us  [neighbours(): return (lax.ppermute(before, axis, up), lax.ppermute(after, axis, down))]
    unnamed x12 -> x8, local copies, waits for them, and re-layouts: 3.51 us -> 0.92 us
    all_to_all x1, starting transfers between devices: 5.53 us -> 7.56 us  [body(): lax.all_to_all(replies.reshape(ndev, cap, sz), AXES, split_axis=0, concat...]
    pallas_call x3 -> x4, Pallas kernels: 28.1 us -> 29.1 us  [the longest x2 23.4 us: fluid_step(): pl.pallas_call(functools.partial(fluid_kernel, opening), grid=(steps + 1,...]
  transfers between devices with their start and end apart: 14 -> 12, of which waited for: 8 -> 6; matrix products, arithmetic and copies ran while one was open for 0% -> 0% of each run, Pallas kernels for 20% -> 25%
where the time goes in v8:
time: 135 us; the launch traced here: 134 us
  waiting for transfers between devices  50.7 us (38%)
  Pallas kernels  46.5 us (34%)
  starting transfers between devices  35.2 us (26%)
    pallas_call x2, Pallas kernels, fluid_step(): pl.pallas_call(functools.partial(fluid_kernel, opening), grid=(steps + 1,...  23.4 us
    all_to_all x1, waiting for transfers between devices, body(): lax.all_to_all(replies.reshape(ndev, cap, sz), AXES, split_axis=0, concat...  22.8 us
    ppermute x10, starting transfers between devices, neighbours(): return (lax.ppermute(before, axis, up), lax.ppermute(after, axis, down))  18.2 us
    ppermute x10, waiting for transfers between devices, neighbours(): return (lax.ppermute(before, axis, up), lax.ppermute(after, axis, down))  17 us
    all_to_all x1, waiting for transfers between devices, body(): lax.all_to_all(outgoing, AXES, split_axis=0, concat_axis=0, tiled=True)  10.9 us
    all_to_all x1, starting transfers between devices, body(): lax.all_to_all(outgoing, AXES, split_axis=0, concat_axis=0, tiled=True)  9.41 us
    all_to_all x1, starting transfers between devices, body(): lax.all_to_all(replies.reshape(ndev, cap, sz), AXES, split_axis=0, concat...  7.56 us
    pallas_call x1, Pallas kernels, solid_steps(): pl.pallas_call(functools.partial(solid_kernel, rim, cap), in_specs=[in_hb...  5.68 us
  transfers between devices with their start and end apart: 12, of which 6 were waited for; matrix products, arithmetic and copies ran while one was open for 0% of the time, Pallas kernels for 25%

profile of v8, /device:TPU:0, one launch (start us, length us, event | category | flops | bytes accessed | tf_op | source)
XLA Modules:
  0.0 134.2 jit_solution(7959906968992462445)
XLA Ops:
  0.6 0.0 copy-start.3
  0.6 0.0 copy-start.2
  0.7 1.6 %x_faces.1 = (f32[112,1024]{1,0:T(8,128)S(1)}, f32[112,1024]{1,0:T(8,128)S(1)}, f32[16,1024]{1,0:T(8,128)S(1)}, f32[16,1024]{1,0:T(8,128)S(1)}) custom-call(f32[16,64,1024]{2,1,0:T(8,128)} %here_ref.1, f32[16,64,1024]{2,1,0:T(8,128)} %here_ref.1, f32[16,64,1024]{2,1,0:T(8,128)} %here_ref.1, f32[16,64,1024]{2,1,0:T(8,128)} %here_ref.1, ...), custom_call_target="tpu_custom_call" | custom-call | flops 1000 | bytes 1835008 | tf_op jit(solution)/shard_map/x_faces/pallas_call | solution.py:280
  2.3 1.3 collective-permute-start.1
  3.6 3.1 %collective-permute-start = (f32[112,1024]{1,0:T(8,128)S(1)}, f32[112,1024]{1,0:T(8,128)S(1)}, u32[]{:S(2)}, u32[]{:S(2)}) collective-permute-start(f32[112,1024]{1,0:T(8,128)S(1)} %get-tuple-element.44.refs_1_), channel_id=1, source_target_pairs={{0,4},{4,8},{8,12},{12,16},{16,20},{20,24},{24,28},{1,5},{5,9},{9,... | collective-permute-start | bytes 1376264 | tf_op jit(solution)/shard_map/ppermute | solution.py:48
  6.6 0.0 copy-done.3
  6.6 0.0 copy-done.2
  6.6 0.9 rank.1
  7.5 4.4 %pack.1 = (f32[32,104,128]{2,1,0:T(8,128)}, f32[16,64,128]{2,1,0:T(8,128)S(1)}) custom-call(s32[1,1024]{1,0:T(1,128)S(1)} %get-tuple-element.41.where_ref, f32[32,128]{1,0:T(8,128)S(1)} %get-tuple-element.42.code_ref, f32[16,64,1024]{2,1,0:T(8,128)} %here_ref.1, f32[16,64,128]{2,1,0:T(8,128)} %old_ref.1, s32[16,64,128]{2,1,0:T(8,128)} %mask_ref.1, ...), custom_call_target="tpu_custom_call" | custom-call | flops 1744830464 | bytes 2621440 | tf_op jit(solution)/shard_map/pack/pallas_call | solution.py:151
  12.0 0.0 collective-permute-done.1.xhi_ref.hi_ref
  12.0 0.0 collective-permute-done.xlo_ref.lo_ref
  12.0 9.4 %all-to-all-start = ((f32[32,104,128]{2,1,0:T(8,128)}), f32[32,104,128]{2,1,0:T(8,128)}, u32[]{:S(2)}, u32[]{:S(2)}) async-start(f32[32,104,128]{2,1,0:T(8,128)} %get-tuple-element.52), calls=%async_computation | async-start | bytes 3407872 | tf_op jit(solution)/shard_map/all_to_all | solution.py:734
  21.4 2.4 %y_faces.1 = (f32[64,1024]{1,0:T(8,128)S(1)}, f32[64,1024]{1,0:T(8,128)S(1)}, f32[2,32,48,128]{3,2,1,0:T(8,128)}) custom-call(f32[16,1024]{1,0:T(8,128)S(1)} %get-tuple-element.53.near_ref, f32[16,1024]{1,0:T(8,128)S(1)} %get-tuple-element.54.far_ref, f32[16,32,128]{2,1,0:T(8,128)} %temp_ref.5, s32[16,32,128]{2,1,0:T(8,128)} %kind_ref.3, ...), custom_call_target="tpu_custom_call" | custom-call | flops 1000 | bytes 1048576 | tf_op jit(solution)/shard_map/y_faces/pallas_call | solution.py:338
  23.8 3.6 %collective-permute-start.4 = (f32[64,1024]{1,0:T(8,128)S(1)}, f32[64,1024]{1,0:T(8,128)S(1)}, u32[]{:S(2)}, u32[]{:S(2)}) collective-permute-start(f32[64,1024]{1,0:T(8,128)S(1)} %get-tuple-element.55), channel_id=1, source_target_pairs={{0,1},{1,2},{2,3},{4,5},{5,6},{6,7},{8,9},{9,10},{10,11},{12,13},{... | collective-permute-start | bytes 786440 | tf_op jit(solution)/shard_map/ppermute | solution.py:48
  27.4 1.3 collective-permute-start.5
  28.7 11.8 %fluid_step.2 = (f32[16,64,1024]{2,1,0:T(8,128)}, f32[64,1024]{1,0:T(8,128)S(1)}, f32[64,1024]{1,0:T(8,128)S(1)}, f32[16,1024]{1,0:T(8,128)S(1)}, f32[16,1024]{1...) custom-call(f32[16,64,1024]{2,1,0:T(8,128)} %here_ref.1, ...), custom_call_target="tpu_custom_call" | custom-call | flops 41943040 | bytes 14680064 | tf_op jit(solution)/shard_map/fluid_step/pallas_call | solution.py:697
  40.5 1.8 %collective-permute-start.2 = (f32[64,1024]{1,0:T(8,128)S(1)}, f32[64,1024]{1,0:T(8,128)S(1)}, u32[]{:S(2)}, u32[]{:S(2)}) collective-permute-start(f32[64,1024]{1,0:T(8,128)S(1)} %get-tuple-element.50), channel_id=1, source_target_pairs={{0,4},{4,8},{8,12},{12,16},{16,20},{20,24},{24,28},{1,5},{5,9},{9,... | collective-permute-start | bytes 786440 | tf_op jit(solution)/shard_map/ppermute | solution.py:48
  42.2 1.3 collective-permute-start.3
  43.5 0.0 collective-permute-done.4.ylo_ref
  43.6 7.3 %collective-permute-done.5.yhi_ref = f32[64,1024]{1,0:T(8,128)S(1)} collective-permute-done((f32[64,1024]{1,0:T(8,128)S(1)}, f32[64,1024]{1,0:T(8,128)S(1)}, u32[]{:S(2)}, u32[]{:S(2)}) %collective-permute-start.5) | collective-permute-done | bytes 262176 | tf_op jit(solution)/shard_map/ppermute | solution.py:48
  50.8 0.0 collective-permute-done.2.xfirst_ref.xlo_ref
  50.8 0.0 collective-permute-done.3.xlast_ref.xhi_ref
  50.8 10.9 %all-to-all-done.rows_ref = f32[32,104,128]{2,1,0:T(8,128)} async-done(((f32[32,104,128]{2,1,0:T(8,128)}), f32[32,104,128]{2,1,0:T(8,128)}, u32[]{:S(2)}, u32[]{:S(2)}) %all-to-all-start) | async-done | bytes 1703968 | tf_op jit(solution)/shard_map/all_to_all | solution.py:734
  61.7 3.6 %heat_sum.1 = (f32[16,32,128]{2,1,0:T(8,128)S(1)}, f32[144,128]{1,0:T(8,128)S(1)}, f32[144,128]{1,0:T(8,128)S(1)}, f32[16,1024]{1,0:T(8,128)S(1)}, f32[16,1024]{1,0:T(8,128)S(1)}, /*index=5*/s32[32,128]{1,0:T(8,128)S(1)}) custom-call(f32[32,104,128]{2,1,0:T(8,128)} %all-to-all-done.rows_ref, f32[64,1024]{1,0:T(8,128)S(1)} %collective-permute-done.2.xfirst_ref.xlo_ref, ...), custom_call_target="tpu_custom_call" | custom-call | flops 872415232 | bytes 1703936 | tf_op jit(solution)/shard_map/heat_sum/pallas_call | solution.py:218
  65.3 1.5 %collective-permute-start.6 = (f32[144,128]{1,0:T(8,128)S(1)}, f32[144,128]{1,0:T(8,128)S(1)}, u32[]{:S(2)}, u32[]{:S(2)}) collective-permute-start(f32[144,128]{1,0:T(8,128)S(1)} %get-tuple-element.61), channel_id=1, source_target_pairs={{0,4},{4,8},{8,12},{12,16},{16,20},{20,24},{24,28},{1,5},{5,9},{9,... | collective-permute-start | bytes 221192 | tf_op jit(solution)/shard_map/ppermute | solution.py:48
  66.8 1.3 collective-permute-start.7
  68.1 0.0 collective-permute-done.6.lo_ref.hxlo_ref.refs_0_
  68.1 3.6 %collective-permute-done.7.hi_ref.hxhi_ref.refs_1_ = f32[144,128]{1,0:T(8,128)S(1)} collective-permute-done((f32[144,128]{1,0:T(8,128)S(1)}, f32[144,128]{1,0:T(8,128)S(1)}, u32[]{:S(2)}, u32[]{:S(2)}) %collective-permute-start.7) | collective-permute-done | bytes 73760 | tf_op jit(solution)/shard_map/ppermute | solution.py:48
  71.7 0.1 strips.1
  71.8 1.8 %collective-permute-start.8 = (f32[32,1024]{1,0:T(8,128)S(1)}, f32[32,1024]{1,0:T(8,128)S(1)}, u32[]{:S(2)}, u32[]{:S(2)}) collective-permute-start(f32[32,1024]{1,0:T(8,128)S(1)} %get-tuple-element.66), channel_id=1, source_target_pairs={{0,1},{1,2},{2,3},{4,5},{5,6},{6,7},{8,9},{9,10},{10,11},{12,13},{... | collective-permute-start | bytes 393224 | tf_op jit(solution)/shard_map/ppermute | solution.py:48
  73.6 1.3 collective-permute-start.9
  74.9 1.2 collective-permute-done.8.hylo_ref.refs_4_
  76.1 5.0 %collective-permute-done.9.hyhi_ref.refs_5_ = f32[32,1024]{1,0:T(8,128)S(1)} collective-permute-done((f32[32,1024]{1,0:T(8,128)S(1)}, f32[32,1024]{1,0:T(8,128)S(1)}, u32[]{:S(2)}, u32[]{:S(2)}) %collective-permute-start.9) | collective-permute-done | bytes 131104 | tf_op jit(solution)/shard_map/ppermute | solution.py:48
  81.1 0.0 copy-start
  81.1 5.7 %solid_steps.1 = (f32[16,32,128]{2,1,0:T(8,128)}, f32[18,48,128]{2,1,0:T(8,128)S(1)}, f32[3072,128]{1,0:T(8,128)}) custom-call(f32[2,32,48,128]{3,2,1,0:T(8,128)} %get-tuple-element.68.state_ref, f32[64,1024]{1,0:T(8,128)S(1)} %collective-permute-done.4.ylo_ref, f32[64,1024]{1,0:T(8,128)S(1)} %collective-permute-done.5.yhi_ref, ...), custom_call_target="tpu_custom_call" | custom-call | flops 805306368 | bytes 1572864 | tf_op jit(solution)/shard_map/solid_steps/pallas_call | solution.py:476
  86.7 0.0 copy-done
  86.8 7.6 %all-to-all-start.1 = ((f32[32,96,128]{2,1,0:T(8,128)}), f32[32,96,128]{2,1,0:T(8,128)S(1)}, u32[]{:S(2)}, u32[]{:S(2)}) async-start(f32[32,96,128]{2,1,0:T(8,128)} %bitcast.6), calls=%async_computation.1 | async-start | bytes 3145728 | tf_op jit(solution)/shard_map/all_to_all | solution.py:753
  94.3 2.1 %stress.1 = (f32[3,16,32,128]{3,2,1,0:T(8,128)}, f32[8,128]{1,0:T(8,128)S(1)}) custom-call(f32[18,48,128]{2,1,0:T(8,128)S(1)} %get-tuple-element.70.sigma_ref), custom_call_target="tpu_custom_call" | custom-call | flops 655360 | bytes 1048576 | tf_op jit(solution)/shard_map/stress/pallas_call | solution.py:523
  96.5 0.0 copy-start.1
  96.5 0.9 copy-done.1
  97.4 11.6 %fluid_step.3 = (f32[16,64,1024]{2,1,0:T(8,128)}, f32[8,128]{1,0:T(8,128)S(1)}) custom-call(f32[16,64,1024]{2,1,0:T(8,128)} %get-tuple-element.49.here_ref, f32[64,1024]{1,0:T(8,128)S(1)} %collective-permute-done.2.xfirst_ref.xlo_ref, f32[64,1024]{1,0:T(8,128)S(1)} %collective-permute-done.3.xlast_ref.xhi_ref, bf16[3,16,64,1024]{3,2,1,0:T(8,128)(2,1)} %speed_ref.3, ...), custom_call_target="tpu_custom_call" | custom-call | flops 41943040 | bytes 14680064 | tf_op jit(solution)/shard_map/fluid_step/pallas_call | solution.py:697
  109.0 22.8 %all-to-all-done.1 = f32[32,96,128]{2,1,0:T(8,128)S(1)} async-done(((f32[32,96,128]{2,1,0:T(8,128)}), f32[32,96,128]{2,1,0:T(8,128)S(1)}, u32[]{:S(2)}, u32[]{:S(2)}) %all-to-all-start.1) | async-done | bytes 1572896 | tf_op jit(solution)/shard_map/all_to_all | solution.py:753
  131.8 2.4 %unpack.1 = f32[1024,128]{1,0:T(8,128)} custom-call(s32[1,1024]{1,0:T(1,128)S(1)} %get-tuple-element.73.dest_ref, f32[3072,128]{1,0:T(8,128)S(1)} %bitcast.4, f32[8,128]{1,0:T(8,128)S(1)} %get-tuple-element.75.refs_0_), custom_call_target="tpu_custom_call" | custom-call | flops 131072 | bytes 1048576 | tf_op jit(solution)/shard_map/unpack/pallas_call | solution.py:551
Async XLA Ops:
  0.6 6.0 %copy-start.3 = (s32[1,1024]{1,0:T(1,128)S(1)}, s32[1,1024]{1,0:T(1,128)}, u32[]{:S(2)}) copy-start(s32[1,1024]{1,0:T(1,128)} %slot_ref.1) | copy-start | bytes 12292
  0.6 6.0 %copy-start.2 = (s32[1,1024,1]{1,2,0:T(1,128)S(1)}, s32[1,1024,1]{1,2,0:T(1,128)}, u32[]{:S(2)}) copy-start(s32[1,1024,1]{1,2,0:T(1,128)} %param.12) | copy-start | bytes 12292
  2.3 9.7 %collective-permute-start.1 = (f32[112,1024]{1,0:T(8,128)S(1)}, f32[112,1024]{1,0:T(8,128)S(1)}, u32[]{:S(2)}, u32[]{:S(2)}) collective-permute-start(f32[112,1024]{1,0:T(8,128)S(1)} %get-tuple-element.43.refs_0_), channel_id=1, source_target_pairs={{4,0},{8,4},{12,8},{16,12},{20,16},{24,20},{28,24},{5,1},{9,5},{13... | collective-permute-start | bytes 1376264 | tf_op jit(solution)/shard_map/ppermute | solution.py:48
  3.6 8.4 %collective-permute-start = (f32[112,1024]{1,0:T(8,128)S(1)}, f32[112,1024]{1,0:T(8,128)S(1)}, u32[]{:S(2)}, u32[]{:S(2)}) collective-permute-start(f32[112,1024]{1,0:T(8,128)S(1)} %get-tuple-element.44.refs_1_), channel_id=1, source_target_pairs={{0,4},{4,8},{8,12},{12,16},{16,20},{20,24},{24,28},{1,5},{5,9},{9,... | collective-permute-start | bytes 1376264 | tf_op jit(solution)/shard_map/ppermute | solution.py:48
  12.0 49.7 %all-to-all-start = ((f32[32,104,128]{2,1,0:T(8,128)}), f32[32,104,128]{2,1,0:T(8,128)}, u32[]{:S(2)}, u32[]{:S(2)}) async-start(f32[32,104,128]{2,1,0:T(8,128)} %get-tuple-element.52), calls=%async_computation | async-start | bytes 3407872 | tf_op jit(solution)/shard_map/all_to_all | solution.py:734
  23.8 19.8 %collective-permute-start.4 = (f32[64,1024]{1,0:T(8,128)S(1)}, f32[64,1024]{1,0:T(8,128)S(1)}, u32[]{:S(2)}, u32[]{:S(2)}) collective-permute-start(f32[64,1024]{1,0:T(8,128)S(1)} %get-tuple-element.55), channel_id=1, source_target_pairs={{0,1},{1,2},{2,3},{4,5},{5,6},{6,7},{8,9},{9,10},{10,11},{12,13},{... | collective-permute-start | bytes 786440 | tf_op jit(solution)/shard_map/ppermute | solution.py:48
  27.4 23.4 %collective-permute-start.5 = (f32[64,1024]{1,0:T(8,128)S(1)}, f32[64,1024]{1,0:T(8,128)S(1)}, u32[]{:S(2)}, u32[]{:S(2)}) collective-permute-start(f32[64,1024]{1,0:T(8,128)S(1)} %get-tuple-element.56), channel_id=1, source_target_pairs={{1,0},{2,1},{3,2},{5,4},{6,5},{7,6},{9,8},{10,9},{11,10},{13,12},{... | collective-permute-start | bytes 786440 | tf_op jit(solution)/shard_map/ppermute | solution.py:48
  40.5 10.4 %collective-permute-start.2 = (f32[64,1024]{1,0:T(8,128)S(1)}, f32[64,1024]{1,0:T(8,128)S(1)}, u32[]{:S(2)}, u32[]{:S(2)}) collective-permute-start(f32[64,1024]{1,0:T(8,128)S(1)} %get-tuple-element.50), channel_id=1, source_target_pairs={{0,4},{4,8},{8,12},{12,16},{16,20},{20,24},{24,28},{1,5},{5,9},{9,... | collective-permute-start | bytes 786440 | tf_op jit(solution)/shard_map/ppermute | solution.py:48
  42.2 8.6 %collective-permute-start.3 = (f32[64,1024]{1,0:T(8,128)S(1)}, f32[64,1024]{1,0:T(8,128)S(1)}, u32[]{:S(2)}, u32[]{:S(2)}) collective-permute-start(f32[64,1024]{1,0:T(8,128)S(1)} %get-tuple-element.51), channel_id=1, source_target_pairs={{4,0},{8,4},{12,8},{16,12},{20,16},{24,20},{28,24},{5,1},{9,5},{13... | collective-permute-start | bytes 786440 | tf_op jit(solution)/shard_map/ppermute | solution.py:48
  65.3 2.9 %collective-permute-start.6 = (f32[144,128]{1,0:T(8,128)S(1)}, f32[144,128]{1,0:T(8,128)S(1)}, u32[]{:S(2)}, u32[]{:S(2)}) collective-permute-start(f32[144,128]{1,0:T(8,128)S(1)} %get-tuple-element.61), channel_id=1, source_target_pairs={{0,4},{4,8},{8,12},{12,16},{16,20},{20,24},{24,28},{1,5},{5,9},{9,... | collective-permute-start | bytes 221192 | tf_op jit(solution)/shard_map/ppermute | solution.py:48
  66.8 4.9 %collective-permute-start.7 = (f32[144,128]{1,0:T(8,128)S(1)}, f32[144,128]{1,0:T(8,128)S(1)}, u32[]{:S(2)}, u32[]{:S(2)}) collective-permute-start(f32[144,128]{1,0:T(8,128)S(1)} %get-tuple-element.62), channel_id=1, source_target_pairs={{4,0},{8,4},{12,8},{16,12},{20,16},{24,20},{28,24},{5,1},{9,5},{13... | collective-permute-start | bytes 221192 | tf_op jit(solution)/shard_map/ppermute | solution.py:48
  71.8 4.3 %collective-permute-start.8 = (f32[32,1024]{1,0:T(8,128)S(1)}, f32[32,1024]{1,0:T(8,128)S(1)}, u32[]{:S(2)}, u32[]{:S(2)}) collective-permute-start(f32[32,1024]{1,0:T(8,128)S(1)} %get-tuple-element.66), channel_id=1, source_target_pairs={{0,1},{1,2},{2,3},{4,5},{5,6},{6,7},{8,9},{9,10},{10,11},{12,13},{... | collective-permute-start | bytes 393224 | tf_op jit(solution)/shard_map/ppermute | solution.py:48
  73.6 7.5 %collective-permute-start.9 = (f32[32,1024]{1,0:T(8,128)S(1)}, f32[32,1024]{1,0:T(8,128)S(1)}, u32[]{:S(2)}, u32[]{:S(2)}) collective-permute-start(f32[32,1024]{1,0:T(8,128)S(1)} %get-tuple-element.67), channel_id=1, source_target_pairs={{1,0},{2,1},{3,2},{5,4},{6,5},{7,6},{9,8},{10,9},{11,10},{13,12},{... | collective-permute-start | bytes 393224 | tf_op jit(solution)/shard_map/ppermute | solution.py:48
  81.1 5.7 %copy-start = (f32[32,1024]{1,0:T(8,128)}, f32[32,1024]{1,0:T(8,128)S(1)}, u32[]{:S(2)}) copy-start(f32[32,1024]{1,0:T(8,128)S(1)} %collective-permute-done.9.hyhi_ref.refs_5_) | copy-start | bytes 393220
  86.8 45.0 %all-to-all-start.1 = ((f32[32,96,128]{2,1,0:T(8,128)}), f32[32,96,128]{2,1,0:T(8,128)S(1)}, u32[]{:S(2)}, u32[]{:S(2)}) async-start(f32[32,96,128]{2,1,0:T(8,128)} %bitcast.6), calls=%async_computation.1 | async-start | bytes 3145728 | tf_op jit(solution)/shard_map/all_to_all | solution.py:753
  96.5 0.9 copy-start.1

commit v9 on v8

--- a/solution.py
+++ b/solution.py
@@ -65,18 +65,18 @@
     return pltpu.with_memory_space_constraint(value, pltpu.VMEM)
 
 
-def rank_kernel(cap, owner_ref, slot_ref, dest_ref, where_ref, code_ref):
-    rows = owner_ref.shape[1]
-    ndev = code_ref.shape[0]
-    tall = cap + 8
-    tri = ones_where(
+def triangle():
+    return ones_where(
         lax.broadcasted_iota(jnp.int32, (LANE, LANE), 0)
         <= lax.broadcasted_iota(jnp.int32, (LANE, LANE), 1)
     )
+
+
+def rank_kernel(ndev, cap, owner_ref, dest_ref):
+    rows = owner_ref.shape[1]
+    tri = triangle()
     names = lax.broadcasted_iota(jnp.int32, (ndev, LANE), 0)
-    steps = lax.broadcasted_iota(jnp.int32, (LANE, LANE), 0)
     carry = jnp.zeros((ndev, 1), F32)
-    codes = jnp.zeros((2 * ndev, LANE), F32)
     for chunk in range(rows // LANE):
         cols = slice(chunk * LANE, (chunk + 1) * LANE)
         own = owner_ref[:, cols]
@@ -85,37 +85,74 @@
         carry = ranks[:, LANE - 1:]
         place = jnp.sum(hit * ranks, axis=0, keepdims=True).astype(jnp.int32) - 1
         dest_ref[:, cols] = own * cap + place
-        where_ref[:, cols] = own * tall + place
-        code = slot_ref[:, cols] + 1
-        pieces = jnp.concatenate(
-            [hit * (code // 32).astype(F32), hit * (code % 32).astype(F32)], axis=0
-        ).astype(BF16)
-        codes = codes + lax.dot_general(
-            pieces, ones_where(steps == place), (((1,), (1,)), ((), ())),
-            preferred_element_type=F32,
-        )
-    code_ref[...] = codes[:ndev] * 32.0 + codes[ndev:]
-
-
-def rank(owner, slot, ndev, cap):
+
+
+def rank(owner, ndev, cap):
     rows = owner.shape[1]
-    line = jax.ShapeDtypeStruct((1, rows), jnp.int32)
-    return pl.pallas_call(
-        functools.partial(rank_kernel, cap),
+    return pl.pallas_call(
+        functools.partial(rank_kernel, ndev, cap),
         grid=(1,),
-        in_specs=[whole((1, rows))] * 2,
-        out_specs=[whole((1, rows))] * 2 + [whole((ndev, LANE))],
-        out_shape=[line, line, jax.ShapeDtypeStruct((ndev, LANE), F32)],
+        in_specs=[whole((1, rows))],
+        out_specs=whole((1, rows)),
+        out_shape=jax.ShapeDtypeStruct((1, rows), jnp.int32),
         compiler_params=params(8),
         cost_estimate=cost(8 * ndev * LANE * rows, 20 * rows),
         name="rank",
-    )(owner, slot)
+    )(owner)
+
+
+def columns_kernel(slots, me_ref, maps_ref, *refs):
+    code_ref, hit_ref, place_ref = refs[-3:]
+    ndev, rows = maps_ref.shape
+    tri = triangle()
+    base = me_ref[0, 0] * slots
+    carry = jnp.zeros((ndev, 1), F32)
+    for chunk in range(rows // LANE):
+        cols = slice(chunk * LANE, (chunk + 1) * LANE)
+        slot = maps_ref[:, cols] - base
+        hit = jnp.where((slot >= 0) & (slot < slots), 1.0, 0.0)
+        ranks = jnp.dot(hit.astype(BF16), tri, preferred_element_type=F32) + carry
+        carry = ranks[:, LANE - 1:]
+        hit_ref[:, cols] = jnp.where(hit > 0.0, slot + 1, 0)
+        place_ref[:, cols] = jnp.where(hit > 0.0, ranks.astype(jnp.int32) - 1, -1)
+    steps = lax.broadcasted_iota(jnp.int32, (LANE, rows), 0)
+
+    def source(index, none):
+        one = pl.ds(index, 1)
+        code = hit_ref[one, :]
+        pieces = jnp.concatenate(
+            [(code >> 5).astype(F32), (code & 31).astype(F32), jnp.zeros((6, rows), F32)], axis=0
+        ).astype(BF16)
+        found = lax.dot_general(
+            pieces, ones_where(steps == place_ref[one, :]), (((1,), (1,)), ((), ())),
+            preferred_element_type=F32,
+        )
+        code_ref[one, :] = (found[0:1] * 32.0 + found[1:2]).astype(jnp.int32) - 1
+        return none
+
+    lax.fori_loop(0, ndev, source, 0, unroll=2)
+
+
+def columns(slots, me, maps, after):
+    ndev, rows = maps.shape
+    return pl.pallas_call(
+        functools.partial(columns_kernel, slots),
+        grid=(1,),
+        in_specs=[pl.BlockSpec(memory_space=pltpu.SMEM), whole(maps.shape)]
+        + [anywhere] * len(after),
+        out_specs=whole((ndev, LANE)),
+        out_shape=jax.ShapeDtypeStruct((ndev, LANE), jnp.int32),
+        scratch_shapes=[pltpu.VMEM((ndev, rows), jnp.int32)] * 2,
+        compiler_params=params(16),
+        cost_estimate=cost(16 * ndev * LANE * rows, 4 * ndev * rows),
+        name="columns",
+    )(me, maps, *after)
 
 
 GROUPS = 4
 
 
-def pack_kernel(cap, where_ref, code_ref, temp_ref, old_ref, mask_ref, *refs):
+def pack_kernel(where_ref, temp_ref, old_ref, mask_ref, *refs):
     out_ref, flux_ref, rhs_ref, stage_ref, sems = refs[-5:]
     rows = where_ref.shape[1]
     ndev, tall, row_len = stage_ref.shape
@@ -135,23 +172,21 @@
         both = jnp.dot(pick, rhs_ref[...], preferred_element_type=F32)
         both = both[:, :row_len] + both[:, row_len:]
         stage_ref[cut] = both.reshape(group, tall, row_len)
-        stage_ref[cut, cap, :] = code_ref[cut, :]
         copies.append(pltpu.make_async_copy(stage_ref.at[cut], out_ref.at[cut], sems.at[index]))
         copies[-1].start()
     for copy in copies:
         copy.wait()
 
 
-def pack(where, code, temp, old, mask, cap, after):
+def pack(where, temp, old, mask, ndev, cap, after):
     cx, cy, _ = temp.shape
     row_len = old.shape[2]
     rows = cx * cy
-    ndev = code.shape[0]
-    tall = cap + 8
-    return pl.pallas_call(
-        functools.partial(pack_kernel, cap),
+    tall = cap
+    return pl.pallas_call(
+        pack_kernel,
         grid=(1,),
-        in_specs=[whole((1, rows)), whole(code.shape)]
+        in_specs=[whole((1, rows))]
         + [whole((cx, cy, row_len))] * 3
         + [anywhere] * len(after),
         out_specs=[in_hbm, whole((cx, cy, row_len))],
@@ -167,12 +202,12 @@
         compiler_params=params(24),
         cost_estimate=cost(4 * ndev * tall * rows * row_len, 5 * rows * row_len * 4),
         name="pack",
-    )(where, code, far(temp), far(old), far(mask), *after)
-
-
-def heat_kernel(cap, thin, rows_ref, xfirst_ref, xlast_ref, ylo_ref, yhi_ref,
+    )(where, far(temp), far(old), far(mask), *after)
+
+
+def heat_kernel(thin, rows_ref, code_ref, xfirst_ref, xlast_ref, ylo_ref, yhi_ref,
                 yfirst_ref, ylast_ref, clo_ref, chi_ref,
-                heat_ref, low_ref, high_ref, left_ref, right_ref, code_ref):
+                heat_ref, low_ref, high_ref, left_ref, right_ref):
     ndev, tall, row_len = rows_ref.shape
     cx, depth = yfirst_ref.shape
     sx, sy, _ = heat_ref.shape
@@ -186,8 +221,7 @@
         for at, line in ((edge, left[x:x + 1]), (edge + depth // LANE, right[x:x + 1])):
             for i in range(depth // LANE):
                 ref[at + i:at + i + 1, :] = line[:, i * LANE:(i + 1) * LANE]
-    codes = rows_ref[:, cap, :].astype(jnp.int32) - 1
-    code_ref[...] = codes
+    codes = code_ref[...]
     group = ndev // GROUPS
     names = lax.broadcasted_iota(jnp.int32, (slots, tall), 0)
     total = jnp.zeros((slots, 2 * row_len), F32)
@@ -210,27 +244,29 @@
     high_ref[:edge, :] = heat[slots - edge:]
 
 
-def heat_sum(incoming, cap, block, thin, faces, edges):
+def heat_sum(incoming, code, block, thin, faces, edges):
     ndev, tall, row_len = incoming.shape
     sx, sy, _ = block
     line = edges[2].shape
     edge = (thin * sy + 2 * (line[1] // LANE), row_len)
     return pl.pallas_call(
-        functools.partial(heat_kernel, cap, thin),
-        in_specs=[in_vmem] + [anywhere] * 2 + [in_vmem] * 6,
-        out_specs=[in_vmem] * 6,
+        functools.partial(heat_kernel, thin),
+        grid=(1,),
+        in_specs=[whole(incoming.shape), whole(code.shape)]
+        + [anywhere] * 2
+        + [whole(x.shape) for x in edges],
+        out_specs=[whole(block), whole(edge), whole(edge), whole(line), whole(line)],
         out_shape=[
             jax.ShapeDtypeStruct(block, F32),
             jax.ShapeDtypeStruct(edge, F32),
             jax.ShapeDtypeStruct(edge, F32),
             jax.ShapeDtypeStruct(line, F32),
             jax.ShapeDtypeStruct(line, F32),
-            jax.ShapeDtypeStruct((ndev, row_len), jnp.int32),
         ],
         compiler_params=params(20),
         cost_estimate=cost(4 * ndev * tall * sx * sy * row_len, 4 * ndev * tall * row_len),
         name="heat_sum",
-    )(near(incoming), *faces, *edges)
+    )(incoming, code, *faces, *edges)
 
 
 def put_rim(ref, base, slabs):
@@ -728,8 +764,11 @@
 
     first, last, left, right = x_faces(rim, temp_fluid, temp_solid, material)
     xlo, xhi = neighbours(last, first, "gx")
-    dest, where, codes = rank(owner_map.reshape(1, rows), slot_map, ndev, cap)
-    outgoing, flux = pack(where, codes, temp_fluid, wall_old, wall_mask, cap, (first, last))
+    owner = owner_map.reshape(1, rows)
+    maps = lax.all_gather(owner * (sx * sy) + slot_map, AXES, axis=0, tiled=True)
+    me = lax.axis_index("gx") * lax.axis_size("gy") + lax.axis_index("gy")
+    dest = rank(owner, ndev, cap)
+    outgoing, flux = pack(dest, temp_fluid, wall_old, wall_mask, ndev, cap, (first, last))
     outgoing, xlo, xhi = lax.optimization_barrier((outgoing, xlo, xhi))
     incoming = lax.all_to_all(outgoing, AXES, split_axis=0, concat_axis=0, tiled=True)
 
@@ -739,10 +778,11 @@
         True, temp_fluid, (xlo, xhi), velocity, flux, (), ()
     )
     sides = neighbours(last, first, "gx")
+    code = columns(sx * sy, me.reshape(1, 1), maps, (edges[0],))
 
     thin = rim - 1
-    heat, first, last, left, right, code = heat_sum(
-        incoming, cap, temp_solid.shape, thin, sides, (ylo, yhi, *edges)
+    heat, first, last, left, right = heat_sum(
+        incoming, code, temp_solid.shape, thin, sides, (ylo, yhi, *edges)
     )
     hxlo, hxhi = neighbours(last, first, "gx")
     first, last = strips(thin, heat, hxlo, hxhi, left, right)

time: 135 us -> 190 us (1.41)
  blocking collectives: 0 us -> 71.5 us
  waiting for transfers between devices: 50.7 us -> 30.8 us
  starting transfers between devices: 35.2 us -> 30.1 us
  Pallas kernels: 46.5 us -> 50.8 us
  local copies, waits for them, and re-layouts: 0.92 us -> 4.7 us
    all_gather x0 -> x1, blocking collectives: none -> 71.5 us  [body(): lax.all_gather(owner * (sx * sy) + slot_map, AXES, axis=0, tiled=True)]
    all_to_all x1, waiting for transfers between devices: 10.9 us -> 0.01 us  [body(): lax.all_to_all(outgoing, AXES, split_axis=0, concat_axis=0, tiled=True)]
    ppermute x10, waiting for transfers between devices: 17 us -> 8.02 us  [neighbours(): return (lax.ppermute(before, axis, up), lax.ppermute(after, axis, down))]
    all_to_all x1, starting transfers between devices: 7.56 us -> 2.7 us  [body(): lax.all_to_all(replies.reshape(ndev, cap, sz), AXES, split_axis=0, concat...]
    pallas_call x3 -> x4, Pallas kernels: 8.88 us -> 13 us  [the longest x1 4.81 us: columns(): pl.pallas_call(functools.partial(columns_kernel, slots), grid=(1,), in_sp...]
    unnamed x8 -> x21, local copies, waits for them, and re-layouts: 0.92 us -> 4.7 us
  transfers between devices with their start and end apart: 12 -> 12, of which waited for: 6 -> 4; matrix products, arithmetic and copies ran while one was open for 0% -> 0% of each run, Pallas kernels for 25% -> 20%
where the time goes in v9:
time: 190 us; the launch traced here: 189 us
  blocking collectives  71.5 us (38%)
  Pallas kernels  50.8 us (27%)
  waiting for transfers between devices  30.8 us (16%)
  starting transfers between devices  30.1 us (16%)
  local copies, waits for them, and re-layouts  4.7 us (2%)
    all_gather x1, blocking collectives, body(): lax.all_gather(owner * (sx * sy) + slot_map, AXES, axis=0, tiled=True)  71.5 us
    pallas_call x2, Pallas kernels, fluid_step(): pl.pallas_call(functools.partial(fluid_kernel, opening), grid=(steps + 1,...  23.5 us
    all_to_all x1, waiting for transfers between devices, body(): lax.all_to_all(replies.reshape(ndev, cap, sz), AXES, split_axis=0, concat...  22.8 us
    ppermute x10, starting transfers between devices, neighbours(): return (lax.ppermute(before, axis, up), lax.ppermute(after, axis, down))  17.5 us
    all_to_all x1, starting transfers between devices, body(): lax.all_to_all(outgoing, AXES, split_axis=0, concat_axis=0, tiled=True)  9.89 us
    ppermute x10, waiting for transfers between devices, neighbours(): return (lax.ppermute(before, axis, up), lax.ppermute(after, axis, down))  8.02 us
    pallas_call x1, Pallas kernels, solid_steps(): pl.pallas_call(functools.partial(solid_kernel, rim, cap), in_specs=[in_hb...  5.64 us
    pallas_call x1, Pallas kernels, columns(): pl.pallas_call(functools.partial(columns_kernel, slots), grid=(1,), in_sp...  4.81 us
  transfers between devices with their start and end apart: 12, of which 4 were waited for; matrix products, arithmetic and copies ran while one was open for 0% of the time, Pallas kernels for 20%

profile of v9, /device:TPU:0, one launch (start us, length us, event | category | flops | bytes accessed | tf_op | source)
XLA Modules:
  0.0 188.8 jit_solution(8562175010744696860)
XLA Ops:
  0.6 0.0 copy-start.2
  0.6 1.6 x_faces.1
  2.2 1.3 collective-permute-start.1
  3.5 3.1 %collective-permute-start = (f32[112,1024]{1,0:T(8,128)S(1)}, f32[112,1024]{1,0:T(8,128)S(1)}, u32[]{:S(2)}, u32[]{:S(2)}) collective-permute-start(f32[112,1024]{1,0:T(8,128)S(1)} %get-tuple-element.38.refs_1_), channel_id=1, source_target_pairs={{0,4},{4,8},{8,12},{12,16},{16,20},{20,24},{24,28},{1,5},{5,9},{9,... | collective-permute-start | bytes 1376264 | tf_op jit(solution)/shard_map/ppermute | solution.py:48
  6.6 0.0 copy-done.2
  6.6 0.6 rank.1.where_ref.dest_ref
  7.3 4.2 %pack.1 = (f32[32,96,128]{2,1,0:T(8,128)}, f32[16,64,128]{2,1,0:T(8,128)S(1)}) custom-call(s32[1,1024]{1,0:T(1,128)S(1)} %rank.1.where_ref.dest_ref, f32[16,64,1024]{2,1,0:T(8,128)} %here_ref.1, f32[16,64,128]{2,1,0:T(8,128)} %old_ref.1, s32[16,64,128]{2,1,0:T(8,128)} %mask_ref.1, f32[112,1024]{1,0:T(8,128)S(1)} %get-tuple-element.37.refs_0_, ...), custom_call_target="tpu_custom_call" | custom-call | flops 1610612736 | bytes 2621440 | tf_op jit(solution)/shard_map/pack/pallas_call | solution.py:186
  11.5 0.0 collective-permute-done.1.xhi_ref.hi_ref
  11.5 0.0 collective-permute-done.xlo_ref.lo_ref
  11.5 9.9 %all-to-all-start = ((f32[32,96,128]{2,1,0:T(8,128)}), f32[32,96,128]{2,1,0:T(8,128)}, u32[]{:S(2)}, u32[]{:S(2)}) async-start(f32[32,96,128]{2,1,0:T(8,128)} %get-tuple-element.46), calls=%async_computation | async-start | bytes 3145728 | tf_op jit(solution)/shard_map/all_to_all | solution.py:773
  21.4 2.4 %y_faces.1 = (f32[64,1024]{1,0:T(8,128)S(1)}, f32[64,1024]{1,0:T(8,128)S(1)}, f32[2,32,48,128]{3,2,1,0:T(8,128)}) custom-call(f32[16,1024]{1,0:T(8,128)S(1)} %get-tuple-element.48.near_ref, f32[16,1024]{1,0:T(8,128)S(1)} %get-tuple-element.49.far_ref, f32[16,32,128]{2,1,0:T(8,128)} %temp_ref.5, s32[16,32,128]{2,1,0:T(8,128)} %kind_ref.3, ...), custom_call_target="tpu_custom_call" | custom-call | flops 1000 | bytes 1048576 | tf_op jit(solution)/shard_map/y_faces/pallas_call | solution.py:374
  23.8 3.6 %collective-permute-start.4 = (f32[64,1024]{1,0:T(8,128)S(1)}, f32[64,1024]{1,0:T(8,128)S(1)}, u32[]{:S(2)}, u32[]{:S(2)}) collective-permute-start(f32[64,1024]{1,0:T(8,128)S(1)} %get-tuple-element.50), channel_id=1, source_target_pairs={{0,1},{1,2},{2,3},{4,5},{5,6},{6,7},{8,9},{9,10},{10,11},{12,13},{... | collective-permute-start | bytes 786440 | tf_op jit(solution)/shard_map/ppermute | solution.py:48
  27.4 1.3 collective-permute-start.5
  28.7 0.0 copy-start.9
  28.7 11.9 %fluid_step.2 = (f32[16,64,1024]{2,1,0:T(8,128)}, f32[64,1024]{1,0:T(8,128)}, f32[64,1024]{1,0:T(8,128)}, f32[16,1024]{1,0:T(8,128)S(1)}, f32[16,1024]{1,0:T(8,1...) custom-call(f32[16,64,1024]{2,1,0:T(8,128)} %here_ref.1, f32[112,1024]{1,0:T(8,128)S(1)} %collective-permute-done.xlo_ref.lo_ref, ...), custom_call_target="tpu_custom_call" | custom-call | flops 41943040 | bytes 14680064 | tf_op jit(solution)/shard_map/fluid_step/pallas_call | solution.py:733
  40.7 0.0 copy-start.5
  40.7 0.6 copy-done.5
  41.3 0.0 copy-start.7
  41.3 0.6 copy-done.7
  41.9 0.0 copy-start.3
  41.9 1.8 collective-permute-start.2
  43.7 1.3 collective-permute-start.3
  45.0 0.0 copy-done.9
  45.0 71.5 %all-gather = s32[32,1,1024]{2,1,0:T(1,128)S(1)} all-gather(s32[1,1,1024]{2,1,0:T(1,128)S(1)} %add_bitcast_fusion), channel_id=1, replica_groups=mesh['gx'=8,'gy'=4] {'gx','gy'}, dimensions={0}, use_global_device_ids=true | all-gather | bytes 135168 | tf_op jit(solution)/shard_map/all_gather | solution.py:768
  116.5 4.8 %columns.1.code_ref = s32[32,128]{1,0:T(8,128)S(1)} custom-call(s32[1,1]{1,0:T(1,128)} %bitcast.1.me_ref, s32[32,1024]{1,0:T(8,128)S(1)} %bitcast.12, f32[16,1024]{1,0:T(8,128)S(1)} %get-tuple-element.47.refs_0_.yfirst_ref), custom_call_target="tpu_custom_call" | custom-call | flops 67108864 | bytes 131072 | tf_op jit(solution)/shard_map/columns/pallas_call | solution.py:138
  121.4 0.0 collective-permute-done.4.ylo_ref
  121.4 0.0 collective-permute-done.5.yhi_ref
  121.4 0.0 collective-permute-done.2.xfirst_ref.xlo_ref
  121.4 0.0 collective-permute-done.3.xlast_ref.xhi_ref
  121.4 0.0 all-to-all-done.rows_ref
  121.4 0.0 copy-done.3
  121.4 0.0 copy-start.4
  121.4 0.8 copy-done.4
  122.3 0.0 copy-start.6
  122.3 0.8 copy-done.6
  123.1 0.0 copy-start.8
  123.1 0.8 copy-done.8
  123.9 3.3 %heat_sum.1 = (f32[16,32,128]{2,1,0:T(8,128)S(1)}, f32[144,128]{1,0:T(8,128)S(1)}, f32[144,128]{1,0:T(8,128)S(1)}, f32[16,1024]{1,0:T(8,128)S(1)}, f32[16,1024]{1,0:T(8,128)S(1)}) custom-call(f32[32,96,128]{2,1,0:T(8,128)} %all-to-all-done.rows_ref, s32[32,128]{1,0:T(8,128)S(1)} %columns.1.code_ref, ...), custom_call_target="tpu_custom_call" | custom-call | flops 805306368 | bytes 1572864 | tf_op jit(solution)/shard_map/heat_sum/pallas_call | solution.py:252
  127.3 1.3 collective-permute-start.6
  128.6 1.3 collective-permute-start.7
  129.9 0.0 collective-permute-done.6.lo_ref.hxlo_ref.refs_0_
  129.9 1.8 collective-permute-done.7.hi_ref.hxhi_ref.refs_1_
  131.7 0.1 strips.1
  131.8 1.3 collective-permute-start.8
  133.1 1.3 collective-permute-start.9
  134.4 2.0 %collective-permute-done.8.hylo_ref.refs_4_ = f32[32,1024]{1,0:T(8,128)S(1)} collective-permute-done((f32[32,1024]{1,0:T(8,128)S(1)}, f32[32,1024]{1,0:T(8,128)S(1)}, u32[]{:S(2)}, u32[]{:S(2)}) %collective-permute-start.8) | collective-permute-done | bytes 131104 | tf_op jit(solution)/shard_map/ppermute | solution.py:48
  136.5 4.1 %collective-permute-done.9.hyhi_ref.refs_5_ = f32[32,1024]{1,0:T(8,128)S(1)} collective-permute-done((f32[32,1024]{1,0:T(8,128)S(1)}, f32[32,1024]{1,0:T(8,128)S(1)}, u32[]{:S(2)}, u32[]{:S(2)}) %collective-permute-start.9) | collective-permute-done | bytes 131104 | tf_op jit(solution)/shard_map/ppermute | solution.py:48
  140.6 0.0 copy-start
  140.6 5.6 %solid_steps.1 = (f32[16,32,128]{2,1,0:T(8,128)}, f32[18,48,128]{2,1,0:T(8,128)S(1)}, f32[3072,128]{1,0:T(8,128)}) custom-call(f32[2,32,48,128]{3,2,1,0:T(8,128)} %get-tuple-element.62.state_ref, f32[64,1024]{1,0:T(8,128)S(1)} %collective-permute-done.4.ylo_ref, f32[64,1024]{1,0:T(8,128)S(1)} %collective-permute-done.5.yhi_ref, ...), custom_call_target="tpu_custom_call" | custom-call | flops 805306368 | bytes 1572864 | tf_op jit(solution)/shard_map/solid_steps/pallas_call | solution.py:512
  146.2 0.0 copy-done
  146.2 2.7 %all-to-all-start.1 = ((f32[32,96,128]{2,1,0:T(8,128)}), f32[32,96,128]{2,1,0:T(8,128)S(1)}, u32[]{:S(2)}, u32[]{:S(2)}) async-start(f32[32,96,128]{2,1,0:T(8,128)} %bitcast.14), calls=%async_computation.1 | async-start | bytes 3145728 | tf_op jit(solution)/shard_map/all_to_all | solution.py:793
  149.0 2.1 %stress.1 = (f32[3,16,32,128]{3,2,1,0:T(8,128)}, f32[8,128]{1,0:T(8,128)S(1)}) custom-call(f32[18,48,128]{2,1,0:T(8,128)S(1)} %get-tuple-element.63.sigma_ref), custom_call_target="tpu_custom_call" | custom-call | flops 655360 | bytes 1048576 | tf_op jit(solution)/shard_map/stress/pallas_call | solution.py:559
  151.1 0.0 copy-start.1
  151.1 0.9 copy-done.1
  152.0 11.6 %fluid_step.3 = (f32[16,64,1024]{2,1,0:T(8,128)}, f32[8,128]{1,0:T(8,128)S(1)}) custom-call(f32[16,64,1024]{2,1,0:T(8,128)} %get-tuple-element.43.here_ref, f32[64,1024]{1,0:T(8,128)S(1)} %collective-permute-done.2.xfirst_ref.xlo_ref, f32[64,1024]{1,0:T(8,128)S(1)} %collective-permute-done.3.xlast_ref.xhi_ref, bf16[3,16,64,1024]{3,2,1,0:T(8,128)(2,1)} %speed_ref.3, ...), custom_call_target="tpu_custom_call" | custom-call | flops 41943040 | bytes 14680064 | tf_op jit(solution)/shard_map/fluid_step/pallas_call | solution.py:733
  163.6 22.8 %all-to-all-done.1 = f32[32,96,128]{2,1,0:T(8,128)S(1)} async-done(((f32[32,96,128]{2,1,0:T(8,128)}), f32[32,96,128]{2,1,0:T(8,128)S(1)}, u32[]{:S(2)}, u32[]{:S(2)}) %all-to-all-start.1) | async-done | bytes 1572896 | tf_op jit(solution)/shard_map/all_to_all | solution.py:793
  186.4 2.4 %unpack.1 = f32[1024,128]{1,0:T(8,128)} custom-call(s32[1,1024]{1,0:T(1,128)S(1)} %rank.1.where_ref.dest_ref, f32[3072,128]{1,0:T(8,128)S(1)} %bitcast.11, f32[8,128]{1,0:T(8,128)S(1)} %get-tuple-element.67.refs_0_), custom_call_target="tpu_custom_call" | custom-call | flops 131072 | bytes 1048576 | tf_op jit(solution)/shard_map/unpack/pallas_call | solution.py:587
  (2 shorter events, 0.0 us)
Async XLA Ops:
  0.6 6.0 %copy-start.2 = (s32[1,1024,1]{1,2,0:T(1,128)S(1)}, s32[1,1024,1]{1,2,0:T(1,128)}, u32[]{:S(2)}) copy-start(s32[1,1024,1]{1,2,0:T(1,128)} %param.12) | copy-start | bytes 12292
  2.2 9.2 %collective-permute-start.1 = (f32[112,1024]{1,0:T(8,128)S(1)}, f32[112,1024]{1,0:T(8,128)S(1)}, u32[]{:S(2)}, u32[]{:S(2)}) collective-permute-start(f32[112,1024]{1,0:T(8,128)S(1)} %get-tuple-element.37.refs_0_), channel_id=1, source_target_pairs={{4,0},{8,4},{12,8},{16,12},{20,16},{24,20},{28,24},{5,1},{9,5},{13... | collective-permute-start | bytes 1376264 | tf_op jit(solution)/shard_map/ppermute | solution.py:48
  3.5 7.9 %collective-permute-start = (f32[112,1024]{1,0:T(8,128)S(1)}, f32[112,1024]{1,0:T(8,128)S(1)}, u32[]{:S(2)}, u32[]{:S(2)}) collective-permute-start(f32[112,1024]{1,0:T(8,128)S(1)} %get-tuple-element.38.refs_1_), channel_id=1, source_target_pairs={{0,4},{4,8},{8,12},{12,16},{16,20},{20,24},{24,28},{1,5},{5,9},{9,... | collective-permute-start | bytes 1376264 | tf_op jit(solution)/shard_map/ppermute | solution.py:48
  11.5 109.9 %all-to-all-start = ((f32[32,96,128]{2,1,0:T(8,128)}), f32[32,96,128]{2,1,0:T(8,128)}, u32[]{:S(2)}, u32[]{:S(2)}) async-start(f32[32,96,128]{2,1,0:T(8,128)} %get-tuple-element.46), calls=%async_computation | async-start | bytes 3145728 | tf_op jit(solution)/shard_map/all_to_all | solution.py:773
  23.8 97.6 %collective-permute-start.4 = (f32[64,1024]{1,0:T(8,128)S(1)}, f32[64,1024]{1,0:T(8,128)S(1)}, u32[]{:S(2)}, u32[]{:S(2)}) collective-permute-start(f32[64,1024]{1,0:T(8,128)S(1)} %get-tuple-element.50), channel_id=1, source_target_pairs={{0,1},{1,2},{2,3},{4,5},{5,6},{6,7},{8,9},{9,10},{10,11},{12,13},{... | collective-permute-start | bytes 786440 | tf_op jit(solution)/shard_map/ppermute | solution.py:48
  27.4 94.0 %collective-permute-start.5 = (f32[64,1024]{1,0:T(8,128)S(1)}, f32[64,1024]{1,0:T(8,128)S(1)}, u32[]{:S(2)}, u32[]{:S(2)}) collective-permute-start(f32[64,1024]{1,0:T(8,128)S(1)} %get-tuple-element.51), channel_id=1, source_target_pairs={{1,0},{2,1},{3,2},{5,4},{6,5},{7,6},{9,8},{10,9},{11,10},{13,12},{... | collective-permute-start | bytes 786440 | tf_op jit(solution)/shard_map/ppermute | solution.py:48
  28.7 16.3 %copy-start.9 = (s32[1,1024]{1,0:T(1,128)S(1)}, s32[1,1024]{1,0:T(1,128)}, u32[]{:S(2)}) copy-start(s32[1,1024]{1,0:T(1,128)} %param.13) | copy-start | bytes 12292
  40.7 0.6 copy-start.5
  41.3 0.6 copy-start.7
  41.9 79.5 %copy-start.3 = (f32[16,1024]{1,0:T(8,128)}, f32[16,1024]{1,0:T(8,128)S(1)}, u32[]{:S(2)}) copy-start(f32[16,1024]{1,0:T(8,128)S(1)} %get-tuple-element.52.ylast_ref) | copy-start | bytes 196612
  41.9 79.5 %collective-permute-start.2 = (f32[64,1024]{1,0:T(8,128)}, f32[64,1024]{1,0:T(8,128)S(1)}, u32[]{:S(2)}, u32[]{:S(2)}) collective-permute-start(f32[64,1024]{1,0:T(8,128)} %get-tuple-element.44), channel_id=1, source_target_pairs={{0,4},{4,8},{8,12},{12,16},{16,20},{20,24},{24,28},{1,5},{5,9},{9,... | collective-permute-start | bytes 786440 | tf_op jit(solution)/shard_map/ppermute | solution.py:48
  43.7 77.7 %collective-permute-start.3 = (f32[64,1024]{1,0:T(8,128)}, f32[64,1024]{1,0:T(8,128)S(1)}, u32[]{:S(2)}, u32[]{:S(2)}) collective-permute-start(f32[64,1024]{1,0:T(8,128)} %get-tuple-element.45), channel_id=1, source_target_pairs={{4,0},{8,4},{12,8},{16,12},{20,16},{24,20},{28,24},{5,1},{9,5},{13... | collective-permute-start | bytes 786440 | tf_op jit(solution)/shard_map/ppermute | solution.py:48
  121.4 0.8 copy-start.4
  122.3 0.8 copy-start.6
  123.1 0.8 copy-start.8
  127.3 2.6 %collective-permute-start.6 = (f32[144,128]{1,0:T(8,128)S(1)}, f32[144,128]{1,0:T(8,128)S(1)}, u32[]{:S(2)}, u32[]{:S(2)}) collective-permute-start(f32[144,128]{1,0:T(8,128)S(1)} %get-tuple-element.55), channel_id=1, source_target_pairs={{0,4},{4,8},{8,12},{12,16},{16,20},{20,24},{24,28},{1,5},{5,9},{9,... | collective-permute-start | bytes 221192 | tf_op jit(solution)/shard_map/ppermute | solution.py:48
  128.6 3.2 %collective-permute-start.7 = (f32[144,128]{1,0:T(8,128)S(1)}, f32[144,128]{1,0:T(8,128)S(1)}, u32[]{:S(2)}, u32[]{:S(2)}) collective-permute-start(f32[144,128]{1,0:T(8,128)S(1)} %get-tuple-element.56), channel_id=1, source_target_pairs={{4,0},{8,4},{12,8},{16,12},{20,16},{24,20},{28,24},{5,1},{9,5},{13... | collective-permute-start | bytes 221192 | tf_op jit(solution)/shard_map/ppermute | solution.py:48
  131.8 4.6 %collective-permute-start.8 = (f32[32,1024]{1,0:T(8,128)S(1)}, f32[32,1024]{1,0:T(8,128)S(1)}, u32[]{:S(2)}, u32[]{:S(2)}) collective-permute-start(f32[32,1024]{1,0:T(8,128)S(1)} %get-tuple-element.60), channel_id=1, source_target_pairs={{0,1},{1,2},{2,3},{4,5},{5,6},{6,7},{8,9},{9,10},{10,11},{12,13},{... | collective-permute-start | bytes 393224 | tf_op jit(solution)/shard_map/ppermute | solution.py:48
  133.1 7.5 %collective-permute-start.9 = (f32[32,1024]{1,0:T(8,128)S(1)}, f32[32,1024]{1,0:T(8,128)S(1)}, u32[]{:S(2)}, u32[]{:S(2)}) collective-permute-start(f32[32,1024]{1,0:T(8,128)S(1)} %get-tuple-element.61), channel_id=1, source_target_pairs={{1,0},{2,1},{3,2},{5,4},{6,5},{7,6},{9,8},{10,9},{11,10},{13,12},{... | collective-permute-start | bytes 393224 | tf_op jit(solution)/shard_map/ppermute | solution.py:48
  140.6 5.6 %copy-start = (f32[32,1024]{1,0:T(8,128)}, f32[32,1024]{1,0:T(8,128)S(1)}, u32[]{:S(2)}) copy-start(f32[32,1024]{1,0:T(8,128)S(1)} %collective-permute-done.9.hyhi_ref.refs_5_) | copy-start | bytes 393220
  146.2 40.2 %all-to-all-start.1 = ((f32[32,96,128]{2,1,0:T(8,128)}), f32[32,96,128]{2,1,0:T(8,128)S(1)}, u32[]{:S(2)}, u32[]{:S(2)}) async-start(f32[32,96,128]{2,1,0:T(8,128)} %bitcast.14), calls=%async_computation.1 | async-start | bytes 3145728 | tf_op jit(solution)/shard_map/all_to_all | solution.py:793
  151.1 0.9 copy-start.1

commit v10 on v8

--- a/solution.py
+++ b/solution.py
@@ -164,7 +164,7 @@
             pltpu.VMEM((ndev, tall, row_len), F32),
             pltpu.SemaphoreType.DMA((GROUPS,)),
         ],
-        compiler_params=params(24),
+        compiler_params=params(18),
         cost_estimate=cost(4 * ndev * tall * rows * row_len, 5 * rows * row_len * 4),
         name="pack",
     )(where, code, far(temp), far(old), far(mask), *after)
@@ -217,8 +217,10 @@
     edge = (thin * sy + 2 * (line[1] // LANE), row_len)
     return pl.pallas_call(
         functools.partial(heat_kernel, cap, thin),
-        in_specs=[in_vmem] + [anywhere] * 2 + [in_vmem] * 6,
-        out_specs=[in_vmem] * 6,
+        grid=(1,),
+        in_specs=[whole(incoming.shape)] + [anywhere] * 2 + [whole(x.shape) for x in edges],
+        out_specs=[whole(block), whole(edge), whole(edge), whole(line), whole(line)]
+        + [whole((ndev, row_len))],
         out_shape=[
             jax.ShapeDtypeStruct(block, F32),
             jax.ShapeDtypeStruct(edge, F32),
@@ -227,10 +229,10 @@
             jax.ShapeDtypeStruct(line, F32),
             jax.ShapeDtypeStruct((ndev, row_len), jnp.int32),
         ],
-        compiler_params=params(20),
+        compiler_params=params(14),
         cost_estimate=cost(4 * ndev * tall * sx * sy * row_len, 4 * ndev * tall * row_len),
         name="heat_sum",
-    )(near(incoming), *faces, *edges)
+    )(incoming, *faces, *edges)
 
 
 def put_rim(ref, base, slabs):
@@ -342,7 +344,7 @@
         out_specs=[whole((height, depth))] * 2 + [whole((2, long, sy + 2 * OFF, sz))],
         out_shape=[jax.ShapeDtypeStruct((height, depth), F32)] * 2
         + [pltpu.HBM((2, long, sy + 2 * OFF, sz), F32)],
-        compiler_params=params(16),
+        compiler_params=params(10),
         cost_estimate=cost(1000, 4 * 4 * height * depth),
         name="y_faces",
     )(*args)
@@ -391,25 +393,67 @@
     return out
 
 
-def solid_kernel(rim, cap, state_ref, ylo_ref, yhi_ref,
-                 heat_ref, hxlo_ref, hxhi_ref, hylo_ref, hyhi_ref, code_ref,
-                 next_ref, sigma_ref, reply_ref, work_ref, src_ref, rhs_ref,
-                 pick_ref, stage_ref, load, sems):
+def ready_kernel(rim, cap, state_ref, ylo_ref, yhi_ref, code_ref,
+                 temp_ref, cond_ref, sigma_ref, pick_ref):
+    _, long, height, sz = state_ref.shape
+    ndev = code_ref.shape[0]
+    slots = pick_ref.shape[1]
+    sx = sigma_ref.shape[0] - 2
+    sy = height - 2 * OFF
+    pieces = long // PART
+    turned = jnp.transpose(code_ref[...])
+    names = lax.broadcasted_iota(jnp.int32, (cap, slots), 1)
+    for source in range(0, ndev, 2):
+        pick_ref[source * cap:(source + 2) * cap, :] = jnp.concatenate(
+            [
+                jnp.where(names == turned[:cap, one:one + 1], 1.0, 0.0)
+                for one in (source, source + 1)
+            ],
+            axis=0,
+        ).astype(BF16)
+    base = ylo_ref.shape[0] - rim_rows(2 * rim * pieces, ylo_ref.shape[1])
+    for which, ref in enumerate((temp_ref, cond_ref)):
+        ref[...] = state_ref[which]
+        for k in range(rim):
+            for h in range(pieces):
+                n = (which * rim + k) * pieces + h
+                cut = slice(h * PART, (h + 1) * PART)
+                ref[cut, OFF - rim + k, :] = get_rim(ylo_ref, base, n)
+                ref[cut, OFF + sy + k, :] = get_rim(yhi_ref, base, n)
+    kind = cond_ref[...]
+    sigma_ref[...] = table(kind[rim - 1:rim + sx + 1], modulus_table)
+    cond_ref[...] = solid_step * table(kind, conduct_table)
+
+
+def ready(rim, cap, state, ylo, yhi, code, block):
+    sx, sy, sz = block
+    _, long, height, _ = state.shape
+    ndev = code.shape[0]
+    args = (far(state), ylo, yhi, code)
+    return pl.pallas_call(
+        functools.partial(ready_kernel, rim, cap),
+        grid=(1,),
+        in_specs=[whole(x.shape) for x in args],
+        out_specs=[in_vmem] * 4,
+        out_shape=[
+            pltpu.VMEM((long, height, sz), F32),
+            pltpu.VMEM((long, height, sz), F32),
+            pltpu.VMEM((sx + 2, height, sz), F32),
+            pltpu.VMEM((ndev * cap, sx * sy), BF16),
+        ],
+        compiler_params=params(14),
+        cost_estimate=cost(4 * ndev * cap * sx * sy, 4 * ndev * cap * sx * sy),
+        name="ready",
+    )(*args)
+
+
+def solid_kernel(rim, start_ref, cond_ref, modulus_ref, pick_ref,
+                 heat_ref, hxlo_ref, hxhi_ref, hylo_ref, hyhi_ref,
+                 next_ref, sigma_ref, reply_ref, even_ref, odd_ref, src_ref, rhs_ref,
+                 stage_ref, sems):
     sx, sy, sz = heat_ref.shape
-    ndev = code_ref.shape[0]
-    slots = sx * sy
     wide = sx + 2 * rim
     thin = rim - 1
-    long = state_ref.shape[1]
-    pieces = long // PART
-    loading = pltpu.make_async_copy(state_ref, work_ref.at[:2], load)
-    loading.start()
-    turned = jnp.transpose(code_ref[...])
-    names = lax.broadcasted_iota(jnp.int32, (cap, slots), 1)
-    for source in range(ndev):
-        pick_ref[source * cap:(source + 1) * cap, :] = ones_where(
-            names == turned[:cap, source:source + 1]
-        )
     edge = thin * sy
     src_ref[rim:rim + sx, OFF:OFF + sy, :] = heat_ref[...]
     src_ref[1:rim, OFF:OFF + sy, :] = hxlo_ref[:edge, :].reshape(thin, sy, sz)
@@ -423,26 +467,13 @@
             cut = slice(1 + h * PART, 1 + h * PART + count)
             src_ref[cut, OFF - thin + k, :] = get_rim(hylo_ref, base, n)[:count]
             src_ref[cut, OFF + sy + k, :] = get_rim(hyhi_ref, base, n)[:count]
-    loading.wait()
-    base = ylo_ref.shape[0] - rim_rows(2 * rim * pieces, ylo_ref.shape[1])
-    for which in range(2):
-        for k in range(rim):
-            for h in range(pieces):
-                n = (which * rim + k) * pieces + h
-                cut = slice(h * PART, (h + 1) * PART)
-                work_ref[which, cut, OFF - rim + k, :] = get_rim(ylo_ref, base, n)
-                work_ref[which, cut, OFF + sy + k, :] = get_rim(yhi_ref, base, n)
-    temp_ref, cond_ref, work_ref = work_ref.at[0], work_ref.at[1], work_ref.at[2]
-    kind = cond_ref[:wide]
-    sigma_ref[...] = table(kind[rim - 1:rim + sx + 1], modulus_table)
-    cond_ref[:wide] = solid_step * table(kind, conduct_table)
     src_ref[...] = (solid_step * source_gain) * src_ref[...]
-    height = state_ref.shape[2]
+    height = start_ref.shape[1]
     first = lax.broadcasted_iota(jnp.int32, (height, sz), 1) == 0
     last = lax.broadcasted_iota(jnp.int32, (height, sz), 1) == sz - 1
-    pair = (temp_ref, work_ref)
+    now = start_ref
     for turn in range(rim - 1):
-        now, later = pair[turn % 2], pair[(turn + 1) % 2]
+        later = (odd_ref, even_ref)[turn % 2]
         for x in range(1 + turn, wide - 1 - turn):
             centre = now[x]
             beside = now[x - 1] + now[x + 1]
@@ -450,14 +481,14 @@
             beside += jnp.where(first, 0.0, pltpu.roll(centre, 1, 1))
             beside += jnp.where(last, 0.0, pltpu.roll(centre, sz - 1, 1))
             later[x] = centre + (cond_ref[x] * (beside - 6.0 * centre) + src_ref[x])
-    final = pair[(rim - 1) % 2]
-    solid = final[rim:rim + sx, OFF:OFF + sy, :]
+        now = later
+    solid = now[rim:rim + sx, OFF:OFF + sy, :]
     next_ref[...] = solid
-    sigma_ref[...] = sigma_ref[...] * final[rim - 1:rim + sx + 1]
+    sigma_ref[...] = modulus_ref[...] * now[rim - 1:rim + sx + 1]
     high, low = halves(solid.reshape(sx * sy, sz))
     rhs_ref[:, :sz] = high
     rhs_ref[:, sz:] = low
-    block = ndev // GROUPS * cap
+    block = pick_ref.shape[0] // GROUPS
     copies = []
     for index in range(GROUPS):
         cut = slice(index * block, (index + 1) * block)
@@ -469,32 +500,30 @@
         copy.wait()
 
 
-def solid_steps(rim, cap, state, state_rim, heat, heat_rim, code):
+def solid_steps(rim, prepared, heat, heat_rim):
     sx, sy, sz = heat.shape
-    _, long, height, _ = state.shape
-    total = code.shape[0] * cap
-    return pl.pallas_call(
-        functools.partial(solid_kernel, rim, cap),
-        in_specs=[in_hbm] + [in_vmem] * 8,
+    long, height, _ = prepared[0].shape
+    total = prepared[3].shape[0]
+    return pl.pallas_call(
+        functools.partial(solid_kernel, rim),
+        in_specs=[in_vmem] * 9,
         out_specs=[in_vmem, in_vmem, in_hbm],
         out_shape=[
             jax.ShapeDtypeStruct((sx, sy, sz), F32),
             jax.ShapeDtypeStruct((sx + 2, height, sz), F32),
             pltpu.HBM((total, sz), F32),
         ],
-        scratch_shapes=[
-            pltpu.VMEM((3, long, height, sz), F32),
+        scratch_shapes=[pltpu.VMEM((long, height, sz), F32)] * 2
+        + [
             pltpu.VMEM((sx + 2 * rim, height, sz), F32),
             pltpu.VMEM((sx * sy, 2 * sz), BF16),
-            pltpu.VMEM((total, sx * sy), BF16),
             pltpu.VMEM((total, sz), F32),
-            pltpu.SemaphoreType.DMA,
             pltpu.SemaphoreType.DMA((GROUPS,)),
         ],
-        compiler_params=params(24),
+        compiler_params=params(14),
         cost_estimate=cost(4 * total * sx * sy * sz, 4 * total * sz),
         name="solid_steps",
-    )(far(state), *state_rim, heat, *heat_rim, code)
+    )(*[near(x) for x in prepared], heat, *heat_rim)
 
 
 def stress_kernel(sigma_ref, out_ref, tick_ref):
@@ -709,7 +738,7 @@
         out_specs=outs,
         out_shape=shapes,
         scratch_shapes=[pltpu.VMEM((RING, cy + 2 * OFF, depth), F32)],
-        compiler_params=params(24),
+        compiler_params=params(16),
         cost_estimate=cost(40 * cx * cy * depth, 14 * cx * cy * depth),
         name="fluid_step",
     )(far(temp), *sides, far(velocity), flux, *lines, *after)
@@ -747,9 +776,8 @@
     hxlo, hxhi = neighbours(last, first, "gx")
     first, last = strips(thin, heat, hxlo, hxhi, left, right)
     hylo, hyhi = neighbours(last, first, "gy")
-    solid, sigma, replies = solid_steps(
-        rim, cap, state, (ylo, yhi), heat, (hxlo, hxhi, hylo, hyhi), code
-    )
+    prepared = ready(rim, cap, state, ylo, yhi, code, heat.shape)
+    solid, sigma, replies = solid_steps(rim, prepared, heat, (hxlo, hxhi, hylo, hyhi))
     returned = lax.all_to_all(
         replies.reshape(ndev, cap, sz), AXES, split_axis=0, concat_axis=0, tiled=True
     )

time: 135 us -> 134 us (level)
  waiting for transfers between devices: 50.7 us -> 47.7 us
    ppermute x10, waiting for transfers between devices: 17 us -> 14.1 us  [neighbours(): return (lax.ppermute(before, axis, up), lax.ppermute(after, axis, down))]
    pallas_call x2 -> x3, Pallas kernels: 9.24 us -> 10.2 us  [the longest x1 3.76 us: solid_steps(): pl.pallas_call(functools.partial(solid_kernel, rim), in_specs=[in_vmem] *...]
  transfers between devices with their start and end apart: 12 -> 12, of which waited for: 6 -> 5; matrix products, arithmetic and copies ran while one was open for 0% -> 0% of each run, Pallas kernels for 25% -> 27%
where the time goes in v10:
time: 134 us; the launch traced here: 132 us
  waiting for transfers between devices  47.7 us (36%)
  Pallas kernels  47.4 us (35%)
  starting transfers between devices  35.4 us (26%)
    pallas_call x2, Pallas kernels, fluid_step(): pl.pallas_call(functools.partial(fluid_kernel, opening), grid=(steps + 1,...  23.3 us
    all_to_all x1, waiting for transfers between devices, body(): lax.all_to_all(replies.reshape(ndev, cap, sz), AXES, split_axis=0, concat...  22.8 us
    ppermute x10, starting transfers between devices, neighbours(): return (lax.ppermute(before, axis, up), lax.ppermute(after, axis, down))  18.2 us
    ppermute x10, waiting for transfers between devices, neighbours(): return (lax.ppermute(before, axis, up), lax.ppermute(after, axis, down))  14.1 us
    all_to_all x1, waiting for transfers between devices, body(): lax.all_to_all(outgoing, AXES, split_axis=0, concat_axis=0, tiled=True)  10.9 us
    all_to_all x1, starting transfers between devices, body(): lax.all_to_all(outgoing, AXES, split_axis=0, concat_axis=0, tiled=True)  9.41 us
    all_to_all x1, starting transfers between devices, body(): lax.all_to_all(replies.reshape(ndev, cap, sz), AXES, split_axis=0, concat...  7.77 us
    pallas_call x1, Pallas kernels, pack(): pl.pallas_call(functools.partial(pack_kernel, cap), grid=(1,), in_specs=[...  4.41 us
  transfers between devices with their start and end apart: 12, of which 5 were waited for; matrix products, arithmetic and copies ran while one was open for 0% of the time, Pallas kernels for 27%

profile of v10, /device:TPU:0, one launch (start us, length us, event | category | flops | bytes accessed | tf_op | source)
XLA Modules:
  0.0 132.4 jit_solution(15113832815223148898)
XLA Ops:
  0.6 0.0 copy-start.3
  0.6 0.0 copy-start.2
  0.7 1.6 %x_faces.1 = (f32[112,1024]{1,0:T(8,128)S(1)}, f32[112,1024]{1,0:T(8,128)S(1)}, f32[16,1024]{1,0:T(8,128)S(1)}, f32[16,1024]{1,0:T(8,128)S(1)}) custom-call(f32[16,64,1024]{2,1,0:T(8,128)} %here_ref.1, f32[16,64,1024]{2,1,0:T(8,128)} %here_ref.1, f32[16,64,1024]{2,1,0:T(8,128)} %here_ref.1, f32[16,64,1024]{2,1,0:T(8,128)} %here_ref.1, ...), custom_call_target="tpu_custom_call" | custom-call | flops 1000 | bytes 1835008 | tf_op jit(solution)/shard_map/x_faces/pallas_call | solution.py:282
  2.3 1.3 collective-permute-start.1
  3.6 3.1 %collective-permute-start = (f32[112,1024]{1,0:T(8,128)S(1)}, f32[112,1024]{1,0:T(8,128)S(1)}, u32[]{:S(2)}, u32[]{:S(2)}) collective-permute-start(f32[112,1024]{1,0:T(8,128)S(1)} %get-tuple-element.48.refs_1_), channel_id=1, source_target_pairs={{0,4},{4,8},{8,12},{12,16},{16,20},{20,24},{24,28},{1,5},{5,9},{9,... | collective-permute-start | bytes 1376264 | tf_op jit(solution)/shard_map/ppermute | solution.py:48
  6.6 0.0 copy-done.3
  6.6 0.0 copy-done.2
  6.6 0.9 rank.1
  7.5 4.4 %pack.1 = (f32[32,104,128]{2,1,0:T(8,128)}, f32[16,64,128]{2,1,0:T(8,128)S(1)}) custom-call(s32[1,1024]{1,0:T(1,128)S(1)} %get-tuple-element.45.where_ref, f32[32,128]{1,0:T(8,128)S(1)} %get-tuple-element.46.code_ref, f32[16,64,1024]{2,1,0:T(8,128)} %here_ref.1, f32[16,64,128]{2,1,0:T(8,128)} %old_ref.1, s32[16,64,128]{2,1,0:T(8,128)} %mask_ref.1, ...), custom_call_target="tpu_custom_call" | custom-call | flops 1744830464 | bytes 2621440 | tf_op jit(solution)/shard_map/pack/pallas_call | solution.py:151
  12.0 0.0 collective-permute-done.1.xhi_ref.hi_ref
  12.0 0.0 collective-permute-done.xlo_ref.lo_ref
  12.0 9.4 %all-to-all-start = ((f32[32,104,128]{2,1,0:T(8,128)}), f32[32,104,128]{2,1,0:T(8,128)}, u32[]{:S(2)}, u32[]{:S(2)}) async-start(f32[32,104,128]{2,1,0:T(8,128)} %get-tuple-element.56), calls=%async_computation | async-start | bytes 3407872 | tf_op jit(solution)/shard_map/all_to_all | solution.py:763
  21.4 2.4 %y_faces.1 = (f32[64,1024]{1,0:T(8,128)S(1)}, f32[64,1024]{1,0:T(8,128)S(1)}, f32[2,32,48,128]{3,2,1,0:T(8,128)}) custom-call(f32[16,1024]{1,0:T(8,128)S(1)} %get-tuple-element.57.near_ref, f32[16,1024]{1,0:T(8,128)S(1)} %get-tuple-element.58.far_ref, f32[16,32,128]{2,1,0:T(8,128)} %temp_ref.5, s32[16,32,128]{2,1,0:T(8,128)} %kind_ref.3, ...), custom_call_target="tpu_custom_call" | custom-call | flops 1000 | bytes 1048576 | tf_op jit(solution)/shard_map/y_faces/pallas_call | solution.py:340
  23.8 3.6 %collective-permute-start.4 = (f32[64,1024]{1,0:T(8,128)S(1)}, f32[64,1024]{1,0:T(8,128)S(1)}, u32[]{:S(2)}, u32[]{:S(2)}) collective-permute-start(f32[64,1024]{1,0:T(8,128)S(1)} %get-tuple-element.59), channel_id=1, source_target_pairs={{0,1},{1,2},{2,3},{4,5},{5,6},{6,7},{8,9},{9,10},{10,11},{12,13},{... | collective-permute-start | bytes 786440 | tf_op jit(solution)/shard_map/ppermute | solution.py:48
  27.4 1.3 collective-permute-start.5
  28.7 11.7 %fluid_step.2 = (f32[16,64,1024]{2,1,0:T(8,128)}, f32[64,1024]{1,0:T(8,128)S(1)}, f32[64,1024]{1,0:T(8,128)S(1)}, f32[16,1024]{1,0:T(8,128)S(1)}, f32[16,1024]{1...) custom-call(f32[16,64,1024]{2,1,0:T(8,128)} %here_ref.1, ...), custom_call_target="tpu_custom_call" | custom-call | flops 41943040 | bytes 14680064 | tf_op jit(solution)/shard_map/fluid_step/pallas_call | solution.py:726
  40.4 1.8 %collective-permute-start.2 = (f32[64,1024]{1,0:T(8,128)S(1)}, f32[64,1024]{1,0:T(8,128)S(1)}, u32[]{:S(2)}, u32[]{:S(2)}) collective-permute-start(f32[64,1024]{1,0:T(8,128)S(1)} %get-tuple-element.54), channel_id=1, source_target_pairs={{0,4},{4,8},{8,12},{12,16},{16,20},{20,24},{24,28},{1,5},{5,9},{9,... | collective-permute-start | bytes 786440 | tf_op jit(solution)/shard_map/ppermute | solution.py:48
  42.2 1.3 collective-permute-start.3
  43.5 0.0 collective-permute-done.4.ylo_ref
  43.5 7.3 %collective-permute-done.5.yhi_ref = f32[64,1024]{1,0:T(8,128)S(1)} collective-permute-done((f32[64,1024]{1,0:T(8,128)S(1)}, f32[64,1024]{1,0:T(8,128)S(1)}, u32[]{:S(2)}, u32[]{:S(2)}) %collective-permute-start.5) | collective-permute-done | bytes 262176 | tf_op jit(solution)/shard_map/ppermute | solution.py:48
  50.8 0.0 collective-permute-done.2.xfirst_ref.xlo_ref
  50.8 0.0 collective-permute-done.3.xlast_ref.xhi_ref
  50.8 0.0 copy-start
  50.8 10.9 %all-to-all-done.rows_ref = f32[32,104,128]{2,1,0:T(8,128)} async-done(((f32[32,104,128]{2,1,0:T(8,128)}), f32[32,104,128]{2,1,0:T(8,128)}, u32[]{:S(2)}, u32[]{:S(2)}) %all-to-all-start) | async-done | bytes 1703968 | tf_op jit(solution)/shard_map/all_to_all | solution.py:763
  61.7 3.6 %heat_sum.1 = (f32[16,32,128]{2,1,0:T(8,128)S(1)}, f32[144,128]{1,0:T(8,128)S(1)}, f32[144,128]{1,0:T(8,128)S(1)}, f32[16,1024]{1,0:T(8,128)S(1)}, f32[16,1024]{1,0:T(8,128)S(1)}, /*index=5*/s32[32,128]{1,0:T(8,128)S(1)}) custom-call(f32[32,104,128]{2,1,0:T(8,128)} %all-to-all-done.rows_ref, f32[64,1024]{1,0:T(8,128)S(1)} %collective-permute-done.2.xfirst_ref.xlo_ref, ...), custom_call_target="tpu_custom_call" | custom-call | flops 872415232 | bytes 1703936 | tf_op jit(solution)/shard_map/heat_sum/pallas_call | solution.py:218
  65.3 0.0 copy-done
  65.3 1.5 %collective-permute-start.6 = (f32[144,128]{1,0:T(8,128)S(1)}, f32[144,128]{1,0:T(8,128)S(1)}, u32[]{:S(2)}, u32[]{:S(2)}) collective-permute-start(f32[144,128]{1,0:T(8,128)S(1)} %get-tuple-element.65), channel_id=1, source_target_pairs={{0,4},{4,8},{8,12},{12,16},{16,20},{20,24},{24,28},{1,5},{5,9},{9,... | collective-permute-start | bytes 221192 | tf_op jit(solution)/shard_map/ppermute | solution.py:48
  66.8 1.3 collective-permute-start.7
  68.1 0.0 collective-permute-done.6.lo_ref.hxlo_ref.refs_0_
  68.2 3.6 %collective-permute-done.7.hi_ref.hxhi_ref.refs_1_ = f32[144,128]{1,0:T(8,128)S(1)} collective-permute-done((f32[144,128]{1,0:T(8,128)S(1)}, f32[144,128]{1,0:T(8,128)S(1)}, u32[]{:S(2)}, u32[]{:S(2)}) %collective-permute-start.7) | collective-permute-done | bytes 73760 | tf_op jit(solution)/shard_map/ppermute | solution.py:48
  71.7 0.1 strips.1
  71.8 1.8 %collective-permute-start.8 = (f32[32,1024]{1,0:T(8,128)S(1)}, f32[32,1024]{1,0:T(8,128)S(1)}, u32[]{:S(2)}, u32[]{:S(2)}) collective-permute-start(f32[32,1024]{1,0:T(8,128)S(1)} %get-tuple-element.70), channel_id=1, source_target_pairs={{0,1},{1,2},{2,3},{4,5},{5,6},{6,7},{8,9},{9,10},{10,11},{12,13},{... | collective-permute-start | bytes 393224 | tf_op jit(solution)/shard_map/ppermute | solution.py:48
  73.6 1.3 collective-permute-start.9
  74.9 2.8 %ready.1 = (f32[32,48,128]{2,1,0:T(8,128)S(1)}, f32[32,48,128]{2,1,0:T(8,128)S(1)}, f32[18,48,128]{2,1,0:T(8,128)S(1)}, bf16[3072,512]{1,0:T(8,128)(2,1)S(1)}) custom-call(f32[2,32,48,128]{3,2,1,0:T(8,128)} %get-tuple-element.72.state_ref, f32[64,1024]{1,0:T(8,128)S(1)} %collective-permute-done.4.ylo_ref, f32[64,1024]{1,0:T(8,128)S(1)} %collective-permute-done.5.yhi_ref, ...), custom_call_target="tpu_custom_call" | custom-call | flops 6291456 | bytes 6291456 | tf_op jit(solution)/shard_map/ready/pallas_call | solution.py:433
  77.7 0.0 collective-permute-done.8.hylo_ref.refs_4_
  77.7 3.2 %collective-permute-done.9.hyhi_ref.refs_5_ = f32[32,1024]{1,0:T(8,128)S(1)} collective-permute-done((f32[32,1024]{1,0:T(8,128)S(1)}, f32[32,1024]{1,0:T(8,128)S(1)}, u32[]{:S(2)}, u32[]{:S(2)}) %collective-permute-start.9) | collective-permute-done | bytes 131104 | tf_op jit(solution)/shard_map/ppermute | solution.py:48
  81.0 3.8 %solid_steps.1 = (f32[16,32,128]{2,1,0:T(8,128)}, f32[18,48,128]{2,1,0:T(8,128)S(1)}, f32[3072,128]{1,0:T(8,128)}) custom-call(f32[32,48,128]{2,1,0:T(8,128)S(1)} %get-tuple-element.74.start_ref, f32[32,48,128]{2,1,0:T(8,128)S(1)} %get-tuple-element.75.cond_ref, f32[18,48,128]{2,1,0:T(8,128)S(1)} %get-tuple-element.76.modulus_ref, ...), custom_call_target="tpu_custom_call" | custom-call | flops 805306368 | bytes 1572864 | tf_op jit(solution)/shard_map/solid_steps/pallas_call | solution.py:507
  84.7 7.8 %all-to-all-start.1 = ((f32[32,96,128]{2,1,0:T(8,128)}), f32[32,96,128]{2,1,0:T(8,128)S(1)}, u32[]{:S(2)}, u32[]{:S(2)}) async-start(f32[32,96,128]{2,1,0:T(8,128)} %bitcast.6), calls=%async_computation.1 | async-start | bytes 3145728 | tf_op jit(solution)/shard_map/all_to_all | solution.py:781
  92.5 2.1 %stress.1 = (f32[3,16,32,128]{3,2,1,0:T(8,128)}, f32[8,128]{1,0:T(8,128)S(1)}) custom-call(f32[18,48,128]{2,1,0:T(8,128)S(1)} %get-tuple-element.78.sigma_ref), custom_call_target="tpu_custom_call" | custom-call | flops 655360 | bytes 1048576 | tf_op jit(solution)/shard_map/stress/pallas_call | solution.py:552
  94.6 0.0 copy-start.1
  94.6 0.9 copy-done.1
  95.6 11.6 %fluid_step.3 = (f32[16,64,1024]{2,1,0:T(8,128)}, f32[8,128]{1,0:T(8,128)S(1)}) custom-call(f32[16,64,1024]{2,1,0:T(8,128)} %get-tuple-element.53.here_ref, f32[64,1024]{1,0:T(8,128)S(1)} %collective-permute-done.2.xfirst_ref.xlo_ref, f32[64,1024]{1,0:T(8,128)S(1)} %copy-done.1, bf16[3,16,64,1024]{3,2,1,0:T(8,128)(2,1)} %speed_ref.3, ...), custom_call_target="tpu_custom_call" | custom-call | flops 41943040 | bytes 14680064 | tf_op jit(solution)/shard_map/fluid_step/pallas_call | solution.py:726
  107.2 22.8 %all-to-all-done.1 = f32[32,96,128]{2,1,0:T(8,128)S(1)} async-done(((f32[32,96,128]{2,1,0:T(8,128)}), f32[32,96,128]{2,1,0:T(8,128)S(1)}, u32[]{:S(2)}, u32[]{:S(2)}) %all-to-all-start.1) | async-done | bytes 1572896 | tf_op jit(solution)/shard_map/all_to_all | solution.py:781
  130.0 2.4 %unpack.1 = f32[1024,128]{1,0:T(8,128)} custom-call(s32[1,1024]{1,0:T(1,128)S(1)} %get-tuple-element.81.dest_ref, f32[3072,128]{1,0:T(8,128)S(1)} %bitcast.4, f32[8,128]{1,0:T(8,128)S(1)} %get-tuple-element.83.refs_0_), custom_call_target="tpu_custom_call" | custom-call | flops 131072 | bytes 1048576 | tf_op jit(solution)/shard_map/unpack/pallas_call | solution.py:580
Async XLA Ops:
  0.6 6.0 %copy-start.3 = (s32[1,1024]{1,0:T(1,128)S(1)}, s32[1,1024]{1,0:T(1,128)}, u32[]{:S(2)}) copy-start(s32[1,1024]{1,0:T(1,128)} %slot_ref.1) | copy-start | bytes 12292
  0.6 6.0 %copy-start.2 = (s32[1,1024,1]{1,2,0:T(1,128)S(1)}, s32[1,1024,1]{1,2,0:T(1,128)}, u32[]{:S(2)}) copy-start(s32[1,1024,1]{1,2,0:T(1,128)} %param.12) | copy-start | bytes 12292
  2.3 9.7 %collective-permute-start.1 = (f32[112,1024]{1,0:T(8,128)S(1)}, f32[112,1024]{1,0:T(8,128)S(1)}, u32[]{:S(2)}, u32[]{:S(2)}) collective-permute-start(f32[112,1024]{1,0:T(8,128)S(1)} %get-tuple-element.47.refs_0_), channel_id=1, source_target_pairs={{4,0},{8,4},{12,8},{16,12},{20,16},{24,20},{28,24},{5,1},{9,5},{13... | collective-permute-start | bytes 1376264 | tf_op jit(solution)/shard_map/ppermute | solution.py:48
  3.6 8.4 %collective-permute-start = (f32[112,1024]{1,0:T(8,128)S(1)}, f32[112,1024]{1,0:T(8,128)S(1)}, u32[]{:S(2)}, u32[]{:S(2)}) collective-permute-start(f32[112,1024]{1,0:T(8,128)S(1)} %get-tuple-element.48.refs_1_), channel_id=1, source_target_pairs={{0,4},{4,8},{8,12},{12,16},{16,20},{20,24},{24,28},{1,5},{5,9},{9,... | collective-permute-start | bytes 1376264 | tf_op jit(solution)/shard_map/ppermute | solution.py:48
  12.0 49.7 %all-to-all-start = ((f32[32,104,128]{2,1,0:T(8,128)}), f32[32,104,128]{2,1,0:T(8,128)}, u32[]{:S(2)}, u32[]{:S(2)}) async-start(f32[32,104,128]{2,1,0:T(8,128)} %get-tuple-element.56), calls=%async_computation | async-start | bytes 3407872 | tf_op jit(solution)/shard_map/all_to_all | solution.py:763
  23.8 19.8 %collective-permute-start.4 = (f32[64,1024]{1,0:T(8,128)S(1)}, f32[64,1024]{1,0:T(8,128)S(1)}, u32[]{:S(2)}, u32[]{:S(2)}) collective-permute-start(f32[64,1024]{1,0:T(8,128)S(1)} %get-tuple-element.59), channel_id=1, source_target_pairs={{0,1},{1,2},{2,3},{4,5},{5,6},{6,7},{8,9},{9,10},{10,11},{12,13},{... | collective-permute-start | bytes 786440 | tf_op jit(solution)/shard_map/ppermute | solution.py:48
  27.4 23.4 %collective-permute-start.5 = (f32[64,1024]{1,0:T(8,128)S(1)}, f32[64,1024]{1,0:T(8,128)S(1)}, u32[]{:S(2)}, u32[]{:S(2)}) collective-permute-start(f32[64,1024]{1,0:T(8,128)S(1)} %get-tuple-element.60), channel_id=1, source_target_pairs={{1,0},{2,1},{3,2},{5,4},{6,5},{7,6},{9,8},{10,9},{11,10},{13,12},{... | collective-permute-start | bytes 786440 | tf_op jit(solution)/shard_map/ppermute | solution.py:48
  40.4 10.4 %collective-permute-start.2 = (f32[64,1024]{1,0:T(8,128)S(1)}, f32[64,1024]{1,0:T(8,128)S(1)}, u32[]{:S(2)}, u32[]{:S(2)}) collective-permute-start(f32[64,1024]{1,0:T(8,128)S(1)} %get-tuple-element.54), channel_id=1, source_target_pairs={{0,4},{4,8},{8,12},{12,16},{16,20},{20,24},{24,28},{1,5},{5,9},{9,... | collective-permute-start | bytes 786440 | tf_op jit(solution)/shard_map/ppermute | solution.py:48
  42.2 8.6 %collective-permute-start.3 = (f32[64,1024]{1,0:T(8,128)S(1)}, f32[64,1024]{1,0:T(8,128)S(1)}, u32[]{:S(2)}, u32[]{:S(2)}) collective-permute-start(f32[64,1024]{1,0:T(8,128)S(1)} %get-tuple-element.55), channel_id=1, source_target_pairs={{4,0},{8,4},{12,8},{16,12},{20,16},{24,20},{28,24},{5,1},{9,5},{13... | collective-permute-start | bytes 786440 | tf_op jit(solution)/shard_map/ppermute | solution.py:48
  50.8 14.4 %copy-start = (f32[64,1024]{1,0:T(8,128)}, f32[64,1024]{1,0:T(8,128)S(1)}, u32[]{:S(2)}) copy-start(f32[64,1024]{1,0:T(8,128)S(1)} %collective-permute-done.3.xlast_ref.xhi_ref) | copy-start | bytes 786436
  65.3 2.9 %collective-permute-start.6 = (f32[144,128]{1,0:T(8,128)S(1)}, f32[144,128]{1,0:T(8,128)S(1)}, u32[]{:S(2)}, u32[]{:S(2)}) collective-permute-start(f32[144,128]{1,0:T(8,128)S(1)} %get-tuple-element.65), channel_id=1, source_target_pairs={{0,4},{4,8},{8,12},{12,16},{16,20},{20,24},{24,28},{1,5},{5,9},{9,... | collective-permute-start | bytes 221192 | tf_op jit(solution)/shard_map/ppermute | solution.py:48
  66.8 4.9 %collective-permute-start.7 = (f32[144,128]{1,0:T(8,128)S(1)}, f32[144,128]{1,0:T(8,128)S(1)}, u32[]{:S(2)}, u32[]{:S(2)}) collective-permute-start(f32[144,128]{1,0:T(8,128)S(1)} %get-tuple-element.66), channel_id=1, source_target_pairs={{4,0},{8,4},{12,8},{16,12},{20,16},{24,20},{28,24},{5,1},{9,5},{13... | collective-permute-start | bytes 221192 | tf_op jit(solution)/shard_map/ppermute | solution.py:48
  71.8 5.9 %collective-permute-start.8 = (f32[32,1024]{1,0:T(8,128)S(1)}, f32[32,1024]{1,0:T(8,128)S(1)}, u32[]{:S(2)}, u32[]{:S(2)}) collective-permute-start(f32[32,1024]{1,0:T(8,128)S(1)} %get-tuple-element.70), channel_id=1, source_target_pairs={{0,1},{1,2},{2,3},{4,5},{5,6},{6,7},{8,9},{9,10},{10,11},{12,13},{... | collective-permute-start | bytes 393224 | tf_op jit(solution)/shard_map/ppermute | solution.py:48
  73.6 7.4 %collective-permute-start.9 = (f32[32,1024]{1,0:T(8,128)S(1)}, f32[32,1024]{1,0:T(8,128)S(1)}, u32[]{:S(2)}, u32[]{:S(2)}) collective-permute-start(f32[32,1024]{1,0:T(8,128)S(1)} %get-tuple-element.71), channel_id=1, source_target_pairs={{1,0},{2,1},{3,2},{5,4},{6,5},{7,6},{9,8},{10,9},{11,10},{13,12},{... | collective-permute-start | bytes 393224 | tf_op jit(solution)/shard_map/ppermute | solution.py:48
  84.7 45.3 %all-to-all-start.1 = ((f32[32,96,128]{2,1,0:T(8,128)}), f32[32,96,128]{2,1,0:T(8,128)S(1)}, u32[]{:S(2)}, u32[]{:S(2)}) async-start(f32[32,96,128]{2,1,0:T(8,128)} %bitcast.6), calls=%async_computation.1 | async-start | bytes 3145728 | tf_op jit(solution)/shard_map/all_to_all | solution.py:781
  94.6 0.9 copy-start.1

commit v11 on v10

--- a/solution.py
+++ b/solution.py
@@ -253,11 +253,8 @@
     return -(-count // across) * PART
 
 
-def x_faces_kernel(rim, bottom_ref, top_ref, near_ref, far_ref, temp_ref, kind_ref,
-                   low_ref, high_ref, left_ref, right_ref):
+def x_faces_kernel(rim, bottom_ref, top_ref, temp_ref, kind_ref, low_ref, high_ref):
     _, cy, _ = bottom_ref.shape
-    left_ref[...] = near_ref[:, 0, :]
-    right_ref[...] = far_ref[:, near_ref.shape[1] - 1, :]
     sx, sy, _ = temp_ref.shape
     low_ref[:cy, :] = bottom_ref[0]
     high_ref[:cy, :] = top_ref[0]
@@ -285,18 +282,15 @@
         in_specs=[
             pl.BlockSpec(plane, lambda i: (0, 0, 0)),
             pl.BlockSpec(plane, lambda i: (cx - 1, 0, 0)),
-            pl.BlockSpec((cx, 8, depth), lambda i: (0, 0, 0)),
-            pl.BlockSpec((cx, 8, depth), lambda i: (0, cy // 8 - 1, 0)),
             whole(temp.shape),
             whole(temp.shape),
         ],
-        out_specs=[whole((height, depth))] * 2 + [whole((cx, depth))] * 2,
-        out_shape=[jax.ShapeDtypeStruct((height, depth), F32)] * 2
-        + [jax.ShapeDtypeStruct((cx, depth), F32)] * 2,
+        out_specs=[whole((height, depth))] * 2,
+        out_shape=[jax.ShapeDtypeStruct((height, depth), F32)] * 2,
         compiler_params=params(16),
         cost_estimate=cost(1000, 4 * 4 * height * depth),
         name="x_faces",
-    )(far(fluid), far(fluid), far(fluid), far(fluid), far(temp), far(kind))
+    )(far(fluid), far(fluid), far(temp), far(kind))
 
 
 def fill_x(rim, ref, which, own, lo_ref, hi_ref):
@@ -314,10 +308,10 @@
 
 def y_faces_kernel(rim, near_ref, far_ref, temp_ref, kind_ref, lo_ref, hi_ref,
                    left_ref, right_ref, state_ref):
-    cx = near_ref.shape[0]
+    cx, near_rows, _ = near_ref.shape
     sx, sy, _ = temp_ref.shape
-    left_ref[:cx, :] = near_ref[...]
-    right_ref[:cx, :] = far_ref[...]
+    left_ref[:cx, :] = near_ref[:, 0, :]
+    right_ref[:cx, :] = far_ref[:, near_rows - 1, :]
     slabs = ([], [])
     long = state_ref.shape[1]
     state_ref[...] = jnp.zeros_like(state_ref)
@@ -331,23 +325,28 @@
     put_rim(right_ref, cx, slabs[1])
 
 
-def y_faces(rim, left, right, temp, kind, lo, hi):
-    cx, depth = left.shape
+def y_faces(rim, fluid, temp, kind, lo, hi):
+    cx, cy, depth = fluid.shape
     sx, sy, sz = temp.shape
     long = -(-(sx + 2 * rim) // PART) * PART
     height = cx + rim_rows(2 * rim * (long // PART), depth)
-    args = (left, right, far(temp), far(kind), lo, hi)
+    args = (far(temp), far(kind), lo, hi)
+    edge = (cx, 8, depth)
     return pl.pallas_call(
         functools.partial(y_faces_kernel, rim),
         grid=(1,),
-        in_specs=[whole(x.shape) for x in args],
+        in_specs=[
+            pl.BlockSpec(edge, lambda i: (0, 0, 0)),
+            pl.BlockSpec(edge, lambda i: (0, cy // 8 - 1, 0)),
+        ]
+        + [whole(x.shape) for x in args],
         out_specs=[whole((height, depth))] * 2 + [whole((2, long, sy + 2 * OFF, sz))],
         out_shape=[jax.ShapeDtypeStruct((height, depth), F32)] * 2
         + [pltpu.HBM((2, long, sy + 2 * OFF, sz), F32)],
         compiler_params=params(10),
         cost_estimate=cost(1000, 4 * 4 * height * depth),
         name="y_faces",
-    )(*args)
+    )(far(fluid), far(fluid), *args)
 
 
 def strips_kernel(thin, heat_ref, lo_ref, hi_ref, near_ref, away_ref,
@@ -568,7 +567,8 @@
     def step(index, none):
         base = pl.multiple_of(index * 8, 8)
         lines = [back_ref[pl.ds(dest_ref[0, base + i], 1), :] for i in range(8)]
-        out_ref[pl.ds(base, 8), :] = jnp.concatenate(lines, axis=0)
+        for i, line in enumerate(lines):
+            out_ref[pl.ds(base + i, 1), :] = line
         return none
 
     lax.fori_loop(0, rows // 8, step, 0, unroll=4)
@@ -755,14 +755,14 @@
     total = ndev * cap
     rim = SSTEPS + 1
 
-    first, last, left, right = x_faces(rim, temp_fluid, temp_solid, material)
+    first, last = x_faces(rim, temp_fluid, temp_solid, material)
     xlo, xhi = neighbours(last, first, "gx")
     dest, where, codes = rank(owner_map.reshape(1, rows), slot_map, ndev, cap)
     outgoing, flux = pack(where, codes, temp_fluid, wall_old, wall_mask, cap, (first, last))
     outgoing, xlo, xhi = lax.optimization_barrier((outgoing, xlo, xhi))
     incoming = lax.all_to_all(outgoing, AXES, split_axis=0, concat_axis=0, tiled=True)
 
-    left, right, state = y_faces(rim, left, right, temp_solid, material, xlo, xhi)
+    left, right, state = y_faces(rim, temp_fluid, temp_solid, material, xlo, xhi)
     ylo, yhi = neighbours(right, left, "gy")
     fluid, first, last, *edges = fluid_step(
         True, temp_fluid, (xlo, xhi), velocity, flux, (), ()

time: 134 us -> 133 us (level)
  transfers between devices with their start and end apart: 12 -> 12, of which waited for: 5 -> 5; matrix products, arithmetic and copies ran while one was open for 0% -> 0% of each run, Pallas kernels for 27% -> 28%
where the time goes in v11:
time: 133 us; the launch traced here: 132 us
  Pallas kernels  47.4 us (36%)
  waiting for transfers between devices  47.4 us (36%)
  starting transfers between devices  35.4 us (27%)
    pallas_call x2, Pallas kernels, fluid_step(): pl.pallas_call(functools.partial(fluid_kernel, opening), grid=(steps + 1,...  23.3 us
    all_to_all x1, waiting for transfers between devices, body(): lax.all_to_all(replies.reshape(ndev, cap, sz), AXES, split_axis=0, concat...  22.8 us
    ppermute x10, starting transfers between devices, neighbours(): return (lax.ppermute(before, axis, up), lax.ppermute(after, axis, down))  18.2 us
    ppermute x10, waiting for transfers between devices, neighbours(): return (lax.ppermute(before, axis, up), lax.ppermute(after, axis, down))  13.7 us
    all_to_all x1, waiting for transfers between devices, body(): lax.all_to_all(outgoing, AXES, split_axis=0, concat_axis=0, tiled=True)  10.9 us
    all_to_all x1, starting transfers between devices, body(): lax.all_to_all(outgoing, AXES, split_axis=0, concat_axis=0, tiled=True)  9.41 us
    all_to_all x1, starting transfers between devices, body(): lax.all_to_all(replies.reshape(ndev, cap, sz), AXES, split_axis=0, concat...  7.86 us
    pallas_call x1, Pallas kernels, pack(): pl.pallas_call(functools.partial(pack_kernel, cap), grid=(1,), in_specs=[...  4.41 us
  transfers between devices with their start and end apart: 12, of which 5 were waited for; matrix products, arithmetic and copies ran while one was open for 0% of the time, Pallas kernels for 28%

profile of v11, /device:TPU:0, one launch (start us, length us, event | category | flops | bytes accessed | tf_op | source)
XLA Modules:
  0.0 132.0 jit_solution(9284751463671296355)
XLA Ops:
  0.6 0.0 copy-start.3
  0.6 0.0 copy-start.2
  0.7 1.3 x_faces.1
  1.9 1.3 collective-permute-start.1
  3.2 3.1 %collective-permute-start = (f32[112,1024]{1,0:T(8,128)S(1)}, f32[112,1024]{1,0:T(8,128)S(1)}, u32[]{:S(2)}, u32[]{:S(2)}) collective-permute-start(f32[112,1024]{1,0:T(8,128)S(1)} %get-tuple-element.46.refs_1_), channel_id=1, source_target_pairs={{0,4},{4,8},{8,12},{12,16},{16,20},{20,24},{24,28},{1,5},{5,9},{9,... | collective-permute-start | bytes 1376264 | tf_op jit(solution)/shard_map/ppermute | solution.py:48
  6.3 0.0 copy-done.3
  6.3 0.0 copy-done.2
  6.3 0.9 rank.1
  7.2 4.4 %pack.1 = (f32[32,104,128]{2,1,0:T(8,128)}, f32[16,64,128]{2,1,0:T(8,128)S(1)}) custom-call(s32[1,1024]{1,0:T(1,128)S(1)} %get-tuple-element.43.where_ref, f32[32,128]{1,0:T(8,128)S(1)} %get-tuple-element.44.code_ref, f32[16,64,1024]{2,1,0:T(8,128)} %far_ref.1, f32[16,64,128]{2,1,0:T(8,128)} %old_ref.1, s32[16,64,128]{2,1,0:T(8,128)} %mask_ref.1, ...), custom_call_target="tpu_custom_call" | custom-call | flops 1744830464 | bytes 2621440 | tf_op jit(solution)/shard_map/pack/pallas_call | solution.py:151
  11.6 0.0 collective-permute-done.1.xhi_ref.hi_ref
  11.6 0.0 collective-permute-done.xlo_ref.lo_ref
  11.6 9.4 %all-to-all-start = ((f32[32,104,128]{2,1,0:T(8,128)}), f32[32,104,128]{2,1,0:T(8,128)}, u32[]{:S(2)}, u32[]{:S(2)}) async-start(f32[32,104,128]{2,1,0:T(8,128)} %get-tuple-element.54), calls=%async_computation | async-start | bytes 3407872 | tf_op jit(solution)/shard_map/all_to_all | solution.py:763
  21.1 2.7 %y_faces.1 = (f32[64,1024]{1,0:T(8,128)S(1)}, f32[64,1024]{1,0:T(8,128)S(1)}, f32[2,32,48,128]{3,2,1,0:T(8,128)}) custom-call(f32[16,64,1024]{2,1,0:T(8,128)} %far_ref.1, f32[16,64,1024]{2,1,0:T(8,128)} %far_ref.1, f32[16,32,128]{2,1,0:T(8,128)} %temp_ref.5, s32[16,32,128]{2,1,0:T(8,128)} %kind_ref.3, f32[112,1024]{1,0:T(8,128)S(1)} %collective-permute-done.xlo_ref.lo_ref, ...), custom_call_target="tpu_custom_call" | custom-call | flops 1000 | bytes 1048576 | tf_op jit(solution)/shard_map/y_faces/pallas_call | solution.py:335
  23.8 3.6 %collective-permute-start.4 = (f32[64,1024]{1,0:T(8,128)S(1)}, f32[64,1024]{1,0:T(8,128)S(1)}, u32[]{:S(2)}, u32[]{:S(2)}) collective-permute-start(f32[64,1024]{1,0:T(8,128)S(1)} %get-tuple-element.55), channel_id=1, source_target_pairs={{0,1},{1,2},{2,3},{4,5},{5,6},{6,7},{8,9},{9,10},{10,11},{12,13},{... | collective-permute-start | bytes 786440 | tf_op jit(solution)/shard_map/ppermute | solution.py:48
  27.4 1.3 collective-permute-start.5
  28.7 11.7 %fluid_step.2 = (f32[16,64,1024]{2,1,0:T(8,128)}, f32[64,1024]{1,0:T(8,128)S(1)}, f32[64,1024]{1,0:T(8,128)S(1)}, f32[16,1024]{1,0:T(8,128)S(1)}, f32[16,1024]{1...) custom-call(f32[16,64,1024]{2,1,0:T(8,128)} %far_ref.1, ...), custom_call_target="tpu_custom_call" | custom-call | flops 41943040 | bytes 14680064 | tf_op jit(solution)/shard_map/fluid_step/pallas_call | solution.py:726
  40.4 1.8 %collective-permute-start.2 = (f32[64,1024]{1,0:T(8,128)S(1)}, f32[64,1024]{1,0:T(8,128)S(1)}, u32[]{:S(2)}, u32[]{:S(2)}) collective-permute-start(f32[64,1024]{1,0:T(8,128)S(1)} %get-tuple-element.52), channel_id=1, source_target_pairs={{0,4},{4,8},{8,12},{12,16},{16,20},{20,24},{24,28},{1,5},{5,9},{9,... | collective-permute-start | bytes 786440 | tf_op jit(solution)/shard_map/ppermute | solution.py:48
  42.2 1.3 collective-permute-start.3
  43.5 0.0 collective-permute-done.4.ylo_ref
  43.5 7.0 %collective-permute-done.5.yhi_ref = f32[64,1024]{1,0:T(8,128)S(1)} collective-permute-done((f32[64,1024]{1,0:T(8,128)S(1)}, f32[64,1024]{1,0:T(8,128)S(1)}, u32[]{:S(2)}, u32[]{:S(2)}) %collective-permute-start.5) | collective-permute-done | bytes 262176 | tf_op jit(solution)/shard_map/ppermute | solution.py:48
  50.5 0.0 collective-permute-done.2.xfirst_ref.xlo_ref
  50.5 0.0 collective-permute-done.3.xlast_ref.xhi_ref
  50.5 0.0 copy-start
  50.5 10.9 %all-to-all-done.rows_ref = f32[32,104,128]{2,1,0:T(8,128)} async-done(((f32[32,104,128]{2,1,0:T(8,128)}), f32[32,104,128]{2,1,0:T(8,128)}, u32[]{:S(2)}, u32[]{:S(2)}) %all-to-all-start) | async-done | bytes 1703968 | tf_op jit(solution)/shard_map/all_to_all | solution.py:763
  61.4 3.6 %heat_sum.1 = (f32[16,32,128]{2,1,0:T(8,128)S(1)}, f32[144,128]{1,0:T(8,128)S(1)}, f32[144,128]{1,0:T(8,128)S(1)}, f32[16,1024]{1,0:T(8,128)S(1)}, f32[16,1024]{1,0:T(8,128)S(1)}, /*index=5*/s32[32,128]{1,0:T(8,128)S(1)}) custom-call(f32[32,104,128]{2,1,0:T(8,128)} %all-to-all-done.rows_ref, f32[64,1024]{1,0:T(8,128)S(1)} %collective-permute-done.2.xfirst_ref.xlo_ref, ...), custom_call_target="tpu_custom_call" | custom-call | flops 872415232 | bytes 1703936 | tf_op jit(solution)/shard_map/heat_sum/pallas_call | solution.py:218
  64.9 0.0 copy-done
  64.9 1.5 %collective-permute-start.6 = (f32[144,128]{1,0:T(8,128)S(1)}, f32[144,128]{1,0:T(8,128)S(1)}, u32[]{:S(2)}, u32[]{:S(2)}) collective-permute-start(f32[144,128]{1,0:T(8,128)S(1)} %get-tuple-element.61), channel_id=1, source_target_pairs={{0,4},{4,8},{8,12},{12,16},{16,20},{20,24},{24,28},{1,5},{5,9},{9,... | collective-permute-start | bytes 221192 | tf_op jit(solution)/shard_map/ppermute | solution.py:48
  66.5 1.3 collective-permute-start.7
  67.8 0.0 collective-permute-done.6.lo_ref.hxlo_ref.refs_0_
  67.8 3.6 %collective-permute-done.7.hi_ref.hxhi_ref.refs_1_ = f32[144,128]{1,0:T(8,128)S(1)} collective-permute-done((f32[144,128]{1,0:T(8,128)S(1)}, f32[144,128]{1,0:T(8,128)S(1)}, u32[]{:S(2)}, u32[]{:S(2)}) %collective-permute-start.7) | collective-permute-done | bytes 73760 | tf_op jit(solution)/shard_map/ppermute | solution.py:48
  71.4 0.1 strips.1
  71.5 1.7 %collective-permute-start.8 = (f32[32,1024]{1,0:T(8,128)S(1)}, f32[32,1024]{1,0:T(8,128)S(1)}, u32[]{:S(2)}, u32[]{:S(2)}) collective-permute-start(f32[32,1024]{1,0:T(8,128)S(1)} %get-tuple-element.66), channel_id=1, source_target_pairs={{0,1},{1,2},{2,3},{4,5},{5,6},{6,7},{8,9},{9,10},{10,11},{12,13},{... | collective-permute-start | bytes 393224 | tf_op jit(solution)/shard_map/ppermute | solution.py:48
  73.2 1.3 collective-permute-start.9
  74.5 2.8 %ready.1 = (f32[32,48,128]{2,1,0:T(8,128)S(1)}, f32[32,48,128]{2,1,0:T(8,128)S(1)}, f32[18,48,128]{2,1,0:T(8,128)S(1)}, bf16[3072,512]{1,0:T(8,128)(2,1)S(1)}) custom-call(f32[2,32,48,128]{3,2,1,0:T(8,128)} %get-tuple-element.68.state_ref, f32[64,1024]{1,0:T(8,128)S(1)} %collective-permute-done.4.ylo_ref, f32[64,1024]{1,0:T(8,128)S(1)} %collective-permute-done.5.yhi_ref, ...), custom_call_target="tpu_custom_call" | custom-call | flops 6291456 | bytes 6291456 | tf_op jit(solution)/shard_map/ready/pallas_call | solution.py:432
  77.3 0.0 collective-permute-done.8.hylo_ref.refs_4_
  77.3 3.2 %collective-permute-done.9.hyhi_ref.refs_5_ = f32[32,1024]{1,0:T(8,128)S(1)} collective-permute-done((f32[32,1024]{1,0:T(8,128)S(1)}, f32[32,1024]{1,0:T(8,128)S(1)}, u32[]{:S(2)}, u32[]{:S(2)}) %collective-permute-start.9) | collective-permute-done | bytes 131104 | tf_op jit(solution)/shard_map/ppermute | solution.py:48
  80.5 3.8 %solid_steps.1 = (f32[16,32,128]{2,1,0:T(8,128)}, f32[18,48,128]{2,1,0:T(8,128)S(1)}, f32[3072,128]{1,0:T(8,128)}) custom-call(f32[32,48,128]{2,1,0:T(8,128)S(1)} %get-tuple-element.70.start_ref, f32[32,48,128]{2,1,0:T(8,128)S(1)} %get-tuple-element.71.cond_ref, f32[18,48,128]{2,1,0:T(8,128)S(1)} %get-tuple-element.72.modulus_ref, ...), custom_call_target="tpu_custom_call" | custom-call | flops 805306368 | bytes 1572864 | tf_op jit(solution)/shard_map/solid_steps/pallas_call | solution.py:506
  84.3 7.9 %all-to-all-start.1 = ((f32[32,96,128]{2,1,0:T(8,128)}), f32[32,96,128]{2,1,0:T(8,128)S(1)}, u32[]{:S(2)}, u32[]{:S(2)}) async-start(f32[32,96,128]{2,1,0:T(8,128)} %bitcast.6), calls=%async_computation.1 | async-start | bytes 3145728 | tf_op jit(solution)/shard_map/all_to_all | solution.py:781
  92.2 2.1 %stress.1 = (f32[3,16,32,128]{3,2,1,0:T(8,128)}, f32[8,128]{1,0:T(8,128)S(1)}) custom-call(f32[18,48,128]{2,1,0:T(8,128)S(1)} %get-tuple-element.74.sigma_ref), custom_call_target="tpu_custom_call" | custom-call | flops 655360 | bytes 1048576 | tf_op jit(solution)/shard_map/stress/pallas_call | solution.py:551
  94.3 0.0 copy-start.1
  94.3 0.9 copy-done.1
  95.2 11.6 %fluid_step.3 = (f32[16,64,1024]{2,1,0:T(8,128)}, f32[8,128]{1,0:T(8,128)S(1)}) custom-call(f32[16,64,1024]{2,1,0:T(8,128)} %get-tuple-element.51.here_ref, f32[64,1024]{1,0:T(8,128)S(1)} %collective-permute-done.2.xfirst_ref.xlo_ref, f32[64,1024]{1,0:T(8,128)S(1)} %copy-done.1, bf16[3,16,64,1024]{3,2,1,0:T(8,128)(2,1)} %speed_ref.3, ...), custom_call_target="tpu_custom_call" | custom-call | flops 41943040 | bytes 14680064 | tf_op jit(solution)/shard_map/fluid_step/pallas_call | solution.py:726
  106.8 22.8 %all-to-all-done.1 = f32[32,96,128]{2,1,0:T(8,128)S(1)} async-done(((f32[32,96,128]{2,1,0:T(8,128)}), f32[32,96,128]{2,1,0:T(8,128)S(1)}, u32[]{:S(2)}, u32[]{:S(2)}) %all-to-all-start.1) | async-done | bytes 1572896 | tf_op jit(solution)/shard_map/all_to_all | solution.py:781
  129.6 2.4 %unpack.1 = f32[1024,128]{1,0:T(8,128)} custom-call(s32[1,1024]{1,0:T(1,128)S(1)} %get-tuple-element.77.dest_ref, f32[3072,128]{1,0:T(8,128)S(1)} %bitcast.4, f32[8,128]{1,0:T(8,128)S(1)} %get-tuple-element.79.refs_0_), custom_call_target="tpu_custom_call" | custom-call | flops 131072 | bytes 1048576 | tf_op jit(solution)/shard_map/unpack/pallas_call | solution.py:580
Async XLA Ops:
  0.6 5.6 %copy-start.3 = (s32[1,1024]{1,0:T(1,128)S(1)}, s32[1,1024]{1,0:T(1,128)}, u32[]{:S(2)}) copy-start(s32[1,1024]{1,0:T(1,128)} %slot_ref.1) | copy-start | bytes 12292
  0.6 5.6 %copy-start.2 = (s32[1,1024,1]{1,2,0:T(1,128)S(1)}, s32[1,1024,1]{1,2,0:T(1,128)}, u32[]{:S(2)}) copy-start(s32[1,1024,1]{1,2,0:T(1,128)} %param.12) | copy-start | bytes 12292
  1.9 9.7 %collective-permute-start.1 = (f32[112,1024]{1,0:T(8,128)S(1)}, f32[112,1024]{1,0:T(8,128)S(1)}, u32[]{:S(2)}, u32[]{:S(2)}) collective-permute-start(f32[112,1024]{1,0:T(8,128)S(1)} %get-tuple-element.45.refs_0_), channel_id=1, source_target_pairs={{4,0},{8,4},{12,8},{16,12},{20,16},{24,20},{28,24},{5,1},{9,5},{13... | collective-permute-start | bytes 1376264 | tf_op jit(solution)/shard_map/ppermute | solution.py:48
  3.2 8.4 %collective-permute-start = (f32[112,1024]{1,0:T(8,128)S(1)}, f32[112,1024]{1,0:T(8,128)S(1)}, u32[]{:S(2)}, u32[]{:S(2)}) collective-permute-start(f32[112,1024]{1,0:T(8,128)S(1)} %get-tuple-element.46.refs_1_), channel_id=1, source_target_pairs={{0,4},{4,8},{8,12},{12,16},{16,20},{20,24},{24,28},{1,5},{5,9},{9,... | collective-permute-start | bytes 1376264 | tf_op jit(solution)/shard_map/ppermute | solution.py:48
  11.6 49.7 %all-to-all-start = ((f32[32,104,128]{2,1,0:T(8,128)}), f32[32,104,128]{2,1,0:T(8,128)}, u32[]{:S(2)}, u32[]{:S(2)}) async-start(f32[32,104,128]{2,1,0:T(8,128)} %get-tuple-element.54), calls=%async_computation | async-start | bytes 3407872 | tf_op jit(solution)/shard_map/all_to_all | solution.py:763
  23.8 19.8 %collective-permute-start.4 = (f32[64,1024]{1,0:T(8,128)S(1)}, f32[64,1024]{1,0:T(8,128)S(1)}, u32[]{:S(2)}, u32[]{:S(2)}) collective-permute-start(f32[64,1024]{1,0:T(8,128)S(1)} %get-tuple-element.55), channel_id=1, source_target_pairs={{0,1},{1,2},{2,3},{4,5},{5,6},{6,7},{8,9},{9,10},{10,11},{12,13},{... | collective-permute-start | bytes 786440 | tf_op jit(solution)/shard_map/ppermute | solution.py:48
  27.4 23.1 %collective-permute-start.5 = (f32[64,1024]{1,0:T(8,128)S(1)}, f32[64,1024]{1,0:T(8,128)S(1)}, u32[]{:S(2)}, u32[]{:S(2)}) collective-permute-start(f32[64,1024]{1,0:T(8,128)S(1)} %get-tuple-element.56), channel_id=1, source_target_pairs={{1,0},{2,1},{3,2},{5,4},{6,5},{7,6},{9,8},{10,9},{11,10},{13,12},{... | collective-permute-start | bytes 786440 | tf_op jit(solution)/shard_map/ppermute | solution.py:48
  40.4 10.1 %collective-permute-start.2 = (f32[64,1024]{1,0:T(8,128)S(1)}, f32[64,1024]{1,0:T(8,128)S(1)}, u32[]{:S(2)}, u32[]{:S(2)}) collective-permute-start(f32[64,1024]{1,0:T(8,128)S(1)} %get-tuple-element.52), channel_id=1, source_target_pairs={{0,4},{4,8},{8,12},{12,16},{16,20},{20,24},{24,28},{1,5},{5,9},{9,... | collective-permute-start | bytes 786440 | tf_op jit(solution)/shard_map/ppermute | solution.py:48
  42.2 8.3 %collective-permute-start.3 = (f32[64,1024]{1,0:T(8,128)S(1)}, f32[64,1024]{1,0:T(8,128)S(1)}, u32[]{:S(2)}, u32[]{:S(2)}) collective-permute-start(f32[64,1024]{1,0:T(8,128)S(1)} %get-tuple-element.53), channel_id=1, source_target_pairs={{4,0},{8,4},{12,8},{16,12},{20,16},{24,20},{28,24},{5,1},{9,5},{13... | collective-permute-start | bytes 786440 | tf_op jit(solution)/shard_map/ppermute | solution.py:48
  50.5 14.4 %copy-start = (f32[64,1024]{1,0:T(8,128)}, f32[64,1024]{1,0:T(8,128)S(1)}, u32[]{:S(2)}) copy-start(f32[64,1024]{1,0:T(8,128)S(1)} %collective-permute-done.3.xlast_ref.xhi_ref) | copy-start | bytes 786436
  64.9 2.9 %collective-permute-start.6 = (f32[144,128]{1,0:T(8,128)S(1)}, f32[144,128]{1,0:T(8,128)S(1)}, u32[]{:S(2)}, u32[]{:S(2)}) collective-permute-start(f32[144,128]{1,0:T(8,128)S(1)} %get-tuple-element.61), channel_id=1, source_target_pairs={{0,4},{4,8},{8,12},{12,16},{16,20},{20,24},{24,28},{1,5},{5,9},{9,... | collective-permute-start | bytes 221192 | tf_op jit(solution)/shard_map/ppermute | solution.py:48
  66.5 4.9 %collective-permute-start.7 = (f32[144,128]{1,0:T(8,128)S(1)}, f32[144,128]{1,0:T(8,128)S(1)}, u32[]{:S(2)}, u32[]{:S(2)}) collective-permute-start(f32[144,128]{1,0:T(8,128)S(1)} %get-tuple-element.62), channel_id=1, source_target_pairs={{4,0},{8,4},{12,8},{16,12},{20,16},{24,20},{28,24},{5,1},{9,5},{13... | collective-permute-start | bytes 221192 | tf_op jit(solution)/shard_map/ppermute | solution.py:48
  71.5 5.9 %collective-permute-start.8 = (f32[32,1024]{1,0:T(8,128)S(1)}, f32[32,1024]{1,0:T(8,128)S(1)}, u32[]{:S(2)}, u32[]{:S(2)}) collective-permute-start(f32[32,1024]{1,0:T(8,128)S(1)} %get-tuple-element.66), channel_id=1, source_target_pairs={{0,1},{1,2},{2,3},{4,5},{5,6},{6,7},{8,9},{9,10},{10,11},{12,13},{... | collective-permute-start | bytes 393224 | tf_op jit(solution)/shard_map/ppermute | solution.py:48
  73.2 7.3 %collective-permute-start.9 = (f32[32,1024]{1,0:T(8,128)S(1)}, f32[32,1024]{1,0:T(8,128)S(1)}, u32[]{:S(2)}, u32[]{:S(2)}) collective-permute-start(f32[32,1024]{1,0:T(8,128)S(1)} %get-tuple-element.67), channel_id=1, source_target_pairs={{1,0},{2,1},{3,2},{5,4},{6,5},{7,6},{9,8},{10,9},{11,10},{13,12},{... | collective-permute-start | bytes 393224 | tf_op jit(solution)/shard_map/ppermute | solution.py:48
  84.3 45.3 %all-to-all-start.1 = ((f32[32,96,128]{2,1,0:T(8,128)}), f32[32,96,128]{2,1,0:T(8,128)S(1)}, u32[]{:S(2)}, u32[]{:S(2)}) async-start(f32[32,96,128]{2,1,0:T(8,128)} %bitcast.6), calls=%async_computation.1 | async-start | bytes 3145728 | tf_op jit(solution)/shard_map/all_to_all | solution.py:781
  94.3 0.9 copy-start.1

commit v12 on v11

--- a/solution.py
+++ b/solution.py
@@ -19,7 +19,7 @@
 BF16 = jnp.bfloat16
 AXES = ("gx", "gy")
 LANE = 128
-PART = 16
+PART = 8
 OFF = 8
 
 
@@ -759,7 +759,7 @@
     xlo, xhi = neighbours(last, first, "gx")
     dest, where, codes = rank(owner_map.reshape(1, rows), slot_map, ndev, cap)
     outgoing, flux = pack(where, codes, temp_fluid, wall_old, wall_mask, cap, (first, last))
-    outgoing, xlo, xhi = lax.optimization_barrier((outgoing, xlo, xhi))
+    outgoing, xhi = lax.optimization_barrier((outgoing, xhi))
     incoming = lax.all_to_all(outgoing, AXES, split_axis=0, concat_axis=0, tiled=True)
 
     left, right, state = y_faces(rim, temp_fluid, temp_solid, material, xlo, xhi)

time: 133 us -> 164 us (1.23)
  starting transfers between devices: 35.4 us -> 66.5 us
    ppermute x10, starting transfers between devices: 18.2 us -> 51.3 us  [neighbours(): return (lax.ppermute(before, axis, up), lax.ppermute(after, axis, down))]
    all_to_all x1, waiting for transfers between devices: 10.9 us -> 0.01 us  [body(): lax.all_to_all(outgoing, AXES, split_axis=0, concat_axis=0, tiled=True)]
    ppermute x10, waiting for transfers between devices: 13.7 us -> 24.5 us  [neighbours(): return (lax.ppermute(before, axis, up), lax.ppermute(after, axis, down))]
  transfers between devices with their start and end apart: 12 -> 12, of which waited for: 5 -> 6; matrix products, arithmetic and copies ran while one was open for 0% -> 0% of each run, Pallas kernels for 28% -> 22%
where the time goes in v12:
time: 164 us; the launch traced here: 163 us
  starting transfers between devices  66.5 us (41%)
  Pallas kernels  47.5 us (29%)
  waiting for transfers between devices  47.3 us (29%)
    ppermute x10, starting transfers between devices, neighbours(): return (lax.ppermute(before, axis, up), lax.ppermute(after, axis, down))  51.3 us
    ppermute x10, waiting for transfers between devices, neighbours(): return (lax.ppermute(before, axis, up), lax.ppermute(after, axis, down))  24.5 us
    pallas_call x2, Pallas kernels, fluid_step(): pl.pallas_call(functools.partial(fluid_kernel, opening), grid=(steps + 1,...  23.3 us
    all_to_all x1, waiting for transfers between devices, body(): lax.all_to_all(replies.reshape(ndev, cap, sz), AXES, split_axis=0, concat...  22.8 us
    all_to_all x1, starting transfers between devices, body(): lax.all_to_all(outgoing, AXES, split_axis=0, concat_axis=0, tiled=True)  8.76 us
    all_to_all x1, starting transfers between devices, body(): lax.all_to_all(replies.reshape(ndev, cap, sz), AXES, split_axis=0, concat...  6.48 us
    pallas_call x1, Pallas kernels, pack(): pl.pallas_call(functools.partial(pack_kernel, cap), grid=(1,), in_specs=[...  4.41 us
    pallas_call x1, Pallas kernels, solid_steps(): pl.pallas_call(functools.partial(solid_kernel, rim), in_specs=[in_vmem] *...  3.88 us
  transfers between devices with their start and end apart: 12, of which 6 were waited for; matrix products, arithmetic and copies ran while one was open for 0% of the time, Pallas kernels for 22%

profile of v12, /device:TPU:0, one launch (start us, length us, event | category | flops | bytes accessed | tf_op | source)
XLA Modules:
  0.0 163.2 jit_solution(681821827503779844)
XLA Ops:
  0.6 0.0 copy-start.3
  0.6 0.0 copy-start.2
  0.7 1.3 x_faces.1
  1.9 1.3 collective-permute-start.1
  3.2 0.0 copy-done.3
  3.2 0.0 copy-done.2
  3.2 0.9 rank.1
  4.1 4.4 %pack.1 = (f32[32,104,128]{2,1,0:T(8,128)}, f32[16,64,128]{2,1,0:T(8,128)S(1)}) custom-call(s32[1,1024]{1,0:T(1,128)S(1)} %get-tuple-element.43.where_ref, f32[32,128]{1,0:T(8,128)S(1)} %get-tuple-element.44.code_ref, f32[16,64,1024]{2,1,0:T(8,128)} %far_ref.1, f32[16,64,128]{2,1,0:T(8,128)} %old_ref.1, s32[16,64,128]{2,1,0:T(8,128)} %mask_ref.1, ...), custom_call_target="tpu_custom_call" | custom-call | flops 1744830464 | bytes 2621440 | tf_op jit(solution)/shard_map/pack/pallas_call | solution.py:151
  8.6 0.0 collective-permute-done.1.xhi_ref.hi_ref
  8.6 8.8 %all-to-all-start = ((f32[32,104,128]{2,1,0:T(8,128)}), f32[32,104,128]{2,1,0:T(8,128)}, u32[]{:S(2)}, u32[]{:S(2)}) async-start(f32[32,104,128]{2,1,0:T(8,128)} %get-tuple-element.52), calls=%async_computation | async-start | bytes 3407872 | tf_op jit(solution)/shard_map/all_to_all | solution.py:763
  17.3 2.1 %collective-permute-start = (f32[104,1024]{1,0:T(8,128)S(1)}, f32[104,1024]{1,0:T(8,128)S(1)}, u32[]{:S(2)}, u32[]{:S(2)}) collective-permute-start(f32[104,1024]{1,0:T(8,128)S(1)} %get-tuple-element.42.refs_1_), channel_id=1, source_target_pairs={{0,4},{4,8},{8,12},{12,16},{16,20},{20,24},{24,28},{1,5},{5,9},{9,... | collective-permute-start | bytes 1277960 | tf_op jit(solution)/shard_map/ppermute | solution.py:48
  19.4 1.4 collective-permute-done.xlo_ref.lo_ref
  20.8 11.7 %fluid_step.2 = (f32[16,64,1024]{2,1,0:T(8,128)}, f32[64,1024]{1,0:T(8,128)S(1)}, f32[64,1024]{1,0:T(8,128)S(1)}, f32[16,1024]{1,0:T(8,128)S(1)}, f32[16,1024]{1...) custom-call(f32[16,64,1024]{2,1,0:T(8,128)} %far_ref.1, ...), custom_call_target="tpu_custom_call" | custom-call | flops 41943040 | bytes 14680064 | tf_op jit(solution)/shard_map/fluid_step/pallas_call | solution.py:726
  32.5 31.2 %collective-permute-start.2 = (f32[64,1024]{1,0:T(8,128)S(1)}, f32[64,1024]{1,0:T(8,128)S(1)}, u32[]{:S(2)}, u32[]{:S(2)}) collective-permute-start(f32[64,1024]{1,0:T(8,128)S(1)} %get-tuple-element.50), channel_id=1, source_target_pairs={{0,4},{4,8},{8,12},{12,16},{16,20},{20,24},{24,28},{1,5},{5,9},{9,... | collective-permute-start | bytes 786440 | tf_op jit(solution)/shard_map/ppermute | solution.py:48
  63.8 1.3 collective-permute-start.3
  65.1 2.7 %y_faces.1 = (f32[56,1024]{1,0:T(8,128)S(1)}, f32[56,1024]{1,0:T(8,128)S(1)}, f32[2,32,48,128]{3,2,1,0:T(8,128)}) custom-call(f32[16,64,1024]{2,1,0:T(8,128)} %far_ref.1, f32[16,64,1024]{2,1,0:T(8,128)} %far_ref.1, f32[16,32,128]{2,1,0:T(8,128)} %temp_ref.5, s32[16,32,128]{2,1,0:T(8,128)} %kind_ref.3, f32[104,1024]{1,0:T(8,128)S(1)} %collective-permute-done.xlo_ref.lo_ref, ...), custom_call_target="tpu_custom_call" | custom-call | flops 1000 | bytes 917504 | tf_op jit(solution)/shard_map/y_faces/pallas_call | solution.py:335
  67.8 3.7 %collective-permute-start.4 = (f32[56,1024]{1,0:T(8,128)S(1)}, f32[56,1024]{1,0:T(8,128)S(1)}, u32[]{:S(2)}, u32[]{:S(2)}) collective-permute-start(f32[56,1024]{1,0:T(8,128)S(1)} %get-tuple-element.53), channel_id=1, source_target_pairs={{0,1},{1,2},{2,3},{4,5},{5,6},{6,7},{8,9},{9,10},{10,11},{12,13},{... | collective-permute-start | bytes 688136 | tf_op jit(solution)/shard_map/ppermute | solution.py:48
  71.5 1.3 collective-permute-start.5
  72.8 2.5 %collective-permute-done.4.ylo_ref = f32[56,1024]{1,0:T(8,128)S(1)} collective-permute-done((f32[56,1024]{1,0:T(8,128)S(1)}, f32[56,1024]{1,0:T(8,128)S(1)}, u32[]{:S(2)}, u32[]{:S(2)}) %collective-permute-start.4) | collective-permute-done | bytes 229408 | tf_op jit(solution)/shard_map/ppermute | solution.py:48
  75.3 6.8 %collective-permute-done.5.yhi_ref = f32[56,1024]{1,0:T(8,128)S(1)} collective-permute-done((f32[56,1024]{1,0:T(8,128)S(1)}, f32[56,1024]{1,0:T(8,128)S(1)}, u32[]{:S(2)}, u32[]{:S(2)}) %collective-permute-start.5) | collective-permute-done | bytes 229408 | tf_op jit(solution)/shard_map/ppermute | solution.py:48
  82.1 0.0 collective-permute-done.2.xfirst_ref.xlo_ref
  82.1 0.0 collective-permute-done.3.xlast_ref.xhi_ref
  82.1 0.0 copy-start
  82.1 0.0 all-to-all-done.rows_ref
  82.1 3.7 %heat_sum.1 = (f32[16,32,128]{2,1,0:T(8,128)S(1)}, f32[144,128]{1,0:T(8,128)S(1)}, f32[144,128]{1,0:T(8,128)S(1)}, f32[16,1024]{1,0:T(8,128)S(1)}, f32[16,1024]{1,0:T(8,128)S(1)}, /*index=5*/s32[32,128]{1,0:T(8,128)S(1)}) custom-call(f32[32,104,128]{2,1,0:T(8,128)} %all-to-all-done.rows_ref, f32[64,1024]{1,0:T(8,128)S(1)} %collective-permute-done.2.xfirst_ref.xlo_ref, ...), custom_call_target="tpu_custom_call" | custom-call | flops 872415232 | bytes 1703936 | tf_op jit(solution)/shard_map/heat_sum/pallas_call | solution.py:218
  85.8 0.0 copy-done
  85.8 3.9 %collective-permute-start.6 = (f32[144,128]{1,0:T(8,128)S(1)}, f32[144,128]{1,0:T(8,128)S(1)}, u32[]{:S(2)}, u32[]{:S(2)}) collective-permute-start(f32[144,128]{1,0:T(8,128)S(1)} %get-tuple-element.59), channel_id=1, source_target_pairs={{0,4},{4,8},{8,12},{12,16},{16,20},{20,24},{24,28},{1,5},{5,9},{9,... | collective-permute-start | bytes 221192 | tf_op jit(solution)/shard_map/ppermute | solution.py:48
  89.7 1.3 collective-permute-start.7
  91.0 0.0 collective-permute-done.6.lo_ref.hxlo_ref.refs_0_
  91.0 11.1 %collective-permute-done.7.hi_ref.hxhi_ref.refs_1_ = f32[144,128]{1,0:T(8,128)S(1)} collective-permute-done((f32[144,128]{1,0:T(8,128)S(1)}, f32[144,128]{1,0:T(8,128)S(1)}, u32[]{:S(2)}, u32[]{:S(2)}) %collective-permute-start.7) | collective-permute-done | bytes 73760 | tf_op jit(solution)/shard_map/ppermute | solution.py:48
  102.2 0.1 strips.1
  102.2 3.9 %collective-permute-start.8 = (f32[32,1024]{1,0:T(8,128)S(1)}, f32[32,1024]{1,0:T(8,128)S(1)}, u32[]{:S(2)}, u32[]{:S(2)}) collective-permute-start(f32[32,1024]{1,0:T(8,128)S(1)} %get-tuple-element.64), channel_id=1, source_target_pairs={{0,1},{1,2},{2,3},{4,5},{5,6},{6,7},{8,9},{9,10},{10,11},{12,13},{... | collective-permute-start | bytes 393224 | tf_op jit(solution)/shard_map/ppermute | solution.py:48
  106.1 1.3 collective-permute-start.9
  107.4 2.8 %ready.1 = (f32[32,48,128]{2,1,0:T(8,128)S(1)}, f32[32,48,128]{2,1,0:T(8,128)S(1)}, f32[18,48,128]{2,1,0:T(8,128)S(1)}, bf16[3072,512]{1,0:T(8,128)(2,1)S(1)}) custom-call(f32[2,32,48,128]{3,2,1,0:T(8,128)} %get-tuple-element.66.state_ref, f32[56,1024]{1,0:T(8,128)S(1)} %collective-permute-done.4.ylo_ref, f32[56,1024]{1,0:T(8,128)S(1)} %collective-permute-done.5.yhi_ref, ...), custom_call_target="tpu_custom_call" | custom-call | flops 6291456 | bytes 6291456 | tf_op jit(solution)/shard_map/ready/pallas_call | solution.py:432
  110.3 0.0 collective-permute-done.8.hylo_ref.refs_4_
  110.3 2.7 %collective-permute-done.9.hyhi_ref.refs_5_ = f32[32,1024]{1,0:T(8,128)S(1)} collective-permute-done((f32[32,1024]{1,0:T(8,128)S(1)}, f32[32,1024]{1,0:T(8,128)S(1)}, u32[]{:S(2)}, u32[]{:S(2)}) %collective-permute-start.9) | collective-permute-done | bytes 131104 | tf_op jit(solution)/shard_map/ppermute | solution.py:48
  113.0 3.9 %solid_steps.1 = (f32[16,32,128]{2,1,0:T(8,128)}, f32[18,48,128]{2,1,0:T(8,128)S(1)}, f32[3072,128]{1,0:T(8,128)}) custom-call(f32[32,48,128]{2,1,0:T(8,128)S(1)} %get-tuple-element.68.start_ref, f32[32,48,128]{2,1,0:T(8,128)S(1)} %get-tuple-element.69.cond_ref, f32[18,48,128]{2,1,0:T(8,128)S(1)} %get-tuple-element.70.modulus_ref, ...), custom_call_target="tpu_custom_call" | custom-call | flops 805306368 | bytes 1572864 | tf_op jit(solution)/shard_map/solid_steps/pallas_call | solution.py:506
  116.9 6.5 %all-to-all-start.1 = ((f32[32,96,128]{2,1,0:T(8,128)}), f32[32,96,128]{2,1,0:T(8,128)S(1)}, u32[]{:S(2)}, u32[]{:S(2)}) async-start(f32[32,96,128]{2,1,0:T(8,128)} %bitcast.6), calls=%async_computation.1 | async-start | bytes 3145728 | tf_op jit(solution)/shard_map/all_to_all | solution.py:781
  123.4 2.1 %stress.1 = (f32[3,16,32,128]{3,2,1,0:T(8,128)}, f32[8,128]{1,0:T(8,128)S(1)}) custom-call(f32[18,48,128]{2,1,0:T(8,128)S(1)} %get-tuple-element.72.sigma_ref), custom_call_target="tpu_custom_call" | custom-call | flops 655360 | bytes 1048576 | tf_op jit(solution)/shard_map/stress/pallas_call | solution.py:551
  125.5 0.0 copy-start.1
  125.5 0.9 copy-done.1
  126.5 11.6 %fluid_step.3 = (f32[16,64,1024]{2,1,0:T(8,128)}, f32[8,128]{1,0:T(8,128)S(1)}) custom-call(f32[16,64,1024]{2,1,0:T(8,128)} %get-tuple-element.49.here_ref, f32[64,1024]{1,0:T(8,128)S(1)} %collective-permute-done.2.xfirst_ref.xlo_ref, f32[64,1024]{1,0:T(8,128)S(1)} %copy-done.1, bf16[3,16,64,1024]{3,2,1,0:T(8,128)(2,1)} %speed_ref.3, ...), custom_call_target="tpu_custom_call" | custom-call | flops 41943040 | bytes 14680064 | tf_op jit(solution)/shard_map/fluid_step/pallas_call | solution.py:726
  138.1 22.8 %all-to-all-done.1 = f32[32,96,128]{2,1,0:T(8,128)S(1)} async-done(((f32[32,96,128]{2,1,0:T(8,128)}), f32[32,96,128]{2,1,0:T(8,128)S(1)}, u32[]{:S(2)}, u32[]{:S(2)}) %all-to-all-start.1) | async-done | bytes 1572896 | tf_op jit(solution)/shard_map/all_to_all | solution.py:781
  160.8 2.4 %unpack.1 = f32[1024,128]{1,0:T(8,128)} custom-call(s32[1,1024]{1,0:T(1,128)S(1)} %get-tuple-element.75.dest_ref, f32[3072,128]{1,0:T(8,128)S(1)} %bitcast.4, f32[8,128]{1,0:T(8,128)S(1)} %get-tuple-element.77.refs_0_), custom_call_target="tpu_custom_call" | custom-call | flops 131072 | bytes 1048576 | tf_op jit(solution)/shard_map/unpack/pallas_call | solution.py:580
Async XLA Ops:
  0.6 2.6 %copy-start.3 = (s32[1,1024]{1,0:T(1,128)S(1)}, s32[1,1024]{1,0:T(1,128)}, u32[]{:S(2)}) copy-start(s32[1,1024]{1,0:T(1,128)} %slot_ref.1) | copy-start | bytes 12292
  0.6 2.6 %copy-start.2 = (s32[1,1024,1]{1,2,0:T(1,128)S(1)}, s32[1,1024,1]{1,2,0:T(1,128)}, u32[]{:S(2)}) copy-start(s32[1,1024,1]{1,2,0:T(1,128)} %param.12) | copy-start | bytes 12292
  1.9 6.6 %collective-permute-start.1 = (f32[104,1024]{1,0:T(8,128)S(1)}, f32[104,1024]{1,0:T(8,128)S(1)}, u32[]{:S(2)}, u32[]{:S(2)}) collective-permute-start(f32[104,1024]{1,0:T(8,128)S(1)} %get-tuple-element.45.refs_0_), channel_id=1, source_target_pairs={{4,0},{8,4},{12,8},{16,12},{20,16},{24,20},{28,24},{5,1},{9,5},{13... | collective-permute-start | bytes 1277960 | tf_op jit(solution)/shard_map/ppermute | solution.py:48
  8.6 73.5 %all-to-all-start = ((f32[32,104,128]{2,1,0:T(8,128)}), f32[32,104,128]{2,1,0:T(8,128)}, u32[]{:S(2)}, u32[]{:S(2)}) async-start(f32[32,104,128]{2,1,0:T(8,128)} %get-tuple-element.52), calls=%async_computation | async-start | bytes 3407872 | tf_op jit(solution)/shard_map/all_to_all | solution.py:763
  17.3 3.5 %collective-permute-start = (f32[104,1024]{1,0:T(8,128)S(1)}, f32[104,1024]{1,0:T(8,128)S(1)}, u32[]{:S(2)}, u32[]{:S(2)}) collective-permute-start(f32[104,1024]{1,0:T(8,128)S(1)} %get-tuple-element.42.refs_1_), channel_id=1, source_target_pairs={{0,4},{4,8},{8,12},{12,16},{16,20},{20,24},{24,28},{1,5},{5,9},{9,... | collective-permute-start | bytes 1277960 | tf_op jit(solution)/shard_map/ppermute | solution.py:48
  32.5 49.6 %collective-permute-start.2 = (f32[64,1024]{1,0:T(8,128)S(1)}, f32[64,1024]{1,0:T(8,128)S(1)}, u32[]{:S(2)}, u32[]{:S(2)}) collective-permute-start(f32[64,1024]{1,0:T(8,128)S(1)} %get-tuple-element.50), channel_id=1, source_target_pairs={{0,4},{4,8},{8,12},{12,16},{16,20},{20,24},{24,28},{1,5},{5,9},{9,... | collective-permute-start | bytes 786440 | tf_op jit(solution)/shard_map/ppermute | solution.py:48
  63.8 18.3 %collective-permute-start.3 = (f32[64,1024]{1,0:T(8,128)S(1)}, f32[64,1024]{1,0:T(8,128)S(1)}, u32[]{:S(2)}, u32[]{:S(2)}) collective-permute-start(f32[64,1024]{1,0:T(8,128)S(1)} %get-tuple-element.51), channel_id=1, source_target_pairs={{4,0},{8,4},{12,8},{16,12},{20,16},{24,20},{28,24},{5,1},{9,5},{13... | collective-permute-start | bytes 786440 | tf_op jit(solution)/shard_map/ppermute | solution.py:48
  67.8 7.5 %collective-permute-start.4 = (f32[56,1024]{1,0:T(8,128)S(1)}, f32[56,1024]{1,0:T(8,128)S(1)}, u32[]{:S(2)}, u32[]{:S(2)}) collective-permute-start(f32[56,1024]{1,0:T(8,128)S(1)} %get-tuple-element.53), channel_id=1, source_target_pairs={{0,1},{1,2},{2,3},{4,5},{5,6},{6,7},{8,9},{9,10},{10,11},{12,13},{... | collective-permute-start | bytes 688136 | tf_op jit(solution)/shard_map/ppermute | solution.py:48
  71.5 10.6 %collective-permute-start.5 = (f32[56,1024]{1,0:T(8,128)S(1)}, f32[56,1024]{1,0:T(8,128)S(1)}, u32[]{:S(2)}, u32[]{:S(2)}) collective-permute-start(f32[56,1024]{1,0:T(8,128)S(1)} %get-tuple-element.54), channel_id=1, source_target_pairs={{1,0},{2,1},{3,2},{5,4},{6,5},{7,6},{9,8},{10,9},{11,10},{13,12},{... | collective-permute-start | bytes 688136 | tf_op jit(solution)/shard_map/ppermute | solution.py:48
  82.1 3.7 %copy-start = (f32[64,1024]{1,0:T(8,128)}, f32[64,1024]{1,0:T(8,128)S(1)}, u32[]{:S(2)}) copy-start(f32[64,1024]{1,0:T(8,128)S(1)} %collective-permute-done.3.xlast_ref.xhi_ref) | copy-start | bytes 786436
  85.8 5.2 %collective-permute-start.6 = (f32[144,128]{1,0:T(8,128)S(1)}, f32[144,128]{1,0:T(8,128)S(1)}, u32[]{:S(2)}, u32[]{:S(2)}) collective-permute-start(f32[144,128]{1,0:T(8,128)S(1)} %get-tuple-element.59), channel_id=1, source_target_pairs={{0,4},{4,8},{8,12},{12,16},{16,20},{20,24},{24,28},{1,5},{5,9},{9,... | collective-permute-start | bytes 221192 | tf_op jit(solution)/shard_map/ppermute | solution.py:48
  89.7 12.4 %collective-permute-start.7 = (f32[144,128]{1,0:T(8,128)S(1)}, f32[144,128]{1,0:T(8,128)S(1)}, u32[]{:S(2)}, u32[]{:S(2)}) collective-permute-start(f32[144,128]{1,0:T(8,128)S(1)} %get-tuple-element.60), channel_id=1, source_target_pairs={{4,0},{8,4},{12,8},{16,12},{20,16},{24,20},{28,24},{5,1},{9,5},{13... | collective-permute-start | bytes 221192 | tf_op jit(solution)/shard_map/ppermute | solution.py:48
  102.2 8.0 %collective-permute-start.8 = (f32[32,1024]{1,0:T(8,128)S(1)}, f32[32,1024]{1,0:T(8,128)S(1)}, u32[]{:S(2)}, u32[]{:S(2)}) collective-permute-start(f32[32,1024]{1,0:T(8,128)S(1)} %get-tuple-element.64), channel_id=1, source_target_pairs={{0,1},{1,2},{2,3},{4,5},{5,6},{6,7},{8,9},{9,10},{10,11},{12,13},{... | collective-permute-start | bytes 393224 | tf_op jit(solution)/shard_map/ppermute | solution.py:48
  106.1 6.9 %collective-permute-start.9 = (f32[32,1024]{1,0:T(8,128)S(1)}, f32[32,1024]{1,0:T(8,128)S(1)}, u32[]{:S(2)}, u32[]{:S(2)}) collective-permute-start(f32[32,1024]{1,0:T(8,128)S(1)} %get-tuple-element.65), channel_id=1, source_target_pairs={{1,0},{2,1},{3,2},{5,4},{6,5},{7,6},{9,8},{10,9},{11,10},{13,12},{... | collective-permute-start | bytes 393224 | tf_op jit(solution)/shard_map/ppermute | solution.py:48
  116.9 44.0 %all-to-all-start.1 = ((f32[32,96,128]{2,1,0:T(8,128)}), f32[32,96,128]{2,1,0:T(8,128)S(1)}, u32[]{:S(2)}, u32[]{:S(2)}) async-start(f32[32,96,128]{2,1,0:T(8,128)} %bitcast.6), calls=%async_computation.1 | async-start | bytes 3145728 | tf_op jit(solution)/shard_map/all_to_all | solution.py:781
  125.5 0.9 copy-start.1

commit v13 on v12

--- a/solution.py
+++ b/solution.py
@@ -172,26 +172,32 @@
 
 def heat_kernel(cap, thin, rows_ref, xfirst_ref, xlast_ref, ylo_ref, yhi_ref,
                 yfirst_ref, ylast_ref, clo_ref, chi_ref,
-                heat_ref, low_ref, high_ref, left_ref, right_ref, code_ref):
-    ndev, tall, row_len = rows_ref.shape
+                heat_ref, low_ref, high_ref, left_ref, right_ref, code_ref, total_ref):
+    share, tall, row_len = rows_ref.shape
     cx, depth = yfirst_ref.shape
     sx, sy, _ = heat_ref.shape
     slots = sx * sy
-    left = yfirst_ref[...] + clo_ref[...] * ylo_ref[:cx, :]
-    right = ylast_ref[...] + chi_ref[...] * yhi_ref[:cx, :]
-    left_ref[...] = left
-    right_ref[...] = right
     edge = thin * sy
-    for ref, x in ((low_ref, 0), (high_ref, cx - 1)):
-        for at, line in ((edge, left[x:x + 1]), (edge + depth // LANE, right[x:x + 1])):
-            for i in range(depth // LANE):
-                ref[at + i:at + i + 1, :] = line[:, i * LANE:(i + 1) * LANE]
+    turn, turns = pl.program_id(0), pl.num_programs(0)
+
+    @pl.when(turn == 0)
+    def _():
+        left = yfirst_ref[...] + clo_ref[...] * ylo_ref[:cx, :]
+        right = ylast_ref[...] + chi_ref[...] * yhi_ref[:cx, :]
+        left_ref[...] = left
+        right_ref[...] = right
+        for ref, x in ((low_ref, 0), (high_ref, cx - 1)):
+            for at, line in ((edge, left[x:x + 1]), (edge + depth // LANE, right[x:x + 1])):
+                for i in range(depth // LANE):
+                    ref[at + i:at + i + 1, :] = line[:, i * LANE:(i + 1) * LANE]
+        total_ref[...] = jnp.zeros_like(total_ref)
+
     codes = rows_ref[:, cap, :].astype(jnp.int32) - 1
-    code_ref[...] = codes
-    group = ndev // GROUPS
+    code_ref[pl.ds(pl.multiple_of(turn * share, 8), share), :] = codes
+    group = share // 2
     names = lax.broadcasted_iota(jnp.int32, (slots, tall), 0)
-    total = jnp.zeros((slots, 2 * row_len), F32)
-    for index in range(0, ndev, group):
+    total = total_ref[...]
+    for index in range(0, share, group):
         lines = rows_ref[index:index + group].reshape(group * tall, row_len)
         high, low = halves(lines)
         pick = jnp.concatenate(
@@ -204,10 +210,14 @@
         total = total + jnp.dot(
             pick, jnp.concatenate([high, low], axis=1), preferred_element_type=F32
         )
-    heat = total[:, :row_len] + total[:, row_len:]
-    heat_ref[...] = heat.reshape(sx, sy, row_len)
-    low_ref[:edge, :] = heat[:edge]
-    high_ref[:edge, :] = heat[slots - edge:]
+    total_ref[...] = total
+
+    @pl.when(turn == turns - 1)
+    def _():
+        heat = total[:, :row_len] + total[:, row_len:]
+        heat_ref[...] = heat.reshape(sx, sy, row_len)
+        low_ref[:edge, :] = heat[:edge]
+        high_ref[:edge, :] = heat[slots - edge:]
 
 
 def heat_sum(incoming, cap, block, thin, faces, edges):
@@ -217,8 +227,10 @@
     edge = (thin * sy + 2 * (line[1] // LANE), row_len)
     return pl.pallas_call(
         functools.partial(heat_kernel, cap, thin),
-        grid=(1,),
-        in_specs=[whole(incoming.shape)] + [anywhere] * 2 + [whole(x.shape) for x in edges],
+        grid=(2,),
+        in_specs=[pl.BlockSpec((ndev // 2, tall, row_len), lambda i: (i, 0, 0))]
+        + [anywhere] * 2
+        + [whole(x.shape) for x in edges],
         out_specs=[whole(block), whole(edge), whole(edge), whole(line), whole(line)]
         + [whole((ndev, row_len))],
         out_shape=[
@@ -229,6 +241,7 @@
             jax.ShapeDtypeStruct(line, F32),
             jax.ShapeDtypeStruct((ndev, row_len), jnp.int32),
         ],
+        scratch_shapes=[pltpu.VMEM((sx * sy, 2 * row_len), F32)],
         compiler_params=params(14),
         cost_estimate=cost(4 * ndev * tall * sx * sy * row_len, 4 * ndev * tall * row_len),
         name="heat_sum",
@@ -580,7 +593,7 @@
     return pl.pallas_call(
         unpack_kernel,
         grid=(1,),
-        in_specs=[pl.BlockSpec(memory_space=pltpu.SMEM), whole(back.shape)]
+        in_specs=[pl.BlockSpec(memory_space=pltpu.SMEM), in_vmem]
         + [anywhere] * len(after),
         out_specs=whole((rows, row_len)),
         out_shape=jax.ShapeDtypeStruct((rows, row_len), F32),
@@ -759,7 +772,7 @@
     xlo, xhi = neighbours(last, first, "gx")
     dest, where, codes = rank(owner_map.reshape(1, rows), slot_map, ndev, cap)
     outgoing, flux = pack(where, codes, temp_fluid, wall_old, wall_mask, cap, (first, last))
-    outgoing, xhi = lax.optimization_barrier((outgoing, xhi))
+    outgoing, xlo, xhi = lax.optimization_barrier((outgoing, xlo, xhi))
     incoming = lax.all_to_all(outgoing, AXES, split_axis=0, concat_axis=0, tiled=True)
 
     left, right, state = y_faces(rim, temp_fluid, temp_solid, material, xlo, xhi)

time: 164 us -> 133 us (0.81)
  starting transfers between devices: 66.5 us -> 34.6 us
    ppermute x10, starting transfers between devices: 51.3 us -> 19.9 us  [neighbours(): return (lax.ppermute(before, axis, up), lax.ppermute(after, axis, down))]
    all_to_all x1, waiting for transfers between devices: 0.01 us -> 4.61 us  [body(): lax.all_to_all(outgoing, AXES, split_axis=0, concat_axis=0, tiled=True)]
    ppermute x10, waiting for transfers between devices: 24.5 us -> 20.6 us  [neighbours(): return (lax.ppermute(before, axis, up), lax.ppermute(after, axis, down))]
  transfers between devices with their start and end apart: 12 -> 12, of which waited for: 6 -> 6; matrix products, arithmetic and copies ran while one was open for 0% -> 0% of each run, Pallas kernels for 22% -> 28%
where the time goes in v13:
time: 133 us; the launch traced here: 132 us
  waiting for transfers between devices  48 us (36%)
  Pallas kernels  47.5 us (36%)
  starting transfers between devices  34.6 us (26%)
    pallas_call x2, Pallas kernels, fluid_step(): pl.pallas_call(functools.partial(fluid_kernel, opening), grid=(steps + 1,...  23.3 us
    all_to_all x1, waiting for transfers between devices, body(): lax.all_to_all(replies.reshape(ndev, cap, sz), AXES, split_axis=0, concat...  22.8 us
    ppermute x10, waiting for transfers between devices, neighbours(): return (lax.ppermute(before, axis, up), lax.ppermute(after, axis, down))  20.6 us
    ppermute x10, starting transfers between devices, neighbours(): return (lax.ppermute(before, axis, up), lax.ppermute(after, axis, down))  19.9 us
    all_to_all x1, starting transfers between devices, body(): lax.all_to_all(outgoing, AXES, split_axis=0, concat_axis=0, tiled=True)  9.06 us
    all_to_all x1, starting transfers between devices, body(): lax.all_to_all(replies.reshape(ndev, cap, sz), AXES, split_axis=0, concat...  5.63 us
    all_to_all x1, waiting for transfers between devices, body(): lax.all_to_all(outgoing, AXES, split_axis=0, concat_axis=0, tiled=True)  4.61 us
    pallas_call x1, Pallas kernels, pack(): pl.pallas_call(functools.partial(pack_kernel, cap), grid=(1,), in_specs=[...  4.41 us
  transfers between devices with their start and end apart: 12, of which 6 were waited for; matrix products, arithmetic and copies ran while one was open for 0% of the time, Pallas kernels for 28%

profile of v13, /device:TPU:0, one launch (start us, length us, event | category | flops | bytes accessed | tf_op | source)
XLA Modules:
  0.0 131.8 jit_solution(627767886493662471)
XLA Ops:
  0.6 0.0 copy-start.3
  0.6 0.0 copy-start.2
  0.7 1.3 x_faces.1
  1.9 1.3 collective-permute-start.1
  3.2 3.1 %collective-permute-start = (f32[104,1024]{1,0:T(8,128)S(1)}, f32[104,1024]{1,0:T(8,128)S(1)}, u32[]{:S(2)}, u32[]{:S(2)}) collective-permute-start(f32[104,1024]{1,0:T(8,128)S(1)} %get-tuple-element.46.refs_1_), channel_id=1, source_target_pairs={{0,4},{4,8},{8,12},{12,16},{16,20},{20,24},{24,28},{1,5},{5,9},{9,... | collective-permute-start | bytes 1277960 | tf_op jit(solution)/shard_map/ppermute | solution.py:48
  6.3 0.0 copy-done.3
  6.3 0.0 copy-done.2
  6.3 0.9 rank.1
  7.2 4.4 %pack.1 = (f32[32,104,128]{2,1,0:T(8,128)}, f32[16,64,128]{2,1,0:T(8,128)S(1)}) custom-call(s32[1,1024]{1,0:T(1,128)S(1)} %get-tuple-element.43.where_ref, f32[32,128]{1,0:T(8,128)S(1)} %get-tuple-element.44.code_ref, f32[16,64,1024]{2,1,0:T(8,128)} %far_ref.1, f32[16,64,128]{2,1,0:T(8,128)} %old_ref.1, s32[16,64,128]{2,1,0:T(8,128)} %mask_ref.1, ...), custom_call_target="tpu_custom_call" | custom-call | flops 1744830464 | bytes 2621440 | tf_op jit(solution)/shard_map/pack/pallas_call | solution.py:151
  11.6 0.0 collective-permute-done.1.xhi_ref.hi_ref
  11.6 0.0 collective-permute-done.xlo_ref.lo_ref
  11.6 9.1 %all-to-all-start = ((f32[32,104,128]{2,1,0:T(8,128)}), f32[32,104,128]{2,1,0:T(8,128)}, u32[]{:S(2)}, u32[]{:S(2)}) async-start(f32[32,104,128]{2,1,0:T(8,128)} %get-tuple-element.54), calls=%async_computation | async-start | bytes 3407872 | tf_op jit(solution)/shard_map/all_to_all | solution.py:776
  20.7 11.7 %fluid_step.2 = (f32[16,64,1024]{2,1,0:T(8,128)}, f32[64,1024]{1,0:T(8,128)S(1)}, f32[64,1024]{1,0:T(8,128)S(1)}, f32[16,1024]{1,0:T(8,128)S(1)}, f32[16,1024]{1...) custom-call(f32[16,64,1024]{2,1,0:T(8,128)} %far_ref.1, ...), custom_call_target="tpu_custom_call" | custom-call | flops 41943040 | bytes 14680064 | tf_op jit(solution)/shard_map/fluid_step/pallas_call | solution.py:739
  32.5 2.1 %collective-permute-start.2 = (f32[64,1024]{1,0:T(8,128)S(1)}, f32[64,1024]{1,0:T(8,128)S(1)}, u32[]{:S(2)}, u32[]{:S(2)}) collective-permute-start(f32[64,1024]{1,0:T(8,128)S(1)} %get-tuple-element.52), channel_id=1, source_target_pairs={{0,4},{4,8},{8,12},{12,16},{16,20},{20,24},{24,28},{1,5},{5,9},{9,... | collective-permute-start | bytes 786440 | tf_op jit(solution)/shard_map/ppermute | solution.py:48
  34.6 1.3 collective-permute-start.3
  35.9 2.7 %y_faces.1 = (f32[56,1024]{1,0:T(8,128)S(1)}, f32[56,1024]{1,0:T(8,128)S(1)}, f32[2,32,48,128]{3,2,1,0:T(8,128)}) custom-call(f32[16,64,1024]{2,1,0:T(8,128)} %far_ref.1, f32[16,64,1024]{2,1,0:T(8,128)} %far_ref.1, f32[16,32,128]{2,1,0:T(8,128)} %temp_ref.5, s32[16,32,128]{2,1,0:T(8,128)} %kind_ref.3, f32[104,1024]{1,0:T(8,128)S(1)} %collective-permute-done.xlo_ref.lo_ref, ...), custom_call_target="tpu_custom_call" | custom-call | flops 1000 | bytes 917504 | tf_op jit(solution)/shard_map/y_faces/pallas_call | solution.py:348
  38.6 3.6 %collective-permute-start.4 = (f32[56,1024]{1,0:T(8,128)S(1)}, f32[56,1024]{1,0:T(8,128)S(1)}, u32[]{:S(2)}, u32[]{:S(2)}) collective-permute-start(f32[56,1024]{1,0:T(8,128)S(1)} %get-tuple-element.55), channel_id=1, source_target_pairs={{0,1},{1,2},{2,3},{4,5},{5,6},{6,7},{8,9},{9,10},{10,11},{12,13},{... | collective-permute-start | bytes 688136 | tf_op jit(solution)/shard_map/ppermute | solution.py:48
  42.1 1.3 collective-permute-start.5
  43.4 5.2 %collective-permute-done.4.ylo_ref = f32[56,1024]{1,0:T(8,128)S(1)} collective-permute-done((f32[56,1024]{1,0:T(8,128)S(1)}, f32[56,1024]{1,0:T(8,128)S(1)}, u32[]{:S(2)}, u32[]{:S(2)}) %collective-permute-start.4) | collective-permute-done | bytes 229408 | tf_op jit(solution)/shard_map/ppermute | solution.py:48
  48.7 7.7 %collective-permute-done.5.yhi_ref = f32[56,1024]{1,0:T(8,128)S(1)} collective-permute-done((f32[56,1024]{1,0:T(8,128)S(1)}, f32[56,1024]{1,0:T(8,128)S(1)}, u32[]{:S(2)}, u32[]{:S(2)}) %collective-permute-start.5) | collective-permute-done | bytes 229408 | tf_op jit(solution)/shard_map/ppermute | solution.py:48
  56.4 0.0 collective-permute-done.2.xfirst_ref.xlo_ref
  56.4 0.0 collective-permute-done.3.xlast_ref.xhi_ref
  56.4 0.0 copy-start
  56.4 4.6 %all-to-all-done.rows_ref = f32[32,104,128]{2,1,0:T(8,128)} async-done(((f32[32,104,128]{2,1,0:T(8,128)}), f32[32,104,128]{2,1,0:T(8,128)}, u32[]{:S(2)}, u32[]{:S(2)}) %all-to-all-start) | async-done | bytes 1703968 | tf_op jit(solution)/shard_map/all_to_all | solution.py:776
  61.0 3.7 %heat_sum.1 = (f32[16,32,128]{2,1,0:T(8,128)S(1)}, f32[144,128]{1,0:T(8,128)S(1)}, f32[144,128]{1,0:T(8,128)S(1)}, f32[16,1024]{1,0:T(8,128)S(1)}, f32[16,1024]{1,0:T(8,128)S(1)}, /*index=5*/s32[32,128]{1,0:T(8,128)S(1)}) custom-call(f32[32,104,128]{2,1,0:T(8,128)} %all-to-all-done.rows_ref, f32[64,1024]{1,0:T(8,128)S(1)} %collective-permute-done.2.xfirst_ref.xlo_ref, ...), custom_call_target="tpu_custom_call" | custom-call | flops 872415232 | bytes 1703936 | tf_op jit(solution)/shard_map/heat_sum/pallas_call | solution.py:228
  64.7 1.5 %collective-permute-start.6 = (f32[144,128]{1,0:T(8,128)S(1)}, f32[144,128]{1,0:T(8,128)S(1)}, u32[]{:S(2)}, u32[]{:S(2)}) collective-permute-start(f32[144,128]{1,0:T(8,128)S(1)} %get-tuple-element.61), channel_id=1, source_target_pairs={{0,4},{4,8},{8,12},{12,16},{16,20},{20,24},{24,28},{1,5},{5,9},{9,... | collective-permute-start | bytes 221192 | tf_op jit(solution)/shard_map/ppermute | solution.py:48
  66.3 1.3 collective-permute-start.7
  67.6 0.0 collective-permute-done.6.lo_ref.hxlo_ref.refs_0_
  67.6 3.6 %collective-permute-done.7.hi_ref.hxhi_ref.refs_1_ = f32[144,128]{1,0:T(8,128)S(1)} collective-permute-done((f32[144,128]{1,0:T(8,128)S(1)}, f32[144,128]{1,0:T(8,128)S(1)}, u32[]{:S(2)}, u32[]{:S(2)}) %collective-permute-start.7) | collective-permute-done | bytes 73760 | tf_op jit(solution)/shard_map/ppermute | solution.py:48
  71.2 0.1 strips.1
  71.3 3.1 %collective-permute-start.8 = (f32[32,1024]{1,0:T(8,128)S(1)}, f32[32,1024]{1,0:T(8,128)S(1)}, u32[]{:S(2)}, u32[]{:S(2)}) collective-permute-start(f32[32,1024]{1,0:T(8,128)S(1)} %get-tuple-element.66), channel_id=1, source_target_pairs={{0,1},{1,2},{2,3},{4,5},{5,6},{6,7},{8,9},{9,10},{10,11},{12,13},{... | collective-permute-start | bytes 393224 | tf_op jit(solution)/shard_map/ppermute | solution.py:48
  74.4 1.3 collective-permute-start.9
  75.7 2.8 %ready.1 = (f32[32,48,128]{2,1,0:T(8,128)S(1)}, f32[32,48,128]{2,1,0:T(8,128)S(1)}, f32[18,48,128]{2,1,0:T(8,128)S(1)}, bf16[3072,512]{1,0:T(8,128)(2,1)S(1)}) custom-call(f32[2,32,48,128]{3,2,1,0:T(8,128)} %get-tuple-element.68.state_ref, f32[56,1024]{1,0:T(8,128)S(1)} %collective-permute-done.4.ylo_ref, f32[56,1024]{1,0:T(8,128)S(1)} %collective-permute-done.5.yhi_ref, ...), custom_call_target="tpu_custom_call" | custom-call | flops 6291456 | bytes 6291456 | tf_op jit(solution)/shard_map/ready/pallas_call | solution.py:445
  78.5 0.0 collective-permute-done.8.hylo_ref.refs_4_
  78.6 4.1 %collective-permute-done.9.hyhi_ref.refs_5_ = f32[32,1024]{1,0:T(8,128)S(1)} collective-permute-done((f32[32,1024]{1,0:T(8,128)S(1)}, f32[32,1024]{1,0:T(8,128)S(1)}, u32[]{:S(2)}, u32[]{:S(2)}) %collective-permute-start.9) | collective-permute-done | bytes 131104 | tf_op jit(solution)/shard_map/ppermute | solution.py:48
  82.6 3.8 %solid_steps.1 = (f32[16,32,128]{2,1,0:T(8,128)}, f32[18,48,128]{2,1,0:T(8,128)S(1)}, f32[3072,128]{1,0:T(8,128)}) custom-call(f32[32,48,128]{2,1,0:T(8,128)S(1)} %get-tuple-element.70.start_ref, f32[32,48,128]{2,1,0:T(8,128)S(1)} %get-tuple-element.71.cond_ref, f32[18,48,128]{2,1,0:T(8,128)S(1)} %get-tuple-element.72.modulus_ref, ...), custom_call_target="tpu_custom_call" | custom-call | flops 805306368 | bytes 1572864 | tf_op jit(solution)/shard_map/solid_steps/pallas_call | solution.py:519
  86.4 0.0 copy-done
  86.4 5.6 %all-to-all-start.1 = ((f32[32,96,128]{2,1,0:T(8,128)}), f32[32,96,128]{2,1,0:T(8,128)S(1)}, u32[]{:S(2)}, u32[]{:S(2)}) async-start(f32[32,96,128]{2,1,0:T(8,128)} %bitcast.6), calls=%async_computation.1 | async-start | bytes 3145728 | tf_op jit(solution)/shard_map/all_to_all | solution.py:794
  92.0 2.1 %stress.1 = (f32[3,16,32,128]{3,2,1,0:T(8,128)}, f32[8,128]{1,0:T(8,128)S(1)}) custom-call(f32[18,48,128]{2,1,0:T(8,128)S(1)} %get-tuple-element.74.sigma_ref), custom_call_target="tpu_custom_call" | custom-call | flops 655360 | bytes 1048576 | tf_op jit(solution)/shard_map/stress/pallas_call | solution.py:564
  94.2 0.0 copy-start.1
  94.2 0.9 copy-done.1
  95.1 11.6 %fluid_step.3 = (f32[16,64,1024]{2,1,0:T(8,128)}, f32[8,128]{1,0:T(8,128)S(1)}) custom-call(f32[16,64,1024]{2,1,0:T(8,128)} %get-tuple-element.51.here_ref, f32[64,1024]{1,0:T(8,128)S(1)} %collective-permute-done.2.xfirst_ref.xlo_ref, f32[64,1024]{1,0:T(8,128)S(1)} %copy-done.1, bf16[3,16,64,1024]{3,2,1,0:T(8,128)(2,1)} %speed_ref.3, ...), custom_call_target="tpu_custom_call" | custom-call | flops 41943040 | bytes 14680064 | tf_op jit(solution)/shard_map/fluid_step/pallas_call | solution.py:739
  106.7 22.8 %all-to-all-done.1 = f32[32,96,128]{2,1,0:T(8,128)S(1)} async-done(((f32[32,96,128]{2,1,0:T(8,128)}), f32[32,96,128]{2,1,0:T(8,128)S(1)}, u32[]{:S(2)}, u32[]{:S(2)}) %all-to-all-start.1) | async-done | bytes 1572896 | tf_op jit(solution)/shard_map/all_to_all | solution.py:794
  129.5 2.4 %unpack.1 = f32[1024,128]{1,0:T(8,128)} custom-call(s32[1,1024]{1,0:T(1,128)S(1)} %get-tuple-element.77.dest_ref, f32[3072,128]{1,0:T(8,128)S(1)} %bitcast.4, f32[8,128]{1,0:T(8,128)S(1)} %get-tuple-element.79.refs_0_), custom_call_target="tpu_custom_call" | custom-call | flops 131072 | bytes 1048576 | tf_op jit(solution)/shard_map/unpack/pallas_call | solution.py:593
Async XLA Ops:
  0.6 5.6 %copy-start.3 = (s32[1,1024]{1,0:T(1,128)S(1)}, s32[1,1024]{1,0:T(1,128)}, u32[]{:S(2)}) copy-start(s32[1,1024]{1,0:T(1,128)} %slot_ref.1) | copy-start | bytes 12292
  0.6 5.6 %copy-start.2 = (s32[1,1024,1]{1,2,0:T(1,128)S(1)}, s32[1,1024,1]{1,2,0:T(1,128)}, u32[]{:S(2)}) copy-start(s32[1,1024,1]{1,2,0:T(1,128)} %param.12) | copy-start | bytes 12292
  1.9 9.7 %collective-permute-start.1 = (f32[104,1024]{1,0:T(8,128)S(1)}, f32[104,1024]{1,0:T(8,128)S(1)}, u32[]{:S(2)}, u32[]{:S(2)}) collective-permute-start(f32[104,1024]{1,0:T(8,128)S(1)} %get-tuple-element.45.refs_0_), channel_id=1, source_target_pairs={{4,0},{8,4},{12,8},{16,12},{20,16},{24,20},{28,24},{5,1},{9,5},{13... | collective-permute-start | bytes 1277960 | tf_op jit(solution)/shard_map/ppermute | solution.py:48
  3.2 8.4 %collective-permute-start = (f32[104,1024]{1,0:T(8,128)S(1)}, f32[104,1024]{1,0:T(8,128)S(1)}, u32[]{:S(2)}, u32[]{:S(2)}) collective-permute-start(f32[104,1024]{1,0:T(8,128)S(1)} %get-tuple-element.46.refs_1_), channel_id=1, source_target_pairs={{0,4},{4,8},{8,12},{12,16},{16,20},{20,24},{24,28},{1,5},{5,9},{9,... | collective-permute-start | bytes 1277960 | tf_op jit(solution)/shard_map/ppermute | solution.py:48
  11.6 49.3 %all-to-all-start = ((f32[32,104,128]{2,1,0:T(8,128)}), f32[32,104,128]{2,1,0:T(8,128)}, u32[]{:S(2)}, u32[]{:S(2)}) async-start(f32[32,104,128]{2,1,0:T(8,128)} %get-tuple-element.54), calls=%async_computation | async-start | bytes 3407872 | tf_op jit(solution)/shard_map/all_to_all | solution.py:776
  32.5 23.9 %collective-permute-start.2 = (f32[64,1024]{1,0:T(8,128)S(1)}, f32[64,1024]{1,0:T(8,128)S(1)}, u32[]{:S(2)}, u32[]{:S(2)}) collective-permute-start(f32[64,1024]{1,0:T(8,128)S(1)} %get-tuple-element.52), channel_id=1, source_target_pairs={{0,4},{4,8},{8,12},{12,16},{16,20},{20,24},{24,28},{1,5},{5,9},{9,... | collective-permute-start | bytes 786440 | tf_op jit(solution)/shard_map/ppermute | solution.py:48
  34.6 21.8 %collective-permute-start.3 = (f32[64,1024]{1,0:T(8,128)S(1)}, f32[64,1024]{1,0:T(8,128)S(1)}, u32[]{:S(2)}, u32[]{:S(2)}) collective-permute-start(f32[64,1024]{1,0:T(8,128)S(1)} %get-tuple-element.53), channel_id=1, source_target_pairs={{4,0},{8,4},{12,8},{16,12},{20,16},{24,20},{28,24},{5,1},{9,5},{13... | collective-permute-start | bytes 786440 | tf_op jit(solution)/shard_map/ppermute | solution.py:48
  38.6 10.1 %collective-permute-start.4 = (f32[56,1024]{1,0:T(8,128)S(1)}, f32[56,1024]{1,0:T(8,128)S(1)}, u32[]{:S(2)}, u32[]{:S(2)}) collective-permute-start(f32[56,1024]{1,0:T(8,128)S(1)} %get-tuple-element.55), channel_id=1, source_target_pairs={{0,1},{1,2},{2,3},{4,5},{5,6},{6,7},{8,9},{9,10},{10,11},{12,13},{... | collective-permute-start | bytes 688136 | tf_op jit(solution)/shard_map/ppermute | solution.py:48
  42.1 14.2 %collective-permute-start.5 = (f32[56,1024]{1,0:T(8,128)S(1)}, f32[56,1024]{1,0:T(8,128)S(1)}, u32[]{:S(2)}, u32[]{:S(2)}) collective-permute-start(f32[56,1024]{1,0:T(8,128)S(1)} %get-tuple-element.56), channel_id=1, source_target_pairs={{1,0},{2,1},{3,2},{5,4},{6,5},{7,6},{9,8},{10,9},{11,10},{13,12},{... | collective-permute-start | bytes 688136 | tf_op jit(solution)/shard_map/ppermute | solution.py:48
  56.4 30.0 %copy-start = (f32[64,1024]{1,0:T(8,128)}, f32[64,1024]{1,0:T(8,128)S(1)}, u32[]{:S(2)}) copy-start(f32[64,1024]{1,0:T(8,128)S(1)} %collective-permute-done.3.xlast_ref.xhi_ref) | copy-start | bytes 786436
  64.7 2.9 %collective-permute-start.6 = (f32[144,128]{1,0:T(8,128)S(1)}, f32[144,128]{1,0:T(8,128)S(1)}, u32[]{:S(2)}, u32[]{:S(2)}) collective-permute-start(f32[144,128]{1,0:T(8,128)S(1)} %get-tuple-element.61), channel_id=1, source_target_pairs={{0,4},{4,8},{8,12},{12,16},{16,20},{20,24},{24,28},{1,5},{5,9},{9,... | collective-permute-start | bytes 221192 | tf_op jit(solution)/shard_map/ppermute | solution.py:48
  66.3 4.9 %collective-permute-start.7 = (f32[144,128]{1,0:T(8,128)S(1)}, f32[144,128]{1,0:T(8,128)S(1)}, u32[]{:S(2)}, u32[]{:S(2)}) collective-permute-start(f32[144,128]{1,0:T(8,128)S(1)} %get-tuple-element.62), channel_id=1, source_target_pairs={{4,0},{8,4},{12,8},{16,12},{20,16},{24,20},{28,24},{5,1},{9,5},{13... | collective-permute-start | bytes 221192 | tf_op jit(solution)/shard_map/ppermute | solution.py:48
  71.3 7.3 %collective-permute-start.8 = (f32[32,1024]{1,0:T(8,128)S(1)}, f32[32,1024]{1,0:T(8,128)S(1)}, u32[]{:S(2)}, u32[]{:S(2)}) collective-permute-start(f32[32,1024]{1,0:T(8,128)S(1)} %get-tuple-element.66), channel_id=1, source_target_pairs={{0,1},{1,2},{2,3},{4,5},{5,6},{6,7},{8,9},{9,10},{10,11},{12,13},{... | collective-permute-start | bytes 393224 | tf_op jit(solution)/shard_map/ppermute | solution.py:48
  74.4 8.2 %collective-permute-start.9 = (f32[32,1024]{1,0:T(8,128)S(1)}, f32[32,1024]{1,0:T(8,128)S(1)}, u32[]{:S(2)}, u32[]{:S(2)}) collective-permute-start(f32[32,1024]{1,0:T(8,128)S(1)} %get-tuple-element.67), channel_id=1, source_target_pairs={{1,0},{2,1},{3,2},{5,4},{6,5},{7,6},{9,8},{10,9},{11,10},{13,12},{... | collective-permute-start | bytes 393224 | tf_op jit(solution)/shard_map/ppermute | solution.py:48
  86.4 43.1 %all-to-all-start.1 = ((f32[32,96,128]{2,1,0:T(8,128)}), f32[32,96,128]{2,1,0:T(8,128)S(1)}, u32[]{:S(2)}, u32[]{:S(2)}) async-start(f32[32,96,128]{2,1,0:T(8,128)} %bitcast.6), calls=%async_computation.1 | async-start | bytes 3145728 | tf_op jit(solution)/shard_map/all_to_all | solution.py:794
  94.2 0.9 copy-start.1

commit v14 on v12

--- a/solution.py
+++ b/solution.py
@@ -449,7 +449,7 @@
 def solid_kernel(rim, start_ref, cond_ref, modulus_ref, pick_ref,
                  heat_ref, hxlo_ref, hxhi_ref, hylo_ref, hyhi_ref,
                  next_ref, sigma_ref, reply_ref, even_ref, odd_ref, src_ref, rhs_ref,
-                 stage_ref, sems):
+                 stage_ref, leave, sems):
     sx, sy, sz = heat_ref.shape
     wide = sx + 2 * rim
     thin = rim - 1
@@ -482,7 +482,10 @@
             later[x] = centre + (cond_ref[x] * (beside - 6.0 * centre) + src_ref[x])
         now = later
     solid = now[rim:rim + sx, OFF:OFF + sy, :]
-    next_ref[...] = solid
+    leaving = pltpu.make_async_copy(
+        now.at[rim:rim + sx, OFF:OFF + sy, :], next_ref, leave
+    )
+    leaving.start()
     sigma_ref[...] = modulus_ref[...] * now[rim - 1:rim + sx + 1]
     high, low = halves(solid.reshape(sx * sy, sz))
     rhs_ref[:, :sz] = high
@@ -495,6 +498,7 @@
         stage_ref[cut, :] = both[:, :sz] + both[:, sz:]
         copies.append(pltpu.make_async_copy(stage_ref.at[cut], reply_ref.at[cut], sems.at[index]))
         copies[-1].start()
+    leaving.wait()
     for copy in copies:
         copy.wait()
 
@@ -506,9 +510,9 @@
     return pl.pallas_call(
         functools.partial(solid_kernel, rim),
         in_specs=[in_vmem] * 9,
-        out_specs=[in_vmem, in_vmem, in_hbm],
+        out_specs=[in_hbm, in_vmem, in_hbm],
         out_shape=[
-            jax.ShapeDtypeStruct((sx, sy, sz), F32),
+            pltpu.HBM((sx, sy, sz), F32),
             jax.ShapeDtypeStruct((sx + 2, height, sz), F32),
             pltpu.HBM((total, sz), F32),
         ],
@@ -517,6 +521,7 @@
             pltpu.VMEM((sx + 2 * rim, height, sz), F32),
             pltpu.VMEM((sx * sy, 2 * sz), BF16),
             pltpu.VMEM((total, sz), F32),
+            pltpu.SemaphoreType.DMA,
             pltpu.SemaphoreType.DMA((GROUPS,)),
         ],
         compiler_params=params(14),
@@ -759,7 +764,7 @@
     xlo, xhi = neighbours(last, first, "gx")
     dest, where, codes = rank(owner_map.reshape(1, rows), slot_map, ndev, cap)
     outgoing, flux = pack(where, codes, temp_fluid, wall_old, wall_mask, cap, (first, last))
-    outgoing, xhi = lax.optimization_barrier((outgoing, xhi))
+    outgoing, xlo, xhi = lax.optimization_barrier((outgoing, xlo, xhi))
     incoming = lax.all_to_all(outgoing, AXES, split_axis=0, concat_axis=0, tiled=True)
 
     left, right, state = y_faces(rim, temp_fluid, temp_solid, material, xlo, xhi)

time: 164 us -> 132 us (0.80)
  starting transfers between devices: 66.5 us -> 34.6 us
    ppermute x10, starting transfers between devices: 51.3 us -> 19.9 us  [neighbours(): return (lax.ppermute(before, axis, up), lax.ppermute(after, axis, down))]
    all_to_all x1, waiting for transfers between devices: 0.01 us -> 4.61 us  [body(): lax.all_to_all(outgoing, AXES, split_axis=0, concat_axis=0, tiled=True)]
    ppermute x10, waiting for transfers between devices: 24.5 us -> 20.6 us  [neighbours(): return (lax.ppermute(before, axis, up), lax.ppermute(after, axis, down))]
  transfers between devices with their start and end apart: 12 -> 12, of which waited for: 6 -> 6; matrix products, arithmetic and copies ran while one was open for 0% -> 0% of each run, Pallas kernels for 22% -> 28%
where the time goes in v14:
time: 132 us; the launch traced here: 131 us
  waiting for transfers between devices  48 us (36%)
  Pallas kernels  46.6 us (35%)
  starting transfers between devices  34.6 us (26%)
    pallas_call x2, Pallas kernels, fluid_step(): pl.pallas_call(functools.partial(fluid_kernel, opening), grid=(steps + 1,...  23.3 us
    all_to_all x1, waiting for transfers between devices, body(): lax.all_to_all(replies.reshape(ndev, cap, sz), AXES, split_axis=0, concat...  22.8 us
    ppermute x10, waiting for transfers between devices, neighbours(): return (lax.ppermute(before, axis, up), lax.ppermute(after, axis, down))  20.6 us
    ppermute x10, starting transfers between devices, neighbours(): return (lax.ppermute(before, axis, up), lax.ppermute(after, axis, down))  19.9 us
    all_to_all x1, starting transfers between devices, body(): lax.all_to_all(outgoing, AXES, split_axis=0, concat_axis=0, tiled=True)  9.06 us
    all_to_all x1, starting transfers between devices, body(): lax.all_to_all(replies.reshape(ndev, cap, sz), AXES, split_axis=0, concat...  5.63 us
    all_to_all x1, waiting for transfers between devices, body(): lax.all_to_all(outgoing, AXES, split_axis=0, concat_axis=0, tiled=True)  4.61 us
    pallas_call x1, Pallas kernels, pack(): pl.pallas_call(functools.partial(pack_kernel, cap), grid=(1,), in_specs=[...  4.41 us
  transfers between devices with their start and end apart: 12, of which 6 were waited for; matrix products, arithmetic and copies ran while one was open for 0% of the time, Pallas kernels for 28%

profile of v14, /device:TPU:0, one launch (start us, length us, event | category | flops | bytes accessed | tf_op | source)
XLA Modules:
  0.0 130.9 jit_solution(17122947546230950489)
XLA Ops:
  0.6 0.0 copy-start.3
  0.6 0.0 copy-start.2
  0.7 1.3 x_faces.1
  1.9 1.3 collective-permute-start.1
  3.2 3.1 %collective-permute-start = (f32[104,1024]{1,0:T(8,128)S(1)}, f32[104,1024]{1,0:T(8,128)S(1)}, u32[]{:S(2)}, u32[]{:S(2)}) collective-permute-start(f32[104,1024]{1,0:T(8,128)S(1)} %get-tuple-element.46.refs_1_), channel_id=1, source_target_pairs={{0,4},{4,8},{8,12},{12,16},{16,20},{20,24},{24,28},{1,5},{5,9},{9,... | collective-permute-start | bytes 1277960 | tf_op jit(solution)/shard_map/ppermute | solution.py:48
  6.3 0.0 copy-done.3
  6.3 0.0 copy-done.2
  6.3 0.9 rank.1
  7.2 4.4 %pack.1 = (f32[32,104,128]{2,1,0:T(8,128)}, f32[16,64,128]{2,1,0:T(8,128)S(1)}) custom-call(s32[1,1024]{1,0:T(1,128)S(1)} %get-tuple-element.43.where_ref, f32[32,128]{1,0:T(8,128)S(1)} %get-tuple-element.44.code_ref, f32[16,64,1024]{2,1,0:T(8,128)} %far_ref.1, f32[16,64,128]{2,1,0:T(8,128)} %old_ref.1, s32[16,64,128]{2,1,0:T(8,128)} %mask_ref.1, ...), custom_call_target="tpu_custom_call" | custom-call | flops 1744830464 | bytes 2621440 | tf_op jit(solution)/shard_map/pack/pallas_call | solution.py:151
  11.6 0.0 collective-permute-done.1.xhi_ref.hi_ref
  11.6 0.0 collective-permute-done.xlo_ref.lo_ref
  11.6 9.1 %all-to-all-start = ((f32[32,104,128]{2,1,0:T(8,128)}), f32[32,104,128]{2,1,0:T(8,128)}, u32[]{:S(2)}, u32[]{:S(2)}) async-start(f32[32,104,128]{2,1,0:T(8,128)} %get-tuple-element.54), calls=%async_computation | async-start | bytes 3407872 | tf_op jit(solution)/shard_map/all_to_all | solution.py:768
  20.7 11.7 %fluid_step.2 = (f32[16,64,1024]{2,1,0:T(8,128)}, f32[64,1024]{1,0:T(8,128)S(1)}, f32[64,1024]{1,0:T(8,128)S(1)}, f32[16,1024]{1,0:T(8,128)S(1)}, f32[16,1024]{1...) custom-call(f32[16,64,1024]{2,1,0:T(8,128)} %far_ref.1, ...), custom_call_target="tpu_custom_call" | custom-call | flops 41943040 | bytes 14680064 | tf_op jit(solution)/shard_map/fluid_step/pallas_call | solution.py:731
  32.5 2.1 %collective-permute-start.2 = (f32[64,1024]{1,0:T(8,128)S(1)}, f32[64,1024]{1,0:T(8,128)S(1)}, u32[]{:S(2)}, u32[]{:S(2)}) collective-permute-start(f32[64,1024]{1,0:T(8,128)S(1)} %get-tuple-element.52), channel_id=1, source_target_pairs={{0,4},{4,8},{8,12},{12,16},{16,20},{20,24},{24,28},{1,5},{5,9},{9,... | collective-permute-start | bytes 786440 | tf_op jit(solution)/shard_map/ppermute | solution.py:48
  34.6 1.3 collective-permute-start.3
  35.9 2.7 %y_faces.1 = (f32[56,1024]{1,0:T(8,128)S(1)}, f32[56,1024]{1,0:T(8,128)S(1)}, f32[2,32,48,128]{3,2,1,0:T(8,128)}) custom-call(f32[16,64,1024]{2,1,0:T(8,128)} %far_ref.1, f32[16,64,1024]{2,1,0:T(8,128)} %far_ref.1, f32[16,32,128]{2,1,0:T(8,128)} %temp_ref.5, s32[16,32,128]{2,1,0:T(8,128)} %kind_ref.3, f32[104,1024]{1,0:T(8,128)S(1)} %collective-permute-done.xlo_ref.lo_ref, ...), custom_call_target="tpu_custom_call" | custom-call | flops 1000 | bytes 917504 | tf_op jit(solution)/shard_map/y_faces/pallas_call | solution.py:335
  38.6 3.6 %collective-permute-start.4 = (f32[56,1024]{1,0:T(8,128)S(1)}, f32[56,1024]{1,0:T(8,128)S(1)}, u32[]{:S(2)}, u32[]{:S(2)}) collective-permute-start(f32[56,1024]{1,0:T(8,128)S(1)} %get-tuple-element.55), channel_id=1, source_target_pairs={{0,1},{1,2},{2,3},{4,5},{5,6},{6,7},{8,9},{9,10},{10,11},{12,13},{... | collective-permute-start | bytes 688136 | tf_op jit(solution)/shard_map/ppermute | solution.py:48
  42.1 1.3 collective-permute-start.5
  43.4 5.2 %collective-permute-done.4.ylo_ref = f32[56,1024]{1,0:T(8,128)S(1)} collective-permute-done((f32[56,1024]{1,0:T(8,128)S(1)}, f32[56,1024]{1,0:T(8,128)S(1)}, u32[]{:S(2)}, u32[]{:S(2)}) %collective-permute-start.4) | collective-permute-done | bytes 229408 | tf_op jit(solution)/shard_map/ppermute | solution.py:48
  48.7 7.7 %collective-permute-done.5.yhi_ref = f32[56,1024]{1,0:T(8,128)S(1)} collective-permute-done((f32[56,1024]{1,0:T(8,128)S(1)}, f32[56,1024]{1,0:T(8,128)S(1)}, u32[]{:S(2)}, u32[]{:S(2)}) %collective-permute-start.5) | collective-permute-done | bytes 229408 | tf_op jit(solution)/shard_map/ppermute | solution.py:48
  56.4 0.0 collective-permute-done.2.xfirst_ref.xlo_ref
  56.4 0.0 collective-permute-done.3.xlast_ref.xhi_ref
  56.4 0.0 copy-start
  56.4 4.6 %all-to-all-done.rows_ref = f32[32,104,128]{2,1,0:T(8,128)} async-done(((f32[32,104,128]{2,1,0:T(8,128)}), f32[32,104,128]{2,1,0:T(8,128)}, u32[]{:S(2)}, u32[]{:S(2)}) %all-to-all-start) | async-done | bytes 1703968 | tf_op jit(solution)/shard_map/all_to_all | solution.py:768
  61.0 3.6 %heat_sum.1 = (f32[16,32,128]{2,1,0:T(8,128)S(1)}, f32[144,128]{1,0:T(8,128)S(1)}, f32[144,128]{1,0:T(8,128)S(1)}, f32[16,1024]{1,0:T(8,128)S(1)}, f32[16,1024]{1,0:T(8,128)S(1)}, /*index=5*/s32[32,128]{1,0:T(8,128)S(1)}) custom-call(f32[32,104,128]{2,1,0:T(8,128)} %all-to-all-done.rows_ref, f32[64,1024]{1,0:T(8,128)S(1)} %collective-permute-done.2.xfirst_ref.xlo_ref, ...), custom_call_target="tpu_custom_call" | custom-call | flops 872415232 | bytes 1703936 | tf_op jit(solution)/shard_map/heat_sum/pallas_call | solution.py:218
  64.5 1.5 %collective-permute-start.6 = (f32[144,128]{1,0:T(8,128)S(1)}, f32[144,128]{1,0:T(8,128)S(1)}, u32[]{:S(2)}, u32[]{:S(2)}) collective-permute-start(f32[144,128]{1,0:T(8,128)S(1)} %get-tuple-element.61), channel_id=1, source_target_pairs={{0,4},{4,8},{8,12},{12,16},{16,20},{20,24},{24,28},{1,5},{5,9},{9,... | collective-permute-start | bytes 221192 | tf_op jit(solution)/shard_map/ppermute | solution.py:48
  66.1 1.3 collective-permute-start.7
  67.4 0.0 collective-permute-done.6.lo_ref.hxlo_ref.refs_0_
  67.4 3.6 %collective-permute-done.7.hi_ref.hxhi_ref.refs_1_ = f32[144,128]{1,0:T(8,128)S(1)} collective-permute-done((f32[144,128]{1,0:T(8,128)S(1)}, f32[144,128]{1,0:T(8,128)S(1)}, u32[]{:S(2)}, u32[]{:S(2)}) %collective-permute-start.7) | collective-permute-done | bytes 73760 | tf_op jit(solution)/shard_map/ppermute | solution.py:48
  71.0 0.1 strips.1
  71.1 3.1 %collective-permute-start.8 = (f32[32,1024]{1,0:T(8,128)S(1)}, f32[32,1024]{1,0:T(8,128)S(1)}, u32[]{:S(2)}, u32[]{:S(2)}) collective-permute-start(f32[32,1024]{1,0:T(8,128)S(1)} %get-tuple-element.66), channel_id=1, source_target_pairs={{0,1},{1,2},{2,3},{4,5},{5,6},{6,7},{8,9},{9,10},{10,11},{12,13},{... | collective-permute-start | bytes 393224 | tf_op jit(solution)/shard_map/ppermute | solution.py:48
  74.2 1.3 collective-permute-start.9
  75.5 2.8 %ready.1 = (f32[32,48,128]{2,1,0:T(8,128)S(1)}, f32[32,48,128]{2,1,0:T(8,128)S(1)}, f32[18,48,128]{2,1,0:T(8,128)S(1)}, bf16[3072,512]{1,0:T(8,128)(2,1)S(1)}) custom-call(f32[2,32,48,128]{3,2,1,0:T(8,128)} %get-tuple-element.68.state_ref, f32[56,1024]{1,0:T(8,128)S(1)} %collective-permute-done.4.ylo_ref, f32[56,1024]{1,0:T(8,128)S(1)} %collective-permute-done.5.yhi_ref, ...), custom_call_target="tpu_custom_call" | custom-call | flops 6291456 | bytes 6291456 | tf_op jit(solution)/shard_map/ready/pallas_call | solution.py:432
  78.4 0.0 collective-permute-done.8.hylo_ref.refs_4_
  78.4 4.0 %collective-permute-done.9.hyhi_ref.refs_5_ = f32[32,1024]{1,0:T(8,128)S(1)} collective-permute-done((f32[32,1024]{1,0:T(8,128)S(1)}, f32[32,1024]{1,0:T(8,128)S(1)}, u32[]{:S(2)}, u32[]{:S(2)}) %collective-permute-start.9) | collective-permute-done | bytes 131104 | tf_op jit(solution)/shard_map/ppermute | solution.py:48
  82.4 3.0 %solid_steps.1 = (f32[16,32,128]{2,1,0:T(8,128)}, f32[18,48,128]{2,1,0:T(8,128)S(1)}, f32[3072,128]{1,0:T(8,128)}) custom-call(f32[32,48,128]{2,1,0:T(8,128)S(1)} %get-tuple-element.70.start_ref, f32[32,48,128]{2,1,0:T(8,128)S(1)} %get-tuple-element.71.cond_ref, f32[18,48,128]{2,1,0:T(8,128)S(1)} %get-tuple-element.72.modulus_ref, ...), custom_call_target="tpu_custom_call" | custom-call | flops 805306368 | bytes 1572864 | tf_op jit(solution)/shard_map/solid_steps/pallas_call | solution.py:510
  85.4 0.0 copy-done
  85.5 5.6 %all-to-all-start.1 = ((f32[32,96,128]{2,1,0:T(8,128)}), f32[32,96,128]{2,1,0:T(8,128)S(1)}, u32[]{:S(2)}, u32[]{:S(2)}) async-start(f32[32,96,128]{2,1,0:T(8,128)} %bitcast.6), calls=%async_computation.1 | async-start | bytes 3145728 | tf_op jit(solution)/shard_map/all_to_all | solution.py:786
  91.1 2.1 %stress.1 = (f32[3,16,32,128]{3,2,1,0:T(8,128)}, f32[8,128]{1,0:T(8,128)S(1)}) custom-call(f32[18,48,128]{2,1,0:T(8,128)S(1)} %get-tuple-element.74.sigma_ref), custom_call_target="tpu_custom_call" | custom-call | flops 655360 | bytes 1048576 | tf_op jit(solution)/shard_map/stress/pallas_call | solution.py:556
  93.2 0.0 copy-start.1
  93.2 0.9 copy-done.1
  94.2 11.6 %fluid_step.3 = (f32[16,64,1024]{2,1,0:T(8,128)}, f32[8,128]{1,0:T(8,128)S(1)}) custom-call(f32[16,64,1024]{2,1,0:T(8,128)} %get-tuple-element.51.here_ref, f32[64,1024]{1,0:T(8,128)S(1)} %collective-permute-done.2.xfirst_ref.xlo_ref, f32[64,1024]{1,0:T(8,128)S(1)} %copy-done.1, bf16[3,16,64,1024]{3,2,1,0:T(8,128)(2,1)} %speed_ref.3, ...), custom_call_target="tpu_custom_call" | custom-call | flops 41943040 | bytes 14680064 | tf_op jit(solution)/shard_map/fluid_step/pallas_call | solution.py:731
  105.8 22.8 %all-to-all-done.1 = f32[32,96,128]{2,1,0:T(8,128)S(1)} async-done(((f32[32,96,128]{2,1,0:T(8,128)}), f32[32,96,128]{2,1,0:T(8,128)S(1)}, u32[]{:S(2)}, u32[]{:S(2)}) %all-to-all-start.1) | async-done | bytes 1572896 | tf_op jit(solution)/shard_map/all_to_all | solution.py:786
  128.6 2.4 %unpack.1 = f32[1024,128]{1,0:T(8,128)} custom-call(s32[1,1024]{1,0:T(1,128)S(1)} %get-tuple-element.77.dest_ref, f32[3072,128]{1,0:T(8,128)S(1)} %bitcast.4, f32[8,128]{1,0:T(8,128)S(1)} %get-tuple-element.79.refs_0_), custom_call_target="tpu_custom_call" | custom-call | flops 131072 | bytes 1048576 | tf_op jit(solution)/shard_map/unpack/pallas_call | solution.py:585
Async XLA Ops:
  0.6 5.6 %copy-start.3 = (s32[1,1024]{1,0:T(1,128)S(1)}, s32[1,1024]{1,0:T(1,128)}, u32[]{:S(2)}) copy-start(s32[1,1024]{1,0:T(1,128)} %slot_ref.1) | copy-start | bytes 12292
  0.6 5.6 %copy-start.2 = (s32[1,1024,1]{1,2,0:T(1,128)S(1)}, s32[1,1024,1]{1,2,0:T(1,128)}, u32[]{:S(2)}) copy-start(s32[1,1024,1]{1,2,0:T(1,128)} %param.12) | copy-start | bytes 12292
  1.9 9.7 %collective-permute-start.1 = (f32[104,1024]{1,0:T(8,128)S(1)}, f32[104,1024]{1,0:T(8,128)S(1)}, u32[]{:S(2)}, u32[]{:S(2)}) collective-permute-start(f32[104,1024]{1,0:T(8,128)S(1)} %get-tuple-element.45.refs_0_), channel_id=1, source_target_pairs={{4,0},{8,4},{12,8},{16,12},{20,16},{24,20},{28,24},{5,1},{9,5},{13... | collective-permute-start | bytes 1277960 | tf_op jit(solution)/shard_map/ppermute | solution.py:48
  3.2 8.4 %collective-permute-start = (f32[104,1024]{1,0:T(8,128)S(1)}, f32[104,1024]{1,0:T(8,128)S(1)}, u32[]{:S(2)}, u32[]{:S(2)}) collective-permute-start(f32[104,1024]{1,0:T(8,128)S(1)} %get-tuple-element.46.refs_1_), channel_id=1, source_target_pairs={{0,4},{4,8},{8,12},{12,16},{16,20},{20,24},{24,28},{1,5},{5,9},{9,... | collective-permute-start | bytes 1277960 | tf_op jit(solution)/shard_map/ppermute | solution.py:48
  11.6 49.3 %all-to-all-start = ((f32[32,104,128]{2,1,0:T(8,128)}), f32[32,104,128]{2,1,0:T(8,128)}, u32[]{:S(2)}, u32[]{:S(2)}) async-start(f32[32,104,128]{2,1,0:T(8,128)} %get-tuple-element.54), calls=%async_computation | async-start | bytes 3407872 | tf_op jit(solution)/shard_map/all_to_all | solution.py:768
  32.5 23.9 %collective-permute-start.2 = (f32[64,1024]{1,0:T(8,128)S(1)}, f32[64,1024]{1,0:T(8,128)S(1)}, u32[]{:S(2)}, u32[]{:S(2)}) collective-permute-start(f32[64,1024]{1,0:T(8,128)S(1)} %get-tuple-element.52), channel_id=1, source_target_pairs={{0,4},{4,8},{8,12},{12,16},{16,20},{20,24},{24,28},{1,5},{5,9},{9,... | collective-permute-start | bytes 786440 | tf_op jit(solution)/shard_map/ppermute | solution.py:48
  34.6 21.8 %collective-permute-start.3 = (f32[64,1024]{1,0:T(8,128)S(1)}, f32[64,1024]{1,0:T(8,128)S(1)}, u32[]{:S(2)}, u32[]{:S(2)}) collective-permute-start(f32[64,1024]{1,0:T(8,128)S(1)} %get-tuple-element.53), channel_id=1, source_target_pairs={{4,0},{8,4},{12,8},{16,12},{20,16},{24,20},{28,24},{5,1},{9,5},{13... | collective-permute-start | bytes 786440 | tf_op jit(solution)/shard_map/ppermute | solution.py:48
  38.6 10.1 %collective-permute-start.4 = (f32[56,1024]{1,0:T(8,128)S(1)}, f32[56,1024]{1,0:T(8,128)S(1)}, u32[]{:S(2)}, u32[]{:S(2)}) collective-permute-start(f32[56,1024]{1,0:T(8,128)S(1)} %get-tuple-element.55), channel_id=1, source_target_pairs={{0,1},{1,2},{2,3},{4,5},{5,6},{6,7},{8,9},{9,10},{10,11},{12,13},{... | collective-permute-start | bytes 688136 | tf_op jit(solution)/shard_map/ppermute | solution.py:48
  42.1 14.2 %collective-permute-start.5 = (f32[56,1024]{1,0:T(8,128)S(1)}, f32[56,1024]{1,0:T(8,128)S(1)}, u32[]{:S(2)}, u32[]{:S(2)}) collective-permute-start(f32[56,1024]{1,0:T(8,128)S(1)} %get-tuple-element.56), channel_id=1, source_target_pairs={{1,0},{2,1},{3,2},{5,4},{6,5},{7,6},{9,8},{10,9},{11,10},{13,12},{... | collective-permute-start | bytes 688136 | tf_op jit(solution)/shard_map/ppermute | solution.py:48
  56.4 29.1 %copy-start = (f32[64,1024]{1,0:T(8,128)}, f32[64,1024]{1,0:T(8,128)S(1)}, u32[]{:S(2)}) copy-start(f32[64,1024]{1,0:T(8,128)S(1)} %collective-permute-done.3.xlast_ref.xhi_ref) | copy-start | bytes 786436
  64.5 2.9 %collective-permute-start.6 = (f32[144,128]{1,0:T(8,128)S(1)}, f32[144,128]{1,0:T(8,128)S(1)}, u32[]{:S(2)}, u32[]{:S(2)}) collective-permute-start(f32[144,128]{1,0:T(8,128)S(1)} %get-tuple-element.61), channel_id=1, source_target_pairs={{0,4},{4,8},{8,12},{12,16},{16,20},{20,24},{24,28},{1,5},{5,9},{9,... | collective-permute-start | bytes 221192 | tf_op jit(solution)/shard_map/ppermute | solution.py:48
  66.1 4.9 %collective-permute-start.7 = (f32[144,128]{1,0:T(8,128)S(1)}, f32[144,128]{1,0:T(8,128)S(1)}, u32[]{:S(2)}, u32[]{:S(2)}) collective-permute-start(f32[144,128]{1,0:T(8,128)S(1)} %get-tuple-element.62), channel_id=1, source_target_pairs={{4,0},{8,4},{12,8},{16,12},{20,16},{24,20},{28,24},{5,1},{9,5},{13... | collective-permute-start | bytes 221192 | tf_op jit(solution)/shard_map/ppermute | solution.py:48
  71.1 7.3 %collective-permute-start.8 = (f32[32,1024]{1,0:T(8,128)S(1)}, f32[32,1024]{1,0:T(8,128)S(1)}, u32[]{:S(2)}, u32[]{:S(2)}) collective-permute-start(f32[32,1024]{1,0:T(8,128)S(1)} %get-tuple-element.66), channel_id=1, source_target_pairs={{0,1},{1,2},{2,3},{4,5},{5,6},{6,7},{8,9},{9,10},{10,11},{12,13},{... | collective-permute-start | bytes 393224 | tf_op jit(solution)/shard_map/ppermute | solution.py:48
  74.2 8.2 %collective-permute-start.9 = (f32[32,1024]{1,0:T(8,128)S(1)}, f32[32,1024]{1,0:T(8,128)S(1)}, u32[]{:S(2)}, u32[]{:S(2)}) collective-permute-start(f32[32,1024]{1,0:T(8,128)S(1)} %get-tuple-element.67), channel_id=1, source_target_pairs={{1,0},{2,1},{3,2},{5,4},{6,5},{7,6},{9,8},{10,9},{11,10},{13,12},{... | collective-permute-start | bytes 393224 | tf_op jit(solution)/shard_map/ppermute | solution.py:48
  85.5 43.1 %all-to-all-start.1 = ((f32[32,96,128]{2,1,0:T(8,128)}), f32[32,96,128]{2,1,0:T(8,128)S(1)}, u32[]{:S(2)}, u32[]{:S(2)}) async-start(f32[32,96,128]{2,1,0:T(8,128)} %bitcast.6), calls=%async_computation.1 | async-start | bytes 3145728 | tf_op jit(solution)/shard_map/all_to_all | solution.py:786
  93.2 0.9 copy-start.1
